TPU v7x, 512 devices: a whole 4x4x16 slice. The times are simulated.
512 devices in a mesh: axial: 16 (over y, x), cross: 32 (over z, core).
Axes of the slice: x: 4, y: 4, z: 16, core: 2. Of those that a mesh axis runs over, the one named last changes fastest.
Arguments:
- force: float32 [16, 32, 8, 3, 128], P('axial', 'cross'), may hold values from -6 to 6
- self_drag: float32 [16, 32, 8, 128], P('axial', 'cross'), may hold values from 0.5 to 4
- tiles: bfloat16 [16, 32, 8, 8, 128, 128], P('axial', 'cross'), may hold values from -0.1875 to 0.1875
- tile_ids: int32 [16, 32, 8, 8], P('axial', 'cross'), may hold values from 8 to 63, as said below
- mig_rows: int32 [16, 32, 2, 64], P('axial', 'cross'), may hold values from 0 to 1023, as said below
- mig_count: int32 [16, 32, 2], P('axial', 'cross'), may hold values from 0 to 64, as said below
Outputs:
- velocity: float32 [16, 32, 8, 3, 128], P('axial', 'cross')
- residual: float32 [16, 32, 8, 3, 128], P('axial', 'cross')
- arrivals: float32 [16, 32, 3, 128], P('axial', 'cross')
Inputs may be any that keep to these rules, and one draw needn't show every extreme that they name: `tile_ids`: each entry is p * 8 + q with p one of 1, 3, 4, 5, 7 and q below 8; the first five tiles of every block name the five values of p. `mig_rows`: the 128 entries of one device are distinct beads. `mig_count`: the lowest slab sends nothing to the lower side and the highest nothing to the upper side; in every axial group one slab sends 64 beads to both sides.
All inputs are finite; a program needn't handle non-finite values.
Results may differ from a plain program's by a relative error of at most 0.024.
Values may be sent and summed in bfloat16 or wider, within the bound.
No kernel may reach another device: no remote copies, remote signals or barrier semaphores. Data moves between devices by JAX's collectives and lax.ppermute only.
A program may use at most 64 MiB of HBM per device.

v0:
```python
import jax
import jax.numpy as jnp
from jax import lax
from jax.sharding import PartitionSpec as P

ITERS = 3


def padded(cells, sides, width, closed):
    for axis, dim in sides:
        count = lax.axis_size(axis)
        ends = count if closed else count - 1
        head = lax.slice_in_dim(cells, 0, width, axis=dim)
        tail = lax.slice_in_dim(cells, cells.shape[dim] - width, cells.shape[dim], axis=dim)
        cells = jnp.concatenate(
            [
                lax.ppermute(tail, axis, [(i, (i + 1) % count) for i in range(ends)]),
                cells,
                lax.ppermute(head, axis, [((i + 1) % count, i) for i in range(ends)]),
            ],
            axis=dim,
        )
    return cells


def passed_along(shard, axis, by):
    devices = lax.axis_size(axis)
    return lax.ppermute(shard, axis, [(i, (i + by) % devices) for i in range(devices)])


def shifted(shard, axis, by):
    devices = lax.axis_size(axis)
    pairs = [(i, i + by) for i in range(devices) if 0 <= i + by < devices]
    return lax.ppermute(shard, axis, pairs)


def neighbour_blocks(lowered):
    centre = lowered[0, 0]
    blanks = jnp.zeros_like(centre)
    axial_pad = padded(lowered, (("axial", 0),), 1, True)
    cross_pad = padded(lowered, (("cross", 1),), 1, False)
    below_axial = axial_pad[0, 0]
    above_axial = axial_pad[2, 0]
    below_cross = cross_pad[0, 0]
    above_cross = cross_pad[0, 2]
    return jnp.concatenate(
        [
            blanks,
            below_axial,
            blanks,
            below_cross,
            centre,
            above_cross,
            blanks,
            above_axial,
            blanks,
        ],
        axis=0,
    )


def apply_operator(direction, self_drag, tiles, tile_ids):
    blocks = tiles.shape[2]
    count = tiles.shape[3]
    width = tiles.shape[4]
    lowered = direction.astype(jnp.bfloat16)
    extended = neighbour_blocks(lowered)
    indices = tile_ids[0, 0].reshape(-1)
    own_tiles = tiles[0, 0]
    entries = lax.broadcasted_iota(jnp.int32, (blocks * count, 9 * blocks), 1)
    selector = entries == indices[:, None]
    picked = jnp.dot(
        selector.astype(jnp.bfloat16),
        extended.reshape(9 * blocks, 3 * width),
        preferred_element_type=jnp.float32,
    )
    picked = picked.astype(jnp.bfloat16).reshape(blocks, count, 3, width)
    coupled = jnp.einsum("bkij,bkcj->bci", own_tiles, picked, preferred_element_type=jnp.float32)
    coupled_low = coupled.astype(jnp.bfloat16)
    spread = jnp.einsum(
        "bkij,bci->bkcj", own_tiles, coupled_low, preferred_element_type=jnp.float32
    )
    summed = jnp.dot(
        selector.astype(jnp.float32).T,
        spread.reshape(blocks * count, 3 * width),
        precision=lax.Precision.HIGHEST,
        preferred_element_type=jnp.float32,
    )
    returned = summed.reshape(9, blocks, 3, width)
    from_upper_axial = passed_along(returned[1], "axial", -1)
    from_lower_axial = passed_along(returned[7], "axial", 1)
    from_upper_cross = shifted(returned[3], "cross", -1)
    from_lower_cross = shifted(returned[5], "cross", 1)
    total = returned[4] + from_upper_axial + from_lower_axial + from_upper_cross + from_lower_cross
    return self_drag[:, :, :, None, :] * direction + total[None, None]


def residual_squares(residual):
    return lax.psum(jnp.sum(residual * residual), ("axial", "cross"))


def on_device(force, self_drag, tiles, tile_ids, mig_rows, mig_count):
    velocity = jnp.zeros_like(force)
    residual = force
    direction = force
    norm_now = residual_squares(residual)
    for sweep in range(ITERS):
        image = apply_operator(direction, self_drag, tiles, tile_ids)
        alpha = norm_now / lax.psum(jnp.sum(direction * image), ("axial", "cross"))
        velocity = velocity + alpha * direction
        residual = residual - alpha * image
        norm_next = residual_squares(residual)
        direction = residual + norm_next / norm_now * direction
        norm_now = norm_next
    blocks = velocity.shape[2]
    width = velocity.shape[4]
    capacity = mig_rows.shape[3]
    flat = jnp.swapaxes(velocity[0, 0], 0, 1).reshape(3, blocks * width)
    picked = flat[:, mig_rows[0, 0].reshape(-1)].reshape(3, 2, capacity)
    live = lax.broadcasted_iota(jnp.int32, (1, 2, capacity), 2) < mig_count[0, 0][None, :, None]
    outgoing = jnp.where(live, picked, jnp.zeros_like(picked))
    from_lower = shifted(outgoing[:, 1], "cross", 1)
    from_upper = shifted(outgoing[:, 0], "cross", -1)
    arrivals = jnp.concatenate([from_lower, from_upper], axis=1)[None, None]
    return (velocity, residual, arrivals)


def solution(mesh):
    placed = (
        P("axial", "cross", None, None, None),
        P("axial", "cross", None, None),
        P("axial", "cross", None, None, None, None),
        P("axial", "cross", None, None),
        P("axial", "cross", None, None),
        P("axial", "cross", None),
    )
    return jax.shard_map(
        on_device,
        mesh=mesh,
        in_specs=placed,
        out_specs=(
            P("axial", "cross", None, None, None),
            P("axial", "cross", None, None, None),
            P("axial", "cross", None, None),
        ),
        check_vma=False,
    )
```

profile of v0, /device:TPU:1, one launch (start us, length us, event | category | flops | bytes accessed | tf_op | source)
XLA Modules:
  0.0 638.1 jit_solution(17687024224916074137)
XLA Ops:
  0.6 0.0 copy-start
  0.6 0.9 convert_element_type.33
  1.5 3.9 collective-permute-start
  5.5 4.4 collective-permute-start.1
  9.8 3.7 collective-permute-start.2
  13.5 7.0 %collective-permute-start.3 = (bf16[1,1,8,3,128]{4,2,3,1,0:T(8,128)(2,1)S(1)}, bf16[1,1,8,3,128]{4,2,3,1,0:T(8,128)(2,1)S(1)}, u32[]{:S(2)}, u32[]{:S(2)}) collective-permute-start(bf16[1,1,8,3,128]{4,2,3,1,0:T(8,128)(2,1)S(1)} %convert_element_type.33), channel_id=1, source_target_pairs={{32,0},{64,32},{96,64},{128,96},{160,128},{192,160},{224,192},{256... | collective-permute-start | bytes 18440 | tf_op jit(solution)/shard_map/ppermute | solution.py:19
  20.5 0.8 eq.6
  21.3 0.7 constant_dynamic-update-slice_fusion.4
  22.1 0.2 fusion.21
  22.3 0.9 fusion.12
  23.3 0.3 fusion.63
  23.6 1.9 collective-permute-start.7
  25.5 2.4 collective-permute-start.6
  28.0 1.9 collective-permute-start.5
  29.9 6.7 %collective-permute-start.4 = (f32[8,3,128]{2,0,1:T(8,128)S(1)}, f32[8,3,128]{2,0,1:T(8,128)S(1)}, u32[]{:S(2)}, u32[]{:S(2)}) collective-permute-start(f32[8,3,128]{2,0,1:T(8,128)S(1)} %get-tuple-element.26), channel_id=1, source_target_pairs={{0,480},{32,0},{64,32},{96,64},{128,96},{160,128},{192,160},{224,1... | collective-permute-start | bytes 36872 | tf_op jit(solution)/shard_map/ppermute | solution.py:28
  36.6 0.1 reshape_squeeze.3
  36.7 0.7 collective-permute-done.4
  37.4 0.6 multiply_reduce_fusion.4
  38.0 109.2 %all-reduce = (f32[]{:T(128)}, f32[]{:T(128)}) all-reduce(f32[]{:T(128)} %get-tuple-element.4, f32[]{:T(128)} %get-tuple-element.3), channel_id=1, replica_groups=mesh['axial'=16,'cross'=32] {'axial','cross'}, use_global_device_ids=true, to_apply=%region_1.0 | all-reduce | flops 2 | bytes 16 | tf_op jit(solution)/shard_map/psum | solution.py:99
  148.6 0.6 multiply_reduce_fusion.3
  149.2 100.0 %psum.44 = f32[]{:T(128)} all-reduce(f32[]{:T(128)} %multiply_reduce_fusion.3), channel_id=1, replica_groups=mesh['axial'=16,'cross'=32] {'axial','cross'}, use_global_device_ids=true, to_apply=%region_5.0 | all-reduce | flops 1 | bytes 8 | tf_op jit(solution)/shard_map/psum | solution.py:99
  250.5 3.0 collective-permute-start.8
  253.6 2.4 collective-permute-start.9
  256.0 1.9 collective-permute-start.10
  257.9 6.3 collective-permute-start.11
  264.3 0.6 collective-permute-done.11
  265.0 0.2 fusion.22
  265.2 0.9 fusion.15
  266.1 0.3 fusion.60
  266.5 4.5 collective-permute-start.15
  271.0 1.9 collective-permute-start.14
  272.9 1.9 collective-permute-start.13
  274.9 7.2 %collective-permute-start.12 = (f32[8,3,128]{2,0,1:T(8,128)S(1)}, f32[8,3,128]{2,0,1:T(8,128)S(1)}, u32[]{:S(2)}, u32[]{:S(2)}) collective-permute-start(f32[8,3,128]{2,0,1:T(8,128)S(1)} %get-tuple-element.22), channel_id=1, source_target_pairs={{0,480},{32,0},{64,32},{96,64},{128,96},{160,128},{192,160},{224,1... | collective-permute-start | bytes 36872 | tf_op jit(solution)/shard_map/ppermute | solution.py:28
  282.1 0.1 iota_compare_fusion.7
  282.2 0.7 collective-permute-done.12
  282.9 0.6 multiply_reduce_fusion.2
  283.5 104.5 %psum.45 = f32[]{:T(128)} all-reduce(f32[]{:T(128)} %get-tuple-element.13), channel_id=1, replica_groups=mesh['axial'=16,'cross'=32] {'axial','cross'}, use_global_device_ids=true, to_apply=%region_7.0 | all-reduce | flops 1 | bytes 8 | tf_op jit(solution)/shard_map/psum | solution.py:109
  389.4 0.6 multiply_reduce_fusion.1
  390.0 100.0 %psum.46 = f32[]{:T(128)} all-reduce(f32[]{:T(128)} %get-tuple-element.11), channel_id=1, replica_groups=mesh['axial'=16,'cross'=32] {'axial','cross'}, use_global_device_ids=true, to_apply=%region_9.0 | all-reduce | flops 1 | bytes 8 | tf_op jit(solution)/shard_map/psum | solution.py:99
  491.3 3.0 collective-permute-start.16
  494.3 2.5 collective-permute-start.17
  496.8 1.9 collective-permute-start.18
  498.8 6.2 collective-permute-start.19
  505.1 0.6 collective-permute-done.19
  505.8 0.2 fusion.23
  506.0 0.9 fusion.18
  506.9 0.3 fusion.57
  507.3 4.5 collective-permute-start.23
  511.8 1.9 collective-permute-start.22
  513.7 1.9 collective-permute-start.21
  515.6 7.2 %collective-permute-start.20 = (f32[8,3,128]{2,0,1:T(8,128)S(1)}, f32[8,3,128]{2,0,1:T(8,128)S(1)}, u32[]{:S(2)}, u32[]{:S(2)}) collective-permute-start(f32[8,3,128]{2,0,1:T(8,128)S(1)} %get-tuple-element.18), channel_id=1, source_target_pairs={{0,480},{32,0},{64,32},{96,64},{128,96},{160,128},{192,160},{224,1... | collective-permute-start | bytes 36872 | tf_op jit(solution)/shard_map/ppermute | solution.py:28
  522.9 0.8 collective-permute-done.20
  523.7 0.6 multiply_reduce_fusion
  524.3 104.5 %psum.47 = f32[]{:T(128)} all-reduce(f32[]{:T(128)} %get-tuple-element.7), channel_id=1, replica_groups=mesh['axial'=16,'cross'=32] {'axial','cross'}, use_global_device_ids=true, to_apply=%region_11.0 | all-reduce | flops 1 | bytes 8 | tf_op jit(solution)/shard_map/psum | solution.py:109
  630.1 0.0 copy-start.2
  630.2 0.2 copy.11
  630.4 0.7 gather_fusion
  631.0 0.1 copy.12
  631.1 2.6 collective-permute-start.25
  633.7 3.0 collective-permute-start.24
  636.7 0.6 multiply_subtract_fusion
  637.3 0.1 collective-permute-done.24
  637.4 0.1 pad_maximum_fusion
  637.5 0.6 broadcast_in_dim.32
  (66 shorter events, 0.3 us)
Async XLA Ops:
  0.6 21.7 %copy-start = (bf16[1,1,8,8,128,128]{5,4,3,2,1,0:T(8,128)(2,1)S(1)}, bf16[1,1,8,8,128,128]{5,4,3,2,1,0:T(8,128)(2,1)}, u32[]{:S(2)}) copy-start(bf16[1,1,8,8,128,128]{5,4,3,2,1,0:T(8,128)(2,1)} %param.8) | copy-start | bytes 6291460
  1.5 19.8 %collective-permute-start = (bf16[1,1,8,3,128]{4,2,3,1,0:T(8,128)(2,1)S(1)}, bf16[1,1,8,3,128]{4,2,3,1,0:T(8,128)(2,1)S(1)}, u32[]{:S(2)}, u32[]{:S(2)}) collective-permute-start(bf16[1,1,8,3,128]{4,2,3,1,0:T(8,128)(2,1)S(1)} %convert_element_type.33), channel_id=1, source_target_pairs={{0,32},{32,64},{64,96},{96,128},{128,160},{160,192},{192,224},{224... | collective-permute-start | bytes 18440 | tf_op jit(solution)/shard_map/ppermute | solution.py:17
  5.5 15.8 %collective-permute-start.1 = (bf16[1,1,8,3,128]{4,2,3,1,0:T(8,128)(2,1)S(1)}, bf16[1,1,8,3,128]{4,2,3,1,0:T(8,128)(2,1)S(1)}, u32[]{:S(2)}, u32[]{:S(2)}) collective-permute-start(bf16[1,1,8,3,128]{4,2,3,1,0:T(8,128)(2,1)S(1)} %convert_element_type.33), channel_id=1, source_target_pairs={{0,1},{1,2},{2,3},{3,4},{4,5},{5,6},{6,7},{7,8},{8,9},{9,10},{10,1... | collective-permute-start | bytes 18440 | tf_op jit(solution)/shard_map/ppermute | solution.py:17
  9.8 12.2 %collective-permute-start.2 = (bf16[1,1,8,3,128]{4,2,3,1,0:T(8,128)(2,1)S(1)}, bf16[1,1,8,3,128]{4,2,3,1,0:T(8,128)(2,1)S(1)}, u32[]{:S(2)}, u32[]{:S(2)}) collective-permute-start(bf16[1,1,8,3,128]{4,2,3,1,0:T(8,128)(2,1)S(1)} %convert_element_type.33), channel_id=1, source_target_pairs={{1,0},{2,1},{3,2},{4,3},{5,4},{6,5},{7,6},{8,7},{9,8},{10,9},{11,1... | collective-permute-start | bytes 18440 | tf_op jit(solution)/shard_map/ppermute | solution.py:19
  13.5 8.5 %collective-permute-start.3 = (bf16[1,1,8,3,128]{4,2,3,1,0:T(8,128)(2,1)S(1)}, bf16[1,1,8,3,128]{4,2,3,1,0:T(8,128)(2,1)S(1)}, u32[]{:S(2)}, u32[]{:S(2)}) collective-permute-start(bf16[1,1,8,3,128]{4,2,3,1,0:T(8,128)(2,1)S(1)} %convert_element_type.33), channel_id=1, source_target_pairs={{32,0},{64,32},{96,64},{128,96},{160,128},{192,160},{224,192},{256... | collective-permute-start | bytes 18440 | tf_op jit(solution)/shard_map/ppermute | solution.py:19
  22.3 14.3 %copy-start.4 = (s32[1,1,2,64]{3,2,1,0:T(2,128)S(1)}, s32[1,1,2,64]{3,2,1,0:T(2,128)}, u32[]{:S(2)}) copy-start(s32[1,1,2,64]{3,2,1,0:T(2,128)} %param.10) | copy-start | bytes 1540
  22.3 15.1 %copy-start.1 = (f32[1,1,8,3,128]{4,2,3,1,0:T(8,128)S(1)}, f32[1,1,8,3,128]{4,2,3,1,0:T(8,128)}, u32[]{:S(2)}) copy-start(f32[1,1,8,3,128]{4,2,3,1,0:T(8,128)} %param.6) | copy-start | bytes 36868
  22.3 15.1 %copy-start.3 = (f32[1,1,8,128]{3,2,1,0:T(8,128)S(1)}, f32[1,1,8,128]{3,2,1,0:T(8,128)}, u32[]{:S(2)}) copy-start(f32[1,1,8,128]{3,2,1,0:T(8,128)} %param.7) | copy-start | bytes 12292
  23.6 13.1 %collective-permute-start.7 = (f32[8,3,128]{2,0,1:T(8,128)S(1)}, f32[8,3,128]{2,0,1:T(8,128)S(1)}, u32[]{:S(2)}, u32[]{:S(2)}) collective-permute-start(f32[8,3,128]{2,0,1:T(8,128)S(1)} %get-tuple-element.27), channel_id=1, source_target_pairs={{0,1},{1,2},{2,3},{3,4},{4,5},{5,6},{6,7},{7,8},{8,9},{9,10},{10,1... | collective-permute-start | bytes 36872 | tf_op jit(solution)/shard_map/ppermute | solution.py:34
  25.5 11.1 %collective-permute-start.6 = (f32[8,3,128]{2,0,1:T(8,128)S(1)}, f32[8,3,128]{2,0,1:T(8,128)S(1)}, u32[]{:S(2)}, u32[]{:S(2)}) collective-permute-start(f32[8,3,128]{2,0,1:T(8,128)S(1)} %get-tuple-element.28), channel_id=1, source_target_pairs={{1,0},{2,1},{3,2},{4,3},{5,4},{6,5},{7,6},{8,7},{9,8},{10,9},{11,1... | collective-permute-start | bytes 36872 | tf_op jit(solution)/shard_map/ppermute | solution.py:34
  28.0 8.7 %collective-permute-start.5 = (f32[8,3,128]{2,0,1:T(8,128)S(1)}, f32[8,3,128]{2,0,1:T(8,128)S(1)}, u32[]{:S(2)}, u32[]{:S(2)}) collective-permute-start(f32[8,3,128]{2,0,1:T(8,128)S(1)} %get-tuple-element.29), channel_id=1, source_target_pairs={{0,32},{32,64},{64,96},{96,128},{128,160},{160,192},{192,224},{224... | collective-permute-start | bytes 36872 | tf_op jit(solution)/shard_map/ppermute | solution.py:28
  29.9 7.5 %collective-permute-start.4 = (f32[8,3,128]{2,0,1:T(8,128)S(1)}, f32[8,3,128]{2,0,1:T(8,128)S(1)}, u32[]{:S(2)}, u32[]{:S(2)}) collective-permute-start(f32[8,3,128]{2,0,1:T(8,128)S(1)} %get-tuple-element.26), channel_id=1, source_target_pairs={{0,480},{32,0},{64,32},{96,64},{128,96},{160,128},{192,160},{224,1... | collective-permute-start | bytes 36872 | tf_op jit(solution)/shard_map/ppermute | solution.py:28
  250.5 13.7 %collective-permute-start.8 = (bf16[1,1,8,3,128]{4,2,3,1,0:T(8,128)(2,1)S(1)}, bf16[1,1,8,3,128]{4,2,3,1,0:T(8,128)(2,1)S(1)}, u32[]{:S(2)}, u32[]{:S(2)}) collective-permute-start(bf16[1,1,8,3,128]{4,2,3,1,0:T(8,128)(2,1)S(1)} %get-tuple-element.15), channel_id=1, source_target_pairs={{0,32},{32,64},{64,96},{96,128},{128,160},{160,192},{192,224},{224... | collective-permute-start | bytes 18440 | tf_op jit(solution)/shard_map/ppermute | solution.py:17
  253.6 10.7 %collective-permute-start.9 = (bf16[1,1,8,3,128]{4,2,3,1,0:T(8,128)(2,1)S(1)}, bf16[1,1,8,3,128]{4,2,3,1,0:T(8,128)(2,1)S(1)}, u32[]{:S(2)}, u32[]{:S(2)}) collective-permute-start(bf16[1,1,8,3,128]{4,2,3,1,0:T(8,128)(2,1)S(1)} %get-tuple-element.15), channel_id=1, source_target_pairs={{0,1},{1,2},{2,3},{3,4},{4,5},{5,6},{6,7},{7,8},{8,9},{9,10},{10,1... | collective-permute-start | bytes 18440 | tf_op jit(solution)/shard_map/ppermute | solution.py:17
  256.0 8.3 %collective-permute-start.10 = (bf16[1,1,8,3,128]{4,2,3,1,0:T(8,128)(2,1)S(1)}, bf16[1,1,8,3,128]{4,2,3,1,0:T(8,128)(2,1)S(1)}, u32[]{:S(2)}, u32[]{:S(2)}) collective-permute-start(bf16[1,1,8,3,128]{4,2,3,1,0:T(8,128)(2,1)S(1)} %get-tuple-element.15), channel_id=1, source_target_pairs={{1,0},{2,1},{3,2},{4,3},{5,4},{6,5},{7,6},{8,7},{9,8},{10,9},{11,1... | collective-permute-start | bytes 18440 | tf_op jit(solution)/shard_map/ppermute | solution.py:19
  257.9 7.1 %collective-permute-start.11 = (bf16[1,1,8,3,128]{4,2,3,1,0:T(8,128)(2,1)S(1)}, bf16[1,1,8,3,128]{4,2,3,1,0:T(8,128)(2,1)S(1)}, u32[]{:S(2)}, u32[]{:S(2)}) collective-permute-start(bf16[1,1,8,3,128]{4,2,3,1,0:T(8,128)(2,1)S(1)} %get-tuple-element.15), channel_id=1, source_target_pairs={{32,0},{64,32},{96,64},{128,96},{160,128},{192,160},{224,192},{256... | collective-permute-start | bytes 18440 | tf_op jit(solution)/shard_map/ppermute | solution.py:19
  265.2 16.9 %copy-start.5 = (s32[1,1,2]{2,1,0:T(1,128)S(1)}, s32[1,1,2]{2,1,0:T(1,128)}, u32[]{:S(2)}) copy-start(s32[1,1,2]{2,1,0:T(1,128)} %param.11) | copy-start | bytes 28
  266.5 15.7 %collective-permute-start.15 = (f32[8,3,128]{2,0,1:T(8,128)S(1)}, f32[8,3,128]{2,0,1:T(8,128)S(1)}, u32[]{:S(2)}, u32[]{:S(2)}) collective-permute-start(f32[8,3,128]{2,0,1:T(8,128)S(1)} %get-tuple-element.23), channel_id=1, source_target_pairs={{0,1},{1,2},{2,3},{3,4},{4,5},{5,6},{6,7},{7,8},{8,9},{9,10},{10,1... | collective-permute-start | bytes 36872 | tf_op jit(solution)/shard_map/ppermute | solution.py:34
  271.0 11.2 %collective-permute-start.14 = (f32[8,3,128]{2,0,1:T(8,128)S(1)}, f32[8,3,128]{2,0,1:T(8,128)S(1)}, u32[]{:S(2)}, u32[]{:S(2)}) collective-permute-start(f32[8,3,128]{2,0,1:T(8,128)S(1)} %get-tuple-element.24), channel_id=1, source_target_pairs={{1,0},{2,1},{3,2},{4,3},{5,4},{6,5},{7,6},{8,7},{9,8},{10,9},{11,1... | collective-permute-start | bytes 36872 | tf_op jit(solution)/shard_map/ppermute | solution.py:34
  272.9 9.3 %collective-permute-start.13 = (f32[8,3,128]{2,0,1:T(8,128)S(1)}, f32[8,3,128]{2,0,1:T(8,128)S(1)}, u32[]{:S(2)}, u32[]{:S(2)}) collective-permute-start(f32[8,3,128]{2,0,1:T(8,128)S(1)} %get-tuple-element.25), channel_id=1, source_target_pairs={{0,32},{32,64},{64,96},{96,128},{128,160},{160,192},{192,224},{224... | collective-permute-start | bytes 36872 | tf_op jit(solution)/shard_map/ppermute | solution.py:28
  274.9 8.1 %collective-permute-start.12 = (f32[8,3,128]{2,0,1:T(8,128)S(1)}, f32[8,3,128]{2,0,1:T(8,128)S(1)}, u32[]{:S(2)}, u32[]{:S(2)}) collective-permute-start(f32[8,3,128]{2,0,1:T(8,128)S(1)} %get-tuple-element.22), channel_id=1, source_target_pairs={{0,480},{32,0},{64,32},{96,64},{128,96},{160,128},{192,160},{224,1... | collective-permute-start | bytes 36872 | tf_op jit(solution)/shard_map/ppermute | solution.py:28
  491.3 13.7 %collective-permute-start.16 = (bf16[1,1,8,3,128]{4,2,3,1,0:T(8,128)(2,1)S(1)}, bf16[1,1,8,3,128]{4,2,3,1,0:T(8,128)(2,1)S(1)}, u32[]{:S(2)}, u32[]{:S(2)}) collective-permute-start(bf16[1,1,8,3,128]{4,2,3,1,0:T(8,128)(2,1)S(1)} %get-tuple-element.9), channel_id=1, source_target_pairs={{0,32},{32,64},{64,96},{96,128},{128,160},{160,192},{192,224},{224... | collective-permute-start | bytes 18440 | tf_op jit(solution)/shard_map/ppermute | solution.py:17
  494.3 10.7 %collective-permute-start.17 = (bf16[1,1,8,3,128]{4,2,3,1,0:T(8,128)(2,1)S(1)}, bf16[1,1,8,3,128]{4,2,3,1,0:T(8,128)(2,1)S(1)}, u32[]{:S(2)}, u32[]{:S(2)}) collective-permute-start(bf16[1,1,8,3,128]{4,2,3,1,0:T(8,128)(2,1)S(1)} %get-tuple-element.9), channel_id=1, source_target_pairs={{0,1},{1,2},{2,3},{3,4},{4,5},{5,6},{6,7},{7,8},{8,9},{9,10},{10,1... | collective-permute-start | bytes 18440 | tf_op jit(solution)/shard_map/ppermute | solution.py:17
  496.8 8.3 %collective-permute-start.18 = (bf16[1,1,8,3,128]{4,2,3,1,0:T(8,128)(2,1)S(1)}, bf16[1,1,8,3,128]{4,2,3,1,0:T(8,128)(2,1)S(1)}, u32[]{:S(2)}, u32[]{:S(2)}) collective-permute-start(bf16[1,1,8,3,128]{4,2,3,1,0:T(8,128)(2,1)S(1)} %get-tuple-element.9), channel_id=1, source_target_pairs={{1,0},{2,1},{3,2},{4,3},{5,4},{6,5},{7,6},{8,7},{9,8},{10,9},{11,1... | collective-permute-start | bytes 18440 | tf_op jit(solution)/shard_map/ppermute | solution.py:19
  498.8 7.0 %collective-permute-start.19 = (bf16[1,1,8,3,128]{4,2,3,1,0:T(8,128)(2,1)S(1)}, bf16[1,1,8,3,128]{4,2,3,1,0:T(8,128)(2,1)S(1)}, u32[]{:S(2)}, u32[]{:S(2)}) collective-permute-start(bf16[1,1,8,3,128]{4,2,3,1,0:T(8,128)(2,1)S(1)} %get-tuple-element.9), channel_id=1, source_target_pairs={{32,0},{64,32},{96,64},{128,96},{160,128},{192,160},{224,192},{256... | collective-permute-start | bytes 18440 | tf_op jit(solution)/shard_map/ppermute | solution.py:19
  507.3 15.6 %collective-permute-start.23 = (f32[8,3,128]{2,0,1:T(8,128)S(1)}, f32[8,3,128]{2,0,1:T(8,128)S(1)}, u32[]{:S(2)}, u32[]{:S(2)}) collective-permute-start(f32[8,3,128]{2,0,1:T(8,128)S(1)} %get-tuple-element.19), channel_id=1, source_target_pairs={{0,1},{1,2},{2,3},{3,4},{4,5},{5,6},{6,7},{7,8},{8,9},{9,10},{10,1... | collective-permute-start | bytes 36872 | tf_op jit(solution)/shard_map/ppermute | solution.py:34
  511.8 11.1 %collective-permute-start.22 = (f32[8,3,128]{2,0,1:T(8,128)S(1)}, f32[8,3,128]{2,0,1:T(8,128)S(1)}, u32[]{:S(2)}, u32[]{:S(2)}) collective-permute-start(f32[8,3,128]{2,0,1:T(8,128)S(1)} %get-tuple-element.20), channel_id=1, source_target_pairs={{1,0},{2,1},{3,2},{4,3},{5,4},{6,5},{7,6},{8,7},{9,8},{10,9},{11,1... | collective-permute-start | bytes 36872 | tf_op jit(solution)/shard_map/ppermute | solution.py:34
  513.7 9.2 %collective-permute-start.21 = (f32[8,3,128]{2,0,1:T(8,128)S(1)}, f32[8,3,128]{2,0,1:T(8,128)S(1)}, u32[]{:S(2)}, u32[]{:S(2)}) collective-permute-start(f32[8,3,128]{2,0,1:T(8,128)S(1)} %get-tuple-element.21), channel_id=1, source_target_pairs={{0,32},{32,64},{64,96},{96,128},{128,160},{160,192},{192,224},{224... | collective-permute-start | bytes 36872 | tf_op jit(solution)/shard_map/ppermute | solution.py:28
  515.6 8.1 %collective-permute-start.20 = (f32[8,3,128]{2,0,1:T(8,128)S(1)}, f32[8,3,128]{2,0,1:T(8,128)S(1)}, u32[]{:S(2)}, u32[]{:S(2)}) collective-permute-start(f32[8,3,128]{2,0,1:T(8,128)S(1)} %get-tuple-element.18), channel_id=1, source_target_pairs={{0,480},{32,0},{64,32},{96,64},{128,96},{160,128},{192,160},{224,1... | collective-permute-start | bytes 36872 | tf_op jit(solution)/shard_map/ppermute | solution.py:28
  630.1 7.9 %copy-start.2 = (f32[1,1,8,3,128]{4,2,3,1,0:T(8,128)}, f32[1,1,8,3,128]{4,2,3,1,0:T(8,128)S(1)}, u32[]{:S(2)}) copy-start(f32[1,1,8,3,128]{4,2,3,1,0:T(8,128)S(1)} %multiply_add_fusion) | copy-start | bytes 36868
  631.1 6.2 collective-permute-start.25
  633.7 3.7 collective-permute-start.24
where the time goes:
time: 640 us; the launch traced here: 638 us
  blocking collectives  518 us (81%)
  starting transfers between devices  95.9 us (15%)
  between operations  7.9 us (1%)
    psum x3, blocking collectives, residual_squares(): return lax.psum(jnp.sum(residual * residual), ('axial', 'cross'))  309 us
    psum x2, blocking collectives, on_device(): alpha = norm_now / lax.psum(jnp.sum(direction * image), ('axial', 'cross'))  209 us
    ppermute x6, starting transfers between devices, padded(): lax.ppermute(head, axis, [((i + 1) % count, i) for i in range(ends)])  27 us
    ppermute x6, starting transfers between devices, passed_along(): lax.ppermute(shard, axis, [(i, (i + by) % devices) for i in range(devices)])  26.9 us
    ppermute x8, starting transfers between devices, shifted(): return lax.ppermute(shard, axis, pairs)  22.7 us
    ppermute x6, starting transfers between devices, padded(): lax.ppermute(tail, axis, [(i, (i + 1) % count) for i in range(ends)])  19.3 us
  transfers between devices with their start and end apart: 26, of which 6 were waited for; matrix products, arithmetic and copies ran while one was open for 0% of the time, Pallas kernels for 0%

commit v1 on v0

v1 whole, which is shorter than its diff:
```python
import jax
import jax.numpy as jnp
from jax import lax
from jax.experimental import pallas as pl
from jax.experimental.pallas import tpu as pltpu
from jax.sharding import PartitionSpec as P

ITERS = 3
PLACES = (1, 3, 4, 5, 7)
SUB = 8
LOW = 4


def ring(count, by):
    return [(i, (i + by) % count) for i in range(count)]


def ring_shift(shard, axis, by):
    return lax.ppermute(shard, axis, ring(lax.axis_size(axis), by))


def high_low(x):
    high = x.astype(jnp.bfloat16).astype(jnp.float32)
    return high, x - high


def operator_kernel(
    ids, own, from_axial_dn, from_cross_dn, from_cross_up, from_axial_up, tiles, drag,
    to_axial_dn, to_cross_dn, to_cross_up, to_axial_up, kept, moments, ext, acc,
):
    blocks, count = ids.shape
    width = tiles.shape[-1]
    slab = lax.axis_index("cross")
    has_dn = jnp.where(slab > 0, 1.0, 0.0).astype(jnp.float32)
    has_up = jnp.where(slab < lax.axis_size("cross") - 1, 1.0, 0.0).astype(jnp.float32)
    sources = (from_axial_dn, from_cross_dn, own, from_cross_up, from_axial_up)
    blank = jnp.zeros((blocks, width), jnp.float32)
    for place, source in zip(PLACES, sources):
        base = place * blocks * SUB
        for comp in range(3):
            x = source[comp]
            if place == 3:
                x = x * has_dn
            if place == 5:
                x = x * has_up
            high, low = high_low(x)
            ext[pl.ds(base + comp, blocks, stride=SUB), :] = high
            ext[pl.ds(base + LOW + comp, blocks, stride=SUB), :] = low
        ext[pl.ds(base + 3, blocks, stride=SUB), :] = blank
        ext[pl.ds(base + LOW + 3, blocks, stride=SUB), :] = blank
    acc[...] = jnp.zeros_like(acc)
    rows = lax.broadcasted_iota(jnp.int32, (SUB, width), 0)
    squares = jnp.zeros((SUB, width), jnp.float32)
    for b in range(blocks):
        starts = [pl.multiple_of(ids[b, k] * SUB, SUB) for k in range(count)]
        coupled = jnp.zeros((SUB, width), jnp.float32)
        for k in range(0, count, 2):
            picked = jnp.concatenate(
                [ext[pl.ds(starts[k], SUB), :], ext[pl.ds(starts[k + 1], SUB), :]], axis=1
            ).astype(jnp.bfloat16)
            pair = jnp.concatenate([tiles[b, k], tiles[b, k + 1]], axis=1)
            coupled += lax.dot_general(
                picked, pair, (((1,), (1,)), ((), ())), preferred_element_type=jnp.float32
            )
        coupled = coupled + pltpu.roll(coupled, LOW, 0)
        squares += jnp.where(rows < LOW, coupled * coupled, 0.0)
        high, low = high_low(coupled)
        parts = jnp.where(rows < LOW, high, low).astype(jnp.bfloat16)
        for k in range(count):
            acc[pl.ds(starts[k], SUB), :] += jnp.dot(
                parts, tiles[b, k], preferred_element_type=jnp.float32
            )
    targets = (to_axial_dn, to_cross_dn, None, to_cross_up, to_axial_up)
    even = jnp.zeros((blocks, width), jnp.float32)
    odd = squares
    for place, target in zip(PLACES, targets):
        base = place * blocks * SUB
        for comp in range(3):
            total = (
                acc[pl.ds(base + comp, blocks, stride=SUB), :]
                + acc[pl.ds(base + LOW + comp, blocks, stride=SUB), :]
            )
            if target is None:
                x = own[comp]
                dragged = drag[...] * x
                even += x * x
                odd += dragged * x
                kept[comp] = dragged + total
            else:
                target[comp] = total
    moments[0] = even
    moments[1] = odd


def operator_call(ids, sources, tiles, drag):
    blocks, width = drag.shape
    vmem = pl.BlockSpec(memory_space=pltpu.VMEM)
    field = jax.ShapeDtypeStruct((3, blocks, width), jnp.float32)
    return pl.pallas_call(
        operator_kernel,
        in_specs=[pl.BlockSpec(memory_space=pltpu.SMEM)] + [vmem] * 7,
        out_specs=[vmem] * 6,
        out_shape=[field] * 5 + [jax.ShapeDtypeStruct((2, blocks, width), jnp.float32)],
        scratch_shapes=[
            pltpu.VMEM((8 * blocks * SUB, width), jnp.float32),
            pltpu.VMEM((8 * blocks * SUB, width), jnp.float32),
        ],
        compiler_params=pltpu.CompilerParams(vmem_limit_bytes=24 << 20),
    )(ids, *sources, tiles, drag)


def shifted_poly(poly):
    return [None] + list(poly)


def combine(left, scale, right):
    out = []
    for i in range(max(len(left), len(right))):
        a = left[i] if i < len(left) else None
        b = right[i] if i < len(right) else None
        b = None if b is None else scale * b
        out.append(b if a is None else a if b is None else a + b)
    return out


def inner(left, right, shift, moment):
    total = None
    for i, a in enumerate(left):
        for j, b in enumerate(right):
            term = a * b * moment[i + j + shift]
            total = term if total is None else total + term
    return total


def cg_coefficients(moment):
    one = jnp.ones_like(moment[0])
    velocity, residual, direction = [], [one], [one]
    norm_now = moment[0]
    for sweep in range(ITERS):
        alpha = norm_now / inner(direction, direction, 1, moment)
        velocity = combine(velocity, alpha, direction)
        residual = combine(residual, -alpha, shifted_poly(direction))
        if sweep < ITERS - 1:
            norm_next = inner(residual, residual, 0, moment)
            direction = combine(residual, norm_next / norm_now, direction)
            norm_now = norm_next
    return velocity, residual


def mixed(coefs, fields):
    total = coefs[0] * fields[0]
    for c, f in zip(coefs[1:], fields[1:]):
        total = total + c * f
    return total


def picked_beads(fields, coefs, wanted, live):
    blocks, width = fields[0][0].shape
    index = jnp.where(live, wanted.astype(jnp.int32), -1)
    block = lax.shift_right_arithmetic(index, 7)
    place = jnp.bitwise_and(index, width - 1)
    parts = []
    for comp in range(3):
        x = mixed(coefs, [f[comp] for f in fields])
        high, rest = high_low(x)
        middle, low = high_low(rest)
        parts += [high, middle, low]
    stacked = jnp.concatenate(parts + [jnp.zeros_like(parts[0])], axis=0).astype(jnp.bfloat16)
    lanes = lax.broadcasted_iota(jnp.int32, (width, width), 0)
    chosen = jnp.where(lanes == place, 1.0, 0.0).astype(jnp.bfloat16)
    found = jnp.dot(stacked, chosen, preferred_element_type=jnp.float32)
    keep = lax.broadcasted_iota(jnp.int32, (blocks, width), 0) == block
    out = []
    for comp in range(3):
        at = 3 * comp * blocks
        x = (
            found[at : at + blocks]
            + found[at + blocks : at + 2 * blocks]
            + found[at + 2 * blocks : at + 3 * blocks]
        )
        out.append(jnp.sum(jnp.where(keep, x, 0.0), axis=0, keepdims=True))
    return out


def finish_kernel(sums, k0, k1, k2, k3, d0, d1, d2, u0, u1, u2, velocity, residual, arrivals):
    blocks, width = k0.shape[1:]
    slab = lax.axis_index("cross")
    total = jnp.sum(sums[...], axis=0)
    moment = [
        jnp.broadcast_to(jnp.sum(total[i : i + 1], axis=1, keepdims=True), (blocks, width))
        for i in range(2 * ITERS)
    ]
    vel, res = cg_coefficients(moment)
    own = (k0, k1, k2, k3)
    for comp in range(3):
        velocity[comp] = mixed(vel, [k[comp] for k in own[:ITERS]])
        residual[comp] = mixed(res, [k[comp] for k in own])
    lower = picked_beads((d0, d1, d2), vel, d0[3, 1:2, :], slab > 0)
    upper = picked_beads(
        (u0, u1, u2), vel, u0[3, 0:1, :], slab < lax.axis_size("cross") - 1
    )
    for comp in range(3):
        arrivals[comp : comp + 1, :] = lower[comp] + upper[comp]


def finish_call(sums, own, below, above):
    blocks, width = own[1].shape[1:]
    vmem = pl.BlockSpec(memory_space=pltpu.VMEM)
    field = jax.ShapeDtypeStruct((3, blocks, width), jnp.float32)
    return pl.pallas_call(
        finish_kernel,
        in_specs=[vmem] * 11,
        out_specs=[vmem] * 3,
        out_shape=[field, field, jax.ShapeDtypeStruct((3, width), jnp.float32)],
    )(sums, *own, *below, *above)


def leaving_rows(mig_rows, mig_count, blocks, width):
    capacity = mig_rows.shape[-1]
    live = lax.broadcasted_iota(jnp.int32, (2, capacity), 1) < mig_count[0, 0][:, None]
    rows = jnp.where(live, mig_rows[0, 0], -1).astype(jnp.float32)
    none = jnp.full((1, width - capacity), -1.0, jnp.float32)
    to_lower = jnp.concatenate([none, rows[0:1]], axis=1)
    to_upper = jnp.concatenate([rows[1:2], none], axis=1)
    rest = jnp.zeros((blocks - 2, width), jnp.float32)
    return jnp.concatenate([to_lower, to_upper, rest], axis=0)[None]


def spread_sum(part, axis):
    count = lax.axis_size(axis)
    copies = jnp.broadcast_to(part[None], (count,) + part.shape)
    return lax.all_to_all(copies, axis, 0, 0)


def on_device(force, self_drag, tiles, tile_ids, mig_rows, mig_count):
    field = jnp.swapaxes(force[0, 0], 0, 1)
    drag = self_drag[0, 0]
    blocks, width = drag.shape
    ids = tile_ids[0, 0]
    slab = lax.axis_index("cross")
    last = lax.axis_size("cross") - 1
    now = jnp.concatenate([field, leaving_rows(mig_rows, mig_count, blocks, width)], axis=0)
    own, below, above, moments = [], [], [], []
    for sweep in range(ITERS):
        cross_dn = ring_shift(now, "cross", 1)
        cross_up = ring_shift(now, "cross", -1)
        axial_dn = ring_shift(now[:3], "axial", 1)
        axial_up = ring_shift(now[:3], "axial", -1)
        own.append(now)
        below.append(cross_dn)
        above.append(cross_up)
        r1, r3, r5, r7, kept, pair = operator_call(
            ids, (now, axial_dn, cross_dn, cross_up, axial_up), tiles[0, 0], drag
        )
        moments.append(jnp.sum(pair, axis=1))
        from_lower_cross = ring_shift(r5, "cross", 1)
        from_upper_cross = ring_shift(r3, "cross", -1)
        from_lower_axial = ring_shift(r7, "axial", 1)
        from_upper_axial = ring_shift(r1, "axial", -1)
        now = kept + from_lower_axial + from_upper_axial
        now = now + jnp.where(slab > 0, from_lower_cross, 0.0)
        now = now + jnp.where(slab < last, from_upper_cross, 0.0)
    own.append(now)
    part = jnp.concatenate(moments + [jnp.zeros((2, width), jnp.float32)], axis=0)
    part = jnp.sum(spread_sum(part, "axial"), axis=0)
    sums = spread_sum(part, "cross")
    velocity, residual, arrivals = finish_call(sums, own, below, above)
    return (
        jnp.swapaxes(velocity, 0, 1)[None, None],
        jnp.swapaxes(residual, 0, 1)[None, None],
        arrivals[None, None],
    )


def solution(mesh):
    placed = (
        P("axial", "cross", None, None, None),
        P("axial", "cross", None, None),
        P("axial", "cross", None, None, None, None),
        P("axial", "cross", None, None),
        P("axial", "cross", None, None),
        P("axial", "cross", None),
    )
    return jax.shard_map(
        on_device,
        mesh=mesh,
        in_specs=placed,
        out_specs=(
            P("axial", "cross", None, None, None),
            P("axial", "cross", None, None, None),
            P("axial", "cross", None, None),
        ),
        check_vma=False,
    )
```

time: 640 us -> 132 us (0.21)
  blocking collectives: 518 us -> 9.06 us
  waiting for transfers between devices: 3.64 us -> 23.3 us
  starting transfers between devices: 95.9 us -> 81.3 us
  Pallas kernels: 0 us -> 8.17 us
  between operations: 7.9 us -> 0.98 us
    psum x5 -> x0, blocking collectives: 518 us -> none  [the longest x3 309 us: residual_squares(): return lax.psum(jnp.sum(residual * residual), ('axial', 'cross'))]
    ppermute x26 -> x24, starting transfers between devices: 95.9 us -> 71.7 us  [ring_shift(): return lax.ppermute(shard, axis, ring(lax.axis_size(axis), by))]
    ppermute x26 -> x24, waiting for transfers between devices: 3.64 us -> 22.3 us  [ring_shift(): return lax.ppermute(shard, axis, ring(lax.axis_size(axis), by))]
    all_to_all x0 -> x1, starting transfers between devices: none -> 9.62 us  [spread_sum(): return lax.all_to_all(copies, axis, 0, 0)]
    all_to_all x0 -> x1, blocking collectives: none -> 9.06 us  [spread_sum(): return lax.all_to_all(copies, axis, 0, 0)]
    pallas_call x0 -> x4, Pallas kernels: none -> 8.17 us  [the longest x3 6.25 us: operator_call(): pl.pallas_call(operator_kernel, in_specs=[pl.BlockSpec(memory_space=pltpu...]
  transfers between devices with their start and end apart: 26 -> 25, of which waited for: 6 -> 10; matrix products, arithmetic and copies ran while one was open for 0% -> 1% of each run, Pallas kernels for 0% -> 0%
where the time goes in v1:
time: 132 us; the launch traced here: 131 us
  starting transfers between devices  81.3 us (62%)
  waiting for transfers between devices  23.3 us (18%)
  blocking collectives  9.06 us (7%)
  Pallas kernels  8.17 us (6%)
  local copies, waits for them, and re-layouts  5.71 us (4%)
  other arithmetic  2.31 us (2%)
    ppermute x24, starting transfers between devices, ring_shift(): return lax.ppermute(shard, axis, ring(lax.axis_size(axis), by))  71.7 us
    ppermute x24, waiting for transfers between devices, ring_shift(): return lax.ppermute(shard, axis, ring(lax.axis_size(axis), by))  22.3 us
    all_to_all x1, starting transfers between devices, spread_sum(): return lax.all_to_all(copies, axis, 0, 0)  9.62 us
    all_to_all x1, blocking collectives, spread_sum(): return lax.all_to_all(copies, axis, 0, 0)  9.06 us
    pallas_call x3, Pallas kernels, operator_call(): pl.pallas_call(operator_kernel, in_specs=[pl.BlockSpec(memory_space=pltpu...  6.25 us
    unnamed x33, local copies, waits for them, and re-layouts  4.89 us
  transfers between devices with their start and end apart: 25, of which 10 were waited for; matrix products, arithmetic and copies ran while one was open for 1% of the time, Pallas kernels for 0%

profile of v1, /device:TPU:1, one launch (start us, length us, event | category | flops | bytes accessed | tf_op | source)
XLA Modules:
  0.0 130.8 jit_solution(10723517164408562821)
XLA Ops:
  0.6 0.0 copy-start.12
  0.6 0.0 copy-start.14
  0.7 0.8 fusion.3
  1.4 0.1 pad.10.clone
  1.5 0.1 fusion.1
  1.6 0.7 pad_maximum_fusion.own.k0
  2.3 6.9 %collective-permute-start.2 = (f32[4,8,128]{2,1,0:T(8,128)S(1)}, f32[4,8,128]{2,1,0:T(8,128)S(1)}, u32[]{:S(2)}, u32[]{:S(2)}) collective-permute-start(f32[4,8,128]{2,1,0:T(8,128)S(1)} %pad_maximum_fusion.own.k0), channel_id=1, source_target_pairs={{0,31},{1,0},{2,1},{3,2},{4,3},{5,4},{6,5},{7,6},{8,7},{9,8},{10,9... | collective-permute-start | bytes 49160 | tf_op jit(solution)/shard_map/ppermute | solution.py:19
  9.2 0.0 collective-permute-start.1
  9.2 3.0 %collective-permute-start.3 = (f32[3,8,128]{2,1,0:T(8,128)}, f32[3,8,128]{2,1,0:T(8,128)S(1)}, u32[]{:S(2)}, u32[]{:S(2)}) collective-permute-start(f32[3,8,128]{2,1,0:T(8,128)} %bitcast.28), channel_id=1, source_target_pairs={{0,480},{32,0},{64,32},{96,64},{128,96},{160,128},{192,160},{224,1... | collective-permute-start | bytes 36872 | tf_op jit(solution)/shard_map/ppermute | solution.py:19
  12.2 2.3 %collective-permute-start = (f32[3,8,128]{2,1,0:T(8,128)}, f32[3,8,128]{2,1,0:T(8,128)S(1)}, u32[]{:S(2)}, u32[]{:S(2)}) collective-permute-start(f32[3,8,128]{2,1,0:T(8,128)} %bitcast.29), channel_id=1, source_target_pairs={{0,32},{32,64},{64,96},{96,128},{128,160},{160,192},{192,224},{224... | collective-permute-start | bytes 36872 | tf_op jit(solution)/shard_map/ppermute | solution.py:19
  14.5 0.0 collective-permute-done.3.from_axial_up
  14.5 5.7 %collective-permute-done.from_axial_dn = f32[3,8,128]{2,1,0:T(8,128)S(1)} collective-permute-done((f32[3,8,128]{2,1,0:T(8,128)}, f32[3,8,128]{2,1,0:T(8,128)S(1)}, u32[]{:S(2)}, u32[]{:S(2)}) %collective-permute-start) | collective-permute-done | bytes 12320 | tf_op jit(solution)/shard_map/ppermute | solution.py:19
  20.1 0.0 collective-permute-done.2.from_cross_up.u0
  20.1 0.0 collective-permute-done.1.from_cross_dn.d0
  20.2 0.0 copy-start
  20.2 1.6 %copy-done = bf16[1,1,8,8,128,128]{5,4,3,2,1,0:T(8,128)(2,1)S(1)} copy-done((bf16[1,1,8,8,128,128]{5,4,3,2,1,0:T(8,128)(2,1)S(1)}, bf16[1,1,8,8,128,128]{5,4,3,2,1,0:T(8,128)(2,1)}, u32[]{:S(2)}) %copy-start) | copy-done | bytes 2097176
  21.7 0.7 copy-done.11
  22.4 0.7 copy-done.13
  23.1 2.1 %shard_map.85 = (f32[3,8,128]{2,1,0:T(8,128)S(1)}, f32[3,8,128]{2,1,0:T(8,128)S(1)}, f32[3,8,128]{2,1,0:T(8,128)S(1)}, f32[3,8,128]{2,1,0:T(8,128)S(1)}, f32[3,8...) custom-call(s32[8,8]{1,0:T(8,128)S(1)} %bitcast.21, f32[4,8,128]{2,1,0:T(8,128)S(1)} %pad_maximum_fusion.own.k0, ...), custom_call_target="tpu_custom_call" | custom-call | tf_op jit(solution)/shard_map/pallas_call | solution.py:99
  25.2 1.9 %collective-permute-start.4 = (f32[3,8,128]{2,1,0:T(8,128)S(1)}, f32[3,8,128]{2,1,0:T(8,128)S(1)}, u32[]{:S(2)}, u32[]{:S(2)}) collective-permute-start(f32[3,8,128]{2,1,0:T(8,128)S(1)} %get-tuple-element.26), channel_id=1, source_target_pairs={{0,32},{32,64},{64,96},{96,128},{128,160},{160,192},{192,224},{224... | collective-permute-start | bytes 36872 | tf_op jit(solution)/shard_map/ppermute | solution.py:19
  27.1 6.7 %collective-permute-start.5 = (f32[3,8,128]{2,1,0:T(8,128)S(1)}, f32[3,8,128]{2,1,0:T(8,128)S(1)}, u32[]{:S(2)}, u32[]{:S(2)}) collective-permute-start(f32[3,8,128]{2,1,0:T(8,128)S(1)} %get-tuple-element.27), channel_id=1, source_target_pairs={{0,480},{32,0},{64,32},{96,64},{128,96},{160,128},{192,160},{224,1... | collective-permute-start | bytes 36872 | tf_op jit(solution)/shard_map/ppermute | solution.py:19
  33.8 2.5 %collective-permute-start.6 = (f32[3,8,128]{2,1,0:T(8,128)S(1)}, f32[3,8,128]{2,1,0:T(8,128)S(1)}, u32[]{:S(2)}, u32[]{:S(2)}) collective-permute-start(f32[3,8,128]{2,1,0:T(8,128)S(1)} %get-tuple-element.28), channel_id=1, source_target_pairs={{0,1},{1,2},{2,3},{3,4},{4,5},{5,6},{6,7},{7,8},{8,9},{9,10},{10,1... | collective-permute-start | bytes 36872 | tf_op jit(solution)/shard_map/ppermute | solution.py:19
  36.3 6.9 %collective-permute-start.7 = (f32[3,8,128]{2,1,0:T(8,128)S(1)}, f32[3,8,128]{2,1,0:T(8,128)S(1)}, u32[]{:S(2)}, u32[]{:S(2)}) collective-permute-start(f32[3,8,128]{2,1,0:T(8,128)S(1)} %get-tuple-element.29), channel_id=1, source_target_pairs={{0,31},{1,0},{2,1},{3,2},{4,3},{5,4},{6,5},{7,6},{8,7},{9,8},{10,9... | collective-permute-start | bytes 36872 | tf_op jit(solution)/shard_map/ppermute | solution.py:19
  43.3 0.6 collective-permute-done.6
  43.9 0.2 collective-permute-done.7
  44.1 1.9 %collective-permute-start.11 = (f32[3,8,128]{2,1,0:T(8,128)S(1)}, f32[3,8,128]{2,1,0:T(8,128)S(1)}, u32[]{:S(2)}, u32[]{:S(2)}) collective-permute-start(f32[3,8,128]{2,1,0:T(8,128)S(1)} %select_add_fusion.2.own.k1), channel_id=1, source_target_pairs={{0,480},{32,0},{64,32},{96,64},{128,96},{160,128},{192,160},{224,1... | collective-permute-start | bytes 36872 | tf_op jit(solution)/shard_map/ppermute | solution.py:19
  46.0 6.1 %collective-permute-start.10 = (f32[3,8,128]{2,1,0:T(8,128)S(1)}, f32[3,8,128]{2,1,0:T(8,128)S(1)}, u32[]{:S(2)}, u32[]{:S(2)}) collective-permute-start(f32[3,8,128]{2,1,0:T(8,128)S(1)} %select_add_fusion.2.own.k1), channel_id=1, source_target_pairs={{0,31},{1,0},{2,1},{3,2},{4,3},{5,4},{6,5},{7,6},{8,7},{9,8},{10,9... | collective-permute-start | bytes 36872 | tf_op jit(solution)/shard_map/ppermute | solution.py:19
  52.2 0.0 collective-permute-start.9
  52.2 1.9 %collective-permute-start.8 = (f32[3,8,128]{2,1,0:T(8,128)S(1)}, f32[3,8,128]{2,1,0:T(8,128)S(1)}, u32[]{:S(2)}, u32[]{:S(2)}) collective-permute-start(f32[3,8,128]{2,1,0:T(8,128)S(1)} %select_add_fusion.2.own.k1), channel_id=1, source_target_pairs={{0,32},{32,64},{64,96},{96,128},{128,160},{160,192},{192,224},{224... | collective-permute-start | bytes 36872 | tf_op jit(solution)/shard_map/ppermute | solution.py:19
  54.1 0.0 collective-permute-done.11.from_axial_up
  54.1 0.0 collective-permute-done.9.from_cross_dn.d1
  54.2 5.8 %collective-permute-done.8.from_axial_dn = f32[3,8,128]{2,1,0:T(8,128)S(1)} collective-permute-done((f32[3,8,128]{2,1,0:T(8,128)S(1)}, f32[3,8,128]{2,1,0:T(8,128)S(1)}, u32[]{:S(2)}, u32[]{:S(2)}) %collective-permute-start.8) | collective-permute-done | bytes 12320 | tf_op jit(solution)/shard_map/ppermute | solution.py:19
  59.9 2.1 %shard_map.86 = (f32[3,8,128]{2,1,0:T(8,128)S(1)}, f32[3,8,128]{2,1,0:T(8,128)S(1)}, f32[3,8,128]{2,1,0:T(8,128)S(1)}, f32[3,8,128]{2,1,0:T(8,128)S(1)}, f32[3,8...) custom-call(s32[8,8]{1,0:T(8,128)S(1)} %bitcast.22, f32[3,8,128]{2,1,0:T(8,128)S(1)} %select_add_fusion.2.own.k1, ...), custom_call_target="tpu_custom_call" | custom-call | tf_op jit(solution)/shard_map/pallas_call | solution.py:99
  62.1 1.9 %collective-permute-start.12 = (f32[3,8,128]{2,1,0:T(8,128)S(1)}, f32[3,8,128]{2,1,0:T(8,128)S(1)}, u32[]{:S(2)}, u32[]{:S(2)}) collective-permute-start(f32[3,8,128]{2,1,0:T(8,128)S(1)} %get-tuple-element.32), channel_id=1, source_target_pairs={{0,32},{32,64},{64,96},{96,128},{128,160},{160,192},{192,224},{224... | collective-permute-start | bytes 36872 | tf_op jit(solution)/shard_map/ppermute | solution.py:19
  64.0 6.7 %collective-permute-start.13 = (f32[3,8,128]{2,1,0:T(8,128)S(1)}, f32[3,8,128]{2,1,0:T(8,128)S(1)}, u32[]{:S(2)}, u32[]{:S(2)}) collective-permute-start(f32[3,8,128]{2,1,0:T(8,128)S(1)} %get-tuple-element.33), channel_id=1, source_target_pairs={{0,480},{32,0},{64,32},{96,64},{128,96},{160,128},{192,160},{224,1... | collective-permute-start | bytes 36872 | tf_op jit(solution)/shard_map/ppermute | solution.py:19
  70.7 0.0 collective-permute-start.14
  70.7 2.2 %collective-permute-start.15 = (f32[3,8,128]{2,1,0:T(8,128)S(1)}, f32[3,8,128]{2,1,0:T(8,128)S(1)}, u32[]{:S(2)}, u32[]{:S(2)}) collective-permute-start(f32[3,8,128]{2,1,0:T(8,128)S(1)} %get-tuple-element.35), channel_id=1, source_target_pairs={{0,31},{1,0},{2,1},{3,2},{4,3},{5,4},{6,5},{7,6},{8,7},{9,8},{10,9... | collective-permute-start | bytes 36872 | tf_op jit(solution)/shard_map/ppermute | solution.py:19
  72.9 0.0 collective-permute-done.12
  72.9 0.0 collective-permute-done.13
  73.0 0.6 collective-permute-done.14
  73.6 0.3 collective-permute-done.15
  73.9 4.6 %collective-permute-start.19 = (f32[3,8,128]{2,1,0:T(8,128)S(1)}, f32[3,8,128]{2,1,0:T(8,128)S(1)}, u32[]{:S(2)}, u32[]{:S(2)}) collective-permute-start(f32[3,8,128]{2,1,0:T(8,128)S(1)} %select_add_fusion.1.own.k2), channel_id=1, source_target_pairs={{0,480},{32,0},{64,32},{96,64},{128,96},{160,128},{192,160},{224,1... | collective-permute-start | bytes 36872 | tf_op jit(solution)/shard_map/ppermute | solution.py:19
  78.5 3.4 %collective-permute-start.18 = (f32[3,8,128]{2,1,0:T(8,128)S(1)}, f32[3,8,128]{2,1,0:T(8,128)S(1)}, u32[]{:S(2)}, u32[]{:S(2)}) collective-permute-start(f32[3,8,128]{2,1,0:T(8,128)S(1)} %select_add_fusion.1.own.k2), channel_id=1, source_target_pairs={{0,31},{1,0},{2,1},{3,2},{4,3},{5,4},{6,5},{7,6},{8,7},{9,8},{10,9... | collective-permute-start | bytes 36872 | tf_op jit(solution)/shard_map/ppermute | solution.py:19
  81.9 1.9 %collective-permute-start.16 = (f32[3,8,128]{2,1,0:T(8,128)S(1)}, f32[3,8,128]{2,1,0:T(8,128)S(1)}, u32[]{:S(2)}, u32[]{:S(2)}) collective-permute-start(f32[3,8,128]{2,1,0:T(8,128)S(1)} %select_add_fusion.1.own.k2), channel_id=1, source_target_pairs={{0,32},{32,64},{64,96},{96,128},{128,160},{160,192},{192,224},{224... | collective-permute-start | bytes 36872 | tf_op jit(solution)/shard_map/ppermute | solution.py:19
  83.8 0.1 pad.5.clone
  83.9 0.0 collective-permute-done.18.from_cross_up.u2
  83.9 5.7 %collective-permute-done.16.from_axial_dn = f32[3,8,128]{2,1,0:T(8,128)S(1)} collective-permute-done((f32[3,8,128]{2,1,0:T(8,128)S(1)}, f32[3,8,128]{2,1,0:T(8,128)S(1)}, u32[]{:S(2)}, u32[]{:S(2)}) %collective-permute-start.16) | collective-permute-done | bytes 12320 | tf_op jit(solution)/shard_map/ppermute | solution.py:19
  89.6 2.1 %shard_map.87 = (f32[3,8,128]{2,1,0:T(8,128)S(1)}, f32[3,8,128]{2,1,0:T(8,128)S(1)}, f32[3,8,128]{2,1,0:T(8,128)S(1)}, f32[3,8,128]{2,1,0:T(8,128)S(1)}, f32[3,8...) custom-call(s32[8,8]{1,0:T(8,128)S(1)} %bitcast.23, f32[3,8,128]{2,1,0:T(8,128)S(1)} %select_add_fusion.1.own.k2, ...), custom_call_target="tpu_custom_call" | custom-call | tf_op jit(solution)/shard_map/pallas_call | solution.py:99
  91.7 0.1 maximum_maximum_fusion
  91.8 9.1 %all_to_all.10 = f32[16,8,128]{2,1,0:T(8,128)S(1)} all-to-all(f32[16,8,128]{2,1,0:T(8,128)S(1)} %broadcast_in_dim.49), channel_id=1, replica_groups=mesh['axial'=16,'cross'=32] {'axial'}, dimensions={0} | all-to-all | bytes 131072 | tf_op jit(solution)/shard_map/all_to_all | solution.py:232
  100.9 0.7 broadcast_in_dim.50
  101.6 9.6 %all-to-all-start.1 = ((f32[32,8,128]{2,1,0:T(8,128)}), f32[32,8,128]{2,1,0:T(8,128)S(1)}, u32[]{:S(2)}, u32[]{:S(2)}) async-start(f32[32,8,128]{2,1,0:T(8,128)} %broadcast_in_dim.50), calls=%async_computation.1 | async-start | bytes 262144 | tf_op jit(solution)/shard_map/all_to_all | solution.py:232
  111.2 2.2 %collective-permute-start.20 = (f32[3,8,128]{2,1,0:T(8,128)S(1)}, f32[3,8,128]{2,1,0:T(8,128)S(1)}, u32[]{:S(2)}, u32[]{:S(2)}) collective-permute-start(f32[3,8,128]{2,1,0:T(8,128)S(1)} %get-tuple-element.38), channel_id=1, source_target_pairs={{0,32},{32,64},{64,96},{96,128},{128,160},{160,192},{192,224},{224... | collective-permute-start | bytes 36872 | tf_op jit(solution)/shard_map/ppermute | solution.py:19
  113.4 6.4 %collective-permute-start.21 = (f32[3,8,128]{2,1,0:T(8,128)S(1)}, f32[3,8,128]{2,1,0:T(8,128)S(1)}, u32[]{:S(2)}, u32[]{:S(2)}) collective-permute-start(f32[3,8,128]{2,1,0:T(8,128)S(1)} %get-tuple-element.39), channel_id=1, source_target_pairs={{0,480},{32,0},{64,32},{96,64},{128,96},{160,128},{192,160},{224,1... | collective-permute-start | bytes 36872 | tf_op jit(solution)/shard_map/ppermute | solution.py:19
  119.8 2.2 %collective-permute-start.22 = (f32[3,8,128]{2,1,0:T(8,128)S(1)}, f32[3,8,128]{2,1,0:T(8,128)S(1)}, u32[]{:S(2)}, u32[]{:S(2)}) collective-permute-start(f32[3,8,128]{2,1,0:T(8,128)S(1)} %get-tuple-element.40), channel_id=1, source_target_pairs={{0,1},{1,2},{2,3},{3,4},{4,5},{5,6},{6,7},{7,8},{8,9},{9,10},{10,1... | collective-permute-start | bytes 36872 | tf_op jit(solution)/shard_map/ppermute | solution.py:19
  122.0 0.0 collective-permute-done.20
  122.0 0.0 collective-permute-done.21
  122.0 0.8 collective-permute-done.22
  122.8 2.6 %collective-permute-done.23 = f32[3,8,128]{2,1,0:T(8,128)S(1)} collective-permute-done((f32[3,8,128]{2,1,0:T(8,128)S(1)}, f32[3,8,128]{2,1,0:T(8,128)S(1)}, u32[]{:S(2)}, u32[]{:S(2)}) %collective-permute-start.23) | collective-permute-done | bytes 12320 | tf_op jit(solution)/shard_map/ppermute | solution.py:19
  125.4 0.6 select_add_fusion.k3
  126.0 1.0 all-to-all-done.1.sums
  127.0 0.6 copy-done.15
  127.7 1.9 %shard_map.88 = (f32[3,8,128]{2,1,0:T(8,128)}, f32[3,8,128]{2,1,0:T(8,128)}, f32[3,128]{1,0:T(4,128)}) custom-call(f32[32,8,128]{2,1,0:T(8,128)} %copy-done.15, f32[4,8,128]{2,1,0:T(8,128)} %copy-done.2, f32[3,8,128]{2,1,0:T(8,128)} %copy-done.3, f32[3,8,128]{2,1,0:T(8,128)} %copy-done.4, f32[3,8,128]{2,1,0:T(8,128)} %select_add_fusion.k3, ...), custom_call_target="tpu_custom_call" | custom-call | tf_op jit(solution)/shard_map/pallas_call | solution.py:210
  129.6 1.2 copy.10
  (42 shorter events, 0.2 us)
Async XLA Ops:
  0.6 59.3 %copy-start.12 = (s32[1,1,8,8]{3,2,1,0:T(8,128)S(1)}, s32[1,1,8,8]{3,2,1,0:T(8,128)}, u32[]{:S(2)}) copy-start(s32[1,1,8,8]{3,2,1,0:T(8,128)} %param.9) | copy-start | bytes 772
  0.6 59.3 %copy-start.14 = (f32[1,1,8,128]{3,2,1,0:T(8,128)S(1)}, f32[1,1,8,128]{3,2,1,0:T(8,128)}, u32[]{:S(2)}) copy-start(f32[1,1,8,128]{3,2,1,0:T(8,128)} %param.7) | copy-start | bytes 12292
  2.3 59.8 %copy-start.2 = (f32[4,8,128]{2,1,0:T(8,128)}, f32[4,8,128]{2,1,0:T(8,128)S(1)}, u32[]{:S(2)}) copy-start(f32[4,8,128]{2,1,0:T(8,128)S(1)} %pad_maximum_fusion.own.k0) | copy-start | bytes 49156
  2.3 17.8 %collective-permute-start.2 = (f32[4,8,128]{2,1,0:T(8,128)S(1)}, f32[4,8,128]{2,1,0:T(8,128)S(1)}, u32[]{:S(2)}, u32[]{:S(2)}) collective-permute-start(f32[4,8,128]{2,1,0:T(8,128)S(1)} %pad_maximum_fusion.own.k0), channel_id=1, source_target_pairs={{0,31},{1,0},{2,1},{3,2},{4,3},{5,4},{6,5},{7,6},{8,7},{9,8},{10,9... | collective-permute-start | bytes 49160 | tf_op jit(solution)/shard_map/ppermute | solution.py:19
  9.2 11.0 %collective-permute-start.1 = (f32[4,8,128]{2,1,0:T(8,128)S(1)}, f32[4,8,128]{2,1,0:T(8,128)S(1)}, u32[]{:S(2)}, u32[]{:S(2)}) collective-permute-start(f32[4,8,128]{2,1,0:T(8,128)S(1)} %pad_maximum_fusion.own.k0), channel_id=1, source_target_pairs={{0,1},{1,2},{2,3},{3,4},{4,5},{5,6},{6,7},{7,8},{8,9},{9,10},{10,1... | collective-permute-start | bytes 49160 | tf_op jit(solution)/shard_map/ppermute | solution.py:19
  9.2 5.3 %collective-permute-start.3 = (f32[3,8,128]{2,1,0:T(8,128)}, f32[3,8,128]{2,1,0:T(8,128)S(1)}, u32[]{:S(2)}, u32[]{:S(2)}) collective-permute-start(f32[3,8,128]{2,1,0:T(8,128)} %bitcast.28), channel_id=1, source_target_pairs={{0,480},{32,0},{64,32},{96,64},{128,96},{160,128},{192,160},{224,1... | collective-permute-start | bytes 36872 | tf_op jit(solution)/shard_map/ppermute | solution.py:19
  12.2 8.0 %collective-permute-start = (f32[3,8,128]{2,1,0:T(8,128)}, f32[3,8,128]{2,1,0:T(8,128)S(1)}, u32[]{:S(2)}, u32[]{:S(2)}) collective-permute-start(f32[3,8,128]{2,1,0:T(8,128)} %bitcast.29), channel_id=1, source_target_pairs={{0,32},{32,64},{64,96},{96,128},{128,160},{160,192},{192,224},{224... | collective-permute-start | bytes 36872 | tf_op jit(solution)/shard_map/ppermute | solution.py:19
  20.1 41.9 %copy-start.5 = (f32[4,8,128]{2,1,0:T(8,128)}, f32[4,8,128]{2,1,0:T(8,128)S(1)}, u32[]{:S(2)}) copy-start(f32[4,8,128]{2,1,0:T(8,128)S(1)} %collective-permute-done.2.from_cross_up.u0) | copy-start | bytes 49156
  20.1 41.9 %copy-start.6 = (f32[4,8,128]{2,1,0:T(8,128)}, f32[4,8,128]{2,1,0:T(8,128)S(1)}, u32[]{:S(2)}) copy-start(f32[4,8,128]{2,1,0:T(8,128)S(1)} %collective-permute-done.1.from_cross_dn.d0) | copy-start | bytes 49156
  20.2 1.6 %copy-start = (bf16[1,1,8,8,128,128]{5,4,3,2,1,0:T(8,128)(2,1)S(1)}, bf16[1,1,8,8,128,128]{5,4,3,2,1,0:T(8,128)(2,1)}, u32[]{:S(2)}) copy-start(bf16[1,1,8,8,128,128]{5,4,3,2,1,0:T(8,128)(2,1)} %param.8) | copy-start | bytes 6291460
  21.7 0.7 copy-start.11
  22.4 0.7 copy-start.13
  23.1 36.8 %copy-start.1 = (bf16[1,1,8,8,128,128]{5,4,3,2,1,0:T(8,128)(2,1)S(1)}, bf16[1,1,8,8,128,128]{5,4,3,2,1,0:T(8,128)(2,1)}, u32[]{:S(2)}) copy-start(bf16[1,1,8,8,128,128]{5,4,3,2,1,0:T(8,128)(2,1)} %param.8) | copy-start | bytes 6291460
  25.2 18.1 %collective-permute-start.4 = (f32[3,8,128]{2,1,0:T(8,128)S(1)}, f32[3,8,128]{2,1,0:T(8,128)S(1)}, u32[]{:S(2)}, u32[]{:S(2)}) collective-permute-start(f32[3,8,128]{2,1,0:T(8,128)S(1)} %get-tuple-element.26), channel_id=1, source_target_pairs={{0,32},{32,64},{64,96},{96,128},{128,160},{160,192},{192,224},{224... | collective-permute-start | bytes 36872 | tf_op jit(solution)/shard_map/ppermute | solution.py:19
  27.1 16.1 %collective-permute-start.5 = (f32[3,8,128]{2,1,0:T(8,128)S(1)}, f32[3,8,128]{2,1,0:T(8,128)S(1)}, u32[]{:S(2)}, u32[]{:S(2)}) collective-permute-start(f32[3,8,128]{2,1,0:T(8,128)S(1)} %get-tuple-element.27), channel_id=1, source_target_pairs={{0,480},{32,0},{64,32},{96,64},{128,96},{160,128},{192,160},{224,1... | collective-permute-start | bytes 36872 | tf_op jit(solution)/shard_map/ppermute | solution.py:19
  33.8 10.1 %collective-permute-start.6 = (f32[3,8,128]{2,1,0:T(8,128)S(1)}, f32[3,8,128]{2,1,0:T(8,128)S(1)}, u32[]{:S(2)}, u32[]{:S(2)}) collective-permute-start(f32[3,8,128]{2,1,0:T(8,128)S(1)} %get-tuple-element.28), channel_id=1, source_target_pairs={{0,1},{1,2},{2,3},{3,4},{4,5},{5,6},{6,7},{7,8},{8,9},{9,10},{10,1... | collective-permute-start | bytes 36872 | tf_op jit(solution)/shard_map/ppermute | solution.py:19
  36.3 7.8 %collective-permute-start.7 = (f32[3,8,128]{2,1,0:T(8,128)S(1)}, f32[3,8,128]{2,1,0:T(8,128)S(1)}, u32[]{:S(2)}, u32[]{:S(2)}) collective-permute-start(f32[3,8,128]{2,1,0:T(8,128)S(1)} %get-tuple-element.29), channel_id=1, source_target_pairs={{0,31},{1,0},{2,1},{3,2},{4,3},{5,4},{6,5},{7,6},{8,7},{9,8},{10,9... | collective-permute-start | bytes 36872 | tf_op jit(solution)/shard_map/ppermute | solution.py:19
  44.1 47.6 %copy-start.3 = (f32[3,8,128]{2,1,0:T(8,128)}, f32[3,8,128]{2,1,0:T(8,128)S(1)}, u32[]{:S(2)}) copy-start(f32[3,8,128]{2,1,0:T(8,128)S(1)} %select_add_fusion.2.own.k1) | copy-start | bytes 36868
  44.1 10.0 %collective-permute-start.11 = (f32[3,8,128]{2,1,0:T(8,128)S(1)}, f32[3,8,128]{2,1,0:T(8,128)S(1)}, u32[]{:S(2)}, u32[]{:S(2)}) collective-permute-start(f32[3,8,128]{2,1,0:T(8,128)S(1)} %select_add_fusion.2.own.k1), channel_id=1, source_target_pairs={{0,480},{32,0},{64,32},{96,64},{128,96},{160,128},{192,160},{224,1... | collective-permute-start | bytes 36872 | tf_op jit(solution)/shard_map/ppermute | solution.py:19
  46.0 8.1 %collective-permute-start.10 = (f32[3,8,128]{2,1,0:T(8,128)S(1)}, f32[3,8,128]{2,1,0:T(8,128)S(1)}, u32[]{:S(2)}, u32[]{:S(2)}) collective-permute-start(f32[3,8,128]{2,1,0:T(8,128)S(1)} %select_add_fusion.2.own.k1), channel_id=1, source_target_pairs={{0,31},{1,0},{2,1},{3,2},{4,3},{5,4},{6,5},{7,6},{8,7},{9,8},{10,9... | collective-permute-start | bytes 36872 | tf_op jit(solution)/shard_map/ppermute | solution.py:19
  52.2 2.0 %collective-permute-start.9 = (f32[3,8,128]{2,1,0:T(8,128)S(1)}, f32[3,8,128]{2,1,0:T(8,128)S(1)}, u32[]{:S(2)}, u32[]{:S(2)}) collective-permute-start(f32[3,8,128]{2,1,0:T(8,128)S(1)} %select_add_fusion.2.own.k1), channel_id=1, source_target_pairs={{0,1},{1,2},{2,3},{3,4},{4,5},{5,6},{6,7},{7,8},{8,9},{9,10},{10,1... | collective-permute-start | bytes 36872 | tf_op jit(solution)/shard_map/ppermute | solution.py:19
  52.2 7.7 %collective-permute-start.8 = (f32[3,8,128]{2,1,0:T(8,128)S(1)}, f32[3,8,128]{2,1,0:T(8,128)S(1)}, u32[]{:S(2)}, u32[]{:S(2)}) collective-permute-start(f32[3,8,128]{2,1,0:T(8,128)S(1)} %select_add_fusion.2.own.k1), channel_id=1, source_target_pairs={{0,32},{32,64},{64,96},{96,128},{128,160},{160,192},{192,224},{224... | collective-permute-start | bytes 36872 | tf_op jit(solution)/shard_map/ppermute | solution.py:19
  54.1 37.6 %copy-start.7 = (f32[3,8,128]{2,1,0:T(8,128)}, f32[3,8,128]{2,1,0:T(8,128)S(1)}, u32[]{:S(2)}) copy-start(f32[3,8,128]{2,1,0:T(8,128)S(1)} %collective-permute-done.10.from_cross_up.u1) | copy-start | bytes 36868
  54.1 37.6 %copy-start.8 = (f32[3,8,128]{2,1,0:T(8,128)}, f32[3,8,128]{2,1,0:T(8,128)S(1)}, u32[]{:S(2)}) copy-start(f32[3,8,128]{2,1,0:T(8,128)S(1)} %collective-permute-done.9.from_cross_dn.d1) | copy-start | bytes 36868
  62.1 10.9 %collective-permute-start.12 = (f32[3,8,128]{2,1,0:T(8,128)S(1)}, f32[3,8,128]{2,1,0:T(8,128)S(1)}, u32[]{:S(2)}, u32[]{:S(2)}) collective-permute-start(f32[3,8,128]{2,1,0:T(8,128)S(1)} %get-tuple-element.32), channel_id=1, source_target_pairs={{0,32},{32,64},{64,96},{96,128},{128,160},{160,192},{192,224},{224... | collective-permute-start | bytes 36872 | tf_op jit(solution)/shard_map/ppermute | solution.py:19
  64.0 9.0 %collective-permute-start.13 = (f32[3,8,128]{2,1,0:T(8,128)S(1)}, f32[3,8,128]{2,1,0:T(8,128)S(1)}, u32[]{:S(2)}, u32[]{:S(2)}) collective-permute-start(f32[3,8,128]{2,1,0:T(8,128)S(1)} %get-tuple-element.33), channel_id=1, source_target_pairs={{0,480},{32,0},{64,32},{96,64},{128,96},{160,128},{192,160},{224,1... | collective-permute-start | bytes 36872 | tf_op jit(solution)/shard_map/ppermute | solution.py:19
  70.7 2.9 %collective-permute-start.14 = (f32[3,8,128]{2,1,0:T(8,128)S(1)}, f32[3,8,128]{2,1,0:T(8,128)S(1)}, u32[]{:S(2)}, u32[]{:S(2)}) collective-permute-start(f32[3,8,128]{2,1,0:T(8,128)S(1)} %get-tuple-element.34), channel_id=1, source_target_pairs={{0,1},{1,2},{2,3},{3,4},{4,5},{5,6},{6,7},{7,8},{8,9},{9,10},{10,1... | collective-permute-start | bytes 36872 | tf_op jit(solution)/shard_map/ppermute | solution.py:19
  70.7 3.1 %collective-permute-start.15 = (f32[3,8,128]{2,1,0:T(8,128)S(1)}, f32[3,8,128]{2,1,0:T(8,128)S(1)}, u32[]{:S(2)}, u32[]{:S(2)}) collective-permute-start(f32[3,8,128]{2,1,0:T(8,128)S(1)} %get-tuple-element.35), channel_id=1, source_target_pairs={{0,31},{1,0},{2,1},{3,2},{4,3},{5,4},{6,5},{7,6},{8,7},{9,8},{10,9... | collective-permute-start | bytes 36872 | tf_op jit(solution)/shard_map/ppermute | solution.py:19
  73.9 53.2 %copy-start.4 = (f32[3,8,128]{2,1,0:T(8,128)}, f32[3,8,128]{2,1,0:T(8,128)S(1)}, u32[]{:S(2)}) copy-start(f32[3,8,128]{2,1,0:T(8,128)S(1)} %select_add_fusion.1.own.k2) | copy-start | bytes 36868
  73.9 10.0 %collective-permute-start.19 = (f32[3,8,128]{2,1,0:T(8,128)S(1)}, f32[3,8,128]{2,1,0:T(8,128)S(1)}, u32[]{:S(2)}, u32[]{:S(2)}) collective-permute-start(f32[3,8,128]{2,1,0:T(8,128)S(1)} %select_add_fusion.1.own.k2), channel_id=1, source_target_pairs={{0,480},{32,0},{64,32},{96,64},{128,96},{160,128},{192,160},{224,1... | collective-permute-start | bytes 36872 | tf_op jit(solution)/shard_map/ppermute | solution.py:19
  78.5 5.4 %collective-permute-start.18 = (f32[3,8,128]{2,1,0:T(8,128)S(1)}, f32[3,8,128]{2,1,0:T(8,128)S(1)}, u32[]{:S(2)}, u32[]{:S(2)}) collective-permute-start(f32[3,8,128]{2,1,0:T(8,128)S(1)} %select_add_fusion.1.own.k2), channel_id=1, source_target_pairs={{0,31},{1,0},{2,1},{3,2},{4,3},{5,4},{6,5},{7,6},{8,7},{9,8},{10,9... | collective-permute-start | bytes 36872 | tf_op jit(solution)/shard_map/ppermute | solution.py:19
  81.9 2.1 %collective-permute-start.17 = (f32[3,8,128]{2,1,0:T(8,128)S(1)}, f32[3,8,128]{2,1,0:T(8,128)S(1)}, u32[]{:S(2)}, u32[]{:S(2)}) collective-permute-start(f32[3,8,128]{2,1,0:T(8,128)S(1)} %select_add_fusion.1.own.k2), channel_id=1, source_target_pairs={{0,1},{1,2},{2,3},{3,4},{4,5},{5,6},{6,7},{7,8},{8,9},{9,10},{10,1... | collective-permute-start | bytes 36872 | tf_op jit(solution)/shard_map/ppermute | solution.py:19
  81.9 7.7 %collective-permute-start.16 = (f32[3,8,128]{2,1,0:T(8,128)S(1)}, f32[3,8,128]{2,1,0:T(8,128)S(1)}, u32[]{:S(2)}, u32[]{:S(2)}) collective-permute-start(f32[3,8,128]{2,1,0:T(8,128)S(1)} %select_add_fusion.1.own.k2), channel_id=1, source_target_pairs={{0,32},{32,64},{64,96},{96,128},{128,160},{160,192},{192,224},{224... | collective-permute-start | bytes 36872 | tf_op jit(solution)/shard_map/ppermute | solution.py:19
  83.9 43.1 %copy-start.9 = (f32[3,8,128]{2,1,0:T(8,128)}, f32[3,8,128]{2,1,0:T(8,128)S(1)}, u32[]{:S(2)}) copy-start(f32[3,8,128]{2,1,0:T(8,128)S(1)} %collective-permute-done.18.from_cross_up.u2) | copy-start | bytes 36868
  83.9 43.1 %copy-start.10 = (f32[3,8,128]{2,1,0:T(8,128)}, f32[3,8,128]{2,1,0:T(8,128)S(1)}, u32[]{:S(2)}) copy-start(f32[3,8,128]{2,1,0:T(8,128)S(1)} %collective-permute-done.17.from_cross_dn.d2) | copy-start | bytes 36868
  101.6 25.5 %all-to-all-start.1 = ((f32[32,8,128]{2,1,0:T(8,128)}), f32[32,8,128]{2,1,0:T(8,128)S(1)}, u32[]{:S(2)}, u32[]{:S(2)}) async-start(f32[32,8,128]{2,1,0:T(8,128)} %broadcast_in_dim.50), calls=%async_computation.1 | async-start | bytes 262144 | tf_op jit(solution)/shard_map/all_to_all | solution.py:232
  111.2 10.8 %collective-permute-start.20 = (f32[3,8,128]{2,1,0:T(8,128)S(1)}, f32[3,8,128]{2,1,0:T(8,128)S(1)}, u32[]{:S(2)}, u32[]{:S(2)}) collective-permute-start(f32[3,8,128]{2,1,0:T(8,128)S(1)} %get-tuple-element.38), channel_id=1, source_target_pairs={{0,32},{32,64},{64,96},{96,128},{128,160},{160,192},{192,224},{224... | collective-permute-start | bytes 36872 | tf_op jit(solution)/shard_map/ppermute | solution.py:19
  113.4 8.6 %collective-permute-start.21 = (f32[3,8,128]{2,1,0:T(8,128)S(1)}, f32[3,8,128]{2,1,0:T(8,128)S(1)}, u32[]{:S(2)}, u32[]{:S(2)}) collective-permute-start(f32[3,8,128]{2,1,0:T(8,128)S(1)} %get-tuple-element.39), channel_id=1, source_target_pairs={{0,480},{32,0},{64,32},{96,64},{128,96},{160,128},{192,160},{224,1... | collective-permute-start | bytes 36872 | tf_op jit(solution)/shard_map/ppermute | solution.py:19
  119.8 3.0 %collective-permute-start.22 = (f32[3,8,128]{2,1,0:T(8,128)S(1)}, f32[3,8,128]{2,1,0:T(8,128)S(1)}, u32[]{:S(2)}, u32[]{:S(2)}) collective-permute-start(f32[3,8,128]{2,1,0:T(8,128)S(1)} %get-tuple-element.40), channel_id=1, source_target_pairs={{0,1},{1,2},{2,3},{3,4},{4,5},{5,6},{6,7},{7,8},{8,9},{9,10},{10,1... | collective-permute-start | bytes 36872 | tf_op jit(solution)/shard_map/ppermute | solution.py:19
  122.0 3.4 %collective-permute-start.23 = (f32[3,8,128]{2,1,0:T(8,128)S(1)}, f32[3,8,128]{2,1,0:T(8,128)S(1)}, u32[]{:S(2)}, u32[]{:S(2)}) collective-permute-start(f32[3,8,128]{2,1,0:T(8,128)S(1)} %get-tuple-element.41), channel_id=1, source_target_pairs={{0,31},{1,0},{2,1},{3,2},{4,3},{5,4},{6,5},{7,6},{8,7},{9,8},{10,9... | collective-permute-start | bytes 36872 | tf_op jit(solution)/shard_map/ppermute | solution.py:19
  127.0 0.6 copy-start.15

commit v2 on v1

--- a/solution.py
+++ b/solution.py
@@ -1,3 +1,5 @@
+import functools
+
 import jax
 import jax.numpy as jnp
 from jax import lax
@@ -25,7 +27,7 @@
 
 
 def operator_kernel(
-    ids, own, from_axial_dn, from_cross_dn, from_cross_up, from_axial_up, tiles, drag,
+    sweep, ids, own, from_axial_dn, from_cross_dn, from_cross_up, from_axial_up, tiles, drag, carried,
     to_axial_dn, to_cross_dn, to_cross_up, to_axial_up, kept, moments, ext, acc,
 ):
     blocks, count = ids.shape
@@ -88,25 +90,35 @@
                 kept[comp] = dragged + total
             else:
                 target[comp] = total
-    moments[0] = even
-    moments[1] = odd
-
-
-def operator_call(ids, sources, tiles, drag):
+    even = jnp.sum(even, axis=0, keepdims=True)
+    odd = jnp.sum(odd, axis=0, keepdims=True)
+    if sweep == 0:
+        moments[...] = jnp.where(rows == 0, even, jnp.where(rows == 1, odd, 0.0))
+        to_cross_dn[3] = carried[...]
+        to_cross_up[3] = carried[...]
+    else:
+        moments[...] = jnp.where(
+            rows == 2 * sweep, even, jnp.where(rows == 2 * sweep + 1, odd, carried[...])
+        )
+
+
+def operator_call(sweep, ids, sources, tiles, drag, carried):
     blocks, width = drag.shape
     vmem = pl.BlockSpec(memory_space=pltpu.VMEM)
     field = jax.ShapeDtypeStruct((3, blocks, width), jnp.float32)
+    across = jax.ShapeDtypeStruct((4 if sweep == 0 else 3, blocks, width), jnp.float32)
+    plane = jax.ShapeDtypeStruct((SUB, width), jnp.float32)
     return pl.pallas_call(
-        operator_kernel,
-        in_specs=[pl.BlockSpec(memory_space=pltpu.SMEM)] + [vmem] * 7,
+        functools.partial(operator_kernel, sweep),
+        in_specs=[pl.BlockSpec(memory_space=pltpu.SMEM)] + [vmem] * 8,
         out_specs=[vmem] * 6,
-        out_shape=[field] * 5 + [jax.ShapeDtypeStruct((2, blocks, width), jnp.float32)],
+        out_shape=[field, across, across, field, field, plane],
         scratch_shapes=[
             pltpu.VMEM((8 * blocks * SUB, width), jnp.float32),
             pltpu.VMEM((8 * blocks * SUB, width), jnp.float32),
         ],
-        compiler_params=pltpu.CompilerParams(vmem_limit_bytes=24 << 20),
-    )(ids, *sources, tiles, drag)
+        compiler_params=pltpu.CompilerParams(vmem_limit_bytes=4 << 20),
+    )(ids, *sources, tiles, drag, carried)
 
 
 def shifted_poly(poly):
@@ -182,7 +194,9 @@
     return out
 
 
-def finish_kernel(sums, k0, k1, k2, k3, d0, d1, d2, u0, u1, u2, velocity, residual, arrivals):
+def finish_kernel(
+    sums, k0, k1, k2, k3, d0, d1, d2, u0, u1, u2, dn_plane, up_plane, velocity, residual, arrivals
+):
     blocks, width = k0.shape[1:]
     slab = lax.axis_index("cross")
     total = jnp.sum(sums[...], axis=0)
@@ -195,24 +209,51 @@
     for comp in range(3):
         velocity[comp] = mixed(vel, [k[comp] for k in own[:ITERS]])
         residual[comp] = mixed(res, [k[comp] for k in own])
-    lower = picked_beads((d0, d1, d2), vel, d0[3, 1:2, :], slab > 0)
+    lower = picked_beads((d0, d1, d2), vel, dn_plane[3, 1:2, :], slab > 0)
     upper = picked_beads(
-        (u0, u1, u2), vel, u0[3, 0:1, :], slab < lax.axis_size("cross") - 1
+        (u0, u1, u2), vel, up_plane[3, 0:1, :], slab < lax.axis_size("cross") - 1
     )
     for comp in range(3):
-        arrivals[comp : comp + 1, :] = lower[comp] + upper[comp]
-
-
-def finish_call(sums, own, below, above):
+        arrivals[comp] = lower[comp] + upper[comp]
+
+
+def finish_call(sums, own, below, above, planes):
     blocks, width = own[1].shape[1:]
     vmem = pl.BlockSpec(memory_space=pltpu.VMEM)
     field = jax.ShapeDtypeStruct((3, blocks, width), jnp.float32)
     return pl.pallas_call(
         finish_kernel,
-        in_specs=[vmem] * 11,
+        in_specs=[vmem] * 13,
         out_specs=[vmem] * 3,
-        out_shape=[field, field, jax.ShapeDtypeStruct((3, width), jnp.float32)],
-    )(sums, *own, *below, *above)
+        out_shape=[field, field, jax.ShapeDtypeStruct((3, 1, width), jnp.float32)],
+        compiler_params=pltpu.CompilerParams(vmem_limit_bytes=4 << 20),
+    )(sums, *own, *below, *above, *planes)
+
+
+def stage_kernel(tiles, drag, force, tiles_out, drag_out, force_out, sems):
+    copies = [
+        pltpu.make_async_copy(source, target, sems.at[i])
+        for i, (source, target) in enumerate(
+            ((tiles, tiles_out), (drag, drag_out), (force, force_out))
+        )
+    ]
+    for copy in copies:
+        copy.start()
+    for copy in copies:
+        copy.wait()
+
+
+def stage_call(tiles, drag, force):
+    arrays = (tiles, drag, force)
+    return pl.pallas_call(
+        stage_kernel,
+        in_specs=[pl.BlockSpec(memory_space=pltpu.HBM)] * 3,
+        out_specs=[pl.BlockSpec(memory_space=pltpu.VMEM)] * 3,
+        out_shape=[jax.ShapeDtypeStruct(a.shape, a.dtype) for a in arrays],
+        scratch_shapes=[pltpu.SemaphoreType.DMA((3,))],
+        compiler_params=pltpu.CompilerParams(vmem_limit_bytes=4 << 20),
+        cost_estimate=pl.CostEstimate(flops=0, bytes_accessed=2 * tiles.size * 2, transcendentals=0),
+    )(*arrays)
 
 
 def leaving_rows(mig_rows, mig_count, blocks, width):
@@ -223,7 +264,7 @@
     to_lower = jnp.concatenate([none, rows[0:1]], axis=1)
     to_upper = jnp.concatenate([rows[1:2], none], axis=1)
     rest = jnp.zeros((blocks - 2, width), jnp.float32)
-    return jnp.concatenate([to_lower, to_upper, rest], axis=0)[None]
+    return jnp.concatenate([to_lower, to_upper, rest], axis=0)
 
 
 def spread_sum(part, axis):
@@ -239,36 +280,44 @@
     ids = tile_ids[0, 0]
     slab = lax.axis_index("cross")
     last = lax.axis_size("cross") - 1
-    now = jnp.concatenate([field, leaving_rows(mig_rows, mig_count, blocks, width)], axis=0)
-    own, below, above, moments = [], [], [], []
+    carried = leaving_rows(mig_rows, mig_count, blocks, width)
+    now = field
+    held, drag, field = stage_call(tiles[0, 0], drag, field)
+    own, below, above, planes = [], [], [], []
     for sweep in range(ITERS):
         cross_dn = ring_shift(now, "cross", 1)
         cross_up = ring_shift(now, "cross", -1)
-        axial_dn = ring_shift(now[:3], "axial", 1)
-        axial_up = ring_shift(now[:3], "axial", -1)
+        axial_dn = ring_shift(now, "axial", 1)
+        axial_up = ring_shift(now, "axial", -1)
+        now = field if sweep == 0 else now
         own.append(now)
         below.append(cross_dn)
         above.append(cross_up)
-        r1, r3, r5, r7, kept, pair = operator_call(
-            ids, (now, axial_dn, cross_dn, cross_up, axial_up), tiles[0, 0], drag
+        r1, r3, r5, r7, kept, carried = operator_call(
+            sweep, ids, (now, axial_dn, cross_dn, cross_up, axial_up), held, drag, carried
         )
-        moments.append(jnp.sum(pair, axis=1))
+        from_lower_axial = ring_shift(r7, "axial", 1)
+        from_upper_axial = ring_shift(r1, "axial", -1)
+        if sweep == ITERS - 1:
+            part = jnp.sum(spread_sum(carried, "axial"), axis=0)
+            part, r3, r5 = lax.optimization_barrier((part, r3, r5))
+            part, from_lower_axial, from_upper_axial = lax.optimization_barrier(
+                (part, from_lower_axial, from_upper_axial)
+            )
+            sums = spread_sum(part, "cross")
         from_lower_cross = ring_shift(r5, "cross", 1)
         from_upper_cross = ring_shift(r3, "cross", -1)
-        from_lower_axial = ring_shift(r7, "axial", 1)
-        from_upper_axial = ring_shift(r1, "axial", -1)
+        if sweep == 0:
+            planes = [from_lower_cross, from_upper_cross]
         now = kept + from_lower_axial + from_upper_axial
-        now = now + jnp.where(slab > 0, from_lower_cross, 0.0)
-        now = now + jnp.where(slab < last, from_upper_cross, 0.0)
+        now = now + jnp.where(slab > 0, from_lower_cross[:3], 0.0)
+        now = now + jnp.where(slab < last, from_upper_cross[:3], 0.0)
     own.append(now)
-    part = jnp.concatenate(moments + [jnp.zeros((2, width), jnp.float32)], axis=0)
-    part = jnp.sum(spread_sum(part, "axial"), axis=0)
-    sums = spread_sum(part, "cross")
-    velocity, residual, arrivals = finish_call(sums, own, below, above)
+    velocity, residual, arrivals = finish_call(sums, own, below, above, planes)
     return (
         jnp.swapaxes(velocity, 0, 1)[None, None],
         jnp.swapaxes(residual, 0, 1)[None, None],
-        arrivals[None, None],
+        jnp.swapaxes(arrivals, 0, 1)[None],
     )
 
 

time: 132 us -> 132 us (level)
  blocking collectives: 9.06 us -> 0 us
  waiting for transfers between devices: 23.3 us -> 29.8 us
  starting transfers between devices: 81.3 us -> 87.2 us
  other arithmetic: 2.31 us -> 0.87 us
  local copies, waits for them, and re-layouts: 5.71 us -> 4.34 us
    all_to_all x1 -> x0, blocking collectives: 9.06 us -> none  [spread_sum(): return lax.all_to_all(copies, axis, 0, 0)]
    all_to_all x1 -> x2, waiting for transfers between devices: 1.01 us -> 9.41 us  [spread_sum(): return lax.all_to_all(copies, axis, 0, 0)]
    all_to_all x1 -> x2, starting transfers between devices: 9.62 us -> 13.4 us  [spread_sum(): return lax.all_to_all(copies, axis, 0, 0)]
    ppermute x24, starting transfers between devices: 71.7 us -> 73.8 us  [ring_shift(): return lax.ppermute(shard, axis, ring(lax.axis_size(axis), by))]
    unnamed x33 -> x8, local copies, waits for them, and re-layouts: 4.89 us -> 2.99 us
    ppermute x24, waiting for transfers between devices: 22.3 us -> 20.4 us  [ring_shift(): return lax.ppermute(shard, axis, ring(lax.axis_size(axis), by))]
    pallas_call x4 -> x5, Pallas kernels: 8.17 us -> 7.32 us  [the longest x3 6.24 us: operator_call(): pl.pallas_call(functools.partial(operator_kernel, sweep), in_specs=[pl.Bl...]
  transfers between devices with their start and end apart: 25 -> 26, of which waited for: 10 -> 10; matrix products, arithmetic and copies ran while one was open for 1% -> 1% of each run, Pallas kernels for 0% -> 0%
where the time goes in v2:
time: 132 us; the launch traced here: 130 us
  starting transfers between devices  87.2 us (66%)
  waiting for transfers between devices  29.8 us (23%)
  Pallas kernels  7.32 us (6%)
  local copies, waits for them, and re-layouts  4.34 us (3%)
    ppermute x24, starting transfers between devices, ring_shift(): return lax.ppermute(shard, axis, ring(lax.axis_size(axis), by))  73.8 us
    ppermute x24, waiting for transfers between devices, ring_shift(): return lax.ppermute(shard, axis, ring(lax.axis_size(axis), by))  20.4 us
    all_to_all x2, starting transfers between devices, spread_sum(): return lax.all_to_all(copies, axis, 0, 0)  13.4 us
    all_to_all x2, waiting for transfers between devices, spread_sum(): return lax.all_to_all(copies, axis, 0, 0)  9.41 us
    pallas_call x3, Pallas kernels, operator_call(): pl.pallas_call(functools.partial(operator_kernel, sweep), in_specs=[pl.Bl...  6.24 us
    unnamed x8, local copies, waits for them, and re-layouts  2.99 us
  transfers between devices with their start and end apart: 26, of which 10 were waited for; matrix products, arithmetic and copies ran while one was open for 1% of the time, Pallas kernels for 0%

profile of v2, /device:TPU:1, one launch (start us, length us, event | category | flops | bytes accessed | tf_op | source)
XLA Modules:
  0.0 130.4 jit_solution(10908959980961931767)
XLA Ops:
  0.6 7.7 %collective-permute-start.3 = (f32[3,8,128]{2,1,0:T(8,128)}, f32[3,8,128]{2,1,0:T(8,128)S(1)}, u32[]{:S(2)}, u32[]{:S(2)}) collective-permute-start(f32[3,8,128]{2,1,0:T(8,128)} %bitcast.22), channel_id=1, source_target_pairs={{0,480},{32,0},{64,32},{96,64},{128,96},{160,128},{192,160},{224,1... | collective-permute-start | bytes 36872 | tf_op jit(solution)/shard_map/ppermute | solution.py:21
  8.3 1.1 collective-permute-start.2
  9.5 1.4 %collective-permute-start.1 = (f32[3,8,128]{2,1,0:T(8,128)}, f32[3,8,128]{2,1,0:T(8,128)S(1)}, u32[]{:S(2)}, u32[]{:S(2)}) collective-permute-start(f32[3,8,128]{2,1,0:T(8,128)} %bitcast.24), channel_id=1, source_target_pairs={{0,1},{1,2},{2,3},{3,4},{4,5},{5,6},{6,7},{7,8},{8,9},{9,10},{10,1... | collective-permute-start | bytes 36872 | tf_op jit(solution)/shard_map/ppermute | solution.py:21
  10.8 2.3 %collective-permute-start = (f32[3,8,128]{2,1,0:T(8,128)}, f32[3,8,128]{2,1,0:T(8,128)S(1)}, u32[]{:S(2)}, u32[]{:S(2)}) collective-permute-start(f32[3,8,128]{2,1,0:T(8,128)} %bitcast.25), channel_id=1, source_target_pairs={{0,32},{32,64},{64,96},{96,128},{128,160},{160,192},{192,224},{224... | collective-permute-start | bytes 36872 | tf_op jit(solution)/shard_map/ppermute | solution.py:21
  13.1 0.8 fusion.4
  13.9 0.1 pad.4.clone
  13.9 0.1 fusion.2.carried
  14.0 1.6 %copy-done = bf16[1,1,8,8,128,128]{5,4,3,2,1,0:T(8,128)(2,1)S(1)} copy-done((bf16[1,1,8,8,128,128]{5,4,3,2,1,0:T(8,128)(2,1)S(1)}, bf16[1,1,8,8,128,128]{5,4,3,2,1,0:T(8,128)(2,1)}, u32[]{:S(2)}) %copy-start) | copy-done | bytes 2097176
  15.6 0.7 copy-done.2
  16.3 0.7 copy-done.3
  17.0 0.2 shard_map.85
  17.2 0.0 collective-permute-done.3.from_axial_up
  17.2 0.0 collective-permute-done.2.from_cross_up.u0
  17.2 1.6 %collective-permute-done.1.from_cross_dn.d0 = f32[3,8,128]{2,1,0:T(8,128)S(1)} collective-permute-done((f32[3,8,128]{2,1,0:T(8,128)}, f32[3,8,128]{2,1,0:T(8,128)S(1)}, u32[]{:S(2)}, u32[]{:S(2)}) %collective-permute-start.1) | collective-permute-done | bytes 12320 | tf_op jit(solution)/shard_map/ppermute | solution.py:21
  18.8 0.0 collective-permute-done.from_axial_dn
  18.8 2.1 %shard_map.86 = (f32[3,8,128]{2,1,0:T(8,128)S(1)}, f32[4,8,128]{2,1,0:T(8,128)S(1)}, f32[4,8,128]{2,1,0:T(8,128)S(1)}, f32[3,8,128]{2,1,0:T(8,128)S(1)}, f32[3,8,128]{2,1,0:T(8,128)S(1)}, /*index=5*/f32[8,128]{1,0:T(8,128)S(1)}) custom-call(s32[8,8]{1,0:T(8,128)S(1)} %bitcast.19, f32[3,8,128]{2,1,0:T(8,128)S(1)} %get-tuple-element.33.own.k0, ...), custom_call_target="tpu_custom_call" | custom-call | tf_op jit(solution)/shard_map/pallas_call | solution.py:111
  20.9 1.6 %collective-permute-start.6 = (f32[4,8,128]{2,1,0:T(8,128)S(1)}, f32[4,8,128]{2,1,0:T(8,128)S(1)}, u32[]{:S(2)}, u32[]{:S(2)}) collective-permute-start(f32[4,8,128]{2,1,0:T(8,128)S(1)} %get-tuple-element.39), channel_id=1, source_target_pairs={{0,1},{1,2},{2,3},{3,4},{4,5},{5,6},{6,7},{7,8},{8,9},{9,10},{10,1... | collective-permute-start | bytes 49160 | tf_op jit(solution)/shard_map/ppermute | solution.py:21
  22.5 6.7 %collective-permute-start.7 = (f32[4,8,128]{2,1,0:T(8,128)S(1)}, f32[4,8,128]{2,1,0:T(8,128)S(1)}, u32[]{:S(2)}, u32[]{:S(2)}) collective-permute-start(f32[4,8,128]{2,1,0:T(8,128)S(1)} %get-tuple-element.40), channel_id=1, source_target_pairs={{0,31},{1,0},{2,1},{3,2},{4,3},{5,4},{6,5},{7,6},{8,7},{9,8},{10,9... | collective-permute-start | bytes 49160 | tf_op jit(solution)/shard_map/ppermute | solution.py:21
  29.2 1.9 %collective-permute-start.4 = (f32[3,8,128]{2,1,0:T(8,128)S(1)}, f32[3,8,128]{2,1,0:T(8,128)S(1)}, u32[]{:S(2)}, u32[]{:S(2)}) collective-permute-start(f32[3,8,128]{2,1,0:T(8,128)S(1)} %get-tuple-element.37), channel_id=1, source_target_pairs={{0,32},{32,64},{64,96},{96,128},{128,160},{160,192},{192,224},{224... | collective-permute-start | bytes 36872 | tf_op jit(solution)/shard_map/ppermute | solution.py:21
  31.1 6.7 %collective-permute-start.5 = (f32[3,8,128]{2,1,0:T(8,128)S(1)}, f32[3,8,128]{2,1,0:T(8,128)S(1)}, u32[]{:S(2)}, u32[]{:S(2)}) collective-permute-start(f32[3,8,128]{2,1,0:T(8,128)S(1)} %get-tuple-element.38), channel_id=1, source_target_pairs={{0,480},{32,0},{64,32},{96,64},{128,96},{160,128},{192,160},{224,1... | collective-permute-start | bytes 36872 | tf_op jit(solution)/shard_map/ppermute | solution.py:21
  37.8 0.0 collective-permute-done.4
  37.8 0.8 collective-permute-done.5
  38.6 0.0 collective-permute-done.6.dn_plane
  38.6 0.0 collective-permute-done.7.up_plane
  38.6 6.9 %collective-permute-start.11 = (f32[3,8,128]{2,1,0:T(8,128)S(1)}, f32[3,8,128]{2,1,0:T(8,128)S(1)}, u32[]{:S(2)}, u32[]{:S(2)}) collective-permute-start(f32[3,8,128]{2,1,0:T(8,128)S(1)} %fusion.own.k1), channel_id=1, source_target_pairs={{0,480},{32,0},{64,32},{96,64},{128,96},{160,128},{192,160},{224,1... | collective-permute-start | bytes 36872 | tf_op jit(solution)/shard_map/ppermute | solution.py:21
  45.6 4.7 %collective-permute-start.10 = (f32[3,8,128]{2,1,0:T(8,128)S(1)}, f32[3,8,128]{2,1,0:T(8,128)S(1)}, u32[]{:S(2)}, u32[]{:S(2)}) collective-permute-start(f32[3,8,128]{2,1,0:T(8,128)S(1)} %fusion.own.k1), channel_id=1, source_target_pairs={{0,31},{1,0},{2,1},{3,2},{4,3},{5,4},{6,5},{7,6},{8,7},{9,8},{10,9... | collective-permute-start | bytes 36872 | tf_op jit(solution)/shard_map/ppermute | solution.py:21
  50.2 0.0 collective-permute-start.9
  50.2 1.9 %collective-permute-start.8 = (f32[3,8,128]{2,1,0:T(8,128)S(1)}, f32[3,8,128]{2,1,0:T(8,128)S(1)}, u32[]{:S(2)}, u32[]{:S(2)}) collective-permute-start(f32[3,8,128]{2,1,0:T(8,128)S(1)} %fusion.own.k1), channel_id=1, source_target_pairs={{0,32},{32,64},{64,96},{96,128},{128,160},{160,192},{192,224},{224... | collective-permute-start | bytes 36872 | tf_op jit(solution)/shard_map/ppermute | solution.py:21
  52.1 0.0 collective-permute-done.11.from_axial_up
  52.2 0.0 collective-permute-done.10.from_cross_up.u1
  52.2 0.0 collective-permute-done.9.from_cross_dn.d1
  52.2 5.8 %collective-permute-done.8.from_axial_dn = f32[3,8,128]{2,1,0:T(8,128)S(1)} collective-permute-done((f32[3,8,128]{2,1,0:T(8,128)S(1)}, f32[3,8,128]{2,1,0:T(8,128)S(1)}, u32[]{:S(2)}, u32[]{:S(2)}) %collective-permute-start.8) | collective-permute-done | bytes 12320 | tf_op jit(solution)/shard_map/ppermute | solution.py:21
  58.0 2.1 %shard_map.87 = (f32[3,8,128]{2,1,0:T(8,128)S(1)}, f32[3,8,128]{2,1,0:T(8,128)S(1)}, f32[3,8,128]{2,1,0:T(8,128)S(1)}, f32[3,8,128]{2,1,0:T(8,128)S(1)}, f32[3,8,128]{2,1,0:T(8,128)S(1)}, /*index=5*/f32[8,128]{1,0:T(8,128)S(1)}) custom-call(s32[8,8]{1,0:T(8,128)S(1)} %bitcast.20, f32[3,8,128]{2,1,0:T(8,128)S(1)} %fusion.own.k1, ...), custom_call_target="tpu_custom_call" | custom-call | tf_op jit(solution)/shard_map/pallas_call | solution.py:111
  60.1 1.9 %collective-permute-start.12 = (f32[3,8,128]{2,1,0:T(8,128)S(1)}, f32[3,8,128]{2,1,0:T(8,128)S(1)}, u32[]{:S(2)}, u32[]{:S(2)}) collective-permute-start(f32[3,8,128]{2,1,0:T(8,128)S(1)} %get-tuple-element.43), channel_id=1, source_target_pairs={{0,32},{32,64},{64,96},{96,128},{128,160},{160,192},{192,224},{224... | collective-permute-start | bytes 36872 | tf_op jit(solution)/shard_map/ppermute | solution.py:21
  62.0 6.7 %collective-permute-start.13 = (f32[3,8,128]{2,1,0:T(8,128)S(1)}, f32[3,8,128]{2,1,0:T(8,128)S(1)}, u32[]{:S(2)}, u32[]{:S(2)}) collective-permute-start(f32[3,8,128]{2,1,0:T(8,128)S(1)} %get-tuple-element.44), channel_id=1, source_target_pairs={{0,480},{32,0},{64,32},{96,64},{128,96},{160,128},{192,160},{224,1... | collective-permute-start | bytes 36872 | tf_op jit(solution)/shard_map/ppermute | solution.py:21
  68.7 0.0 collective-permute-start.14
  68.7 2.2 %collective-permute-start.15 = (f32[3,8,128]{2,1,0:T(8,128)S(1)}, f32[3,8,128]{2,1,0:T(8,128)S(1)}, u32[]{:S(2)}, u32[]{:S(2)}) collective-permute-start(f32[3,8,128]{2,1,0:T(8,128)S(1)} %get-tuple-element.46), channel_id=1, source_target_pairs={{0,31},{1,0},{2,1},{3,2},{4,3},{5,4},{6,5},{7,6},{8,7},{9,8},{10,9... | collective-permute-start | bytes 36872 | tf_op jit(solution)/shard_map/ppermute | solution.py:21
  70.9 0.0 collective-permute-done.12
  70.9 0.0 collective-permute-done.13
  70.9 0.6 collective-permute-done.14
  71.6 0.3 collective-permute-done.15
  71.8 4.6 %collective-permute-start.19 = (f32[3,8,128]{2,1,0:T(8,128)S(1)}, f32[3,8,128]{2,1,0:T(8,128)S(1)}, u32[]{:S(2)}, u32[]{:S(2)}) collective-permute-start(f32[3,8,128]{2,1,0:T(8,128)S(1)} %select_add_fusion.1.own.k2), channel_id=1, source_target_pairs={{0,480},{32,0},{64,32},{96,64},{128,96},{160,128},{192,160},{224,1... | collective-permute-start | bytes 36872 | tf_op jit(solution)/shard_map/ppermute | solution.py:21
  76.5 3.4 %collective-permute-start.18 = (f32[3,8,128]{2,1,0:T(8,128)S(1)}, f32[3,8,128]{2,1,0:T(8,128)S(1)}, u32[]{:S(2)}, u32[]{:S(2)}) collective-permute-start(f32[3,8,128]{2,1,0:T(8,128)S(1)} %select_add_fusion.1.own.k2), channel_id=1, source_target_pairs={{0,31},{1,0},{2,1},{3,2},{4,3},{5,4},{6,5},{7,6},{8,7},{9,8},{10,9... | collective-permute-start | bytes 36872 | tf_op jit(solution)/shard_map/ppermute | solution.py:21
  79.8 0.0 collective-permute-start.17
  79.8 1.9 %collective-permute-start.16 = (f32[3,8,128]{2,1,0:T(8,128)S(1)}, f32[3,8,128]{2,1,0:T(8,128)S(1)}, u32[]{:S(2)}, u32[]{:S(2)}) collective-permute-start(f32[3,8,128]{2,1,0:T(8,128)S(1)} %select_add_fusion.1.own.k2), channel_id=1, source_target_pairs={{0,32},{32,64},{64,96},{96,128},{128,160},{160,192},{192,224},{224... | collective-permute-start | bytes 36872 | tf_op jit(solution)/shard_map/ppermute | solution.py:21
  81.8 0.0 collective-permute-done.19.from_axial_up
  81.8 0.0 collective-permute-done.18.from_cross_up.u2
  81.8 0.0 collective-permute-done.17.from_cross_dn.d2
  81.8 5.8 %collective-permute-done.16.from_axial_dn = f32[3,8,128]{2,1,0:T(8,128)S(1)} collective-permute-done((f32[3,8,128]{2,1,0:T(8,128)S(1)}, f32[3,8,128]{2,1,0:T(8,128)S(1)}, u32[]{:S(2)}, u32[]{:S(2)}) %collective-permute-start.16) | collective-permute-done | bytes 12320 | tf_op jit(solution)/shard_map/ppermute | solution.py:21
  87.6 2.1 %shard_map.88 = (f32[3,8,128]{2,1,0:T(8,128)S(1)}, f32[3,8,128]{2,1,0:T(8,128)S(1)}, f32[3,8,128]{2,1,0:T(8,128)S(1)}, f32[3,8,128]{2,1,0:T(8,128)S(1)}, f32[3,8,128]{2,1,0:T(8,128)S(1)}, /*index=5*/f32[8,128]{1,0:T(8,128)S(1)}) custom-call(s32[8,8]{1,0:T(8,128)S(1)} %bitcast.21, f32[3,8,128]{2,1,0:T(8,128)S(1)} %select_add_fusion.1.own.k2, ...), custom_call_target="tpu_custom_call" | custom-call | tf_op jit(solution)/shard_map/pallas_call | solution.py:111
  89.7 0.6 broadcast_in_dim.38
  90.3 3.5 %all-to-all-start = ((f32[16,8,128]{2,1,0:T(8,128)}), f32[16,8,128]{2,1,0:T(8,128)S(1)}, u32[]{:S(2)}, u32[]{:S(2)}) async-start(f32[16,8,128]{2,1,0:T(8,128)} %broadcast_in_dim.38), calls=%async_computation | async-start | bytes 131072 | tf_op jit(solution)/shard_map/all_to_all | solution.py:273
  93.8 3.1 %collective-permute-start.20 = (f32[3,8,128]{2,1,0:T(8,128)S(1)}, f32[3,8,128]{2,1,0:T(8,128)S(1)}, u32[]{:S(2)}, u32[]{:S(2)}) collective-permute-start(f32[3,8,128]{2,1,0:T(8,128)S(1)} %get-tuple-element.52), channel_id=1, source_target_pairs={{0,32},{32,64},{64,96},{96,128},{128,160},{160,192},{192,224},{224... | collective-permute-start | bytes 36872 | tf_op jit(solution)/shard_map/ppermute | solution.py:21
  97.0 5.5 %collective-permute-start.21 = (f32[3,8,128]{2,1,0:T(8,128)S(1)}, f32[3,8,128]{2,1,0:T(8,128)S(1)}, u32[]{:S(2)}, u32[]{:S(2)}) collective-permute-start(f32[3,8,128]{2,1,0:T(8,128)S(1)} %get-tuple-element.53), channel_id=1, source_target_pairs={{0,480},{32,0},{64,32},{96,64},{128,96},{160,128},{192,160},{224,1... | collective-permute-start | bytes 36872 | tf_op jit(solution)/shard_map/ppermute | solution.py:21
  102.4 0.0 all-to-all-done
  102.5 0.0 collective-permute-done.20
  102.5 0.8 collective-permute-done.21
  103.2 0.6 broadcast_in_dim.39
  103.9 9.9 %all-to-all-start.1 = ((f32[32,8,128]{2,1,0:T(8,128)}), f32[32,8,128]{2,1,0:T(8,128)S(1)}, u32[]{:S(2)}, u32[]{:S(2)}) async-start(f32[32,8,128]{2,1,0:T(8,128)} %broadcast_in_dim.39), calls=%async_computation.1 | async-start | bytes 262144 | tf_op jit(solution)/shard_map/all_to_all | solution.py:273
  113.8 1.6 %collective-permute-start.22 = (f32[3,8,128]{2,1,0:T(8,128)S(1)}, f32[3,8,128]{2,1,0:T(8,128)S(1)}, u32[]{:S(2)}, u32[]{:S(2)}) collective-permute-start(f32[3,8,128]{2,1,0:T(8,128)S(1)} %get-tuple-element.58), channel_id=1, source_target_pairs={{0,1},{1,2},{2,3},{3,4},{4,5},{5,6},{6,7},{7,8},{8,9},{9,10},{10,1... | collective-permute-start | bytes 36872 | tf_op jit(solution)/shard_map/ppermute | solution.py:21
  115.4 0.8 collective-permute-done.22
  116.2 3.9 %collective-permute-done.23 = f32[3,8,128]{2,1,0:T(8,128)S(1)} collective-permute-done((f32[3,8,128]{2,1,0:T(8,128)S(1)}, f32[3,8,128]{2,1,0:T(8,128)S(1)}, u32[]{:S(2)}, u32[]{:S(2)}) %collective-permute-start.23) | collective-permute-done | bytes 12320 | tf_op jit(solution)/shard_map/ppermute | solution.py:21
  120.1 9.4 %all-to-all-done.1.sums = f32[32,8,128]{2,1,0:T(8,128)S(1)} async-done(((f32[32,8,128]{2,1,0:T(8,128)}), f32[32,8,128]{2,1,0:T(8,128)S(1)}, u32[]{:S(2)}, u32[]{:S(2)}) %all-to-all-start.1) | async-done | bytes 131104 | tf_op jit(solution)/shard_map/all_to_all | solution.py:273
  129.6 0.9 shard_map.89
  (12 shorter events, 0.1 us)
Async XLA Ops:
  0.6 18.2 %copy-start.1 = (s32[1,1,8,8]{3,2,1,0:T(8,128)S(1)}, s32[1,1,8,8]{3,2,1,0:T(8,128)}, u32[]{:S(2)}) copy-start(s32[1,1,8,8]{3,2,1,0:T(8,128)} %param.9) | copy-start | bytes 772
  0.6 16.6 %collective-permute-start.3 = (f32[3,8,128]{2,1,0:T(8,128)}, f32[3,8,128]{2,1,0:T(8,128)S(1)}, u32[]{:S(2)}, u32[]{:S(2)}) collective-permute-start(f32[3,8,128]{2,1,0:T(8,128)} %bitcast.22), channel_id=1, source_target_pairs={{0,480},{32,0},{64,32},{96,64},{128,96},{160,128},{192,160},{224,1... | collective-permute-start | bytes 36872 | tf_op jit(solution)/shard_map/ppermute | solution.py:21
  8.3 8.9 %collective-permute-start.2 = (f32[3,8,128]{2,1,0:T(8,128)}, f32[3,8,128]{2,1,0:T(8,128)S(1)}, u32[]{:S(2)}, u32[]{:S(2)}) collective-permute-start(f32[3,8,128]{2,1,0:T(8,128)} %bitcast.23), channel_id=1, source_target_pairs={{0,31},{1,0},{2,1},{3,2},{4,3},{5,4},{6,5},{7,6},{8,7},{9,8},{10,9... | collective-permute-start | bytes 36872 | tf_op jit(solution)/shard_map/ppermute | solution.py:21
  9.5 9.4 %collective-permute-start.1 = (f32[3,8,128]{2,1,0:T(8,128)}, f32[3,8,128]{2,1,0:T(8,128)S(1)}, u32[]{:S(2)}, u32[]{:S(2)}) collective-permute-start(f32[3,8,128]{2,1,0:T(8,128)} %bitcast.24), channel_id=1, source_target_pairs={{0,1},{1,2},{2,3},{3,4},{4,5},{5,6},{6,7},{7,8},{8,9},{9,10},{10,1... | collective-permute-start | bytes 36872 | tf_op jit(solution)/shard_map/ppermute | solution.py:21
  10.8 8.0 %collective-permute-start = (f32[3,8,128]{2,1,0:T(8,128)}, f32[3,8,128]{2,1,0:T(8,128)S(1)}, u32[]{:S(2)}, u32[]{:S(2)}) collective-permute-start(f32[3,8,128]{2,1,0:T(8,128)} %bitcast.25), channel_id=1, source_target_pairs={{0,32},{32,64},{64,96},{96,128},{128,160},{160,192},{192,224},{224... | collective-permute-start | bytes 36872 | tf_op jit(solution)/shard_map/ppermute | solution.py:21
  14.0 1.6 %copy-start = (bf16[1,1,8,8,128,128]{5,4,3,2,1,0:T(8,128)(2,1)S(1)}, bf16[1,1,8,8,128,128]{5,4,3,2,1,0:T(8,128)(2,1)}, u32[]{:S(2)}) copy-start(bf16[1,1,8,8,128,128]{5,4,3,2,1,0:T(8,128)(2,1)} %param.8) | copy-start | bytes 6291460
  15.6 0.7 copy-start.2
  16.3 0.7 copy-start.3
  20.9 17.7 %collective-permute-start.6 = (f32[4,8,128]{2,1,0:T(8,128)S(1)}, f32[4,8,128]{2,1,0:T(8,128)S(1)}, u32[]{:S(2)}, u32[]{:S(2)}) collective-permute-start(f32[4,8,128]{2,1,0:T(8,128)S(1)} %get-tuple-element.39), channel_id=1, source_target_pairs={{0,1},{1,2},{2,3},{3,4},{4,5},{5,6},{6,7},{7,8},{8,9},{9,10},{10,1... | collective-permute-start | bytes 49160 | tf_op jit(solution)/shard_map/ppermute | solution.py:21
  22.5 16.1 %collective-permute-start.7 = (f32[4,8,128]{2,1,0:T(8,128)S(1)}, f32[4,8,128]{2,1,0:T(8,128)S(1)}, u32[]{:S(2)}, u32[]{:S(2)}) collective-permute-start(f32[4,8,128]{2,1,0:T(8,128)S(1)} %get-tuple-element.40), channel_id=1, source_target_pairs={{0,31},{1,0},{2,1},{3,2},{4,3},{5,4},{6,5},{7,6},{8,7},{9,8},{10,9... | collective-permute-start | bytes 49160 | tf_op jit(solution)/shard_map/ppermute | solution.py:21
  29.2 8.6 %collective-permute-start.4 = (f32[3,8,128]{2,1,0:T(8,128)S(1)}, f32[3,8,128]{2,1,0:T(8,128)S(1)}, u32[]{:S(2)}, u32[]{:S(2)}) collective-permute-start(f32[3,8,128]{2,1,0:T(8,128)S(1)} %get-tuple-element.37), channel_id=1, source_target_pairs={{0,32},{32,64},{64,96},{96,128},{128,160},{160,192},{192,224},{224... | collective-permute-start | bytes 36872 | tf_op jit(solution)/shard_map/ppermute | solution.py:21
  31.1 7.5 %collective-permute-start.5 = (f32[3,8,128]{2,1,0:T(8,128)S(1)}, f32[3,8,128]{2,1,0:T(8,128)S(1)}, u32[]{:S(2)}, u32[]{:S(2)}) collective-permute-start(f32[3,8,128]{2,1,0:T(8,128)S(1)} %get-tuple-element.38), channel_id=1, source_target_pairs={{0,480},{32,0},{64,32},{96,64},{128,96},{160,128},{192,160},{224,1... | collective-permute-start | bytes 36872 | tf_op jit(solution)/shard_map/ppermute | solution.py:21
  38.6 13.5 %collective-permute-start.11 = (f32[3,8,128]{2,1,0:T(8,128)S(1)}, f32[3,8,128]{2,1,0:T(8,128)S(1)}, u32[]{:S(2)}, u32[]{:S(2)}) collective-permute-start(f32[3,8,128]{2,1,0:T(8,128)S(1)} %fusion.own.k1), channel_id=1, source_target_pairs={{0,480},{32,0},{64,32},{96,64},{128,96},{160,128},{192,160},{224,1... | collective-permute-start | bytes 36872 | tf_op jit(solution)/shard_map/ppermute | solution.py:21
  45.6 6.6 %collective-permute-start.10 = (f32[3,8,128]{2,1,0:T(8,128)S(1)}, f32[3,8,128]{2,1,0:T(8,128)S(1)}, u32[]{:S(2)}, u32[]{:S(2)}) collective-permute-start(f32[3,8,128]{2,1,0:T(8,128)S(1)} %fusion.own.k1), channel_id=1, source_target_pairs={{0,31},{1,0},{2,1},{3,2},{4,3},{5,4},{6,5},{7,6},{8,7},{9,8},{10,9... | collective-permute-start | bytes 36872 | tf_op jit(solution)/shard_map/ppermute | solution.py:21
  50.2 1.9 %collective-permute-start.9 = (f32[3,8,128]{2,1,0:T(8,128)S(1)}, f32[3,8,128]{2,1,0:T(8,128)S(1)}, u32[]{:S(2)}, u32[]{:S(2)}) collective-permute-start(f32[3,8,128]{2,1,0:T(8,128)S(1)} %fusion.own.k1), channel_id=1, source_target_pairs={{0,1},{1,2},{2,3},{3,4},{4,5},{5,6},{6,7},{7,8},{8,9},{9,10},{10,1... | collective-permute-start | bytes 36872 | tf_op jit(solution)/shard_map/ppermute | solution.py:21
  50.2 7.7 %collective-permute-start.8 = (f32[3,8,128]{2,1,0:T(8,128)S(1)}, f32[3,8,128]{2,1,0:T(8,128)S(1)}, u32[]{:S(2)}, u32[]{:S(2)}) collective-permute-start(f32[3,8,128]{2,1,0:T(8,128)S(1)} %fusion.own.k1), channel_id=1, source_target_pairs={{0,32},{32,64},{64,96},{96,128},{128,160},{160,192},{192,224},{224... | collective-permute-start | bytes 36872 | tf_op jit(solution)/shard_map/ppermute | solution.py:21
  60.1 10.9 %collective-permute-start.12 = (f32[3,8,128]{2,1,0:T(8,128)S(1)}, f32[3,8,128]{2,1,0:T(8,128)S(1)}, u32[]{:S(2)}, u32[]{:S(2)}) collective-permute-start(f32[3,8,128]{2,1,0:T(8,128)S(1)} %get-tuple-element.43), channel_id=1, source_target_pairs={{0,32},{32,64},{64,96},{96,128},{128,160},{160,192},{192,224},{224... | collective-permute-start | bytes 36872 | tf_op jit(solution)/shard_map/ppermute | solution.py:21
  62.0 9.0 %collective-permute-start.13 = (f32[3,8,128]{2,1,0:T(8,128)S(1)}, f32[3,8,128]{2,1,0:T(8,128)S(1)}, u32[]{:S(2)}, u32[]{:S(2)}) collective-permute-start(f32[3,8,128]{2,1,0:T(8,128)S(1)} %get-tuple-element.44), channel_id=1, source_target_pairs={{0,480},{32,0},{64,32},{96,64},{128,96},{160,128},{192,160},{224,1... | collective-permute-start | bytes 36872 | tf_op jit(solution)/shard_map/ppermute | solution.py:21
  68.7 2.9 %collective-permute-start.14 = (f32[3,8,128]{2,1,0:T(8,128)S(1)}, f32[3,8,128]{2,1,0:T(8,128)S(1)}, u32[]{:S(2)}, u32[]{:S(2)}) collective-permute-start(f32[3,8,128]{2,1,0:T(8,128)S(1)} %get-tuple-element.45), channel_id=1, source_target_pairs={{0,1},{1,2},{2,3},{3,4},{4,5},{5,6},{6,7},{7,8},{8,9},{9,10},{10,1... | collective-permute-start | bytes 36872 | tf_op jit(solution)/shard_map/ppermute | solution.py:21
  68.7 3.1 %collective-permute-start.15 = (f32[3,8,128]{2,1,0:T(8,128)S(1)}, f32[3,8,128]{2,1,0:T(8,128)S(1)}, u32[]{:S(2)}, u32[]{:S(2)}) collective-permute-start(f32[3,8,128]{2,1,0:T(8,128)S(1)} %get-tuple-element.46), channel_id=1, source_target_pairs={{0,31},{1,0},{2,1},{3,2},{4,3},{5,4},{6,5},{7,6},{8,7},{9,8},{10,9... | collective-permute-start | bytes 36872 | tf_op jit(solution)/shard_map/ppermute | solution.py:21
  71.8 9.9 %collective-permute-start.19 = (f32[3,8,128]{2,1,0:T(8,128)S(1)}, f32[3,8,128]{2,1,0:T(8,128)S(1)}, u32[]{:S(2)}, u32[]{:S(2)}) collective-permute-start(f32[3,8,128]{2,1,0:T(8,128)S(1)} %select_add_fusion.1.own.k2), channel_id=1, source_target_pairs={{0,480},{32,0},{64,32},{96,64},{128,96},{160,128},{192,160},{224,1... | collective-permute-start | bytes 36872 | tf_op jit(solution)/shard_map/ppermute | solution.py:21
  76.5 5.3 %collective-permute-start.18 = (f32[3,8,128]{2,1,0:T(8,128)S(1)}, f32[3,8,128]{2,1,0:T(8,128)S(1)}, u32[]{:S(2)}, u32[]{:S(2)}) collective-permute-start(f32[3,8,128]{2,1,0:T(8,128)S(1)} %select_add_fusion.1.own.k2), channel_id=1, source_target_pairs={{0,31},{1,0},{2,1},{3,2},{4,3},{5,4},{6,5},{7,6},{8,7},{9,8},{10,9... | collective-permute-start | bytes 36872 | tf_op jit(solution)/shard_map/ppermute | solution.py:21
  79.8 1.9 %collective-permute-start.17 = (f32[3,8,128]{2,1,0:T(8,128)S(1)}, f32[3,8,128]{2,1,0:T(8,128)S(1)}, u32[]{:S(2)}, u32[]{:S(2)}) collective-permute-start(f32[3,8,128]{2,1,0:T(8,128)S(1)} %select_add_fusion.1.own.k2), channel_id=1, source_target_pairs={{0,1},{1,2},{2,3},{3,4},{4,5},{5,6},{6,7},{7,8},{8,9},{9,10},{10,1... | collective-permute-start | bytes 36872 | tf_op jit(solution)/shard_map/ppermute | solution.py:21
  79.8 7.7 %collective-permute-start.16 = (f32[3,8,128]{2,1,0:T(8,128)S(1)}, f32[3,8,128]{2,1,0:T(8,128)S(1)}, u32[]{:S(2)}, u32[]{:S(2)}) collective-permute-start(f32[3,8,128]{2,1,0:T(8,128)S(1)} %select_add_fusion.1.own.k2), channel_id=1, source_target_pairs={{0,32},{32,64},{64,96},{96,128},{128,160},{160,192},{192,224},{224... | collective-permute-start | bytes 36872 | tf_op jit(solution)/shard_map/ppermute | solution.py:21
  90.3 12.1 %all-to-all-start = ((f32[16,8,128]{2,1,0:T(8,128)}), f32[16,8,128]{2,1,0:T(8,128)S(1)}, u32[]{:S(2)}, u32[]{:S(2)}) async-start(f32[16,8,128]{2,1,0:T(8,128)} %broadcast_in_dim.38), calls=%async_computation | async-start | bytes 131072 | tf_op jit(solution)/shard_map/all_to_all | solution.py:273
  93.8 8.7 %collective-permute-start.20 = (f32[3,8,128]{2,1,0:T(8,128)S(1)}, f32[3,8,128]{2,1,0:T(8,128)S(1)}, u32[]{:S(2)}, u32[]{:S(2)}) collective-permute-start(f32[3,8,128]{2,1,0:T(8,128)S(1)} %get-tuple-element.52), channel_id=1, source_target_pairs={{0,32},{32,64},{64,96},{96,128},{128,160},{160,192},{192,224},{224... | collective-permute-start | bytes 36872 | tf_op jit(solution)/shard_map/ppermute | solution.py:21
  97.0 6.3 %collective-permute-start.21 = (f32[3,8,128]{2,1,0:T(8,128)S(1)}, f32[3,8,128]{2,1,0:T(8,128)S(1)}, u32[]{:S(2)}, u32[]{:S(2)}) collective-permute-start(f32[3,8,128]{2,1,0:T(8,128)S(1)} %get-tuple-element.53), channel_id=1, source_target_pairs={{0,480},{32,0},{64,32},{96,64},{128,96},{160,128},{192,160},{224,1... | collective-permute-start | bytes 36872 | tf_op jit(solution)/shard_map/ppermute | solution.py:21
  103.9 25.7 %all-to-all-start.1 = ((f32[32,8,128]{2,1,0:T(8,128)}), f32[32,8,128]{2,1,0:T(8,128)S(1)}, u32[]{:S(2)}, u32[]{:S(2)}) async-start(f32[32,8,128]{2,1,0:T(8,128)} %broadcast_in_dim.39), calls=%async_computation.1 | async-start | bytes 262144 | tf_op jit(solution)/shard_map/all_to_all | solution.py:273
  113.8 2.5 %collective-permute-start.22 = (f32[3,8,128]{2,1,0:T(8,128)S(1)}, f32[3,8,128]{2,1,0:T(8,128)S(1)}, u32[]{:S(2)}, u32[]{:S(2)}) collective-permute-start(f32[3,8,128]{2,1,0:T(8,128)S(1)} %get-tuple-element.58), channel_id=1, source_target_pairs={{0,1},{1,2},{2,3},{3,4},{4,5},{5,6},{6,7},{7,8},{8,9},{9,10},{10,1... | collective-permute-start | bytes 36872 | tf_op jit(solution)/shard_map/ppermute | solution.py:21
  115.4 4.7 %collective-permute-start.23 = (f32[3,8,128]{2,1,0:T(8,128)S(1)}, f32[3,8,128]{2,1,0:T(8,128)S(1)}, u32[]{:S(2)}, u32[]{:S(2)}) collective-permute-start(f32[3,8,128]{2,1,0:T(8,128)S(1)} %get-tuple-element.59), channel_id=1, source_target_pairs={{0,31},{1,0},{2,1},{3,2},{4,3},{5,4},{6,5},{7,6},{8,7},{9,8},{10,9... | collective-permute-start | bytes 36872 | tf_op jit(solution)/shard_map/ppermute | solution.py:21

commit v3 on v2

--- a/solution.py
+++ b/solution.py
@@ -97,17 +97,19 @@
         to_cross_dn[3] = carried[...]
         to_cross_up[3] = carried[...]
     else:
-        moments[...] = jnp.where(
+        merged = jnp.where(
             rows == 2 * sweep, even, jnp.where(rows == 2 * sweep + 1, odd, carried[...])
         )
-
-
-def operator_call(sweep, ids, sources, tiles, drag, carried):
+        moments[...] = jnp.broadcast_to(merged, moments.shape)
+
+
+def operator_call(sweep, ids, sources, tiles, drag, carried, copies):
     blocks, width = drag.shape
     vmem = pl.BlockSpec(memory_space=pltpu.VMEM)
     field = jax.ShapeDtypeStruct((3, blocks, width), jnp.float32)
     across = jax.ShapeDtypeStruct((4 if sweep == 0 else 3, blocks, width), jnp.float32)
-    plane = jax.ShapeDtypeStruct((SUB, width), jnp.float32)
+    plane = (SUB, width) if copies is None else (copies, SUB, width)
+    plane = jax.ShapeDtypeStruct(plane, jnp.float32)
     return pl.pallas_call(
         functools.partial(operator_kernel, sweep),
         in_specs=[pl.BlockSpec(memory_space=pltpu.SMEM)] + [vmem] * 8,
@@ -267,10 +269,16 @@
     return jnp.concatenate([to_lower, to_upper, rest], axis=0)
 
 
-def spread_sum(part, axis):
-    count = lax.axis_size(axis)
-    copies = jnp.broadcast_to(part[None], (count,) + part.shape)
-    return lax.all_to_all(copies, axis, 0, 0)
+def spread_sum(part, key):
+    axial, cross = lax.axis_size("axial"), lax.axis_size("cross")
+    groups = {}
+    for a in range(axial):
+        for c in range(cross):
+            groups.setdefault(key(a, c), []).append(a * cross + c)
+    groups = list(groups.values())
+    if part.ndim == 2:
+        part = jnp.broadcast_to(part[None], (len(groups[0]),) + part.shape)
+    return lax.all_to_all(part, ("axial", "cross"), 0, 0, axis_index_groups=groups)
 
 
 def on_device(force, self_drag, tiles, tile_ids, mig_rows, mig_count):
@@ -294,19 +302,21 @@
         below.append(cross_dn)
         above.append(cross_up)
         r1, r3, r5, r7, kept, carried = operator_call(
-            sweep, ids, (now, axial_dn, cross_dn, cross_up, axial_up), held, drag, carried
+            sweep, ids, (now, axial_dn, cross_dn, cross_up, axial_up), held, drag, carried,
+            2 * lax.axis_size("axial") if sweep == ITERS - 1 else None,
         )
+        if sweep == ITERS - 1:
+            part = jnp.sum(spread_sum(carried, lambda a, c: c // 2), axis=0)
+            part, r1, r7 = lax.optimization_barrier((part, r1, r7))
+        from_lower_cross = ring_shift(r5, "cross", 1)
+        from_upper_cross = ring_shift(r3, "cross", -1)
+        if sweep == ITERS - 1:
+            part, from_lower_cross, from_upper_cross = lax.optimization_barrier(
+                (part, from_lower_cross, from_upper_cross)
+            )
+            sums = spread_sum(part, lambda a, c: (a, c % 2))
         from_lower_axial = ring_shift(r7, "axial", 1)
         from_upper_axial = ring_shift(r1, "axial", -1)
-        if sweep == ITERS - 1:
-            part = jnp.sum(spread_sum(carried, "axial"), axis=0)
-            part, r3, r5 = lax.optimization_barrier((part, r3, r5))
-            part, from_lower_axial, from_upper_axial = lax.optimization_barrier(
-                (part, from_lower_axial, from_upper_axial)
-            )
-            sums = spread_sum(part, "cross")
-        from_lower_cross = ring_shift(r5, "cross", 1)
-        from_upper_cross = ring_shift(r3, "cross", -1)
         if sweep == 0:
             planes = [from_lower_cross, from_upper_cross]
         now = kept + from_lower_axial + from_upper_axial

time: 132 us -> 124 us (0.939)
  waiting for transfers between devices: 29.8 us -> 25.1 us
  starting transfers between devices: 87.2 us -> 84.6 us
    ppermute x24, waiting for transfers between devices: 20.4 us -> 15.7 us  [ring_shift(): return lax.ppermute(shard, axis, ring(lax.axis_size(axis), by))]
    all_to_all x2, starting transfers between devices: 13.4 us -> 11.9 us  [spread_sum(): lax.all_to_all(part, ('axial', 'cross'), 0, 0, axis_index_groups=groups)]
  transfers between devices with their start and end apart: 26 -> 26, of which waited for: 10 -> 9; matrix products, arithmetic and copies ran while one was open for 1% -> 1% of each run, Pallas kernels for 0% -> 0%
where the time goes in v3:
time: 124 us; the launch traced here: 123 us
  starting transfers between devices  84.6 us (68%)
  waiting for transfers between devices  25.1 us (20%)
  Pallas kernels  7.73 us (6%)
  local copies, waits for them, and re-layouts  3.7 us (3%)
    ppermute x24, starting transfers between devices, ring_shift(): return lax.ppermute(shard, axis, ring(lax.axis_size(axis), by))  72.7 us
    ppermute x24, waiting for transfers between devices, ring_shift(): return lax.ppermute(shard, axis, ring(lax.axis_size(axis), by))  15.7 us
    all_to_all x2, starting transfers between devices, spread_sum(): lax.all_to_all(part, ('axial', 'cross'), 0, 0, axis_index_groups=groups)  11.9 us
    all_to_all x2, waiting for transfers between devices, spread_sum(): lax.all_to_all(part, ('axial', 'cross'), 0, 0, axis_index_groups=groups)  9.37 us
    pallas_call x3, Pallas kernels, operator_call(): pl.pallas_call(functools.partial(operator_kernel, sweep), in_specs=[pl.Bl...  6.67 us
    unnamed x8, local copies, waits for them, and re-layouts  2.99 us
  transfers between devices with their start and end apart: 26, of which 9 were waited for; matrix products, arithmetic and copies ran while one was open for 1% of the time, Pallas kernels for 0%

profile of v3, /device:TPU:1, one launch (start us, length us, event | category | flops | bytes accessed | tf_op | source)
XLA Modules:
  0.0 122.9 jit_solution(4725086809694156689)
XLA Ops:
  0.6 7.7 %collective-permute-start.3 = (f32[3,8,128]{2,1,0:T(8,128)}, f32[3,8,128]{2,1,0:T(8,128)S(1)}, u32[]{:S(2)}, u32[]{:S(2)}) collective-permute-start(f32[3,8,128]{2,1,0:T(8,128)} %bitcast.22), channel_id=1, source_target_pairs={{0,480},{32,0},{64,32},{96,64},{128,96},{160,128},{192,160},{224,1... | collective-permute-start | bytes 36872 | tf_op jit(solution)/shard_map/ppermute | solution.py:21
  8.3 1.1 collective-permute-start.2
  9.5 1.4 %collective-permute-start.1 = (f32[3,8,128]{2,1,0:T(8,128)}, f32[3,8,128]{2,1,0:T(8,128)S(1)}, u32[]{:S(2)}, u32[]{:S(2)}) collective-permute-start(f32[3,8,128]{2,1,0:T(8,128)} %bitcast.24), channel_id=1, source_target_pairs={{0,1},{1,2},{2,3},{3,4},{4,5},{5,6},{6,7},{7,8},{8,9},{9,10},{10,1... | collective-permute-start | bytes 36872 | tf_op jit(solution)/shard_map/ppermute | solution.py:21
  10.8 2.3 %collective-permute-start = (f32[3,8,128]{2,1,0:T(8,128)}, f32[3,8,128]{2,1,0:T(8,128)S(1)}, u32[]{:S(2)}, u32[]{:S(2)}) collective-permute-start(f32[3,8,128]{2,1,0:T(8,128)} %bitcast.25), channel_id=1, source_target_pairs={{0,32},{32,64},{64,96},{96,128},{128,160},{160,192},{192,224},{224... | collective-permute-start | bytes 36872 | tf_op jit(solution)/shard_map/ppermute | solution.py:21
  13.1 0.8 fusion.4
  13.9 0.1 pad.4.clone
  13.9 0.1 fusion.2.carried
  14.0 1.6 %copy-done = bf16[1,1,8,8,128,128]{5,4,3,2,1,0:T(8,128)(2,1)S(1)} copy-done((bf16[1,1,8,8,128,128]{5,4,3,2,1,0:T(8,128)(2,1)S(1)}, bf16[1,1,8,8,128,128]{5,4,3,2,1,0:T(8,128)(2,1)}, u32[]{:S(2)}) %copy-start) | copy-done | bytes 2097176
  15.6 0.7 copy-done.2
  16.3 0.7 copy-done.3
  17.0 0.2 shard_map.85
  17.2 0.0 collective-permute-done.3.from_axial_up
  17.2 0.0 collective-permute-done.2.from_cross_up.u0
  17.2 1.6 %collective-permute-done.1.from_cross_dn.d0 = f32[3,8,128]{2,1,0:T(8,128)S(1)} collective-permute-done((f32[3,8,128]{2,1,0:T(8,128)}, f32[3,8,128]{2,1,0:T(8,128)S(1)}, u32[]{:S(2)}, u32[]{:S(2)}) %collective-permute-start.1) | collective-permute-done | bytes 12320 | tf_op jit(solution)/shard_map/ppermute | solution.py:21
  18.8 0.0 collective-permute-done.from_axial_dn
  18.8 2.1 %shard_map.86 = (f32[3,8,128]{2,1,0:T(8,128)S(1)}, f32[4,8,128]{2,1,0:T(8,128)S(1)}, f32[4,8,128]{2,1,0:T(8,128)S(1)}, f32[3,8,128]{2,1,0:T(8,128)S(1)}, f32[3,8,128]{2,1,0:T(8,128)S(1)}, /*index=5*/f32[8,128]{1,0:T(8,128)S(1)}) custom-call(s32[8,8]{1,0:T(8,128)S(1)} %bitcast.19, f32[3,8,128]{2,1,0:T(8,128)S(1)} %get-tuple-element.33.own.k0, ...), custom_call_target="tpu_custom_call" | custom-call | tf_op jit(solution)/shard_map/pallas_call | solution.py:113
  20.9 1.6 %collective-permute-start.6 = (f32[4,8,128]{2,1,0:T(8,128)S(1)}, f32[4,8,128]{2,1,0:T(8,128)S(1)}, u32[]{:S(2)}, u32[]{:S(2)}) collective-permute-start(f32[4,8,128]{2,1,0:T(8,128)S(1)} %get-tuple-element.39), channel_id=1, source_target_pairs={{0,1},{1,2},{2,3},{3,4},{4,5},{5,6},{6,7},{7,8},{8,9},{9,10},{10,1... | collective-permute-start | bytes 49160 | tf_op jit(solution)/shard_map/ppermute | solution.py:21
  22.5 6.6 %collective-permute-start.7 = (f32[4,8,128]{2,1,0:T(8,128)S(1)}, f32[4,8,128]{2,1,0:T(8,128)S(1)}, u32[]{:S(2)}, u32[]{:S(2)}) collective-permute-start(f32[4,8,128]{2,1,0:T(8,128)S(1)} %get-tuple-element.40), channel_id=1, source_target_pairs={{0,31},{1,0},{2,1},{3,2},{4,3},{5,4},{6,5},{7,6},{8,7},{9,8},{10,9... | collective-permute-start | bytes 49160 | tf_op jit(solution)/shard_map/ppermute | solution.py:21
  29.2 1.9 %collective-permute-start.4 = (f32[3,8,128]{2,1,0:T(8,128)S(1)}, f32[3,8,128]{2,1,0:T(8,128)S(1)}, u32[]{:S(2)}, u32[]{:S(2)}) collective-permute-start(f32[3,8,128]{2,1,0:T(8,128)S(1)} %get-tuple-element.37), channel_id=1, source_target_pairs={{0,32},{32,64},{64,96},{96,128},{128,160},{160,192},{192,224},{224... | collective-permute-start | bytes 36872 | tf_op jit(solution)/shard_map/ppermute | solution.py:21
  31.1 6.7 %collective-permute-start.5 = (f32[3,8,128]{2,1,0:T(8,128)S(1)}, f32[3,8,128]{2,1,0:T(8,128)S(1)}, u32[]{:S(2)}, u32[]{:S(2)}) collective-permute-start(f32[3,8,128]{2,1,0:T(8,128)S(1)} %get-tuple-element.38), channel_id=1, source_target_pairs={{0,480},{32,0},{64,32},{96,64},{128,96},{160,128},{192,160},{224,1... | collective-permute-start | bytes 36872 | tf_op jit(solution)/shard_map/ppermute | solution.py:21
  37.8 0.0 collective-permute-done.4
  37.8 0.8 collective-permute-done.5
  38.6 0.0 collective-permute-done.6.dn_plane
  38.6 0.0 collective-permute-done.7.up_plane
  38.6 6.9 %collective-permute-start.11 = (f32[3,8,128]{2,1,0:T(8,128)S(1)}, f32[3,8,128]{2,1,0:T(8,128)S(1)}, u32[]{:S(2)}, u32[]{:S(2)}) collective-permute-start(f32[3,8,128]{2,1,0:T(8,128)S(1)} %fusion.own.k1), channel_id=1, source_target_pairs={{0,480},{32,0},{64,32},{96,64},{128,96},{160,128},{192,160},{224,1... | collective-permute-start | bytes 36872 | tf_op jit(solution)/shard_map/ppermute | solution.py:21
  45.6 4.7 %collective-permute-start.10 = (f32[3,8,128]{2,1,0:T(8,128)S(1)}, f32[3,8,128]{2,1,0:T(8,128)S(1)}, u32[]{:S(2)}, u32[]{:S(2)}) collective-permute-start(f32[3,8,128]{2,1,0:T(8,128)S(1)} %fusion.own.k1), channel_id=1, source_target_pairs={{0,31},{1,0},{2,1},{3,2},{4,3},{5,4},{6,5},{7,6},{8,7},{9,8},{10,9... | collective-permute-start | bytes 36872 | tf_op jit(solution)/shard_map/ppermute | solution.py:21
  50.2 0.0 collective-permute-start.9
  50.2 1.9 %collective-permute-start.8 = (f32[3,8,128]{2,1,0:T(8,128)S(1)}, f32[3,8,128]{2,1,0:T(8,128)S(1)}, u32[]{:S(2)}, u32[]{:S(2)}) collective-permute-start(f32[3,8,128]{2,1,0:T(8,128)S(1)} %fusion.own.k1), channel_id=1, source_target_pairs={{0,32},{32,64},{64,96},{96,128},{128,160},{160,192},{192,224},{224... | collective-permute-start | bytes 36872 | tf_op jit(solution)/shard_map/ppermute | solution.py:21
  52.1 0.0 collective-permute-done.11.from_axial_up
  52.1 0.0 collective-permute-done.10.from_cross_up.u1
  52.2 0.0 collective-permute-done.9.from_cross_dn.d1
  52.2 5.8 %collective-permute-done.8.from_axial_dn = f32[3,8,128]{2,1,0:T(8,128)S(1)} collective-permute-done((f32[3,8,128]{2,1,0:T(8,128)S(1)}, f32[3,8,128]{2,1,0:T(8,128)S(1)}, u32[]{:S(2)}, u32[]{:S(2)}) %collective-permute-start.8) | collective-permute-done | bytes 12320 | tf_op jit(solution)/shard_map/ppermute | solution.py:21
  58.0 2.1 %shard_map.87 = (f32[3,8,128]{2,1,0:T(8,128)S(1)}, f32[3,8,128]{2,1,0:T(8,128)S(1)}, f32[3,8,128]{2,1,0:T(8,128)S(1)}, f32[3,8,128]{2,1,0:T(8,128)S(1)}, f32[3,8,128]{2,1,0:T(8,128)S(1)}, /*index=5*/f32[8,128]{1,0:T(8,128)S(1)}) custom-call(s32[8,8]{1,0:T(8,128)S(1)} %bitcast.20, f32[3,8,128]{2,1,0:T(8,128)S(1)} %fusion.own.k1, ...), custom_call_target="tpu_custom_call" | custom-call | tf_op jit(solution)/shard_map/pallas_call | solution.py:113
  60.1 1.9 %collective-permute-start.12 = (f32[3,8,128]{2,1,0:T(8,128)S(1)}, f32[3,8,128]{2,1,0:T(8,128)S(1)}, u32[]{:S(2)}, u32[]{:S(2)}) collective-permute-start(f32[3,8,128]{2,1,0:T(8,128)S(1)} %get-tuple-element.43), channel_id=1, source_target_pairs={{0,32},{32,64},{64,96},{96,128},{128,160},{160,192},{192,224},{224... | collective-permute-start | bytes 36872 | tf_op jit(solution)/shard_map/ppermute | solution.py:21
  62.0 6.7 %collective-permute-start.13 = (f32[3,8,128]{2,1,0:T(8,128)S(1)}, f32[3,8,128]{2,1,0:T(8,128)S(1)}, u32[]{:S(2)}, u32[]{:S(2)}) collective-permute-start(f32[3,8,128]{2,1,0:T(8,128)S(1)} %get-tuple-element.44), channel_id=1, source_target_pairs={{0,480},{32,0},{64,32},{96,64},{128,96},{160,128},{192,160},{224,1... | collective-permute-start | bytes 36872 | tf_op jit(solution)/shard_map/ppermute | solution.py:21
  68.7 0.0 collective-permute-start.14
  68.7 2.2 %collective-permute-start.15 = (f32[3,8,128]{2,1,0:T(8,128)S(1)}, f32[3,8,128]{2,1,0:T(8,128)S(1)}, u32[]{:S(2)}, u32[]{:S(2)}) collective-permute-start(f32[3,8,128]{2,1,0:T(8,128)S(1)} %get-tuple-element.46), channel_id=1, source_target_pairs={{0,31},{1,0},{2,1},{3,2},{4,3},{5,4},{6,5},{7,6},{8,7},{9,8},{10,9... | collective-permute-start | bytes 36872 | tf_op jit(solution)/shard_map/ppermute | solution.py:21
  70.9 0.0 collective-permute-done.12
  70.9 0.0 collective-permute-done.13
  70.9 0.6 collective-permute-done.14
  71.6 0.3 collective-permute-done.15
  71.8 4.6 %collective-permute-start.19 = (f32[3,8,128]{2,1,0:T(8,128)S(1)}, f32[3,8,128]{2,1,0:T(8,128)S(1)}, u32[]{:S(2)}, u32[]{:S(2)}) collective-permute-start(f32[3,8,128]{2,1,0:T(8,128)S(1)} %select_add_fusion.1.own.k2), channel_id=1, source_target_pairs={{0,480},{32,0},{64,32},{96,64},{128,96},{160,128},{192,160},{224,1... | collective-permute-start | bytes 36872 | tf_op jit(solution)/shard_map/ppermute | solution.py:21
  76.4 3.4 %collective-permute-start.18 = (f32[3,8,128]{2,1,0:T(8,128)S(1)}, f32[3,8,128]{2,1,0:T(8,128)S(1)}, u32[]{:S(2)}, u32[]{:S(2)}) collective-permute-start(f32[3,8,128]{2,1,0:T(8,128)S(1)} %select_add_fusion.1.own.k2), channel_id=1, source_target_pairs={{0,31},{1,0},{2,1},{3,2},{4,3},{5,4},{6,5},{7,6},{8,7},{9,8},{10,9... | collective-permute-start | bytes 36872 | tf_op jit(solution)/shard_map/ppermute | solution.py:21
  79.8 0.0 collective-permute-start.17
  79.8 1.9 %collective-permute-start.16 = (f32[3,8,128]{2,1,0:T(8,128)S(1)}, f32[3,8,128]{2,1,0:T(8,128)S(1)}, u32[]{:S(2)}, u32[]{:S(2)}) collective-permute-start(f32[3,8,128]{2,1,0:T(8,128)S(1)} %select_add_fusion.1.own.k2), channel_id=1, source_target_pairs={{0,32},{32,64},{64,96},{96,128},{128,160},{160,192},{192,224},{224... | collective-permute-start | bytes 36872 | tf_op jit(solution)/shard_map/ppermute | solution.py:21
  81.7 0.0 collective-permute-done.19.from_axial_up
  81.8 0.0 collective-permute-done.18.from_cross_up.u2
  81.8 0.0 collective-permute-done.17.from_cross_dn.d2
  81.8 5.8 %collective-permute-done.16.from_axial_dn = f32[3,8,128]{2,1,0:T(8,128)S(1)} collective-permute-done((f32[3,8,128]{2,1,0:T(8,128)S(1)}, f32[3,8,128]{2,1,0:T(8,128)S(1)}, u32[]{:S(2)}, u32[]{:S(2)}) %collective-permute-start.16) | collective-permute-done | bytes 12320 | tf_op jit(solution)/shard_map/ppermute | solution.py:21
  87.6 2.5 %shard_map.88 = (f32[3,8,128]{2,1,0:T(8,128)S(1)}, f32[3,8,128]{2,1,0:T(8,128)S(1)}, f32[3,8,128]{2,1,0:T(8,128)S(1)}, f32[3,8,128]{2,1,0:T(8,128)S(1)}, f32[3,8...) custom-call(s32[8,8]{1,0:T(8,128)S(1)} %bitcast.21, f32[3,8,128]{2,1,0:T(8,128)S(1)} %select_add_fusion.1.own.k2, ...), custom_call_target="tpu_custom_call" | custom-call | tf_op jit(solution)/shard_map/pallas_call | solution.py:113
  90.1 5.2 %all-to-all-start = ((f32[32,8,128]{2,1,0:T(8,128)}), f32[32,8,128]{2,1,0:T(8,128)S(1)}, u32[]{:S(2)}, u32[]{:S(2)}) async-start(f32[32,8,128]{2,1,0:T(8,128)} %get-tuple-element.48), calls=%async_computation | async-start | bytes 262144 | tf_op jit(solution)/shard_map/all_to_all | solution.py:281
  95.3 0.0 collective-permute-start.20
  95.3 0.5 collective-permute-start.21
  95.8 7.2 %all-to-all-done = f32[32,8,128]{2,1,0:T(8,128)S(1)} async-done(((f32[32,8,128]{2,1,0:T(8,128)}), f32[32,8,128]{2,1,0:T(8,128)S(1)}, u32[]{:S(2)}, u32[]{:S(2)}) %all-to-all-start) | async-done | bytes 131104 | tf_op jit(solution)/shard_map/all_to_all | solution.py:281
  103.0 0.0 collective-permute-done.20
  103.1 0.0 collective-permute-done.21
  103.1 0.6 broadcast_in_dim.32
  103.7 6.8 %all-to-all-start.1 = ((f32[16,8,128]{2,1,0:T(8,128)}), f32[16,8,128]{2,1,0:T(8,128)S(1)}, u32[]{:S(2)}, u32[]{:S(2)}) async-start(f32[16,8,128]{2,1,0:T(8,128)} %broadcast_in_dim.32), calls=%async_computation.1 | async-start | bytes 131072 | tf_op jit(solution)/shard_map/all_to_all | solution.py:281
  110.5 2.3 %collective-permute-start.22 = (f32[3,8,128]{2,1,0:T(8,128)S(1)}, f32[3,8,128]{2,1,0:T(8,128)S(1)}, u32[]{:S(2)}, u32[]{:S(2)}) collective-permute-start(f32[3,8,128]{2,1,0:T(8,128)S(1)} %get-tuple-element.56), channel_id=1, source_target_pairs={{0,32},{32,64},{64,96},{96,128},{128,160},{160,192},{192,224},{224... | collective-permute-start | bytes 36872 | tf_op jit(solution)/shard_map/ppermute | solution.py:21
  112.8 6.3 %collective-permute-start.23 = (f32[3,8,128]{2,1,0:T(8,128)S(1)}, f32[3,8,128]{2,1,0:T(8,128)S(1)}, u32[]{:S(2)}, u32[]{:S(2)}) collective-permute-start(f32[3,8,128]{2,1,0:T(8,128)S(1)} %get-tuple-element.57), channel_id=1, source_target_pairs={{0,480},{32,0},{64,32},{96,64},{128,96},{160,128},{192,160},{224,1... | collective-permute-start | bytes 36872 | tf_op jit(solution)/shard_map/ppermute | solution.py:21
  119.1 0.0 collective-permute-done.22
  119.1 0.8 collective-permute-done.23
  119.9 2.2 %all-to-all-done.1.sums = f32[16,8,128]{2,1,0:T(8,128)S(1)} async-done(((f32[16,8,128]{2,1,0:T(8,128)}), f32[16,8,128]{2,1,0:T(8,128)S(1)}, u32[]{:S(2)}, u32[]{:S(2)}) %all-to-all-start.1) | async-done | bytes 65568 | tf_op jit(solution)/shard_map/all_to_all | solution.py:281
  122.1 0.9 shard_map.89
  (11 shorter events, 0.1 us)
Async XLA Ops:
  0.6 18.2 %copy-start.1 = (s32[1,1,8,8]{3,2,1,0:T(8,128)S(1)}, s32[1,1,8,8]{3,2,1,0:T(8,128)}, u32[]{:S(2)}) copy-start(s32[1,1,8,8]{3,2,1,0:T(8,128)} %param.9) | copy-start | bytes 772
  0.6 16.6 %collective-permute-start.3 = (f32[3,8,128]{2,1,0:T(8,128)}, f32[3,8,128]{2,1,0:T(8,128)S(1)}, u32[]{:S(2)}, u32[]{:S(2)}) collective-permute-start(f32[3,8,128]{2,1,0:T(8,128)} %bitcast.22), channel_id=1, source_target_pairs={{0,480},{32,0},{64,32},{96,64},{128,96},{160,128},{192,160},{224,1... | collective-permute-start | bytes 36872 | tf_op jit(solution)/shard_map/ppermute | solution.py:21
  8.3 8.9 %collective-permute-start.2 = (f32[3,8,128]{2,1,0:T(8,128)}, f32[3,8,128]{2,1,0:T(8,128)S(1)}, u32[]{:S(2)}, u32[]{:S(2)}) collective-permute-start(f32[3,8,128]{2,1,0:T(8,128)} %bitcast.23), channel_id=1, source_target_pairs={{0,31},{1,0},{2,1},{3,2},{4,3},{5,4},{6,5},{7,6},{8,7},{9,8},{10,9... | collective-permute-start | bytes 36872 | tf_op jit(solution)/shard_map/ppermute | solution.py:21
  9.5 9.4 %collective-permute-start.1 = (f32[3,8,128]{2,1,0:T(8,128)}, f32[3,8,128]{2,1,0:T(8,128)S(1)}, u32[]{:S(2)}, u32[]{:S(2)}) collective-permute-start(f32[3,8,128]{2,1,0:T(8,128)} %bitcast.24), channel_id=1, source_target_pairs={{0,1},{1,2},{2,3},{3,4},{4,5},{5,6},{6,7},{7,8},{8,9},{9,10},{10,1... | collective-permute-start | bytes 36872 | tf_op jit(solution)/shard_map/ppermute | solution.py:21
  10.8 8.0 %collective-permute-start = (f32[3,8,128]{2,1,0:T(8,128)}, f32[3,8,128]{2,1,0:T(8,128)S(1)}, u32[]{:S(2)}, u32[]{:S(2)}) collective-permute-start(f32[3,8,128]{2,1,0:T(8,128)} %bitcast.25), channel_id=1, source_target_pairs={{0,32},{32,64},{64,96},{96,128},{128,160},{160,192},{192,224},{224... | collective-permute-start | bytes 36872 | tf_op jit(solution)/shard_map/ppermute | solution.py:21
  14.0 1.6 %copy-start = (bf16[1,1,8,8,128,128]{5,4,3,2,1,0:T(8,128)(2,1)S(1)}, bf16[1,1,8,8,128,128]{5,4,3,2,1,0:T(8,128)(2,1)}, u32[]{:S(2)}) copy-start(bf16[1,1,8,8,128,128]{5,4,3,2,1,0:T(8,128)(2,1)} %param.8) | copy-start | bytes 6291460
  15.6 0.7 copy-start.2
  16.3 0.7 copy-start.3
  20.9 17.7 %collective-permute-start.6 = (f32[4,8,128]{2,1,0:T(8,128)S(1)}, f32[4,8,128]{2,1,0:T(8,128)S(1)}, u32[]{:S(2)}, u32[]{:S(2)}) collective-permute-start(f32[4,8,128]{2,1,0:T(8,128)S(1)} %get-tuple-element.39), channel_id=1, source_target_pairs={{0,1},{1,2},{2,3},{3,4},{4,5},{5,6},{6,7},{7,8},{8,9},{9,10},{10,1... | collective-permute-start | bytes 49160 | tf_op jit(solution)/shard_map/ppermute | solution.py:21
  22.5 16.1 %collective-permute-start.7 = (f32[4,8,128]{2,1,0:T(8,128)S(1)}, f32[4,8,128]{2,1,0:T(8,128)S(1)}, u32[]{:S(2)}, u32[]{:S(2)}) collective-permute-start(f32[4,8,128]{2,1,0:T(8,128)S(1)} %get-tuple-element.40), channel_id=1, source_target_pairs={{0,31},{1,0},{2,1},{3,2},{4,3},{5,4},{6,5},{7,6},{8,7},{9,8},{10,9... | collective-permute-start | bytes 49160 | tf_op jit(solution)/shard_map/ppermute | solution.py:21
  29.2 8.6 %collective-permute-start.4 = (f32[3,8,128]{2,1,0:T(8,128)S(1)}, f32[3,8,128]{2,1,0:T(8,128)S(1)}, u32[]{:S(2)}, u32[]{:S(2)}) collective-permute-start(f32[3,8,128]{2,1,0:T(8,128)S(1)} %get-tuple-element.37), channel_id=1, source_target_pairs={{0,32},{32,64},{64,96},{96,128},{128,160},{160,192},{192,224},{224... | collective-permute-start | bytes 36872 | tf_op jit(solution)/shard_map/ppermute | solution.py:21
  31.1 7.5 %collective-permute-start.5 = (f32[3,8,128]{2,1,0:T(8,128)S(1)}, f32[3,8,128]{2,1,0:T(8,128)S(1)}, u32[]{:S(2)}, u32[]{:S(2)}) collective-permute-start(f32[3,8,128]{2,1,0:T(8,128)S(1)} %get-tuple-element.38), channel_id=1, source_target_pairs={{0,480},{32,0},{64,32},{96,64},{128,96},{160,128},{192,160},{224,1... | collective-permute-start | bytes 36872 | tf_op jit(solution)/shard_map/ppermute | solution.py:21
  38.6 13.5 %collective-permute-start.11 = (f32[3,8,128]{2,1,0:T(8,128)S(1)}, f32[3,8,128]{2,1,0:T(8,128)S(1)}, u32[]{:S(2)}, u32[]{:S(2)}) collective-permute-start(f32[3,8,128]{2,1,0:T(8,128)S(1)} %fusion.own.k1), channel_id=1, source_target_pairs={{0,480},{32,0},{64,32},{96,64},{128,96},{160,128},{192,160},{224,1... | collective-permute-start | bytes 36872 | tf_op jit(solution)/shard_map/ppermute | solution.py:21
  45.6 6.6 %collective-permute-start.10 = (f32[3,8,128]{2,1,0:T(8,128)S(1)}, f32[3,8,128]{2,1,0:T(8,128)S(1)}, u32[]{:S(2)}, u32[]{:S(2)}) collective-permute-start(f32[3,8,128]{2,1,0:T(8,128)S(1)} %fusion.own.k1), channel_id=1, source_target_pairs={{0,31},{1,0},{2,1},{3,2},{4,3},{5,4},{6,5},{7,6},{8,7},{9,8},{10,9... | collective-permute-start | bytes 36872 | tf_op jit(solution)/shard_map/ppermute | solution.py:21
  50.2 1.9 %collective-permute-start.9 = (f32[3,8,128]{2,1,0:T(8,128)S(1)}, f32[3,8,128]{2,1,0:T(8,128)S(1)}, u32[]{:S(2)}, u32[]{:S(2)}) collective-permute-start(f32[3,8,128]{2,1,0:T(8,128)S(1)} %fusion.own.k1), channel_id=1, source_target_pairs={{0,1},{1,2},{2,3},{3,4},{4,5},{5,6},{6,7},{7,8},{8,9},{9,10},{10,1... | collective-permute-start | bytes 36872 | tf_op jit(solution)/shard_map/ppermute | solution.py:21
  50.2 7.7 %collective-permute-start.8 = (f32[3,8,128]{2,1,0:T(8,128)S(1)}, f32[3,8,128]{2,1,0:T(8,128)S(1)}, u32[]{:S(2)}, u32[]{:S(2)}) collective-permute-start(f32[3,8,128]{2,1,0:T(8,128)S(1)} %fusion.own.k1), channel_id=1, source_target_pairs={{0,32},{32,64},{64,96},{96,128},{128,160},{160,192},{192,224},{224... | collective-permute-start | bytes 36872 | tf_op jit(solution)/shard_map/ppermute | solution.py:21
  60.1 10.9 %collective-permute-start.12 = (f32[3,8,128]{2,1,0:T(8,128)S(1)}, f32[3,8,128]{2,1,0:T(8,128)S(1)}, u32[]{:S(2)}, u32[]{:S(2)}) collective-permute-start(f32[3,8,128]{2,1,0:T(8,128)S(1)} %get-tuple-element.43), channel_id=1, source_target_pairs={{0,32},{32,64},{64,96},{96,128},{128,160},{160,192},{192,224},{224... | collective-permute-start | bytes 36872 | tf_op jit(solution)/shard_map/ppermute | solution.py:21
  62.0 9.0 %collective-permute-start.13 = (f32[3,8,128]{2,1,0:T(8,128)S(1)}, f32[3,8,128]{2,1,0:T(8,128)S(1)}, u32[]{:S(2)}, u32[]{:S(2)}) collective-permute-start(f32[3,8,128]{2,1,0:T(8,128)S(1)} %get-tuple-element.44), channel_id=1, source_target_pairs={{0,480},{32,0},{64,32},{96,64},{128,96},{160,128},{192,160},{224,1... | collective-permute-start | bytes 36872 | tf_op jit(solution)/shard_map/ppermute | solution.py:21
  68.7 2.9 %collective-permute-start.14 = (f32[3,8,128]{2,1,0:T(8,128)S(1)}, f32[3,8,128]{2,1,0:T(8,128)S(1)}, u32[]{:S(2)}, u32[]{:S(2)}) collective-permute-start(f32[3,8,128]{2,1,0:T(8,128)S(1)} %get-tuple-element.45), channel_id=1, source_target_pairs={{0,1},{1,2},{2,3},{3,4},{4,5},{5,6},{6,7},{7,8},{8,9},{9,10},{10,1... | collective-permute-start | bytes 36872 | tf_op jit(solution)/shard_map/ppermute | solution.py:21
  68.7 3.1 %collective-permute-start.15 = (f32[3,8,128]{2,1,0:T(8,128)S(1)}, f32[3,8,128]{2,1,0:T(8,128)S(1)}, u32[]{:S(2)}, u32[]{:S(2)}) collective-permute-start(f32[3,8,128]{2,1,0:T(8,128)S(1)} %get-tuple-element.46), channel_id=1, source_target_pairs={{0,31},{1,0},{2,1},{3,2},{4,3},{5,4},{6,5},{7,6},{8,7},{9,8},{10,9... | collective-permute-start | bytes 36872 | tf_op jit(solution)/shard_map/ppermute | solution.py:21
  71.8 9.9 %collective-permute-start.19 = (f32[3,8,128]{2,1,0:T(8,128)S(1)}, f32[3,8,128]{2,1,0:T(8,128)S(1)}, u32[]{:S(2)}, u32[]{:S(2)}) collective-permute-start(f32[3,8,128]{2,1,0:T(8,128)S(1)} %select_add_fusion.1.own.k2), channel_id=1, source_target_pairs={{0,480},{32,0},{64,32},{96,64},{128,96},{160,128},{192,160},{224,1... | collective-permute-start | bytes 36872 | tf_op jit(solution)/shard_map/ppermute | solution.py:21
  76.4 5.3 %collective-permute-start.18 = (f32[3,8,128]{2,1,0:T(8,128)S(1)}, f32[3,8,128]{2,1,0:T(8,128)S(1)}, u32[]{:S(2)}, u32[]{:S(2)}) collective-permute-start(f32[3,8,128]{2,1,0:T(8,128)S(1)} %select_add_fusion.1.own.k2), channel_id=1, source_target_pairs={{0,31},{1,0},{2,1},{3,2},{4,3},{5,4},{6,5},{7,6},{8,7},{9,8},{10,9... | collective-permute-start | bytes 36872 | tf_op jit(solution)/shard_map/ppermute | solution.py:21
  79.8 1.9 %collective-permute-start.17 = (f32[3,8,128]{2,1,0:T(8,128)S(1)}, f32[3,8,128]{2,1,0:T(8,128)S(1)}, u32[]{:S(2)}, u32[]{:S(2)}) collective-permute-start(f32[3,8,128]{2,1,0:T(8,128)S(1)} %select_add_fusion.1.own.k2), channel_id=1, source_target_pairs={{0,1},{1,2},{2,3},{3,4},{4,5},{5,6},{6,7},{7,8},{8,9},{9,10},{10,1... | collective-permute-start | bytes 36872 | tf_op jit(solution)/shard_map/ppermute | solution.py:21
  79.8 7.7 %collective-permute-start.16 = (f32[3,8,128]{2,1,0:T(8,128)S(1)}, f32[3,8,128]{2,1,0:T(8,128)S(1)}, u32[]{:S(2)}, u32[]{:S(2)}) collective-permute-start(f32[3,8,128]{2,1,0:T(8,128)S(1)} %select_add_fusion.1.own.k2), channel_id=1, source_target_pairs={{0,32},{32,64},{64,96},{96,128},{128,160},{160,192},{192,224},{224... | collective-permute-start | bytes 36872 | tf_op jit(solution)/shard_map/ppermute | solution.py:21
  90.1 12.9 %all-to-all-start = ((f32[32,8,128]{2,1,0:T(8,128)}), f32[32,8,128]{2,1,0:T(8,128)S(1)}, u32[]{:S(2)}, u32[]{:S(2)}) async-start(f32[32,8,128]{2,1,0:T(8,128)} %get-tuple-element.48), calls=%async_computation | async-start | bytes 262144 | tf_op jit(solution)/shard_map/all_to_all | solution.py:281
  95.3 7.8 %collective-permute-start.20 = (f32[3,8,128]{2,1,0:T(8,128)S(1)}, f32[3,8,128]{2,1,0:T(8,128)S(1)}, u32[]{:S(2)}, u32[]{:S(2)}) collective-permute-start(f32[3,8,128]{2,1,0:T(8,128)S(1)} %get-tuple-element.52), channel_id=1, source_target_pairs={{0,1},{1,2},{2,3},{3,4},{4,5},{5,6},{6,7},{7,8},{8,9},{9,10},{10,1... | collective-permute-start | bytes 36872 | tf_op jit(solution)/shard_map/ppermute | solution.py:21
  95.3 7.8 %collective-permute-start.21 = (f32[3,8,128]{2,1,0:T(8,128)S(1)}, f32[3,8,128]{2,1,0:T(8,128)S(1)}, u32[]{:S(2)}, u32[]{:S(2)}) collective-permute-start(f32[3,8,128]{2,1,0:T(8,128)S(1)} %get-tuple-element.53), channel_id=1, source_target_pairs={{0,31},{1,0},{2,1},{3,2},{4,3},{5,4},{6,5},{7,6},{8,7},{9,8},{10,9... | collective-permute-start | bytes 36872 | tf_op jit(solution)/shard_map/ppermute | solution.py:21
  103.7 18.4 %all-to-all-start.1 = ((f32[16,8,128]{2,1,0:T(8,128)}), f32[16,8,128]{2,1,0:T(8,128)S(1)}, u32[]{:S(2)}, u32[]{:S(2)}) async-start(f32[16,8,128]{2,1,0:T(8,128)} %broadcast_in_dim.32), calls=%async_computation.1 | async-start | bytes 131072 | tf_op jit(solution)/shard_map/all_to_all | solution.py:281
  110.5 8.6 %collective-permute-start.22 = (f32[3,8,128]{2,1,0:T(8,128)S(1)}, f32[3,8,128]{2,1,0:T(8,128)S(1)}, u32[]{:S(2)}, u32[]{:S(2)}) collective-permute-start(f32[3,8,128]{2,1,0:T(8,128)S(1)} %get-tuple-element.56), channel_id=1, source_target_pairs={{0,32},{32,64},{64,96},{96,128},{128,160},{160,192},{192,224},{224... | collective-permute-start | bytes 36872 | tf_op jit(solution)/shard_map/ppermute | solution.py:21
  112.8 7.1 %collective-permute-start.23 = (f32[3,8,128]{2,1,0:T(8,128)S(1)}, f32[3,8,128]{2,1,0:T(8,128)S(1)}, u32[]{:S(2)}, u32[]{:S(2)}) collective-permute-start(f32[3,8,128]{2,1,0:T(8,128)S(1)} %get-tuple-element.57), channel_id=1, source_target_pairs={{0,480},{32,0},{64,32},{96,64},{128,96},{160,128},{192,160},{224,1... | collective-permute-start | bytes 36872 | tf_op jit(solution)/shard_map/ppermute | solution.py:21

commit v4 on v3

--- a/solution.py
+++ b/solution.py
@@ -307,14 +307,10 @@
         )
         if sweep == ITERS - 1:
             part = jnp.sum(spread_sum(carried, lambda a, c: c // 2), axis=0)
-            part, r1, r7 = lax.optimization_barrier((part, r1, r7))
+            part, r1, r3, r5, r7 = lax.optimization_barrier((part, r1, r3, r5, r7))
+            sums = spread_sum(part, lambda a, c: (a, c % 2))
         from_lower_cross = ring_shift(r5, "cross", 1)
         from_upper_cross = ring_shift(r3, "cross", -1)
-        if sweep == ITERS - 1:
-            part, from_lower_cross, from_upper_cross = lax.optimization_barrier(
-                (part, from_lower_cross, from_upper_cross)
-            )
-            sums = spread_sum(part, lambda a, c: (a, c % 2))
         from_lower_axial = ring_shift(r7, "axial", 1)
         from_upper_axial = ring_shift(r1, "axial", -1)
         if sweep == 0:

time: 124 us -> 125 us (level)
  blocking collectives: 0 us -> 12 us
  waiting for transfers between devices: 25.1 us -> 18 us
  starting transfers between devices: 84.6 us -> 81.7 us
    all_to_all x0 -> x1, blocking collectives: none -> 12 us  [spread_sum(): lax.all_to_all(part, ('axial', 'cross'), 0, 0, axis_index_groups=groups)]
    all_to_all x2 -> x1, waiting for transfers between devices: 9.37 us -> 0.01 us  [spread_sum(): lax.all_to_all(part, ('axial', 'cross'), 0, 0, axis_index_groups=groups)]
    all_to_all x2 -> x1, starting transfers between devices: 11.9 us -> 6.76 us  [spread_sum(): lax.all_to_all(part, ('axial', 'cross'), 0, 0, axis_index_groups=groups)]
    ppermute x24, waiting for transfers between devices: 15.7 us -> 18 us  [ring_shift(): return lax.ppermute(shard, axis, ring(lax.axis_size(axis), by))]
    ppermute x24, starting transfers between devices: 72.7 us -> 75 us  [ring_shift(): return lax.ppermute(shard, axis, ring(lax.axis_size(axis), by))]
  transfers between devices with their start and end apart: 26 -> 25, of which waited for: 9 -> 8; matrix products, arithmetic and copies ran while one was open for 1% -> 1% of each run, Pallas kernels for 0% -> 0%
where the time goes in v4:
time: 125 us
  starting transfers between devices  81.7 us (65%)
  waiting for transfers between devices  18 us (14%)
  blocking collectives  12 us (10%)
  Pallas kernels  7.29 us (6%)
  local copies, waits for them, and re-layouts  3.7 us (3%)
    ppermute x24, starting transfers between devices, ring_shift(): return lax.ppermute(shard, axis, ring(lax.axis_size(axis), by))  75 us
    ppermute x24, waiting for transfers between devices, ring_shift(): return lax.ppermute(shard, axis, ring(lax.axis_size(axis), by))  18 us
    all_to_all x1, blocking collectives, spread_sum(): lax.all_to_all(part, ('axial', 'cross'), 0, 0, axis_index_groups=groups)  12 us
    all_to_all x1, starting transfers between devices, spread_sum(): lax.all_to_all(part, ('axial', 'cross'), 0, 0, axis_index_groups=groups)  6.76 us
    pallas_call x3, Pallas kernels, operator_call(): pl.pallas_call(functools.partial(operator_kernel, sweep), in_specs=[pl.Bl...  6.23 us
    unnamed x8, local copies, waits for them, and re-layouts  2.99 us
  transfers between devices with their start and end apart: 25, of which 8 were waited for; matrix products, arithmetic and copies ran while one was open for 1% of the time, Pallas kernels for 0%

profile of v4, /device:TPU:1, one launch (start us, length us, event | category | flops | bytes accessed | tf_op | source)
XLA Modules:
  0.0 124.5 jit_solution(13126235851055732768)
XLA Ops:
  0.6 0.0 copy-start.1
  0.6 7.7 %collective-permute-start.3 = (f32[3,8,128]{2,1,0:T(8,128)}, f32[3,8,128]{2,1,0:T(8,128)S(1)}, u32[]{:S(2)}, u32[]{:S(2)}) collective-permute-start(f32[3,8,128]{2,1,0:T(8,128)} %bitcast.22), channel_id=1, source_target_pairs={{0,480},{32,0},{64,32},{96,64},{128,96},{160,128},{192,160},{224,1... | collective-permute-start | bytes 36872 | tf_op jit(solution)/shard_map/ppermute | solution.py:21
  8.3 1.1 collective-permute-start.2
  9.5 1.4 %collective-permute-start.1 = (f32[3,8,128]{2,1,0:T(8,128)}, f32[3,8,128]{2,1,0:T(8,128)S(1)}, u32[]{:S(2)}, u32[]{:S(2)}) collective-permute-start(f32[3,8,128]{2,1,0:T(8,128)} %bitcast.24), channel_id=1, source_target_pairs={{0,1},{1,2},{2,3},{3,4},{4,5},{5,6},{6,7},{7,8},{8,9},{9,10},{10,1... | collective-permute-start | bytes 36872 | tf_op jit(solution)/shard_map/ppermute | solution.py:21
  10.8 2.3 %collective-permute-start = (f32[3,8,128]{2,1,0:T(8,128)}, f32[3,8,128]{2,1,0:T(8,128)S(1)}, u32[]{:S(2)}, u32[]{:S(2)}) collective-permute-start(f32[3,8,128]{2,1,0:T(8,128)} %bitcast.25), channel_id=1, source_target_pairs={{0,32},{32,64},{64,96},{96,128},{128,160},{160,192},{192,224},{224... | collective-permute-start | bytes 36872 | tf_op jit(solution)/shard_map/ppermute | solution.py:21
  13.1 0.8 fusion.4
  13.9 0.1 pad.4.clone
  13.9 0.1 fusion.2.carried
  14.0 1.6 %copy-done = bf16[1,1,8,8,128,128]{5,4,3,2,1,0:T(8,128)(2,1)S(1)} copy-done((bf16[1,1,8,8,128,128]{5,4,3,2,1,0:T(8,128)(2,1)S(1)}, bf16[1,1,8,8,128,128]{5,4,3,2,1,0:T(8,128)(2,1)}, u32[]{:S(2)}) %copy-start) | copy-done | bytes 2097176
  15.6 0.7 copy-done.2
  16.3 0.7 copy-done.3
  17.0 0.2 shard_map.85
  17.2 0.0 collective-permute-done.3.from_axial_up
  17.2 0.0 collective-permute-done.2.from_cross_up.u0
  17.2 1.6 %collective-permute-done.1.from_cross_dn.d0 = f32[3,8,128]{2,1,0:T(8,128)S(1)} collective-permute-done((f32[3,8,128]{2,1,0:T(8,128)}, f32[3,8,128]{2,1,0:T(8,128)S(1)}, u32[]{:S(2)}, u32[]{:S(2)}) %collective-permute-start.1) | collective-permute-done | bytes 12320 | tf_op jit(solution)/shard_map/ppermute | solution.py:21
  18.8 0.0 collective-permute-done.from_axial_dn
  18.8 2.1 %shard_map.86 = (f32[3,8,128]{2,1,0:T(8,128)S(1)}, f32[4,8,128]{2,1,0:T(8,128)S(1)}, f32[4,8,128]{2,1,0:T(8,128)S(1)}, f32[3,8,128]{2,1,0:T(8,128)S(1)}, f32[3,8,128]{2,1,0:T(8,128)S(1)}, /*index=5*/f32[8,128]{1,0:T(8,128)S(1)}) custom-call(s32[8,8]{1,0:T(8,128)S(1)} %bitcast.19, f32[3,8,128]{2,1,0:T(8,128)S(1)} %get-tuple-element.32.own.k0, ...), custom_call_target="tpu_custom_call" | custom-call | tf_op jit(solution)/shard_map/pallas_call | solution.py:113
  20.9 1.6 %collective-permute-start.6 = (f32[4,8,128]{2,1,0:T(8,128)S(1)}, f32[4,8,128]{2,1,0:T(8,128)S(1)}, u32[]{:S(2)}, u32[]{:S(2)}) collective-permute-start(f32[4,8,128]{2,1,0:T(8,128)S(1)} %get-tuple-element.38), channel_id=1, source_target_pairs={{0,1},{1,2},{2,3},{3,4},{4,5},{5,6},{6,7},{7,8},{8,9},{9,10},{10,1... | collective-permute-start | bytes 49160 | tf_op jit(solution)/shard_map/ppermute | solution.py:21
  22.5 6.7 %collective-permute-start.7 = (f32[4,8,128]{2,1,0:T(8,128)S(1)}, f32[4,8,128]{2,1,0:T(8,128)S(1)}, u32[]{:S(2)}, u32[]{:S(2)}) collective-permute-start(f32[4,8,128]{2,1,0:T(8,128)S(1)} %get-tuple-element.39), channel_id=1, source_target_pairs={{0,31},{1,0},{2,1},{3,2},{4,3},{5,4},{6,5},{7,6},{8,7},{9,8},{10,9... | collective-permute-start | bytes 49160 | tf_op jit(solution)/shard_map/ppermute | solution.py:21
  29.2 1.9 %collective-permute-start.4 = (f32[3,8,128]{2,1,0:T(8,128)S(1)}, f32[3,8,128]{2,1,0:T(8,128)S(1)}, u32[]{:S(2)}, u32[]{:S(2)}) collective-permute-start(f32[3,8,128]{2,1,0:T(8,128)S(1)} %get-tuple-element.36), channel_id=1, source_target_pairs={{0,32},{32,64},{64,96},{96,128},{128,160},{160,192},{192,224},{224... | collective-permute-start | bytes 36872 | tf_op jit(solution)/shard_map/ppermute | solution.py:21
  31.1 6.7 %collective-permute-start.5 = (f32[3,8,128]{2,1,0:T(8,128)S(1)}, f32[3,8,128]{2,1,0:T(8,128)S(1)}, u32[]{:S(2)}, u32[]{:S(2)}) collective-permute-start(f32[3,8,128]{2,1,0:T(8,128)S(1)} %get-tuple-element.37), channel_id=1, source_target_pairs={{0,480},{32,0},{64,32},{96,64},{128,96},{160,128},{192,160},{224,1... | collective-permute-start | bytes 36872 | tf_op jit(solution)/shard_map/ppermute | solution.py:21
  37.8 0.0 collective-permute-done.4
  37.8 0.8 collective-permute-done.5
  38.6 0.0 collective-permute-done.6.dn_plane
  38.6 0.0 collective-permute-done.7.up_plane
  38.6 6.9 %collective-permute-start.11 = (f32[3,8,128]{2,1,0:T(8,128)S(1)}, f32[3,8,128]{2,1,0:T(8,128)S(1)}, u32[]{:S(2)}, u32[]{:S(2)}) collective-permute-start(f32[3,8,128]{2,1,0:T(8,128)S(1)} %fusion.own.k1), channel_id=1, source_target_pairs={{0,480},{32,0},{64,32},{96,64},{128,96},{160,128},{192,160},{224,1... | collective-permute-start | bytes 36872 | tf_op jit(solution)/shard_map/ppermute | solution.py:21
  45.6 4.7 %collective-permute-start.10 = (f32[3,8,128]{2,1,0:T(8,128)S(1)}, f32[3,8,128]{2,1,0:T(8,128)S(1)}, u32[]{:S(2)}, u32[]{:S(2)}) collective-permute-start(f32[3,8,128]{2,1,0:T(8,128)S(1)} %fusion.own.k1), channel_id=1, source_target_pairs={{0,31},{1,0},{2,1},{3,2},{4,3},{5,4},{6,5},{7,6},{8,7},{9,8},{10,9... | collective-permute-start | bytes 36872 | tf_op jit(solution)/shard_map/ppermute | solution.py:21
  50.2 0.0 collective-permute-start.9
  50.2 1.9 %collective-permute-start.8 = (f32[3,8,128]{2,1,0:T(8,128)S(1)}, f32[3,8,128]{2,1,0:T(8,128)S(1)}, u32[]{:S(2)}, u32[]{:S(2)}) collective-permute-start(f32[3,8,128]{2,1,0:T(8,128)S(1)} %fusion.own.k1), channel_id=1, source_target_pairs={{0,32},{32,64},{64,96},{96,128},{128,160},{160,192},{192,224},{224... | collective-permute-start | bytes 36872 | tf_op jit(solution)/shard_map/ppermute | solution.py:21
  52.1 0.0 collective-permute-done.11.from_axial_up
  52.2 0.0 collective-permute-done.10.from_cross_up.u1
  52.2 0.0 collective-permute-done.9.from_cross_dn.d1
  52.2 5.8 %collective-permute-done.8.from_axial_dn = f32[3,8,128]{2,1,0:T(8,128)S(1)} collective-permute-done((f32[3,8,128]{2,1,0:T(8,128)S(1)}, f32[3,8,128]{2,1,0:T(8,128)S(1)}, u32[]{:S(2)}, u32[]{:S(2)}) %collective-permute-start.8) | collective-permute-done | bytes 12320 | tf_op jit(solution)/shard_map/ppermute | solution.py:21
  58.0 2.1 %shard_map.87 = (f32[3,8,128]{2,1,0:T(8,128)S(1)}, f32[3,8,128]{2,1,0:T(8,128)S(1)}, f32[3,8,128]{2,1,0:T(8,128)S(1)}, f32[3,8,128]{2,1,0:T(8,128)S(1)}, f32[3,8,128]{2,1,0:T(8,128)S(1)}, /*index=5*/f32[8,128]{1,0:T(8,128)S(1)}) custom-call(s32[8,8]{1,0:T(8,128)S(1)} %bitcast.20, f32[3,8,128]{2,1,0:T(8,128)S(1)} %fusion.own.k1, ...), custom_call_target="tpu_custom_call" | custom-call | tf_op jit(solution)/shard_map/pallas_call | solution.py:113
  60.1 1.9 %collective-permute-start.12 = (f32[3,8,128]{2,1,0:T(8,128)S(1)}, f32[3,8,128]{2,1,0:T(8,128)S(1)}, u32[]{:S(2)}, u32[]{:S(2)}) collective-permute-start(f32[3,8,128]{2,1,0:T(8,128)S(1)} %get-tuple-element.42), channel_id=1, source_target_pairs={{0,32},{32,64},{64,96},{96,128},{128,160},{160,192},{192,224},{224... | collective-permute-start | bytes 36872 | tf_op jit(solution)/shard_map/ppermute | solution.py:21
  62.0 6.7 %collective-permute-start.13 = (f32[3,8,128]{2,1,0:T(8,128)S(1)}, f32[3,8,128]{2,1,0:T(8,128)S(1)}, u32[]{:S(2)}, u32[]{:S(2)}) collective-permute-start(f32[3,8,128]{2,1,0:T(8,128)S(1)} %get-tuple-element.43), channel_id=1, source_target_pairs={{0,480},{32,0},{64,32},{96,64},{128,96},{160,128},{192,160},{224,1... | collective-permute-start | bytes 36872 | tf_op jit(solution)/shard_map/ppermute | solution.py:21
  68.7 0.0 collective-permute-start.14
  68.7 2.2 %collective-permute-start.15 = (f32[3,8,128]{2,1,0:T(8,128)S(1)}, f32[3,8,128]{2,1,0:T(8,128)S(1)}, u32[]{:S(2)}, u32[]{:S(2)}) collective-permute-start(f32[3,8,128]{2,1,0:T(8,128)S(1)} %get-tuple-element.45), channel_id=1, source_target_pairs={{0,31},{1,0},{2,1},{3,2},{4,3},{5,4},{6,5},{7,6},{8,7},{9,8},{10,9... | collective-permute-start | bytes 36872 | tf_op jit(solution)/shard_map/ppermute | solution.py:21
  70.9 0.0 collective-permute-done.12
  70.9 0.0 collective-permute-done.13
  70.9 0.6 collective-permute-done.14
  71.6 0.2 collective-permute-done.15
  71.8 4.6 %collective-permute-start.19 = (f32[3,8,128]{2,1,0:T(8,128)S(1)}, f32[3,8,128]{2,1,0:T(8,128)S(1)}, u32[]{:S(2)}, u32[]{:S(2)}) collective-permute-start(f32[3,8,128]{2,1,0:T(8,128)S(1)} %select_add_fusion.1.own.k2), channel_id=1, source_target_pairs={{0,480},{32,0},{64,32},{96,64},{128,96},{160,128},{192,160},{224,1... | collective-permute-start | bytes 36872 | tf_op jit(solution)/shard_map/ppermute | solution.py:21
  76.5 3.4 %collective-permute-start.18 = (f32[3,8,128]{2,1,0:T(8,128)S(1)}, f32[3,8,128]{2,1,0:T(8,128)S(1)}, u32[]{:S(2)}, u32[]{:S(2)}) collective-permute-start(f32[3,8,128]{2,1,0:T(8,128)S(1)} %select_add_fusion.1.own.k2), channel_id=1, source_target_pairs={{0,31},{1,0},{2,1},{3,2},{4,3},{5,4},{6,5},{7,6},{8,7},{9,8},{10,9... | collective-permute-start | bytes 36872 | tf_op jit(solution)/shard_map/ppermute | solution.py:21
  79.8 0.0 collective-permute-start.17
  79.8 1.9 %collective-permute-start.16 = (f32[3,8,128]{2,1,0:T(8,128)S(1)}, f32[3,8,128]{2,1,0:T(8,128)S(1)}, u32[]{:S(2)}, u32[]{:S(2)}) collective-permute-start(f32[3,8,128]{2,1,0:T(8,128)S(1)} %select_add_fusion.1.own.k2), channel_id=1, source_target_pairs={{0,32},{32,64},{64,96},{96,128},{128,160},{160,192},{192,224},{224... | collective-permute-start | bytes 36872 | tf_op jit(solution)/shard_map/ppermute | solution.py:21
  81.8 0.0 collective-permute-done.19.from_axial_up
  81.8 0.0 collective-permute-done.18.from_cross_up.u2
  81.8 0.0 collective-permute-done.17.from_cross_dn.d2
  81.8 5.8 %collective-permute-done.16.from_axial_dn = f32[3,8,128]{2,1,0:T(8,128)S(1)} collective-permute-done((f32[3,8,128]{2,1,0:T(8,128)S(1)}, f32[3,8,128]{2,1,0:T(8,128)S(1)}, u32[]{:S(2)}, u32[]{:S(2)}) %collective-permute-start.16) | collective-permute-done | bytes 12320 | tf_op jit(solution)/shard_map/ppermute | solution.py:21
  87.6 2.1 %shard_map.88 = (f32[3,8,128]{2,1,0:T(8,128)S(1)}, f32[3,8,128]{2,1,0:T(8,128)S(1)}, f32[3,8,128]{2,1,0:T(8,128)S(1)}, f32[3,8,128]{2,1,0:T(8,128)S(1)}, f32[3,8...) custom-call(s32[8,8]{1,0:T(8,128)S(1)} %bitcast.21, f32[3,8,128]{2,1,0:T(8,128)S(1)} %select_add_fusion.1.own.k2, ...), custom_call_target="tpu_custom_call" | custom-call | tf_op jit(solution)/shard_map/pallas_call | solution.py:113
  89.7 12.0 %all_to_all.10 = f32[32,8,128]{2,1,0:T(8,128)S(1)} all-to-all(f32[32,8,128]{2,1,0:T(8,128)S(1)} %get-tuple-element.47), channel_id=1, replica_groups={{0,1,32,33,64,65,96,97,128,129,160,161,192,193,224,225,256,257,288,289,..., dimensions={0} | all-to-all | bytes 262144 | tf_op jit(solution)/shard_map/all_to_all | solution.py:281
  101.7 0.6 broadcast_in_dim.32
  102.4 6.8 %all-to-all-start.1 = ((f32[16,8,128]{2,1,0:T(8,128)}), f32[16,8,128]{2,1,0:T(8,128)S(1)}, u32[]{:S(2)}, u32[]{:S(2)}) async-start(f32[16,8,128]{2,1,0:T(8,128)} %broadcast_in_dim.32), calls=%async_computation.1 | async-start | bytes 131072 | tf_op jit(solution)/shard_map/all_to_all | solution.py:281
  109.1 2.3 %collective-permute-start.20 = (f32[3,8,128]{2,1,0:T(8,128)S(1)}, f32[3,8,128]{2,1,0:T(8,128)S(1)}, u32[]{:S(2)}, u32[]{:S(2)}) collective-permute-start(f32[3,8,128]{2,1,0:T(8,128)S(1)} %get-tuple-element.54), channel_id=1, source_target_pairs={{0,32},{32,64},{64,96},{96,128},{128,160},{160,192},{192,224},{224... | collective-permute-start | bytes 36872 | tf_op jit(solution)/shard_map/ppermute | solution.py:21
  111.4 6.3 %collective-permute-start.21 = (f32[3,8,128]{2,1,0:T(8,128)S(1)}, f32[3,8,128]{2,1,0:T(8,128)S(1)}, u32[]{:S(2)}, u32[]{:S(2)}) collective-permute-start(f32[3,8,128]{2,1,0:T(8,128)S(1)} %get-tuple-element.55), channel_id=1, source_target_pairs={{0,480},{32,0},{64,32},{96,64},{128,96},{160,128},{192,160},{224,1... | collective-permute-start | bytes 36872 | tf_op jit(solution)/shard_map/ppermute | solution.py:21
  117.8 2.8 %collective-permute-start.22 = (f32[3,8,128]{2,1,0:T(8,128)S(1)}, f32[3,8,128]{2,1,0:T(8,128)S(1)}, u32[]{:S(2)}, u32[]{:S(2)}) collective-permute-start(f32[3,8,128]{2,1,0:T(8,128)S(1)} %get-tuple-element.56), channel_id=1, source_target_pairs={{0,1},{1,2},{2,3},{3,4},{4,5},{5,6},{6,7},{7,8},{8,9},{9,10},{10,1... | collective-permute-start | bytes 36872 | tf_op jit(solution)/shard_map/ppermute | solution.py:21
  120.5 0.0 collective-permute-start.23
  120.5 0.0 collective-permute-done.20
  120.5 0.0 collective-permute-done.21
  120.5 0.8 collective-permute-done.22
  121.4 2.3 %collective-permute-done.23 = f32[3,8,128]{2,1,0:T(8,128)S(1)} collective-permute-done((f32[3,8,128]{2,1,0:T(8,128)S(1)}, f32[3,8,128]{2,1,0:T(8,128)S(1)}, u32[]{:S(2)}, u32[]{:S(2)}) %collective-permute-start.23) | collective-permute-done | bytes 12320 | tf_op jit(solution)/shard_map/ppermute | solution.py:21
  123.7 0.0 all-to-all-done.1.sums
  123.7 0.9 shard_map.89
  (10 shorter events, 0.1 us)
Async XLA Ops:
  0.6 18.2 %copy-start.1 = (s32[1,1,8,8]{3,2,1,0:T(8,128)S(1)}, s32[1,1,8,8]{3,2,1,0:T(8,128)}, u32[]{:S(2)}) copy-start(s32[1,1,8,8]{3,2,1,0:T(8,128)} %param.9) | copy-start | bytes 772
  0.6 16.6 %collective-permute-start.3 = (f32[3,8,128]{2,1,0:T(8,128)}, f32[3,8,128]{2,1,0:T(8,128)S(1)}, u32[]{:S(2)}, u32[]{:S(2)}) collective-permute-start(f32[3,8,128]{2,1,0:T(8,128)} %bitcast.22), channel_id=1, source_target_pairs={{0,480},{32,0},{64,32},{96,64},{128,96},{160,128},{192,160},{224,1... | collective-permute-start | bytes 36872 | tf_op jit(solution)/shard_map/ppermute | solution.py:21
  8.3 8.9 %collective-permute-start.2 = (f32[3,8,128]{2,1,0:T(8,128)}, f32[3,8,128]{2,1,0:T(8,128)S(1)}, u32[]{:S(2)}, u32[]{:S(2)}) collective-permute-start(f32[3,8,128]{2,1,0:T(8,128)} %bitcast.23), channel_id=1, source_target_pairs={{0,31},{1,0},{2,1},{3,2},{4,3},{5,4},{6,5},{7,6},{8,7},{9,8},{10,9... | collective-permute-start | bytes 36872 | tf_op jit(solution)/shard_map/ppermute | solution.py:21
  9.5 9.4 %collective-permute-start.1 = (f32[3,8,128]{2,1,0:T(8,128)}, f32[3,8,128]{2,1,0:T(8,128)S(1)}, u32[]{:S(2)}, u32[]{:S(2)}) collective-permute-start(f32[3,8,128]{2,1,0:T(8,128)} %bitcast.24), channel_id=1, source_target_pairs={{0,1},{1,2},{2,3},{3,4},{4,5},{5,6},{6,7},{7,8},{8,9},{9,10},{10,1... | collective-permute-start | bytes 36872 | tf_op jit(solution)/shard_map/ppermute | solution.py:21
  10.8 8.0 %collective-permute-start = (f32[3,8,128]{2,1,0:T(8,128)}, f32[3,8,128]{2,1,0:T(8,128)S(1)}, u32[]{:S(2)}, u32[]{:S(2)}) collective-permute-start(f32[3,8,128]{2,1,0:T(8,128)} %bitcast.25), channel_id=1, source_target_pairs={{0,32},{32,64},{64,96},{96,128},{128,160},{160,192},{192,224},{224... | collective-permute-start | bytes 36872 | tf_op jit(solution)/shard_map/ppermute | solution.py:21
  14.0 1.6 %copy-start = (bf16[1,1,8,8,128,128]{5,4,3,2,1,0:T(8,128)(2,1)S(1)}, bf16[1,1,8,8,128,128]{5,4,3,2,1,0:T(8,128)(2,1)}, u32[]{:S(2)}) copy-start(bf16[1,1,8,8,128,128]{5,4,3,2,1,0:T(8,128)(2,1)} %param.8) | copy-start | bytes 6291460
  15.6 0.7 copy-start.2
  16.3 0.7 copy-start.3
  20.9 17.7 %collective-permute-start.6 = (f32[4,8,128]{2,1,0:T(8,128)S(1)}, f32[4,8,128]{2,1,0:T(8,128)S(1)}, u32[]{:S(2)}, u32[]{:S(2)}) collective-permute-start(f32[4,8,128]{2,1,0:T(8,128)S(1)} %get-tuple-element.38), channel_id=1, source_target_pairs={{0,1},{1,2},{2,3},{3,4},{4,5},{5,6},{6,7},{7,8},{8,9},{9,10},{10,1... | collective-permute-start | bytes 49160 | tf_op jit(solution)/shard_map/ppermute | solution.py:21
  22.5 16.1 %collective-permute-start.7 = (f32[4,8,128]{2,1,0:T(8,128)S(1)}, f32[4,8,128]{2,1,0:T(8,128)S(1)}, u32[]{:S(2)}, u32[]{:S(2)}) collective-permute-start(f32[4,8,128]{2,1,0:T(8,128)S(1)} %get-tuple-element.39), channel_id=1, source_target_pairs={{0,31},{1,0},{2,1},{3,2},{4,3},{5,4},{6,5},{7,6},{8,7},{9,8},{10,9... | collective-permute-start | bytes 49160 | tf_op jit(solution)/shard_map/ppermute | solution.py:21
  29.2 8.6 %collective-permute-start.4 = (f32[3,8,128]{2,1,0:T(8,128)S(1)}, f32[3,8,128]{2,1,0:T(8,128)S(1)}, u32[]{:S(2)}, u32[]{:S(2)}) collective-permute-start(f32[3,8,128]{2,1,0:T(8,128)S(1)} %get-tuple-element.36), channel_id=1, source_target_pairs={{0,32},{32,64},{64,96},{96,128},{128,160},{160,192},{192,224},{224... | collective-permute-start | bytes 36872 | tf_op jit(solution)/shard_map/ppermute | solution.py:21
  31.1 7.5 %collective-permute-start.5 = (f32[3,8,128]{2,1,0:T(8,128)S(1)}, f32[3,8,128]{2,1,0:T(8,128)S(1)}, u32[]{:S(2)}, u32[]{:S(2)}) collective-permute-start(f32[3,8,128]{2,1,0:T(8,128)S(1)} %get-tuple-element.37), channel_id=1, source_target_pairs={{0,480},{32,0},{64,32},{96,64},{128,96},{160,128},{192,160},{224,1... | collective-permute-start | bytes 36872 | tf_op jit(solution)/shard_map/ppermute | solution.py:21
  38.6 13.5 %collective-permute-start.11 = (f32[3,8,128]{2,1,0:T(8,128)S(1)}, f32[3,8,128]{2,1,0:T(8,128)S(1)}, u32[]{:S(2)}, u32[]{:S(2)}) collective-permute-start(f32[3,8,128]{2,1,0:T(8,128)S(1)} %fusion.own.k1), channel_id=1, source_target_pairs={{0,480},{32,0},{64,32},{96,64},{128,96},{160,128},{192,160},{224,1... | collective-permute-start | bytes 36872 | tf_op jit(solution)/shard_map/ppermute | solution.py:21
  45.6 6.6 %collective-permute-start.10 = (f32[3,8,128]{2,1,0:T(8,128)S(1)}, f32[3,8,128]{2,1,0:T(8,128)S(1)}, u32[]{:S(2)}, u32[]{:S(2)}) collective-permute-start(f32[3,8,128]{2,1,0:T(8,128)S(1)} %fusion.own.k1), channel_id=1, source_target_pairs={{0,31},{1,0},{2,1},{3,2},{4,3},{5,4},{6,5},{7,6},{8,7},{9,8},{10,9... | collective-permute-start | bytes 36872 | tf_op jit(solution)/shard_map/ppermute | solution.py:21
  50.2 1.9 %collective-permute-start.9 = (f32[3,8,128]{2,1,0:T(8,128)S(1)}, f32[3,8,128]{2,1,0:T(8,128)S(1)}, u32[]{:S(2)}, u32[]{:S(2)}) collective-permute-start(f32[3,8,128]{2,1,0:T(8,128)S(1)} %fusion.own.k1), channel_id=1, source_target_pairs={{0,1},{1,2},{2,3},{3,4},{4,5},{5,6},{6,7},{7,8},{8,9},{9,10},{10,1... | collective-permute-start | bytes 36872 | tf_op jit(solution)/shard_map/ppermute | solution.py:21
  50.2 7.7 %collective-permute-start.8 = (f32[3,8,128]{2,1,0:T(8,128)S(1)}, f32[3,8,128]{2,1,0:T(8,128)S(1)}, u32[]{:S(2)}, u32[]{:S(2)}) collective-permute-start(f32[3,8,128]{2,1,0:T(8,128)S(1)} %fusion.own.k1), channel_id=1, source_target_pairs={{0,32},{32,64},{64,96},{96,128},{128,160},{160,192},{192,224},{224... | collective-permute-start | bytes 36872 | tf_op jit(solution)/shard_map/ppermute | solution.py:21
  60.1 10.9 %collective-permute-start.12 = (f32[3,8,128]{2,1,0:T(8,128)S(1)}, f32[3,8,128]{2,1,0:T(8,128)S(1)}, u32[]{:S(2)}, u32[]{:S(2)}) collective-permute-start(f32[3,8,128]{2,1,0:T(8,128)S(1)} %get-tuple-element.42), channel_id=1, source_target_pairs={{0,32},{32,64},{64,96},{96,128},{128,160},{160,192},{192,224},{224... | collective-permute-start | bytes 36872 | tf_op jit(solution)/shard_map/ppermute | solution.py:21
  62.0 9.0 %collective-permute-start.13 = (f32[3,8,128]{2,1,0:T(8,128)S(1)}, f32[3,8,128]{2,1,0:T(8,128)S(1)}, u32[]{:S(2)}, u32[]{:S(2)}) collective-permute-start(f32[3,8,128]{2,1,0:T(8,128)S(1)} %get-tuple-element.43), channel_id=1, source_target_pairs={{0,480},{32,0},{64,32},{96,64},{128,96},{160,128},{192,160},{224,1... | collective-permute-start | bytes 36872 | tf_op jit(solution)/shard_map/ppermute | solution.py:21
  68.7 2.9 %collective-permute-start.14 = (f32[3,8,128]{2,1,0:T(8,128)S(1)}, f32[3,8,128]{2,1,0:T(8,128)S(1)}, u32[]{:S(2)}, u32[]{:S(2)}) collective-permute-start(f32[3,8,128]{2,1,0:T(8,128)S(1)} %get-tuple-element.44), channel_id=1, source_target_pairs={{0,1},{1,2},{2,3},{3,4},{4,5},{5,6},{6,7},{7,8},{8,9},{9,10},{10,1... | collective-permute-start | bytes 36872 | tf_op jit(solution)/shard_map/ppermute | solution.py:21
  68.7 3.1 %collective-permute-start.15 = (f32[3,8,128]{2,1,0:T(8,128)S(1)}, f32[3,8,128]{2,1,0:T(8,128)S(1)}, u32[]{:S(2)}, u32[]{:S(2)}) collective-permute-start(f32[3,8,128]{2,1,0:T(8,128)S(1)} %get-tuple-element.45), channel_id=1, source_target_pairs={{0,31},{1,0},{2,1},{3,2},{4,3},{5,4},{6,5},{7,6},{8,7},{9,8},{10,9... | collective-permute-start | bytes 36872 | tf_op jit(solution)/shard_map/ppermute | solution.py:21
  71.8 9.9 %collective-permute-start.19 = (f32[3,8,128]{2,1,0:T(8,128)S(1)}, f32[3,8,128]{2,1,0:T(8,128)S(1)}, u32[]{:S(2)}, u32[]{:S(2)}) collective-permute-start(f32[3,8,128]{2,1,0:T(8,128)S(1)} %select_add_fusion.1.own.k2), channel_id=1, source_target_pairs={{0,480},{32,0},{64,32},{96,64},{128,96},{160,128},{192,160},{224,1... | collective-permute-start | bytes 36872 | tf_op jit(solution)/shard_map/ppermute | solution.py:21
  76.5 5.3 %collective-permute-start.18 = (f32[3,8,128]{2,1,0:T(8,128)S(1)}, f32[3,8,128]{2,1,0:T(8,128)S(1)}, u32[]{:S(2)}, u32[]{:S(2)}) collective-permute-start(f32[3,8,128]{2,1,0:T(8,128)S(1)} %select_add_fusion.1.own.k2), channel_id=1, source_target_pairs={{0,31},{1,0},{2,1},{3,2},{4,3},{5,4},{6,5},{7,6},{8,7},{9,8},{10,9... | collective-permute-start | bytes 36872 | tf_op jit(solution)/shard_map/ppermute | solution.py:21
  79.8 1.9 %collective-permute-start.17 = (f32[3,8,128]{2,1,0:T(8,128)S(1)}, f32[3,8,128]{2,1,0:T(8,128)S(1)}, u32[]{:S(2)}, u32[]{:S(2)}) collective-permute-start(f32[3,8,128]{2,1,0:T(8,128)S(1)} %select_add_fusion.1.own.k2), channel_id=1, source_target_pairs={{0,1},{1,2},{2,3},{3,4},{4,5},{5,6},{6,7},{7,8},{8,9},{9,10},{10,1... | collective-permute-start | bytes 36872 | tf_op jit(solution)/shard_map/ppermute | solution.py:21
  79.8 7.7 %collective-permute-start.16 = (f32[3,8,128]{2,1,0:T(8,128)S(1)}, f32[3,8,128]{2,1,0:T(8,128)S(1)}, u32[]{:S(2)}, u32[]{:S(2)}) collective-permute-start(f32[3,8,128]{2,1,0:T(8,128)S(1)} %select_add_fusion.1.own.k2), channel_id=1, source_target_pairs={{0,32},{32,64},{64,96},{96,128},{128,160},{160,192},{192,224},{224... | collective-permute-start | bytes 36872 | tf_op jit(solution)/shard_map/ppermute | solution.py:21
  102.4 21.3 %all-to-all-start.1 = ((f32[16,8,128]{2,1,0:T(8,128)}), f32[16,8,128]{2,1,0:T(8,128)S(1)}, u32[]{:S(2)}, u32[]{:S(2)}) async-start(f32[16,8,128]{2,1,0:T(8,128)} %broadcast_in_dim.32), calls=%async_computation.1 | async-start | bytes 131072 | tf_op jit(solution)/shard_map/all_to_all | solution.py:281
  109.1 11.4 %collective-permute-start.20 = (f32[3,8,128]{2,1,0:T(8,128)S(1)}, f32[3,8,128]{2,1,0:T(8,128)S(1)}, u32[]{:S(2)}, u32[]{:S(2)}) collective-permute-start(f32[3,8,128]{2,1,0:T(8,128)S(1)} %get-tuple-element.54), channel_id=1, source_target_pairs={{0,32},{32,64},{64,96},{96,128},{128,160},{160,192},{192,224},{224... | collective-permute-start | bytes 36872 | tf_op jit(solution)/shard_map/ppermute | solution.py:21
  111.4 9.1 %collective-permute-start.21 = (f32[3,8,128]{2,1,0:T(8,128)S(1)}, f32[3,8,128]{2,1,0:T(8,128)S(1)}, u32[]{:S(2)}, u32[]{:S(2)}) collective-permute-start(f32[3,8,128]{2,1,0:T(8,128)S(1)} %get-tuple-element.55), channel_id=1, source_target_pairs={{0,480},{32,0},{64,32},{96,64},{128,96},{160,128},{192,160},{224,1... | collective-permute-start | bytes 36872 | tf_op jit(solution)/shard_map/ppermute | solution.py:21
  117.8 3.6 %collective-permute-start.22 = (f32[3,8,128]{2,1,0:T(8,128)S(1)}, f32[3,8,128]{2,1,0:T(8,128)S(1)}, u32[]{:S(2)}, u32[]{:S(2)}) collective-permute-start(f32[3,8,128]{2,1,0:T(8,128)S(1)} %get-tuple-element.56), channel_id=1, source_target_pairs={{0,1},{1,2},{2,3},{3,4},{4,5},{5,6},{6,7},{7,8},{8,9},{9,10},{10,1... | collective-permute-start | bytes 36872 | tf_op jit(solution)/shard_map/ppermute | solution.py:21
  120.5 3.1 %collective-permute-start.23 = (f32[3,8,128]{2,1,0:T(8,128)S(1)}, f32[3,8,128]{2,1,0:T(8,128)S(1)}, u32[]{:S(2)}, u32[]{:S(2)}) collective-permute-start(f32[3,8,128]{2,1,0:T(8,128)S(1)} %get-tuple-element.57), channel_id=1, source_target_pairs={{0,31},{1,0},{2,1},{3,2},{4,3},{5,4},{6,5},{7,6},{8,7},{9,8},{10,9... | collective-permute-start | bytes 36872 | tf_op jit(solution)/shard_map/ppermute | solution.py:21

commit v5 on v3

--- a/solution.py
+++ b/solution.py
@@ -27,61 +27,59 @@
 
 
 def operator_kernel(
-    sweep, ids, own, from_axial_dn, from_cross_dn, from_cross_up, from_axial_up, tiles, drag, carried,
-    to_axial_dn, to_cross_dn, to_cross_up, to_axial_up, kept, moments, ext, acc,
+    sweep, own, from_axial_dn, from_cross_dn, from_cross_up, from_axial_up, tiles, drag,
+    picker, adder, carried,
+    to_axial_dn, to_cross_dn, to_cross_up, to_axial_up, kept, moments, products,
 ):
-    blocks, count = ids.shape
-    width = tiles.shape[-1]
+    blocks, count, width = tiles.shape[0], tiles.shape[1], tiles.shape[3]
     slab = lax.axis_index("cross")
     has_dn = jnp.where(slab > 0, 1.0, 0.0).astype(jnp.float32)
     has_up = jnp.where(slab < lax.axis_size("cross") - 1, 1.0, 0.0).astype(jnp.float32)
     sources = (from_axial_dn, from_cross_dn, own, from_cross_up, from_axial_up)
-    blank = jnp.zeros((blocks, width), jnp.float32)
-    for place, source in zip(PLACES, sources):
-        base = place * blocks * SUB
-        for comp in range(3):
-            x = source[comp]
-            if place == 3:
-                x = x * has_dn
-            if place == 5:
-                x = x * has_up
+    scales = (None, has_dn, None, has_up, None)
+    highs, lows = [], []
+    for comp in range(3):
+        for source, scale in zip(sources, scales):
+            x = source[comp] if scale is None else source[comp] * scale
             high, low = high_low(x)
-            ext[pl.ds(base + comp, blocks, stride=SUB), :] = high
-            ext[pl.ds(base + LOW + comp, blocks, stride=SUB), :] = low
-        ext[pl.ds(base + 3, blocks, stride=SUB), :] = blank
-        ext[pl.ds(base + LOW + 3, blocks, stride=SUB), :] = blank
-    acc[...] = jnp.zeros_like(acc)
+            highs.append(high)
+            lows.append(low)
+    spare = picker.shape[1] - 6 * len(PLACES) * blocks
+    listed = jnp.concatenate(highs + lows + [jnp.zeros((spare, width), jnp.float32)], axis=0)
+    picked = jnp.dot(
+        picker[...], listed.astype(jnp.bfloat16), preferred_element_type=jnp.float32
+    ).astype(jnp.bfloat16)
     rows = lax.broadcasted_iota(jnp.int32, (SUB, width), 0)
     squares = jnp.zeros((SUB, width), jnp.float32)
     for b in range(blocks):
-        starts = [pl.multiple_of(ids[b, k] * SUB, SUB) for k in range(count)]
         coupled = jnp.zeros((SUB, width), jnp.float32)
         for k in range(0, count, 2):
-            picked = jnp.concatenate(
-                [ext[pl.ds(starts[k], SUB), :], ext[pl.ds(starts[k + 1], SUB), :]], axis=1
-            ).astype(jnp.bfloat16)
+            at = (b * count + k) * SUB
+            both = jnp.concatenate([picked[at : at + SUB], picked[at + SUB : at + 2 * SUB]], axis=1)
             pair = jnp.concatenate([tiles[b, k], tiles[b, k + 1]], axis=1)
             coupled += lax.dot_general(
-                picked, pair, (((1,), (1,)), ((), ())), preferred_element_type=jnp.float32
+                both, pair, (((1,), (1,)), ((), ())), preferred_element_type=jnp.float32
             )
         coupled = coupled + pltpu.roll(coupled, LOW, 0)
         squares += jnp.where(rows < LOW, coupled * coupled, 0.0)
         high, low = high_low(coupled)
         parts = jnp.where(rows < LOW, high, low).astype(jnp.bfloat16)
         for k in range(count):
-            acc[pl.ds(starts[k], SUB), :] += jnp.dot(
+            at = (b * count + k) * SUB
+            products[at : at + SUB, :] = jnp.dot(
                 parts, tiles[b, k], preferred_element_type=jnp.float32
             )
+    high, low = high_low(products[...])
+    returned = jnp.dot(
+        adder[...], high.astype(jnp.bfloat16), preferred_element_type=jnp.float32
+    ) + jnp.dot(adder[...], low.astype(jnp.bfloat16), preferred_element_type=jnp.float32)
     targets = (to_axial_dn, to_cross_dn, None, to_cross_up, to_axial_up)
     even = jnp.zeros((blocks, width), jnp.float32)
     odd = squares
-    for place, target in zip(PLACES, targets):
-        base = place * blocks * SUB
-        for comp in range(3):
-            total = (
-                acc[pl.ds(base + comp, blocks, stride=SUB), :]
-                + acc[pl.ds(base + LOW + comp, blocks, stride=SUB), :]
-            )
+    for comp in range(3):
+        for place, target in enumerate(targets):
+            at = (comp * len(PLACES) + place) * blocks
+            total = returned[at : at + blocks]
             if target is None:
                 x = own[comp]
                 dragged = drag[...] * x
@@ -103,7 +101,7 @@
         moments[...] = jnp.broadcast_to(merged, moments.shape)
 
 
-def operator_call(sweep, ids, sources, tiles, drag, carried, copies):
+def operator_call(sweep, sources, tiles, drag, picker, adder, carried, copies):
     blocks, width = drag.shape
     vmem = pl.BlockSpec(memory_space=pltpu.VMEM)
     field = jax.ShapeDtypeStruct((3, blocks, width), jnp.float32)
@@ -112,15 +110,28 @@
     plane = jax.ShapeDtypeStruct(plane, jnp.float32)
     return pl.pallas_call(
         functools.partial(operator_kernel, sweep),
-        in_specs=[pl.BlockSpec(memory_space=pltpu.SMEM)] + [vmem] * 8,
+        in_specs=[vmem] * 10,
         out_specs=[vmem] * 6,
         out_shape=[field, across, across, field, field, plane],
-        scratch_shapes=[
-            pltpu.VMEM((8 * blocks * SUB, width), jnp.float32),
-            pltpu.VMEM((8 * blocks * SUB, width), jnp.float32),
-        ],
+        scratch_shapes=[pltpu.VMEM((tiles.shape[0] * tiles.shape[1] * SUB, width), jnp.float32)],
         compiler_params=pltpu.CompilerParams(vmem_limit_bytes=4 << 20),
-    )(ids, *sources, tiles, drag, carried)
+    )(*sources, tiles, drag, picker, adder, carried)
+
+
+def one_hots(tile_ids, blocks):
+    place = tile_ids // blocks
+    order = sum((place >= p).astype(jnp.int32) for p in PLACES[1:])
+    entry = jnp.repeat((order * blocks + tile_ids % blocks).reshape(-1), SUB)
+    row = lax.broadcasted_iota(jnp.int32, entry.shape, 0) % SUB
+    comp, listed = row % LOW, len(PLACES) * blocks
+    used = comp < 3
+    source = jnp.where(used, (comp + 3 * (row // LOW)) * listed + entry, -1)
+    target = jnp.where(used, comp * listed + entry, -1)
+    wide = -(-6 * listed // 128) * 128
+    tall = -(-3 * listed // 16) * 16
+    picker = source[:, None] == lax.broadcasted_iota(jnp.int32, (1, wide), 1)
+    adder = lax.broadcasted_iota(jnp.int32, (tall, 1), 0) == target[None, :]
+    return picker.astype(jnp.bfloat16), adder.astype(jnp.bfloat16)
 
 
 def shifted_poly(poly):
@@ -285,7 +296,7 @@
     field = jnp.swapaxes(force[0, 0], 0, 1)
     drag = self_drag[0, 0]
     blocks, width = drag.shape
-    ids = tile_ids[0, 0]
+    picker, adder = one_hots(tile_ids[0, 0], blocks)
     slab = lax.axis_index("cross")
     last = lax.axis_size("cross") - 1
     carried = leaving_rows(mig_rows, mig_count, blocks, width)
@@ -302,7 +313,7 @@
         below.append(cross_dn)
         above.append(cross_up)
         r1, r3, r5, r7, kept, carried = operator_call(
-            sweep, ids, (now, axial_dn, cross_dn, cross_up, axial_up), held, drag, carried,
+            sweep, (now, axial_dn, cross_dn, cross_up, axial_up), held, drag, picker, adder, carried,
             2 * lax.axis_size("axial") if sweep == ITERS - 1 else None,
         )
         if sweep == ITERS - 1:

time: 124 us -> 123 us (level)
    unnamed x8 -> x6, local copies, waits for them, and re-layouts: 2.99 us -> 2.98 us
  transfers between devices with their start and end apart: 26 -> 26, of which waited for: 9 -> 9; matrix products, arithmetic and copies ran while one was open for 1% -> 2% of each run, Pallas kernels for 0% -> 0%
where the time goes in v5:
time: 123 us
  starting transfers between devices  84.6 us (69%)
  waiting for transfers between devices  23.9 us (19%)
  Pallas kernels  7.35 us (6%)
  local copies, waits for them, and re-layouts  4.62 us (4%)
    ppermute x24, starting transfers between devices, ring_shift(): return lax.ppermute(shard, axis, ring(lax.axis_size(axis), by))  72.7 us
    ppermute x24, waiting for transfers between devices, ring_shift(): return lax.ppermute(shard, axis, ring(lax.axis_size(axis), by))  14.6 us
    all_to_all x2, starting transfers between devices, spread_sum(): lax.all_to_all(part, ('axial', 'cross'), 0, 0, axis_index_groups=groups)  11.9 us
    all_to_all x2, waiting for transfers between devices, spread_sum(): lax.all_to_all(part, ('axial', 'cross'), 0, 0, axis_index_groups=groups)  9.37 us
    pallas_call x3, Pallas kernels, operator_call(): pl.pallas_call(functools.partial(operator_kernel, sweep), in_specs=[vmem]...  6.28 us
    unnamed x6, local copies, waits for them, and re-layouts  2.98 us
  transfers between devices with their start and end apart: 26, of which 9 were waited for; matrix products, arithmetic and copies ran while one was open for 2% of the time, Pallas kernels for 0%

profile of v5, /device:TPU:1, one launch (start us, length us, event | category | flops | bytes accessed | tf_op | source)
XLA Modules:
  0.0 122.5 jit_solution(6767497081135428284)
XLA Ops:
  0.6 7.7 %collective-permute-start.3 = (f32[3,8,128]{2,1,0:T(8,128)}, f32[3,8,128]{2,1,0:T(8,128)S(1)}, u32[]{:S(2)}, u32[]{:S(2)}) collective-permute-start(f32[3,8,128]{2,1,0:T(8,128)} %bitcast.20), channel_id=1, source_target_pairs={{0,480},{32,0},{64,32},{96,64},{128,96},{160,128},{192,160},{224,1... | collective-permute-start | bytes 36872 | tf_op jit(solution)/shard_map/ppermute | solution.py:21
  8.3 1.1 collective-permute-start.2
  9.5 1.4 %collective-permute-start.1 = (f32[3,8,128]{2,1,0:T(8,128)}, f32[3,8,128]{2,1,0:T(8,128)S(1)}, u32[]{:S(2)}, u32[]{:S(2)}) collective-permute-start(f32[3,8,128]{2,1,0:T(8,128)} %bitcast.22), channel_id=1, source_target_pairs={{0,1},{1,2},{2,3},{3,4},{4,5},{5,6},{6,7},{7,8},{8,9},{9,10},{10,1... | collective-permute-start | bytes 36872 | tf_op jit(solution)/shard_map/ppermute | solution.py:21
  10.8 2.3 %collective-permute-start = (f32[3,8,128]{2,1,0:T(8,128)}, f32[3,8,128]{2,1,0:T(8,128)S(1)}, u32[]{:S(2)}, u32[]{:S(2)}) collective-permute-start(f32[3,8,128]{2,1,0:T(8,128)} %bitcast.23), channel_id=1, source_target_pairs={{0,32},{32,64},{64,96},{96,128},{128,160},{160,192},{192,224},{224... | collective-permute-start | bytes 36872 | tf_op jit(solution)/shard_map/ppermute | solution.py:21
  13.1 0.8 squeeze.18
  13.9 0.8 fusion.16
  14.6 0.1 broadcast_in_dim.37
  14.7 0.1 reshape.86
  14.9 0.1 fusion.picker
  15.0 0.1 pad.4.clone
  15.1 0.1 fusion.4.carried
  15.2 1.6 %copy-done = bf16[1,1,8,8,128,128]{5,4,3,2,1,0:T(8,128)(2,1)S(1)} copy-done((bf16[1,1,8,8,128,128]{5,4,3,2,1,0:T(8,128)(2,1)S(1)}, bf16[1,1,8,8,128,128]{5,4,3,2,1,0:T(8,128)(2,1)}, u32[]{:S(2)}) %copy-start) | copy-done | bytes 2097176
  16.8 0.7 copy-done.1
  17.5 0.7 copy-done.2
  18.2 0.2 shard_map.85
  18.4 0.0 collective-permute-done.3.from_axial_up
  18.4 0.0 collective-permute-done.2.from_cross_up.u0
  18.4 0.4 collective-permute-done.1.from_cross_dn.d0
  18.8 0.0 collective-permute-done.from_axial_dn
  18.8 1.9 %shard_map.86 = (f32[3,8,128]{2,1,0:T(8,128)S(1)}, f32[4,8,128]{2,1,0:T(8,128)S(1)}, f32[4,8,128]{2,1,0:T(8,128)S(1)}, f32[3,8,128]{2,1,0:T(8,128)S(1)}, f32[3,8,128]{2,1,0:T(8,128)S(1)}, /*index=5*/f32[8,128]{1,0:T(8,128)S(1)}) custom-call(f32[3,8,128]{2,1,0:T(8,128)S(1)} %get-tuple-element.33.own.k0, f32[3,8,128]{2,1,0:T(8,128)S(1)} %collective-permute-done.from_axial_dn, ...), custom_call_target="tpu_custom_call" | custom-call | tf_op jit(solution)/shard_map/pallas_call | solution.py:111
  20.8 1.6 %collective-permute-start.6 = (f32[4,8,128]{2,1,0:T(8,128)S(1)}, f32[4,8,128]{2,1,0:T(8,128)S(1)}, u32[]{:S(2)}, u32[]{:S(2)}) collective-permute-start(f32[4,8,128]{2,1,0:T(8,128)S(1)} %get-tuple-element.39), channel_id=1, source_target_pairs={{0,1},{1,2},{2,3},{3,4},{4,5},{5,6},{6,7},{7,8},{8,9},{9,10},{10,1... | collective-permute-start | bytes 49160 | tf_op jit(solution)/shard_map/ppermute | solution.py:21
  22.4 6.7 %collective-permute-start.7 = (f32[4,8,128]{2,1,0:T(8,128)S(1)}, f32[4,8,128]{2,1,0:T(8,128)S(1)}, u32[]{:S(2)}, u32[]{:S(2)}) collective-permute-start(f32[4,8,128]{2,1,0:T(8,128)S(1)} %get-tuple-element.40), channel_id=1, source_target_pairs={{0,31},{1,0},{2,1},{3,2},{4,3},{5,4},{6,5},{7,6},{8,7},{9,8},{10,9... | collective-permute-start | bytes 49160 | tf_op jit(solution)/shard_map/ppermute | solution.py:21
  29.0 1.9 %collective-permute-start.4 = (f32[3,8,128]{2,1,0:T(8,128)S(1)}, f32[3,8,128]{2,1,0:T(8,128)S(1)}, u32[]{:S(2)}, u32[]{:S(2)}) collective-permute-start(f32[3,8,128]{2,1,0:T(8,128)S(1)} %get-tuple-element.37), channel_id=1, source_target_pairs={{0,32},{32,64},{64,96},{96,128},{128,160},{160,192},{192,224},{224... | collective-permute-start | bytes 36872 | tf_op jit(solution)/shard_map/ppermute | solution.py:21
  30.9 6.7 %collective-permute-start.5 = (f32[3,8,128]{2,1,0:T(8,128)S(1)}, f32[3,8,128]{2,1,0:T(8,128)S(1)}, u32[]{:S(2)}, u32[]{:S(2)}) collective-permute-start(f32[3,8,128]{2,1,0:T(8,128)S(1)} %get-tuple-element.38), channel_id=1, source_target_pairs={{0,480},{32,0},{64,32},{96,64},{128,96},{160,128},{192,160},{224,1... | collective-permute-start | bytes 36872 | tf_op jit(solution)/shard_map/ppermute | solution.py:21
  37.6 0.0 collective-permute-done.4
  37.6 0.8 collective-permute-done.5
  38.4 0.0 collective-permute-done.6.dn_plane
  38.4 0.0 collective-permute-done.7.up_plane
  38.5 6.9 %collective-permute-start.11 = (f32[3,8,128]{2,1,0:T(8,128)S(1)}, f32[3,8,128]{2,1,0:T(8,128)S(1)}, u32[]{:S(2)}, u32[]{:S(2)}) collective-permute-start(f32[3,8,128]{2,1,0:T(8,128)S(1)} %fusion.2.own.k1), channel_id=1, source_target_pairs={{0,480},{32,0},{64,32},{96,64},{128,96},{160,128},{192,160},{224,1... | collective-permute-start | bytes 36872 | tf_op jit(solution)/shard_map/ppermute | solution.py:21
  45.4 4.7 %collective-permute-start.10 = (f32[3,8,128]{2,1,0:T(8,128)S(1)}, f32[3,8,128]{2,1,0:T(8,128)S(1)}, u32[]{:S(2)}, u32[]{:S(2)}) collective-permute-start(f32[3,8,128]{2,1,0:T(8,128)S(1)} %fusion.2.own.k1), channel_id=1, source_target_pairs={{0,31},{1,0},{2,1},{3,2},{4,3},{5,4},{6,5},{7,6},{8,7},{9,8},{10,9... | collective-permute-start | bytes 36872 | tf_op jit(solution)/shard_map/ppermute | solution.py:21
  50.1 0.0 collective-permute-start.9
  50.1 1.9 %collective-permute-start.8 = (f32[3,8,128]{2,1,0:T(8,128)S(1)}, f32[3,8,128]{2,1,0:T(8,128)S(1)}, u32[]{:S(2)}, u32[]{:S(2)}) collective-permute-start(f32[3,8,128]{2,1,0:T(8,128)S(1)} %fusion.2.own.k1), channel_id=1, source_target_pairs={{0,32},{32,64},{64,96},{96,128},{128,160},{160,192},{192,224},{224... | collective-permute-start | bytes 36872 | tf_op jit(solution)/shard_map/ppermute | solution.py:21
  52.0 0.0 collective-permute-done.11.from_axial_up
  52.0 0.0 collective-permute-done.10.from_cross_up.u1
  52.0 5.8 %collective-permute-done.8.from_axial_dn = f32[3,8,128]{2,1,0:T(8,128)S(1)} collective-permute-done((f32[3,8,128]{2,1,0:T(8,128)S(1)}, f32[3,8,128]{2,1,0:T(8,128)S(1)}, u32[]{:S(2)}, u32[]{:S(2)}) %collective-permute-start.8) | collective-permute-done | bytes 12320 | tf_op jit(solution)/shard_map/ppermute | solution.py:21
  57.8 1.9 %shard_map.87 = (f32[3,8,128]{2,1,0:T(8,128)S(1)}, f32[3,8,128]{2,1,0:T(8,128)S(1)}, f32[3,8,128]{2,1,0:T(8,128)S(1)}, f32[3,8,128]{2,1,0:T(8,128)S(1)}, f32[3,8,128]{2,1,0:T(8,128)S(1)}, /*index=5*/f32[8,128]{1,0:T(8,128)S(1)}) custom-call(f32[3,8,128]{2,1,0:T(8,128)S(1)} %fusion.2.own.k1, f32[3,8,128]{2,1,0:T(8,128)S(1)} %collective-permute-done.8.from_axial_dn, ...), custom_call_target="tpu_custom_call" | custom-call | tf_op jit(solution)/shard_map/pallas_call | solution.py:111
  59.8 1.9 %collective-permute-start.12 = (f32[3,8,128]{2,1,0:T(8,128)S(1)}, f32[3,8,128]{2,1,0:T(8,128)S(1)}, u32[]{:S(2)}, u32[]{:S(2)}) collective-permute-start(f32[3,8,128]{2,1,0:T(8,128)S(1)} %get-tuple-element.43), channel_id=1, source_target_pairs={{0,32},{32,64},{64,96},{96,128},{128,160},{160,192},{192,224},{224... | collective-permute-start | bytes 36872 | tf_op jit(solution)/shard_map/ppermute | solution.py:21
  61.7 6.7 %collective-permute-start.13 = (f32[3,8,128]{2,1,0:T(8,128)S(1)}, f32[3,8,128]{2,1,0:T(8,128)S(1)}, u32[]{:S(2)}, u32[]{:S(2)}) collective-permute-start(f32[3,8,128]{2,1,0:T(8,128)S(1)} %get-tuple-element.44), channel_id=1, source_target_pairs={{0,480},{32,0},{64,32},{96,64},{128,96},{160,128},{192,160},{224,1... | collective-permute-start | bytes 36872 | tf_op jit(solution)/shard_map/ppermute | solution.py:21
  68.4 0.0 collective-permute-start.14
  68.4 2.2 %collective-permute-start.15 = (f32[3,8,128]{2,1,0:T(8,128)S(1)}, f32[3,8,128]{2,1,0:T(8,128)S(1)}, u32[]{:S(2)}, u32[]{:S(2)}) collective-permute-start(f32[3,8,128]{2,1,0:T(8,128)S(1)} %get-tuple-element.46), channel_id=1, source_target_pairs={{0,31},{1,0},{2,1},{3,2},{4,3},{5,4},{6,5},{7,6},{8,7},{9,8},{10,9... | collective-permute-start | bytes 36872 | tf_op jit(solution)/shard_map/ppermute | solution.py:21
  70.6 0.6 collective-permute-done.14
  71.3 0.3 collective-permute-done.15
  71.5 4.6 %collective-permute-start.19 = (f32[3,8,128]{2,1,0:T(8,128)S(1)}, f32[3,8,128]{2,1,0:T(8,128)S(1)}, u32[]{:S(2)}, u32[]{:S(2)}) collective-permute-start(f32[3,8,128]{2,1,0:T(8,128)S(1)} %select_add_fusion.1.own.k2), channel_id=1, source_target_pairs={{0,480},{32,0},{64,32},{96,64},{128,96},{160,128},{192,160},{224,1... | collective-permute-start | bytes 36872 | tf_op jit(solution)/shard_map/ppermute | solution.py:21
  76.1 3.4 %collective-permute-start.18 = (f32[3,8,128]{2,1,0:T(8,128)S(1)}, f32[3,8,128]{2,1,0:T(8,128)S(1)}, u32[]{:S(2)}, u32[]{:S(2)}) collective-permute-start(f32[3,8,128]{2,1,0:T(8,128)S(1)} %select_add_fusion.1.own.k2), channel_id=1, source_target_pairs={{0,31},{1,0},{2,1},{3,2},{4,3},{5,4},{6,5},{7,6},{8,7},{9,8},{10,9... | collective-permute-start | bytes 36872 | tf_op jit(solution)/shard_map/ppermute | solution.py:21
  79.5 0.0 collective-permute-start.17
  79.5 1.9 %collective-permute-start.16 = (f32[3,8,128]{2,1,0:T(8,128)S(1)}, f32[3,8,128]{2,1,0:T(8,128)S(1)}, u32[]{:S(2)}, u32[]{:S(2)}) collective-permute-start(f32[3,8,128]{2,1,0:T(8,128)S(1)} %select_add_fusion.1.own.k2), channel_id=1, source_target_pairs={{0,32},{32,64},{64,96},{96,128},{128,160},{160,192},{192,224},{224... | collective-permute-start | bytes 36872 | tf_op jit(solution)/shard_map/ppermute | solution.py:21
  81.4 0.0 collective-permute-done.19.from_axial_up
  81.5 0.0 collective-permute-done.17.from_cross_dn.d2
  81.5 5.8 %collective-permute-done.16.from_axial_dn = f32[3,8,128]{2,1,0:T(8,128)S(1)} collective-permute-done((f32[3,8,128]{2,1,0:T(8,128)S(1)}, f32[3,8,128]{2,1,0:T(8,128)S(1)}, u32[]{:S(2)}, u32[]{:S(2)}) %collective-permute-start.16) | collective-permute-done | bytes 12320 | tf_op jit(solution)/shard_map/ppermute | solution.py:21
  87.3 2.4 %shard_map.88 = (f32[3,8,128]{2,1,0:T(8,128)S(1)}, f32[3,8,128]{2,1,0:T(8,128)S(1)}, f32[3,8,128]{2,1,0:T(8,128)S(1)}, f32[3,8,128]{2,1,0:T(8,128)S(1)}, f32[3,8...) custom-call(f32[3,8,128]{2,1,0:T(8,128)S(1)} %select_add_fusion.1.own.k2, ...), custom_call_target="tpu_custom_call" | custom-call | tf_op jit(solution)/shard_map/pallas_call | solution.py:111
  89.7 5.2 %all-to-all-start = ((f32[32,8,128]{2,1,0:T(8,128)}), f32[32,8,128]{2,1,0:T(8,128)S(1)}, u32[]{:S(2)}, u32[]{:S(2)}) async-start(f32[32,8,128]{2,1,0:T(8,128)} %get-tuple-element.48), calls=%async_computation | async-start | bytes 262144 | tf_op jit(solution)/shard_map/all_to_all | solution.py:292
  94.9 0.0 collective-permute-start.20
  94.9 0.5 collective-permute-start.21
  95.4 7.2 %all-to-all-done = f32[32,8,128]{2,1,0:T(8,128)S(1)} async-done(((f32[32,8,128]{2,1,0:T(8,128)}), f32[32,8,128]{2,1,0:T(8,128)S(1)}, u32[]{:S(2)}, u32[]{:S(2)}) %all-to-all-start) | async-done | bytes 131104 | tf_op jit(solution)/shard_map/all_to_all | solution.py:292
  102.6 0.0 collective-permute-done.20
  102.7 0.0 collective-permute-done.21
  102.7 0.6 broadcast_in_dim.41
  103.3 6.8 %all-to-all-start.1 = ((f32[16,8,128]{2,1,0:T(8,128)}), f32[16,8,128]{2,1,0:T(8,128)S(1)}, u32[]{:S(2)}, u32[]{:S(2)}) async-start(f32[16,8,128]{2,1,0:T(8,128)} %broadcast_in_dim.41), calls=%async_computation.1 | async-start | bytes 131072 | tf_op jit(solution)/shard_map/all_to_all | solution.py:292
  110.1 2.3 %collective-permute-start.22 = (f32[3,8,128]{2,1,0:T(8,128)S(1)}, f32[3,8,128]{2,1,0:T(8,128)S(1)}, u32[]{:S(2)}, u32[]{:S(2)}) collective-permute-start(f32[3,8,128]{2,1,0:T(8,128)S(1)} %get-tuple-element.56), channel_id=1, source_target_pairs={{0,32},{32,64},{64,96},{96,128},{128,160},{160,192},{192,224},{224... | collective-permute-start | bytes 36872 | tf_op jit(solution)/shard_map/ppermute | solution.py:21
  112.4 6.3 %collective-permute-start.23 = (f32[3,8,128]{2,1,0:T(8,128)S(1)}, f32[3,8,128]{2,1,0:T(8,128)S(1)}, u32[]{:S(2)}, u32[]{:S(2)}) collective-permute-start(f32[3,8,128]{2,1,0:T(8,128)S(1)} %get-tuple-element.57), channel_id=1, source_target_pairs={{0,480},{32,0},{64,32},{96,64},{128,96},{160,128},{192,160},{224,1... | collective-permute-start | bytes 36872 | tf_op jit(solution)/shard_map/ppermute | solution.py:21
  118.7 0.0 collective-permute-done.22
  118.7 0.8 collective-permute-done.23
  119.5 2.2 %all-to-all-done.1.sums = f32[16,8,128]{2,1,0:T(8,128)S(1)} async-done(((f32[16,8,128]{2,1,0:T(8,128)}), f32[16,8,128]{2,1,0:T(8,128)S(1)}, u32[]{:S(2)}, u32[]{:S(2)}) %all-to-all-start.1) | async-done | bytes 65568 | tf_op jit(solution)/shard_map/all_to_all | solution.py:292
  121.7 0.9 shard_map.89
  (16 shorter events, 0.1 us)
Async XLA Ops:
  0.6 17.7 %collective-permute-start.3 = (f32[3,8,128]{2,1,0:T(8,128)}, f32[3,8,128]{2,1,0:T(8,128)S(1)}, u32[]{:S(2)}, u32[]{:S(2)}) collective-permute-start(f32[3,8,128]{2,1,0:T(8,128)} %bitcast.20), channel_id=1, source_target_pairs={{0,480},{32,0},{64,32},{96,64},{128,96},{160,128},{192,160},{224,1... | collective-permute-start | bytes 36872 | tf_op jit(solution)/shard_map/ppermute | solution.py:21
  8.3 10.1 %collective-permute-start.2 = (f32[3,8,128]{2,1,0:T(8,128)}, f32[3,8,128]{2,1,0:T(8,128)S(1)}, u32[]{:S(2)}, u32[]{:S(2)}) collective-permute-start(f32[3,8,128]{2,1,0:T(8,128)} %bitcast.21), channel_id=1, source_target_pairs={{0,31},{1,0},{2,1},{3,2},{4,3},{5,4},{6,5},{7,6},{8,7},{9,8},{10,9... | collective-permute-start | bytes 36872 | tf_op jit(solution)/shard_map/ppermute | solution.py:21
  9.5 9.4 %collective-permute-start.1 = (f32[3,8,128]{2,1,0:T(8,128)}, f32[3,8,128]{2,1,0:T(8,128)S(1)}, u32[]{:S(2)}, u32[]{:S(2)}) collective-permute-start(f32[3,8,128]{2,1,0:T(8,128)} %bitcast.22), channel_id=1, source_target_pairs={{0,1},{1,2},{2,3},{3,4},{4,5},{5,6},{6,7},{7,8},{8,9},{9,10},{10,1... | collective-permute-start | bytes 36872 | tf_op jit(solution)/shard_map/ppermute | solution.py:21
  10.8 8.0 %collective-permute-start = (f32[3,8,128]{2,1,0:T(8,128)}, f32[3,8,128]{2,1,0:T(8,128)S(1)}, u32[]{:S(2)}, u32[]{:S(2)}) collective-permute-start(f32[3,8,128]{2,1,0:T(8,128)} %bitcast.23), channel_id=1, source_target_pairs={{0,32},{32,64},{64,96},{96,128},{128,160},{160,192},{192,224},{224... | collective-permute-start | bytes 36872 | tf_op jit(solution)/shard_map/ppermute | solution.py:21
  15.2 1.6 %copy-start = (bf16[1,1,8,8,128,128]{5,4,3,2,1,0:T(8,128)(2,1)S(1)}, bf16[1,1,8,8,128,128]{5,4,3,2,1,0:T(8,128)(2,1)}, u32[]{:S(2)}) copy-start(bf16[1,1,8,8,128,128]{5,4,3,2,1,0:T(8,128)(2,1)} %param.8) | copy-start | bytes 6291460
  16.8 0.7 copy-start.1
  17.5 0.7 copy-start.2
  20.8 17.7 %collective-permute-start.6 = (f32[4,8,128]{2,1,0:T(8,128)S(1)}, f32[4,8,128]{2,1,0:T(8,128)S(1)}, u32[]{:S(2)}, u32[]{:S(2)}) collective-permute-start(f32[4,8,128]{2,1,0:T(8,128)S(1)} %get-tuple-element.39), channel_id=1, source_target_pairs={{0,1},{1,2},{2,3},{3,4},{4,5},{5,6},{6,7},{7,8},{8,9},{9,10},{10,1... | collective-permute-start | bytes 49160 | tf_op jit(solution)/shard_map/ppermute | solution.py:21
  22.4 16.1 %collective-permute-start.7 = (f32[4,8,128]{2,1,0:T(8,128)S(1)}, f32[4,8,128]{2,1,0:T(8,128)S(1)}, u32[]{:S(2)}, u32[]{:S(2)}) collective-permute-start(f32[4,8,128]{2,1,0:T(8,128)S(1)} %get-tuple-element.40), channel_id=1, source_target_pairs={{0,31},{1,0},{2,1},{3,2},{4,3},{5,4},{6,5},{7,6},{8,7},{9,8},{10,9... | collective-permute-start | bytes 49160 | tf_op jit(solution)/shard_map/ppermute | solution.py:21
  29.0 8.6 %collective-permute-start.4 = (f32[3,8,128]{2,1,0:T(8,128)S(1)}, f32[3,8,128]{2,1,0:T(8,128)S(1)}, u32[]{:S(2)}, u32[]{:S(2)}) collective-permute-start(f32[3,8,128]{2,1,0:T(8,128)S(1)} %get-tuple-element.37), channel_id=1, source_target_pairs={{0,32},{32,64},{64,96},{96,128},{128,160},{160,192},{192,224},{224... | collective-permute-start | bytes 36872 | tf_op jit(solution)/shard_map/ppermute | solution.py:21
  30.9 7.5 %collective-permute-start.5 = (f32[3,8,128]{2,1,0:T(8,128)S(1)}, f32[3,8,128]{2,1,0:T(8,128)S(1)}, u32[]{:S(2)}, u32[]{:S(2)}) collective-permute-start(f32[3,8,128]{2,1,0:T(8,128)S(1)} %get-tuple-element.38), channel_id=1, source_target_pairs={{0,480},{32,0},{64,32},{96,64},{128,96},{160,128},{192,160},{224,1... | collective-permute-start | bytes 36872 | tf_op jit(solution)/shard_map/ppermute | solution.py:21
  38.5 13.5 %collective-permute-start.11 = (f32[3,8,128]{2,1,0:T(8,128)S(1)}, f32[3,8,128]{2,1,0:T(8,128)S(1)}, u32[]{:S(2)}, u32[]{:S(2)}) collective-permute-start(f32[3,8,128]{2,1,0:T(8,128)S(1)} %fusion.2.own.k1), channel_id=1, source_target_pairs={{0,480},{32,0},{64,32},{96,64},{128,96},{160,128},{192,160},{224,1... | collective-permute-start | bytes 36872 | tf_op jit(solution)/shard_map/ppermute | solution.py:21
  45.4 6.6 %collective-permute-start.10 = (f32[3,8,128]{2,1,0:T(8,128)S(1)}, f32[3,8,128]{2,1,0:T(8,128)S(1)}, u32[]{:S(2)}, u32[]{:S(2)}) collective-permute-start(f32[3,8,128]{2,1,0:T(8,128)S(1)} %fusion.2.own.k1), channel_id=1, source_target_pairs={{0,31},{1,0},{2,1},{3,2},{4,3},{5,4},{6,5},{7,6},{8,7},{9,8},{10,9... | collective-permute-start | bytes 36872 | tf_op jit(solution)/shard_map/ppermute | solution.py:21
  50.1 1.9 %collective-permute-start.9 = (f32[3,8,128]{2,1,0:T(8,128)S(1)}, f32[3,8,128]{2,1,0:T(8,128)S(1)}, u32[]{:S(2)}, u32[]{:S(2)}) collective-permute-start(f32[3,8,128]{2,1,0:T(8,128)S(1)} %fusion.2.own.k1), channel_id=1, source_target_pairs={{0,1},{1,2},{2,3},{3,4},{4,5},{5,6},{6,7},{7,8},{8,9},{9,10},{10,1... | collective-permute-start | bytes 36872 | tf_op jit(solution)/shard_map/ppermute | solution.py:21
  50.1 7.7 %collective-permute-start.8 = (f32[3,8,128]{2,1,0:T(8,128)S(1)}, f32[3,8,128]{2,1,0:T(8,128)S(1)}, u32[]{:S(2)}, u32[]{:S(2)}) collective-permute-start(f32[3,8,128]{2,1,0:T(8,128)S(1)} %fusion.2.own.k1), channel_id=1, source_target_pairs={{0,32},{32,64},{64,96},{96,128},{128,160},{160,192},{192,224},{224... | collective-permute-start | bytes 36872 | tf_op jit(solution)/shard_map/ppermute | solution.py:21
  59.8 10.9 %collective-permute-start.12 = (f32[3,8,128]{2,1,0:T(8,128)S(1)}, f32[3,8,128]{2,1,0:T(8,128)S(1)}, u32[]{:S(2)}, u32[]{:S(2)}) collective-permute-start(f32[3,8,128]{2,1,0:T(8,128)S(1)} %get-tuple-element.43), channel_id=1, source_target_pairs={{0,32},{32,64},{64,96},{96,128},{128,160},{160,192},{192,224},{224... | collective-permute-start | bytes 36872 | tf_op jit(solution)/shard_map/ppermute | solution.py:21
  61.7 9.0 %collective-permute-start.13 = (f32[3,8,128]{2,1,0:T(8,128)S(1)}, f32[3,8,128]{2,1,0:T(8,128)S(1)}, u32[]{:S(2)}, u32[]{:S(2)}) collective-permute-start(f32[3,8,128]{2,1,0:T(8,128)S(1)} %get-tuple-element.44), channel_id=1, source_target_pairs={{0,480},{32,0},{64,32},{96,64},{128,96},{160,128},{192,160},{224,1... | collective-permute-start | bytes 36872 | tf_op jit(solution)/shard_map/ppermute | solution.py:21
  68.4 2.9 %collective-permute-start.14 = (f32[3,8,128]{2,1,0:T(8,128)S(1)}, f32[3,8,128]{2,1,0:T(8,128)S(1)}, u32[]{:S(2)}, u32[]{:S(2)}) collective-permute-start(f32[3,8,128]{2,1,0:T(8,128)S(1)} %get-tuple-element.45), channel_id=1, source_target_pairs={{0,1},{1,2},{2,3},{3,4},{4,5},{5,6},{6,7},{7,8},{8,9},{9,10},{10,1... | collective-permute-start | bytes 36872 | tf_op jit(solution)/shard_map/ppermute | solution.py:21
  68.4 3.1 %collective-permute-start.15 = (f32[3,8,128]{2,1,0:T(8,128)S(1)}, f32[3,8,128]{2,1,0:T(8,128)S(1)}, u32[]{:S(2)}, u32[]{:S(2)}) collective-permute-start(f32[3,8,128]{2,1,0:T(8,128)S(1)} %get-tuple-element.46), channel_id=1, source_target_pairs={{0,31},{1,0},{2,1},{3,2},{4,3},{5,4},{6,5},{7,6},{8,7},{9,8},{10,9... | collective-permute-start | bytes 36872 | tf_op jit(solution)/shard_map/ppermute | solution.py:21
  71.5 9.9 %collective-permute-start.19 = (f32[3,8,128]{2,1,0:T(8,128)S(1)}, f32[3,8,128]{2,1,0:T(8,128)S(1)}, u32[]{:S(2)}, u32[]{:S(2)}) collective-permute-start(f32[3,8,128]{2,1,0:T(8,128)S(1)} %select_add_fusion.1.own.k2), channel_id=1, source_target_pairs={{0,480},{32,0},{64,32},{96,64},{128,96},{160,128},{192,160},{224,1... | collective-permute-start | bytes 36872 | tf_op jit(solution)/shard_map/ppermute | solution.py:21
  76.1 5.3 %collective-permute-start.18 = (f32[3,8,128]{2,1,0:T(8,128)S(1)}, f32[3,8,128]{2,1,0:T(8,128)S(1)}, u32[]{:S(2)}, u32[]{:S(2)}) collective-permute-start(f32[3,8,128]{2,1,0:T(8,128)S(1)} %select_add_fusion.1.own.k2), channel_id=1, source_target_pairs={{0,31},{1,0},{2,1},{3,2},{4,3},{5,4},{6,5},{7,6},{8,7},{9,8},{10,9... | collective-permute-start | bytes 36872 | tf_op jit(solution)/shard_map/ppermute | solution.py:21
  79.5 1.9 %collective-permute-start.17 = (f32[3,8,128]{2,1,0:T(8,128)S(1)}, f32[3,8,128]{2,1,0:T(8,128)S(1)}, u32[]{:S(2)}, u32[]{:S(2)}) collective-permute-start(f32[3,8,128]{2,1,0:T(8,128)S(1)} %select_add_fusion.1.own.k2), channel_id=1, source_target_pairs={{0,1},{1,2},{2,3},{3,4},{4,5},{5,6},{6,7},{7,8},{8,9},{9,10},{10,1... | collective-permute-start | bytes 36872 | tf_op jit(solution)/shard_map/ppermute | solution.py:21
  79.5 7.7 %collective-permute-start.16 = (f32[3,8,128]{2,1,0:T(8,128)S(1)}, f32[3,8,128]{2,1,0:T(8,128)S(1)}, u32[]{:S(2)}, u32[]{:S(2)}) collective-permute-start(f32[3,8,128]{2,1,0:T(8,128)S(1)} %select_add_fusion.1.own.k2), channel_id=1, source_target_pairs={{0,32},{32,64},{64,96},{96,128},{128,160},{160,192},{192,224},{224... | collective-permute-start | bytes 36872 | tf_op jit(solution)/shard_map/ppermute | solution.py:21
  89.7 12.9 %all-to-all-start = ((f32[32,8,128]{2,1,0:T(8,128)}), f32[32,8,128]{2,1,0:T(8,128)S(1)}, u32[]{:S(2)}, u32[]{:S(2)}) async-start(f32[32,8,128]{2,1,0:T(8,128)} %get-tuple-element.48), calls=%async_computation | async-start | bytes 262144 | tf_op jit(solution)/shard_map/all_to_all | solution.py:292
  94.9 7.8 %collective-permute-start.20 = (f32[3,8,128]{2,1,0:T(8,128)S(1)}, f32[3,8,128]{2,1,0:T(8,128)S(1)}, u32[]{:S(2)}, u32[]{:S(2)}) collective-permute-start(f32[3,8,128]{2,1,0:T(8,128)S(1)} %get-tuple-element.52), channel_id=1, source_target_pairs={{0,1},{1,2},{2,3},{3,4},{4,5},{5,6},{6,7},{7,8},{8,9},{9,10},{10,1... | collective-permute-start | bytes 36872 | tf_op jit(solution)/shard_map/ppermute | solution.py:21
  94.9 7.8 %collective-permute-start.21 = (f32[3,8,128]{2,1,0:T(8,128)S(1)}, f32[3,8,128]{2,1,0:T(8,128)S(1)}, u32[]{:S(2)}, u32[]{:S(2)}) collective-permute-start(f32[3,8,128]{2,1,0:T(8,128)S(1)} %get-tuple-element.53), channel_id=1, source_target_pairs={{0,31},{1,0},{2,1},{3,2},{4,3},{5,4},{6,5},{7,6},{8,7},{9,8},{10,9... | collective-permute-start | bytes 36872 | tf_op jit(solution)/shard_map/ppermute | solution.py:21
  103.3 18.4 %all-to-all-start.1 = ((f32[16,8,128]{2,1,0:T(8,128)}), f32[16,8,128]{2,1,0:T(8,128)S(1)}, u32[]{:S(2)}, u32[]{:S(2)}) async-start(f32[16,8,128]{2,1,0:T(8,128)} %broadcast_in_dim.41), calls=%async_computation.1 | async-start | bytes 131072 | tf_op jit(solution)/shard_map/all_to_all | solution.py:292
  110.1 8.6 %collective-permute-start.22 = (f32[3,8,128]{2,1,0:T(8,128)S(1)}, f32[3,8,128]{2,1,0:T(8,128)S(1)}, u32[]{:S(2)}, u32[]{:S(2)}) collective-permute-start(f32[3,8,128]{2,1,0:T(8,128)S(1)} %get-tuple-element.56), channel_id=1, source_target_pairs={{0,32},{32,64},{64,96},{96,128},{128,160},{160,192},{192,224},{224... | collective-permute-start | bytes 36872 | tf_op jit(solution)/shard_map/ppermute | solution.py:21
  112.4 7.1 %collective-permute-start.23 = (f32[3,8,128]{2,1,0:T(8,128)S(1)}, f32[3,8,128]{2,1,0:T(8,128)S(1)}, u32[]{:S(2)}, u32[]{:S(2)}) collective-permute-start(f32[3,8,128]{2,1,0:T(8,128)S(1)} %get-tuple-element.57), channel_id=1, source_target_pairs={{0,480},{32,0},{64,32},{96,64},{128,96},{160,128},{192,160},{224,1... | collective-permute-start | bytes 36872 | tf_op jit(solution)/shard_map/ppermute | solution.py:21

commit v6 on v3

--- a/solution.py
+++ b/solution.py
@@ -10,6 +10,7 @@
 ITERS = 3
 PLACES = (1, 3, 4, 5, 7)
 SUB = 8
+FIRST_EXCHANGE_FLOPS = 8 * 10**9
 LOW = 4
 
 
@@ -27,9 +28,13 @@
 
 
 def operator_kernel(
-    sweep, ids, own, from_axial_dn, from_cross_dn, from_cross_up, from_axial_up, tiles, drag, carried,
-    to_axial_dn, to_cross_dn, to_cross_up, to_axial_up, kept, moments, ext, acc,
+    sweep, ids, own, from_axial_dn, from_cross_dn, from_cross_up, from_axial_up, tiles, drag, *rest
 ):
+    many = (1, 2, 1)[sweep]
+    carried, rest = rest[:many], rest[many:]
+    (
+        to_axial_dn, to_cross_dn, to_cross_up, to_axial_up, kept, moments, ext, acc,
+    ) = rest
     blocks, count = ids.shape
     width = tiles.shape[-1]
     slab = lax.axis_index("cross")
@@ -92,35 +97,34 @@
                 target[comp] = total
     even = jnp.sum(even, axis=0, keepdims=True)
     odd = jnp.sum(odd, axis=0, keepdims=True)
-    if sweep == 0:
-        moments[...] = jnp.where(rows == 0, even, jnp.where(rows == 1, odd, 0.0))
-        to_cross_dn[3] = carried[...]
-        to_cross_up[3] = carried[...]
-    else:
-        merged = jnp.where(
-            rows == 2 * sweep, even, jnp.where(rows == 2 * sweep + 1, odd, carried[...])
-        )
-        moments[...] = jnp.broadcast_to(merged, moments.shape)
+    merged = jnp.where(
+        rows == 2 * sweep, even, jnp.where(rows == 2 * sweep + 1, odd, carried[0][...])
+    )
+    moments[...] = jnp.broadcast_to(merged, moments.shape)
+    if sweep == 1:
+        to_cross_dn[3] = carried[1][...]
+        to_cross_up[3] = carried[1][...]
 
 
 def operator_call(sweep, ids, sources, tiles, drag, carried, copies):
     blocks, width = drag.shape
     vmem = pl.BlockSpec(memory_space=pltpu.VMEM)
     field = jax.ShapeDtypeStruct((3, blocks, width), jnp.float32)
-    across = jax.ShapeDtypeStruct((4 if sweep == 0 else 3, blocks, width), jnp.float32)
+    across = jax.ShapeDtypeStruct((4 if sweep == 1 else 3, blocks, width), jnp.float32)
     plane = (SUB, width) if copies is None else (copies, SUB, width)
     plane = jax.ShapeDtypeStruct(plane, jnp.float32)
+    rows = 8 * blocks * SUB
+    scratch = [pltpu.VMEM((rows, width), jnp.float32), pltpu.VMEM((rows, width), jnp.float32)]
     return pl.pallas_call(
         functools.partial(operator_kernel, sweep),
-        in_specs=[pl.BlockSpec(memory_space=pltpu.SMEM)] + [vmem] * 8,
+        in_specs=[pl.BlockSpec(memory_space=pltpu.SMEM)]
+        + [vmem] * 5
+        + [vmem] * (2 + len(carried)),
         out_specs=[vmem] * 6,
         out_shape=[field, across, across, field, field, plane],
-        scratch_shapes=[
-            pltpu.VMEM((8 * blocks * SUB, width), jnp.float32),
-            pltpu.VMEM((8 * blocks * SUB, width), jnp.float32),
-        ],
+        scratch_shapes=scratch,
         compiler_params=pltpu.CompilerParams(vmem_limit_bytes=4 << 20),
-    )(ids, *sources, tiles, drag, carried)
+    )(ids, *sources, tiles, drag, *carried)
 
 
 def shifted_poly(poly):
@@ -232,30 +236,20 @@
     )(sums, *own, *below, *above, *planes)
 
 
-def stage_kernel(tiles, drag, force, tiles_out, drag_out, force_out, sems):
-    copies = [
-        pltpu.make_async_copy(source, target, sems.at[i])
-        for i, (source, target) in enumerate(
-            ((tiles, tiles_out), (drag, drag_out), (force, force_out))
-        )
-    ]
-    for copy in copies:
-        copy.start()
-    for copy in copies:
-        copy.wait()
-
-
-def stage_call(tiles, drag, force):
-    arrays = (tiles, drag, force)
+def no_moments_kernel(moments):
+    moments[...] = jnp.zeros_like(moments)
+
+
+def no_moments(width):
     return pl.pallas_call(
-        stage_kernel,
-        in_specs=[pl.BlockSpec(memory_space=pltpu.HBM)] * 3,
-        out_specs=[pl.BlockSpec(memory_space=pltpu.VMEM)] * 3,
-        out_shape=[jax.ShapeDtypeStruct(a.shape, a.dtype) for a in arrays],
-        scratch_shapes=[pltpu.SemaphoreType.DMA((3,))],
+        no_moments_kernel,
+        out_specs=pl.BlockSpec(memory_space=pltpu.VMEM),
+        out_shape=jax.ShapeDtypeStruct((SUB, width), jnp.float32),
         compiler_params=pltpu.CompilerParams(vmem_limit_bytes=4 << 20),
-        cost_estimate=pl.CostEstimate(flops=0, bytes_accessed=2 * tiles.size * 2, transcendentals=0),
-    )(*arrays)
+        cost_estimate=pl.CostEstimate(
+            flops=FIRST_EXCHANGE_FLOPS, bytes_accessed=4 * SUB * width, transcendentals=0
+        ),
+    )()
 
 
 def leaving_rows(mig_rows, mig_count, blocks, width):
@@ -288,25 +282,23 @@
     ids = tile_ids[0, 0]
     slab = lax.axis_index("cross")
     last = lax.axis_size("cross") - 1
-    carried = leaving_rows(mig_rows, mig_count, blocks, width)
-    now = field
-    held, drag, field = stage_call(tiles[0, 0], drag, field)
+    now, carried = field, (no_moments(width),)
     own, below, above, planes = [], [], [], []
     for sweep in range(ITERS):
         cross_dn = ring_shift(now, "cross", 1)
         cross_up = ring_shift(now, "cross", -1)
         axial_dn = ring_shift(now, "axial", 1)
         axial_up = ring_shift(now, "axial", -1)
-        now = field if sweep == 0 else now
         own.append(now)
         below.append(cross_dn)
         above.append(cross_up)
-        r1, r3, r5, r7, kept, carried = operator_call(
-            sweep, ids, (now, axial_dn, cross_dn, cross_up, axial_up), held, drag, carried,
+        r1, r3, r5, r7, kept, sums = operator_call(
+            sweep, ids, (now, axial_dn, cross_dn, cross_up, axial_up), tiles[0, 0], drag, carried,
             2 * lax.axis_size("axial") if sweep == ITERS - 1 else None,
         )
+        carried = (sums,)
         if sweep == ITERS - 1:
-            part = jnp.sum(spread_sum(carried, lambda a, c: c // 2), axis=0)
+            part = jnp.sum(spread_sum(sums, lambda a, c: c // 2), axis=0)
             part, r1, r7 = lax.optimization_barrier((part, r1, r7))
         from_lower_cross = ring_shift(r5, "cross", 1)
         from_upper_cross = ring_shift(r3, "cross", -1)
@@ -317,11 +309,14 @@
             sums = spread_sum(part, lambda a, c: (a, c % 2))
         from_lower_axial = ring_shift(r7, "axial", 1)
         from_upper_axial = ring_shift(r1, "axial", -1)
-        if sweep == 0:
+        if sweep == 1:
             planes = [from_lower_cross, from_upper_cross]
         now = kept + from_lower_axial + from_upper_axial
         now = now + jnp.where(slab > 0, from_lower_cross[:3], 0.0)
         now = now + jnp.where(slab < last, from_upper_cross[:3], 0.0)
+        if sweep == 0:
+            now, mig_rows, mig_count = lax.optimization_barrier((now, mig_rows, mig_count))
+            carried += (leaving_rows(mig_rows, mig_count, blocks, width),)
     own.append(now)
     velocity, residual, arrivals = finish_call(sums, own, below, above, planes)
     return (

time: 124 us -> 124 us (level)
  waiting for transfers between devices: 25.1 us -> 28.9 us
  local copies, waits for them, and re-layouts: 3.7 us -> 0.75 us
    ppermute x24, waiting for transfers between devices: 15.7 us -> 19.5 us  [ring_shift(): return lax.ppermute(shard, axis, ring(lax.axis_size(axis), by))]
    unnamed x8 -> x12, local copies, waits for them, and re-layouts: 2.99 us -> 0.03 us
  transfers between devices with their start and end apart: 26 -> 26, of which waited for: 9 -> 9; matrix products, arithmetic and copies ran while one was open for 1% -> 0% of each run, Pallas kernels for 0% -> 0%
where the time goes in v6:
time: 124 us; the launch traced here: 123 us
  starting transfers between devices  84.8 us (68%)
  waiting for transfers between devices  28.9 us (23%)
  Pallas kernels  7.57 us (6%)
    ppermute x24, starting transfers between devices, ring_shift(): return lax.ppermute(shard, axis, ring(lax.axis_size(axis), by))  72.8 us
    ppermute x24, waiting for transfers between devices, ring_shift(): return lax.ppermute(shard, axis, ring(lax.axis_size(axis), by))  19.5 us
    all_to_all x2, starting transfers between devices, spread_sum(): lax.all_to_all(part, ('axial', 'cross'), 0, 0, axis_index_groups=groups)  11.9 us
    all_to_all x2, waiting for transfers between devices, spread_sum(): lax.all_to_all(part, ('axial', 'cross'), 0, 0, axis_index_groups=groups)  9.37 us
    pallas_call x3, Pallas kernels, operator_call(): pl.pallas_call(functools.partial(operator_kernel, sweep), in_specs=[pl.Bl...  6.7 us
  transfers between devices with their start and end apart: 26, of which 9 were waited for; matrix products, arithmetic and copies ran while one was open for 0% of the time, Pallas kernels for 0%

profile of v6, /device:TPU:1, one launch (start us, length us, event | category | flops | bytes accessed | tf_op | source)
XLA Modules:
  0.0 123.1 jit_solution(11312676830184067062)
XLA Ops:
  0.6 0.0 copy-start
  0.7 7.8 %collective-permute-start.3 = (f32[3,8,128]{2,1,0:T(8,128)}, f32[3,8,128]{2,1,0:T(8,128)S(1)}, u32[]{:S(2)}, u32[]{:S(2)}) collective-permute-start(f32[3,8,128]{2,1,0:T(8,128)} %bitcast.21), channel_id=1, source_target_pairs={{0,480},{32,0},{64,32},{96,64},{128,96},{160,128},{192,160},{224,1... | collective-permute-start | bytes 36872 | tf_op jit(solution)/shard_map/ppermute | solution.py:22
  8.5 1.1 collective-permute-start.2
  9.6 1.4 %collective-permute-start.1 = (f32[3,8,128]{2,1,0:T(8,128)}, f32[3,8,128]{2,1,0:T(8,128)S(1)}, u32[]{:S(2)}, u32[]{:S(2)}) collective-permute-start(f32[3,8,128]{2,1,0:T(8,128)} %bitcast.23), channel_id=1, source_target_pairs={{0,1},{1,2},{2,3},{3,4},{4,5},{5,6},{6,7},{7,8},{8,9},{9,10},{10,1... | collective-permute-start | bytes 36872 | tf_op jit(solution)/shard_map/ppermute | solution.py:22
  11.0 2.3 %collective-permute-start = (f32[3,8,128]{2,1,0:T(8,128)}, f32[3,8,128]{2,1,0:T(8,128)S(1)}, u32[]{:S(2)}, u32[]{:S(2)}) collective-permute-start(f32[3,8,128]{2,1,0:T(8,128)} %bitcast.24), channel_id=1, source_target_pairs={{0,32},{32,64},{64,96},{96,128},{128,160},{160,192},{192,224},{224... | collective-permute-start | bytes 36872 | tf_op jit(solution)/shard_map/ppermute | solution.py:22
  13.3 0.0 copy-start.4
  13.3 0.0 copy-start.5
  13.3 0.0 collective-permute-done.3.from_axial_up
  13.3 0.0 collective-permute-done.2.from_cross_up.u0
  13.3 5.7 %collective-permute-done.1.from_cross_dn.d0 = f32[3,8,128]{2,1,0:T(8,128)S(1)} collective-permute-done((f32[3,8,128]{2,1,0:T(8,128)}, f32[3,8,128]{2,1,0:T(8,128)S(1)}, u32[]{:S(2)}, u32[]{:S(2)}) %collective-permute-start.1) | collective-permute-done | bytes 12320 | tf_op jit(solution)/shard_map/ppermute | solution.py:22
  19.0 0.0 collective-permute-done.from_axial_dn
  19.0 0.0 copy-done.1
  19.0 2.1 %shard_map.86 = (f32[3,8,128]{2,1,0:T(8,128)S(1)}, f32[3,8,128]{2,1,0:T(8,128)S(1)}, f32[3,8,128]{2,1,0:T(8,128)S(1)}, f32[3,8,128]{2,1,0:T(8,128)S(1)}, f32[3,8,128]{2,1,0:T(8,128)S(1)}, /*index=5*/f32[8,128]{1,0:T(8,128)S(1)}) custom-call(s32[8,8]{1,0:T(8,128)S(1)} %bitcast.27, f32[3,8,128]{2,1,0:T(8,128)S(1)} %bitcast.25, ...), custom_call_target="tpu_custom_call" | custom-call | tf_op jit(solution)/shard_map/pallas_call | solution.py:118
  21.1 1.9 %collective-permute-start.4 = (f32[3,8,128]{2,1,0:T(8,128)S(1)}, f32[3,8,128]{2,1,0:T(8,128)S(1)}, u32[]{:S(2)}, u32[]{:S(2)}) collective-permute-start(f32[3,8,128]{2,1,0:T(8,128)S(1)} %get-tuple-element.34), channel_id=1, source_target_pairs={{0,32},{32,64},{64,96},{96,128},{128,160},{160,192},{192,224},{224... | collective-permute-start | bytes 36872 | tf_op jit(solution)/shard_map/ppermute | solution.py:22
  23.0 6.7 %collective-permute-start.5 = (f32[3,8,128]{2,1,0:T(8,128)S(1)}, f32[3,8,128]{2,1,0:T(8,128)S(1)}, u32[]{:S(2)}, u32[]{:S(2)}) collective-permute-start(f32[3,8,128]{2,1,0:T(8,128)S(1)} %get-tuple-element.35), channel_id=1, source_target_pairs={{0,480},{32,0},{64,32},{96,64},{128,96},{160,128},{192,160},{224,1... | collective-permute-start | bytes 36872 | tf_op jit(solution)/shard_map/ppermute | solution.py:22
  29.7 2.2 %collective-permute-start.6 = (f32[3,8,128]{2,1,0:T(8,128)S(1)}, f32[3,8,128]{2,1,0:T(8,128)S(1)}, u32[]{:S(2)}, u32[]{:S(2)}) collective-permute-start(f32[3,8,128]{2,1,0:T(8,128)S(1)} %get-tuple-element.36), channel_id=1, source_target_pairs={{0,1},{1,2},{2,3},{3,4},{4,5},{5,6},{6,7},{7,8},{8,9},{9,10},{10,1... | collective-permute-start | bytes 36872 | tf_op jit(solution)/shard_map/ppermute | solution.py:22
  31.9 6.7 %collective-permute-start.7 = (f32[3,8,128]{2,1,0:T(8,128)S(1)}, f32[3,8,128]{2,1,0:T(8,128)S(1)}, u32[]{:S(2)}, u32[]{:S(2)}) collective-permute-start(f32[3,8,128]{2,1,0:T(8,128)S(1)} %get-tuple-element.37), channel_id=1, source_target_pairs={{0,31},{1,0},{2,1},{3,2},{4,3},{5,4},{6,5},{7,6},{8,7},{9,8},{10,9... | collective-permute-start | bytes 36872 | tf_op jit(solution)/shard_map/ppermute | solution.py:22
  38.5 0.1 pad.4.clone
  38.6 0.0 collective-permute-done.4
  38.6 0.0 collective-permute-done.5
  38.6 0.6 collective-permute-done.6
  39.2 0.2 collective-permute-done.7
  39.4 1.9 %collective-permute-start.11 = (f32[3,8,128]{2,1,0:T(8,128)S(1)}, f32[3,8,128]{2,1,0:T(8,128)S(1)}, u32[]{:S(2)}, u32[]{:S(2)}) collective-permute-start(f32[3,8,128]{2,1,0:T(8,128)S(1)} %select_add_fusion.1.own.k1), channel_id=1, source_target_pairs={{0,480},{32,0},{64,32},{96,64},{128,96},{160,128},{192,160},{224,1... | collective-permute-start | bytes 36872 | tf_op jit(solution)/shard_map/ppermute | solution.py:22
  41.3 6.1 %collective-permute-start.10 = (f32[3,8,128]{2,1,0:T(8,128)S(1)}, f32[3,8,128]{2,1,0:T(8,128)S(1)}, u32[]{:S(2)}, u32[]{:S(2)}) collective-permute-start(f32[3,8,128]{2,1,0:T(8,128)S(1)} %select_add_fusion.1.own.k1), channel_id=1, source_target_pairs={{0,31},{1,0},{2,1},{3,2},{4,3},{5,4},{6,5},{7,6},{8,7},{9,8},{10,9... | collective-permute-start | bytes 36872 | tf_op jit(solution)/shard_map/ppermute | solution.py:22
  47.4 0.0 collective-permute-start.9
  47.4 1.9 %collective-permute-start.8 = (f32[3,8,128]{2,1,0:T(8,128)S(1)}, f32[3,8,128]{2,1,0:T(8,128)S(1)}, u32[]{:S(2)}, u32[]{:S(2)}) collective-permute-start(f32[3,8,128]{2,1,0:T(8,128)S(1)} %select_add_fusion.1.own.k1), channel_id=1, source_target_pairs={{0,32},{32,64},{64,96},{96,128},{128,160},{160,192},{192,224},{224... | collective-permute-start | bytes 36872 | tf_op jit(solution)/shard_map/ppermute | solution.py:22
  49.4 0.1 fusion.4
  49.5 0.1 fusion.2.rest_1_
  49.5 0.0 collective-permute-done.11.from_axial_up
  49.5 0.0 collective-permute-done.10.from_cross_up.u1
  49.5 0.0 collective-permute-done.9.from_cross_dn.d1
  49.6 5.6 %collective-permute-done.8.from_axial_dn = f32[3,8,128]{2,1,0:T(8,128)S(1)} collective-permute-done((f32[3,8,128]{2,1,0:T(8,128)S(1)}, f32[3,8,128]{2,1,0:T(8,128)S(1)}, u32[]{:S(2)}, u32[]{:S(2)}) %collective-permute-start.8) | collective-permute-done | bytes 12320 | tf_op jit(solution)/shard_map/ppermute | solution.py:22
  55.2 2.1 %shard_map.87 = (f32[3,8,128]{2,1,0:T(8,128)S(1)}, f32[4,8,128]{2,1,0:T(8,128)S(1)}, f32[4,8,128]{2,1,0:T(8,128)S(1)}, f32[3,8,128]{2,1,0:T(8,128)S(1)}, f32[3,8,128]{2,1,0:T(8,128)S(1)}, /*index=5*/f32[8,128]{1,0:T(8,128)S(1)}) custom-call(s32[8,8]{1,0:T(8,128)S(1)} %bitcast.28, f32[3,8,128]{2,1,0:T(8,128)S(1)} %select_add_fusion.1.own.k1, ...), custom_call_target="tpu_custom_call" | custom-call | tf_op jit(solution)/shard_map/pallas_call | solution.py:118
  57.3 0.0 collective-permute-start.14
  57.3 1.7 %collective-permute-start.15 = (f32[4,8,128]{2,1,0:T(8,128)S(1)}, f32[4,8,128]{2,1,0:T(8,128)S(1)}, u32[]{:S(2)}, u32[]{:S(2)}) collective-permute-start(f32[4,8,128]{2,1,0:T(8,128)S(1)} %get-tuple-element.46), channel_id=1, source_target_pairs={{0,31},{1,0},{2,1},{3,2},{4,3},{5,4},{6,5},{7,6},{8,7},{9,8},{10,9... | collective-permute-start | bytes 49160 | tf_op jit(solution)/shard_map/ppermute | solution.py:22
  59.0 1.9 %collective-permute-start.12 = (f32[3,8,128]{2,1,0:T(8,128)S(1)}, f32[3,8,128]{2,1,0:T(8,128)S(1)}, u32[]{:S(2)}, u32[]{:S(2)}) collective-permute-start(f32[3,8,128]{2,1,0:T(8,128)S(1)} %get-tuple-element.43), channel_id=1, source_target_pairs={{0,32},{32,64},{64,96},{96,128},{128,160},{160,192},{192,224},{224... | collective-permute-start | bytes 36872 | tf_op jit(solution)/shard_map/ppermute | solution.py:22
  60.9 6.7 %collective-permute-start.13 = (f32[3,8,128]{2,1,0:T(8,128)S(1)}, f32[3,8,128]{2,1,0:T(8,128)S(1)}, u32[]{:S(2)}, u32[]{:S(2)}) collective-permute-start(f32[3,8,128]{2,1,0:T(8,128)S(1)} %get-tuple-element.44), channel_id=1, source_target_pairs={{0,480},{32,0},{64,32},{96,64},{128,96},{160,128},{192,160},{224,1... | collective-permute-start | bytes 36872 | tf_op jit(solution)/shard_map/ppermute | solution.py:22
  67.6 0.0 collective-permute-done.12
  67.6 0.8 collective-permute-done.13
  68.4 0.0 collective-permute-done.14.dn_plane
  68.4 0.0 collective-permute-done.15.up_plane
  68.4 6.9 %collective-permute-start.19 = (f32[3,8,128]{2,1,0:T(8,128)S(1)}, f32[3,8,128]{2,1,0:T(8,128)S(1)}, u32[]{:S(2)}, u32[]{:S(2)}) collective-permute-start(f32[3,8,128]{2,1,0:T(8,128)S(1)} %fusion.own.k2), channel_id=1, source_target_pairs={{0,480},{32,0},{64,32},{96,64},{128,96},{160,128},{192,160},{224,1... | collective-permute-start | bytes 36872 | tf_op jit(solution)/shard_map/ppermute | solution.py:22
  75.4 4.7 %collective-permute-start.18 = (f32[3,8,128]{2,1,0:T(8,128)S(1)}, f32[3,8,128]{2,1,0:T(8,128)S(1)}, u32[]{:S(2)}, u32[]{:S(2)}) collective-permute-start(f32[3,8,128]{2,1,0:T(8,128)S(1)} %fusion.own.k2), channel_id=1, source_target_pairs={{0,31},{1,0},{2,1},{3,2},{4,3},{5,4},{6,5},{7,6},{8,7},{9,8},{10,9... | collective-permute-start | bytes 36872 | tf_op jit(solution)/shard_map/ppermute | solution.py:22
  80.0 0.0 collective-permute-start.17
  80.0 1.9 %collective-permute-start.16 = (f32[3,8,128]{2,1,0:T(8,128)S(1)}, f32[3,8,128]{2,1,0:T(8,128)S(1)}, u32[]{:S(2)}, u32[]{:S(2)}) collective-permute-start(f32[3,8,128]{2,1,0:T(8,128)S(1)} %fusion.own.k2), channel_id=1, source_target_pairs={{0,32},{32,64},{64,96},{96,128},{128,160},{160,192},{192,224},{224... | collective-permute-start | bytes 36872 | tf_op jit(solution)/shard_map/ppermute | solution.py:22
  81.9 0.0 collective-permute-done.19.from_axial_up
  81.9 0.0 collective-permute-done.18.from_cross_up.u2
  82.0 0.0 collective-permute-done.17.from_cross_dn.d2
  82.0 5.8 %collective-permute-done.16.from_axial_dn = f32[3,8,128]{2,1,0:T(8,128)S(1)} collective-permute-done((f32[3,8,128]{2,1,0:T(8,128)S(1)}, f32[3,8,128]{2,1,0:T(8,128)S(1)}, u32[]{:S(2)}, u32[]{:S(2)}) %collective-permute-start.16) | collective-permute-done | bytes 12320 | tf_op jit(solution)/shard_map/ppermute | solution.py:22
  87.8 2.5 %shard_map.88 = (f32[3,8,128]{2,1,0:T(8,128)S(1)}, f32[3,8,128]{2,1,0:T(8,128)S(1)}, f32[3,8,128]{2,1,0:T(8,128)S(1)}, f32[3,8,128]{2,1,0:T(8,128)S(1)}, f32[3,8...) custom-call(s32[8,8]{1,0:T(8,128)S(1)} %bitcast.29, f32[3,8,128]{2,1,0:T(8,128)S(1)} %fusion.own.k2, ...), custom_call_target="tpu_custom_call" | custom-call | tf_op jit(solution)/shard_map/pallas_call | solution.py:118
  90.3 5.2 %all-to-all-start = ((f32[32,8,128]{2,1,0:T(8,128)}), f32[32,8,128]{2,1,0:T(8,128)S(1)}, u32[]{:S(2)}, u32[]{:S(2)}) async-start(f32[32,8,128]{2,1,0:T(8,128)} %get-tuple-element.48), calls=%async_computation | async-start | bytes 262144 | tf_op jit(solution)/shard_map/all_to_all | solution.py:275
  95.4 0.0 collective-permute-start.20
  95.5 0.5 collective-permute-start.21
  96.0 7.2 %all-to-all-done = f32[32,8,128]{2,1,0:T(8,128)S(1)} async-done(((f32[32,8,128]{2,1,0:T(8,128)}), f32[32,8,128]{2,1,0:T(8,128)S(1)}, u32[]{:S(2)}, u32[]{:S(2)}) %all-to-all-start) | async-done | bytes 131104 | tf_op jit(solution)/shard_map/all_to_all | solution.py:275
  103.2 0.0 collective-permute-done.20
  103.2 0.0 collective-permute-done.21
  103.2 0.6 broadcast_in_dim.32
  103.9 6.8 %all-to-all-start.1 = ((f32[16,8,128]{2,1,0:T(8,128)}), f32[16,8,128]{2,1,0:T(8,128)S(1)}, u32[]{:S(2)}, u32[]{:S(2)}) async-start(f32[16,8,128]{2,1,0:T(8,128)} %broadcast_in_dim.32), calls=%async_computation.1 | async-start | bytes 131072 | tf_op jit(solution)/shard_map/all_to_all | solution.py:275
  110.6 2.3 %collective-permute-start.22 = (f32[3,8,128]{2,1,0:T(8,128)S(1)}, f32[3,8,128]{2,1,0:T(8,128)S(1)}, u32[]{:S(2)}, u32[]{:S(2)}) collective-permute-start(f32[3,8,128]{2,1,0:T(8,128)S(1)} %get-tuple-element.56), channel_id=1, source_target_pairs={{0,32},{32,64},{64,96},{96,128},{128,160},{160,192},{192,224},{224... | collective-permute-start | bytes 36872 | tf_op jit(solution)/shard_map/ppermute | solution.py:22
  113.0 6.3 %collective-permute-start.23 = (f32[3,8,128]{2,1,0:T(8,128)S(1)}, f32[3,8,128]{2,1,0:T(8,128)S(1)}, u32[]{:S(2)}, u32[]{:S(2)}) collective-permute-start(f32[3,8,128]{2,1,0:T(8,128)S(1)} %get-tuple-element.57), channel_id=1, source_target_pairs={{0,480},{32,0},{64,32},{96,64},{128,96},{160,128},{192,160},{224,1... | collective-permute-start | bytes 36872 | tf_op jit(solution)/shard_map/ppermute | solution.py:22
  119.3 0.0 collective-permute-done.22
  119.3 0.8 collective-permute-done.23
  120.1 2.2 %all-to-all-done.1.sums = f32[16,8,128]{2,1,0:T(8,128)S(1)} async-done(((f32[16,8,128]{2,1,0:T(8,128)}), f32[16,8,128]{2,1,0:T(8,128)S(1)}, u32[]{:S(2)}, u32[]{:S(2)}) %all-to-all-start.1) | async-done | bytes 65568 | tf_op jit(solution)/shard_map/all_to_all | solution.py:275
  122.2 0.9 shard_map.89
  (15 shorter events, 0.1 us)
Async XLA Ops:
  0.6 18.4 %copy-start = (bf16[1,1,8,8,128,128]{5,4,3,2,1,0:T(8,128)(2,1)S(1)}, bf16[1,1,8,8,128,128]{5,4,3,2,1,0:T(8,128)(2,1)}, u32[]{:S(2)}) copy-start(bf16[1,1,8,8,128,128]{5,4,3,2,1,0:T(8,128)(2,1)} %param.8) | copy-start | bytes 6291460
  0.6 18.3 %copy-start.1 = (f32[1,1,8,3,128]{4,2,3,1,0:T(8,128)S(1)}, f32[1,1,8,3,128]{4,2,3,1,0:T(8,128)}, u32[]{:S(2)}) copy-start(f32[1,1,8,3,128]{4,2,3,1,0:T(8,128)} %param.6) | copy-start | bytes 36868
  0.7 18.3 %copy-start.2 = (s32[1,1,8,8]{3,2,1,0:T(8,128)S(1)}, s32[1,1,8,8]{3,2,1,0:T(8,128)}, u32[]{:S(2)}) copy-start(s32[1,1,8,8]{3,2,1,0:T(8,128)} %param.9) | copy-start | bytes 772
  0.7 18.3 %copy-start.3 = (f32[1,1,8,128]{3,2,1,0:T(8,128)S(1)}, f32[1,1,8,128]{3,2,1,0:T(8,128)}, u32[]{:S(2)}) copy-start(f32[1,1,8,128]{3,2,1,0:T(8,128)} %param.7) | copy-start | bytes 12292
  0.7 12.6 %collective-permute-start.3 = (f32[3,8,128]{2,1,0:T(8,128)}, f32[3,8,128]{2,1,0:T(8,128)S(1)}, u32[]{:S(2)}, u32[]{:S(2)}) collective-permute-start(f32[3,8,128]{2,1,0:T(8,128)} %bitcast.21), channel_id=1, source_target_pairs={{0,480},{32,0},{64,32},{96,64},{128,96},{160,128},{192,160},{224,1... | collective-permute-start | bytes 36872 | tf_op jit(solution)/shard_map/ppermute | solution.py:22
  8.5 4.8 %collective-permute-start.2 = (f32[3,8,128]{2,1,0:T(8,128)}, f32[3,8,128]{2,1,0:T(8,128)S(1)}, u32[]{:S(2)}, u32[]{:S(2)}) collective-permute-start(f32[3,8,128]{2,1,0:T(8,128)} %bitcast.22), channel_id=1, source_target_pairs={{0,31},{1,0},{2,1},{3,2},{4,3},{5,4},{6,5},{7,6},{8,7},{9,8},{10,9... | collective-permute-start | bytes 36872 | tf_op jit(solution)/shard_map/ppermute | solution.py:22
  9.6 9.4 %collective-permute-start.1 = (f32[3,8,128]{2,1,0:T(8,128)}, f32[3,8,128]{2,1,0:T(8,128)S(1)}, u32[]{:S(2)}, u32[]{:S(2)}) collective-permute-start(f32[3,8,128]{2,1,0:T(8,128)} %bitcast.23), channel_id=1, source_target_pairs={{0,1},{1,2},{2,3},{3,4},{4,5},{5,6},{6,7},{7,8},{8,9},{9,10},{10,1... | collective-permute-start | bytes 36872 | tf_op jit(solution)/shard_map/ppermute | solution.py:22
  11.0 8.0 %collective-permute-start = (f32[3,8,128]{2,1,0:T(8,128)}, f32[3,8,128]{2,1,0:T(8,128)S(1)}, u32[]{:S(2)}, u32[]{:S(2)}) collective-permute-start(f32[3,8,128]{2,1,0:T(8,128)} %bitcast.24), channel_id=1, source_target_pairs={{0,32},{32,64},{64,96},{96,128},{128,160},{160,192},{192,224},{224... | collective-permute-start | bytes 36872 | tf_op jit(solution)/shard_map/ppermute | solution.py:22
  13.3 36.1 %copy-start.4 = (s32[1,1,2,64]{3,2,1,0:T(2,128)S(1)}, s32[1,1,2,64]{3,2,1,0:T(2,128)}, u32[]{:S(2)}) copy-start(s32[1,1,2,64]{3,2,1,0:T(2,128)} %param.10) | copy-start | bytes 1540
  13.3 36.1 %copy-start.5 = (s32[1,1,2]{2,1,0:T(1,128)S(1)}, s32[1,1,2]{2,1,0:T(1,128)}, u32[]{:S(2)}) copy-start(s32[1,1,2]{2,1,0:T(1,128)} %param.11) | copy-start | bytes 28
  21.1 17.5 %collective-permute-start.4 = (f32[3,8,128]{2,1,0:T(8,128)S(1)}, f32[3,8,128]{2,1,0:T(8,128)S(1)}, u32[]{:S(2)}, u32[]{:S(2)}) collective-permute-start(f32[3,8,128]{2,1,0:T(8,128)S(1)} %get-tuple-element.34), channel_id=1, source_target_pairs={{0,32},{32,64},{64,96},{96,128},{128,160},{160,192},{192,224},{224... | collective-permute-start | bytes 36872 | tf_op jit(solution)/shard_map/ppermute | solution.py:22
  23.0 15.6 %collective-permute-start.5 = (f32[3,8,128]{2,1,0:T(8,128)S(1)}, f32[3,8,128]{2,1,0:T(8,128)S(1)}, u32[]{:S(2)}, u32[]{:S(2)}) collective-permute-start(f32[3,8,128]{2,1,0:T(8,128)S(1)} %get-tuple-element.35), channel_id=1, source_target_pairs={{0,480},{32,0},{64,32},{96,64},{128,96},{160,128},{192,160},{224,1... | collective-permute-start | bytes 36872 | tf_op jit(solution)/shard_map/ppermute | solution.py:22
  29.7 9.5 %collective-permute-start.6 = (f32[3,8,128]{2,1,0:T(8,128)S(1)}, f32[3,8,128]{2,1,0:T(8,128)S(1)}, u32[]{:S(2)}, u32[]{:S(2)}) collective-permute-start(f32[3,8,128]{2,1,0:T(8,128)S(1)} %get-tuple-element.36), channel_id=1, source_target_pairs={{0,1},{1,2},{2,3},{3,4},{4,5},{5,6},{6,7},{7,8},{8,9},{9,10},{10,1... | collective-permute-start | bytes 36872 | tf_op jit(solution)/shard_map/ppermute | solution.py:22
  31.9 7.5 %collective-permute-start.7 = (f32[3,8,128]{2,1,0:T(8,128)S(1)}, f32[3,8,128]{2,1,0:T(8,128)S(1)}, u32[]{:S(2)}, u32[]{:S(2)}) collective-permute-start(f32[3,8,128]{2,1,0:T(8,128)S(1)} %get-tuple-element.37), channel_id=1, source_target_pairs={{0,31},{1,0},{2,1},{3,2},{4,3},{5,4},{6,5},{7,6},{8,7},{9,8},{10,9... | collective-permute-start | bytes 36872 | tf_op jit(solution)/shard_map/ppermute | solution.py:22
  39.4 10.2 %collective-permute-start.11 = (f32[3,8,128]{2,1,0:T(8,128)S(1)}, f32[3,8,128]{2,1,0:T(8,128)S(1)}, u32[]{:S(2)}, u32[]{:S(2)}) collective-permute-start(f32[3,8,128]{2,1,0:T(8,128)S(1)} %select_add_fusion.1.own.k1), channel_id=1, source_target_pairs={{0,480},{32,0},{64,32},{96,64},{128,96},{160,128},{192,160},{224,1... | collective-permute-start | bytes 36872 | tf_op jit(solution)/shard_map/ppermute | solution.py:22
  41.3 8.2 %collective-permute-start.10 = (f32[3,8,128]{2,1,0:T(8,128)S(1)}, f32[3,8,128]{2,1,0:T(8,128)S(1)}, u32[]{:S(2)}, u32[]{:S(2)}) collective-permute-start(f32[3,8,128]{2,1,0:T(8,128)S(1)} %select_add_fusion.1.own.k1), channel_id=1, source_target_pairs={{0,31},{1,0},{2,1},{3,2},{4,3},{5,4},{6,5},{7,6},{8,7},{9,8},{10,9... | collective-permute-start | bytes 36872 | tf_op jit(solution)/shard_map/ppermute | solution.py:22
  47.4 2.1 %collective-permute-start.9 = (f32[3,8,128]{2,1,0:T(8,128)S(1)}, f32[3,8,128]{2,1,0:T(8,128)S(1)}, u32[]{:S(2)}, u32[]{:S(2)}) collective-permute-start(f32[3,8,128]{2,1,0:T(8,128)S(1)} %select_add_fusion.1.own.k1), channel_id=1, source_target_pairs={{0,1},{1,2},{2,3},{3,4},{4,5},{5,6},{6,7},{7,8},{8,9},{9,10},{10,1... | collective-permute-start | bytes 36872 | tf_op jit(solution)/shard_map/ppermute | solution.py:22
  47.4 7.7 %collective-permute-start.8 = (f32[3,8,128]{2,1,0:T(8,128)S(1)}, f32[3,8,128]{2,1,0:T(8,128)S(1)}, u32[]{:S(2)}, u32[]{:S(2)}) collective-permute-start(f32[3,8,128]{2,1,0:T(8,128)S(1)} %select_add_fusion.1.own.k1), channel_id=1, source_target_pairs={{0,32},{32,64},{64,96},{96,128},{128,160},{160,192},{192,224},{224... | collective-permute-start | bytes 36872 | tf_op jit(solution)/shard_map/ppermute | solution.py:22
  57.3 11.1 %collective-permute-start.14 = (f32[4,8,128]{2,1,0:T(8,128)S(1)}, f32[4,8,128]{2,1,0:T(8,128)S(1)}, u32[]{:S(2)}, u32[]{:S(2)}) collective-permute-start(f32[4,8,128]{2,1,0:T(8,128)S(1)} %get-tuple-element.45), channel_id=1, source_target_pairs={{0,1},{1,2},{2,3},{3,4},{4,5},{5,6},{6,7},{7,8},{8,9},{9,10},{10,1... | collective-permute-start | bytes 49160 | tf_op jit(solution)/shard_map/ppermute | solution.py:22
  57.3 11.1 %collective-permute-start.15 = (f32[4,8,128]{2,1,0:T(8,128)S(1)}, f32[4,8,128]{2,1,0:T(8,128)S(1)}, u32[]{:S(2)}, u32[]{:S(2)}) collective-permute-start(f32[4,8,128]{2,1,0:T(8,128)S(1)} %get-tuple-element.46), channel_id=1, source_target_pairs={{0,31},{1,0},{2,1},{3,2},{4,3},{5,4},{6,5},{7,6},{8,7},{9,8},{10,9... | collective-permute-start | bytes 49160 | tf_op jit(solution)/shard_map/ppermute | solution.py:22
  59.0 8.6 %collective-permute-start.12 = (f32[3,8,128]{2,1,0:T(8,128)S(1)}, f32[3,8,128]{2,1,0:T(8,128)S(1)}, u32[]{:S(2)}, u32[]{:S(2)}) collective-permute-start(f32[3,8,128]{2,1,0:T(8,128)S(1)} %get-tuple-element.43), channel_id=1, source_target_pairs={{0,32},{32,64},{64,96},{96,128},{128,160},{160,192},{192,224},{224... | collective-permute-start | bytes 36872 | tf_op jit(solution)/shard_map/ppermute | solution.py:22
  60.9 7.5 %collective-permute-start.13 = (f32[3,8,128]{2,1,0:T(8,128)S(1)}, f32[3,8,128]{2,1,0:T(8,128)S(1)}, u32[]{:S(2)}, u32[]{:S(2)}) collective-permute-start(f32[3,8,128]{2,1,0:T(8,128)S(1)} %get-tuple-element.44), channel_id=1, source_target_pairs={{0,480},{32,0},{64,32},{96,64},{128,96},{160,128},{192,160},{224,1... | collective-permute-start | bytes 36872 | tf_op jit(solution)/shard_map/ppermute | solution.py:22
  68.4 13.5 %collective-permute-start.19 = (f32[3,8,128]{2,1,0:T(8,128)S(1)}, f32[3,8,128]{2,1,0:T(8,128)S(1)}, u32[]{:S(2)}, u32[]{:S(2)}) collective-permute-start(f32[3,8,128]{2,1,0:T(8,128)S(1)} %fusion.own.k2), channel_id=1, source_target_pairs={{0,480},{32,0},{64,32},{96,64},{128,96},{160,128},{192,160},{224,1... | collective-permute-start | bytes 36872 | tf_op jit(solution)/shard_map/ppermute | solution.py:22
  75.4 6.6 %collective-permute-start.18 = (f32[3,8,128]{2,1,0:T(8,128)S(1)}, f32[3,8,128]{2,1,0:T(8,128)S(1)}, u32[]{:S(2)}, u32[]{:S(2)}) collective-permute-start(f32[3,8,128]{2,1,0:T(8,128)S(1)} %fusion.own.k2), channel_id=1, source_target_pairs={{0,31},{1,0},{2,1},{3,2},{4,3},{5,4},{6,5},{7,6},{8,7},{9,8},{10,9... | collective-permute-start | bytes 36872 | tf_op jit(solution)/shard_map/ppermute | solution.py:22
  80.0 1.9 %collective-permute-start.17 = (f32[3,8,128]{2,1,0:T(8,128)S(1)}, f32[3,8,128]{2,1,0:T(8,128)S(1)}, u32[]{:S(2)}, u32[]{:S(2)}) collective-permute-start(f32[3,8,128]{2,1,0:T(8,128)S(1)} %fusion.own.k2), channel_id=1, source_target_pairs={{0,1},{1,2},{2,3},{3,4},{4,5},{5,6},{6,7},{7,8},{8,9},{9,10},{10,1... | collective-permute-start | bytes 36872 | tf_op jit(solution)/shard_map/ppermute | solution.py:22
  80.0 7.7 %collective-permute-start.16 = (f32[3,8,128]{2,1,0:T(8,128)S(1)}, f32[3,8,128]{2,1,0:T(8,128)S(1)}, u32[]{:S(2)}, u32[]{:S(2)}) collective-permute-start(f32[3,8,128]{2,1,0:T(8,128)S(1)} %fusion.own.k2), channel_id=1, source_target_pairs={{0,32},{32,64},{64,96},{96,128},{128,160},{160,192},{192,224},{224... | collective-permute-start | bytes 36872 | tf_op jit(solution)/shard_map/ppermute | solution.py:22
  90.3 12.9 %all-to-all-start = ((f32[32,8,128]{2,1,0:T(8,128)}), f32[32,8,128]{2,1,0:T(8,128)S(1)}, u32[]{:S(2)}, u32[]{:S(2)}) async-start(f32[32,8,128]{2,1,0:T(8,128)} %get-tuple-element.48), calls=%async_computation | async-start | bytes 262144 | tf_op jit(solution)/shard_map/all_to_all | solution.py:275
  95.4 7.8 %collective-permute-start.20 = (f32[3,8,128]{2,1,0:T(8,128)S(1)}, f32[3,8,128]{2,1,0:T(8,128)S(1)}, u32[]{:S(2)}, u32[]{:S(2)}) collective-permute-start(f32[3,8,128]{2,1,0:T(8,128)S(1)} %get-tuple-element.52), channel_id=1, source_target_pairs={{0,1},{1,2},{2,3},{3,4},{4,5},{5,6},{6,7},{7,8},{8,9},{9,10},{10,1... | collective-permute-start | bytes 36872 | tf_op jit(solution)/shard_map/ppermute | solution.py:22
  95.5 7.8 %collective-permute-start.21 = (f32[3,8,128]{2,1,0:T(8,128)S(1)}, f32[3,8,128]{2,1,0:T(8,128)S(1)}, u32[]{:S(2)}, u32[]{:S(2)}) collective-permute-start(f32[3,8,128]{2,1,0:T(8,128)S(1)} %get-tuple-element.53), channel_id=1, source_target_pairs={{0,31},{1,0},{2,1},{3,2},{4,3},{5,4},{6,5},{7,6},{8,7},{9,8},{10,9... | collective-permute-start | bytes 36872 | tf_op jit(solution)/shard_map/ppermute | solution.py:22
  103.9 18.4 %all-to-all-start.1 = ((f32[16,8,128]{2,1,0:T(8,128)}), f32[16,8,128]{2,1,0:T(8,128)S(1)}, u32[]{:S(2)}, u32[]{:S(2)}) async-start(f32[16,8,128]{2,1,0:T(8,128)} %broadcast_in_dim.32), calls=%async_computation.1 | async-start | bytes 131072 | tf_op jit(solution)/shard_map/all_to_all | solution.py:275
  110.6 8.6 %collective-permute-start.22 = (f32[3,8,128]{2,1,0:T(8,128)S(1)}, f32[3,8,128]{2,1,0:T(8,128)S(1)}, u32[]{:S(2)}, u32[]{:S(2)}) collective-permute-start(f32[3,8,128]{2,1,0:T(8,128)S(1)} %get-tuple-element.56), channel_id=1, source_target_pairs={{0,32},{32,64},{64,96},{96,128},{128,160},{160,192},{192,224},{224... | collective-permute-start | bytes 36872 | tf_op jit(solution)/shard_map/ppermute | solution.py:22
  113.0 7.1 %collective-permute-start.23 = (f32[3,8,128]{2,1,0:T(8,128)S(1)}, f32[3,8,128]{2,1,0:T(8,128)S(1)}, u32[]{:S(2)}, u32[]{:S(2)}) collective-permute-start(f32[3,8,128]{2,1,0:T(8,128)S(1)} %get-tuple-element.57), channel_id=1, source_target_pairs={{0,480},{32,0},{64,32},{96,64},{128,96},{160,128},{192,160},{224,1... | collective-permute-start | bytes 36872 | tf_op jit(solution)/shard_map/ppermute | solution.py:22

commit v7 on v6

--- a/solution.py
+++ b/solution.py
@@ -30,7 +30,7 @@
 def operator_kernel(
     sweep, ids, own, from_axial_dn, from_cross_dn, from_cross_up, from_axial_up, tiles, drag, *rest
 ):
-    many = (1, 2, 1)[sweep]
+    many = 2 if sweep == ITERS - 1 else 1
     carried, rest = rest[:many], rest[many:]
     (
         to_axial_dn, to_cross_dn, to_cross_up, to_axial_up, kept, moments, ext, acc,
@@ -101,7 +101,7 @@
         rows == 2 * sweep, even, jnp.where(rows == 2 * sweep + 1, odd, carried[0][...])
     )
     moments[...] = jnp.broadcast_to(merged, moments.shape)
-    if sweep == 1:
+    if sweep == ITERS - 1:
         to_cross_dn[3] = carried[1][...]
         to_cross_up[3] = carried[1][...]
 
@@ -110,7 +110,7 @@
     blocks, width = drag.shape
     vmem = pl.BlockSpec(memory_space=pltpu.VMEM)
     field = jax.ShapeDtypeStruct((3, blocks, width), jnp.float32)
-    across = jax.ShapeDtypeStruct((4 if sweep == 1 else 3, blocks, width), jnp.float32)
+    across = jax.ShapeDtypeStruct((4 if sweep == ITERS - 1 else 3, blocks, width), jnp.float32)
     plane = (SUB, width) if copies is None else (copies, SUB, width)
     plane = jax.ShapeDtypeStruct(plane, jnp.float32)
     rows = 8 * blocks * SUB
@@ -309,12 +309,12 @@
             sums = spread_sum(part, lambda a, c: (a, c % 2))
         from_lower_axial = ring_shift(r7, "axial", 1)
         from_upper_axial = ring_shift(r1, "axial", -1)
-        if sweep == 1:
+        if sweep == ITERS - 1:
             planes = [from_lower_cross, from_upper_cross]
         now = kept + from_lower_axial + from_upper_axial
         now = now + jnp.where(slab > 0, from_lower_cross[:3], 0.0)
         now = now + jnp.where(slab < last, from_upper_cross[:3], 0.0)
-        if sweep == 0:
+        if sweep == ITERS - 2:
             now, mig_rows, mig_count = lax.optimization_barrier((now, mig_rows, mig_count))
             carried += (leaving_rows(mig_rows, mig_count, blocks, width),)
     own.append(now)

time: 124 us -> 121 us (0.976)
  starting transfers between devices: 84.8 us -> 81.8 us
    ppermute x24, starting transfers between devices: 72.8 us -> 69.8 us  [ring_shift(): return lax.ppermute(shard, axis, ring(lax.axis_size(axis), by))]
  transfers between devices with their start and end apart: 26 -> 26, of which waited for: 9 -> 10; matrix products, arithmetic and copies ran while one was open for 0% -> 0% of each run, Pallas kernels for 0% -> 0%
where the time goes in v7:
time: 121 us; the launch traced here: 120 us
  starting transfers between devices  81.8 us (68%)
  waiting for transfers between devices  29 us (24%)
  Pallas kernels  7.55 us (6%)
    ppermute x24, starting transfers between devices, ring_shift(): return lax.ppermute(shard, axis, ring(lax.axis_size(axis), by))  69.8 us
    ppermute x24, waiting for transfers between devices, ring_shift(): return lax.ppermute(shard, axis, ring(lax.axis_size(axis), by))  19.6 us
    all_to_all x2, starting transfers between devices, spread_sum(): lax.all_to_all(part, ('axial', 'cross'), 0, 0, axis_index_groups=groups)  11.9 us
    all_to_all x2, waiting for transfers between devices, spread_sum(): lax.all_to_all(part, ('axial', 'cross'), 0, 0, axis_index_groups=groups)  9.37 us
    pallas_call x3, Pallas kernels, operator_call(): pl.pallas_call(functools.partial(operator_kernel, sweep), in_specs=[pl.Bl...  6.67 us
  transfers between devices with their start and end apart: 26, of which 10 were waited for; matrix products, arithmetic and copies ran while one was open for 0% of the time, Pallas kernels for 0%

profile of v7, /device:TPU:1, one launch (start us, length us, event | category | flops | bytes accessed | tf_op | source)
XLA Modules:
  0.0 120.2 jit_solution(13279831975535785017)
XLA Ops:
  0.6 0.0 copy-start
  0.7 7.8 %collective-permute-start.3 = (f32[3,8,128]{2,1,0:T(8,128)}, f32[3,8,128]{2,1,0:T(8,128)S(1)}, u32[]{:S(2)}, u32[]{:S(2)}) collective-permute-start(f32[3,8,128]{2,1,0:T(8,128)} %bitcast.21), channel_id=1, source_target_pairs={{0,480},{32,0},{64,32},{96,64},{128,96},{160,128},{192,160},{224,1... | collective-permute-start | bytes 36872 | tf_op jit(solution)/shard_map/ppermute | solution.py:22
  8.5 1.1 collective-permute-start.2
  9.6 1.4 %collective-permute-start.1 = (f32[3,8,128]{2,1,0:T(8,128)}, f32[3,8,128]{2,1,0:T(8,128)S(1)}, u32[]{:S(2)}, u32[]{:S(2)}) collective-permute-start(f32[3,8,128]{2,1,0:T(8,128)} %bitcast.23), channel_id=1, source_target_pairs={{0,1},{1,2},{2,3},{3,4},{4,5},{5,6},{6,7},{7,8},{8,9},{9,10},{10,1... | collective-permute-start | bytes 36872 | tf_op jit(solution)/shard_map/ppermute | solution.py:22
  11.0 2.3 %collective-permute-start = (f32[3,8,128]{2,1,0:T(8,128)}, f32[3,8,128]{2,1,0:T(8,128)S(1)}, u32[]{:S(2)}, u32[]{:S(2)}) collective-permute-start(f32[3,8,128]{2,1,0:T(8,128)} %bitcast.24), channel_id=1, source_target_pairs={{0,32},{32,64},{64,96},{96,128},{128,160},{160,192},{192,224},{224... | collective-permute-start | bytes 36872 | tf_op jit(solution)/shard_map/ppermute | solution.py:22
  13.3 0.0 collective-permute-done.3.from_axial_up
  13.3 0.0 collective-permute-done.2.from_cross_up.u0
  13.3 5.7 %collective-permute-done.1.from_cross_dn.d0 = f32[3,8,128]{2,1,0:T(8,128)S(1)} collective-permute-done((f32[3,8,128]{2,1,0:T(8,128)}, f32[3,8,128]{2,1,0:T(8,128)S(1)}, u32[]{:S(2)}, u32[]{:S(2)}) %collective-permute-start.1) | collective-permute-done | bytes 12320 | tf_op jit(solution)/shard_map/ppermute | solution.py:22
  19.0 0.0 collective-permute-done.from_axial_dn
  19.0 0.0 copy-done.1
  19.0 0.0 copy-start.4
  19.0 0.0 copy-start.5
  19.0 2.1 %shard_map.86 = (f32[3,8,128]{2,1,0:T(8,128)S(1)}, f32[3,8,128]{2,1,0:T(8,128)S(1)}, f32[3,8,128]{2,1,0:T(8,128)S(1)}, f32[3,8,128]{2,1,0:T(8,128)S(1)}, f32[3,8,128]{2,1,0:T(8,128)S(1)}, /*index=5*/f32[8,128]{1,0:T(8,128)S(1)}) custom-call(s32[8,8]{1,0:T(8,128)S(1)} %bitcast.27, f32[3,8,128]{2,1,0:T(8,128)S(1)} %bitcast.25, ...), custom_call_target="tpu_custom_call" | custom-call | tf_op jit(solution)/shard_map/pallas_call | solution.py:118
  21.1 1.9 %collective-permute-start.4 = (f32[3,8,128]{2,1,0:T(8,128)S(1)}, f32[3,8,128]{2,1,0:T(8,128)S(1)}, u32[]{:S(2)}, u32[]{:S(2)}) collective-permute-start(f32[3,8,128]{2,1,0:T(8,128)S(1)} %get-tuple-element.34), channel_id=1, source_target_pairs={{0,32},{32,64},{64,96},{96,128},{128,160},{160,192},{192,224},{224... | collective-permute-start | bytes 36872 | tf_op jit(solution)/shard_map/ppermute | solution.py:22
  23.1 6.7 %collective-permute-start.5 = (f32[3,8,128]{2,1,0:T(8,128)S(1)}, f32[3,8,128]{2,1,0:T(8,128)S(1)}, u32[]{:S(2)}, u32[]{:S(2)}) collective-permute-start(f32[3,8,128]{2,1,0:T(8,128)S(1)} %get-tuple-element.35), channel_id=1, source_target_pairs={{0,480},{32,0},{64,32},{96,64},{128,96},{160,128},{192,160},{224,1... | collective-permute-start | bytes 36872 | tf_op jit(solution)/shard_map/ppermute | solution.py:22
  29.7 2.2 %collective-permute-start.6 = (f32[3,8,128]{2,1,0:T(8,128)S(1)}, f32[3,8,128]{2,1,0:T(8,128)S(1)}, u32[]{:S(2)}, u32[]{:S(2)}) collective-permute-start(f32[3,8,128]{2,1,0:T(8,128)S(1)} %get-tuple-element.36), channel_id=1, source_target_pairs={{0,1},{1,2},{2,3},{3,4},{4,5},{5,6},{6,7},{7,8},{8,9},{9,10},{10,1... | collective-permute-start | bytes 36872 | tf_op jit(solution)/shard_map/ppermute | solution.py:22
  31.9 6.6 %collective-permute-start.7 = (f32[3,8,128]{2,1,0:T(8,128)S(1)}, f32[3,8,128]{2,1,0:T(8,128)S(1)}, u32[]{:S(2)}, u32[]{:S(2)}) collective-permute-start(f32[3,8,128]{2,1,0:T(8,128)S(1)} %get-tuple-element.37), channel_id=1, source_target_pairs={{0,31},{1,0},{2,1},{3,2},{4,3},{5,4},{6,5},{7,6},{8,7},{9,8},{10,9... | collective-permute-start | bytes 36872 | tf_op jit(solution)/shard_map/ppermute | solution.py:22
  38.6 0.0 collective-permute-done.4
  38.6 0.0 collective-permute-done.5
  38.6 0.6 collective-permute-done.6
  39.2 0.2 collective-permute-done.7
  39.4 1.9 %collective-permute-start.11 = (f32[3,8,128]{2,1,0:T(8,128)S(1)}, f32[3,8,128]{2,1,0:T(8,128)S(1)}, u32[]{:S(2)}, u32[]{:S(2)}) collective-permute-start(f32[3,8,128]{2,1,0:T(8,128)S(1)} %select_add_fusion.2.own.k1), channel_id=1, source_target_pairs={{0,480},{32,0},{64,32},{96,64},{128,96},{160,128},{192,160},{224,1... | collective-permute-start | bytes 36872 | tf_op jit(solution)/shard_map/ppermute | solution.py:22
  41.3 6.1 %collective-permute-start.10 = (f32[3,8,128]{2,1,0:T(8,128)S(1)}, f32[3,8,128]{2,1,0:T(8,128)S(1)}, u32[]{:S(2)}, u32[]{:S(2)}) collective-permute-start(f32[3,8,128]{2,1,0:T(8,128)S(1)} %select_add_fusion.2.own.k1), channel_id=1, source_target_pairs={{0,31},{1,0},{2,1},{3,2},{4,3},{5,4},{6,5},{7,6},{8,7},{9,8},{10,9... | collective-permute-start | bytes 36872 | tf_op jit(solution)/shard_map/ppermute | solution.py:22
  47.5 0.0 collective-permute-start.9
  47.5 1.9 %collective-permute-start.8 = (f32[3,8,128]{2,1,0:T(8,128)S(1)}, f32[3,8,128]{2,1,0:T(8,128)S(1)}, u32[]{:S(2)}, u32[]{:S(2)}) collective-permute-start(f32[3,8,128]{2,1,0:T(8,128)S(1)} %select_add_fusion.2.own.k1), channel_id=1, source_target_pairs={{0,32},{32,64},{64,96},{96,128},{128,160},{160,192},{192,224},{224... | collective-permute-start | bytes 36872 | tf_op jit(solution)/shard_map/ppermute | solution.py:22
  49.4 0.0 collective-permute-done.11.from_axial_up
  49.4 0.0 collective-permute-done.10.from_cross_up.u1
  49.4 0.0 collective-permute-done.9.from_cross_dn.d1
  49.4 5.8 %collective-permute-done.8.from_axial_dn = f32[3,8,128]{2,1,0:T(8,128)S(1)} collective-permute-done((f32[3,8,128]{2,1,0:T(8,128)S(1)}, f32[3,8,128]{2,1,0:T(8,128)S(1)}, u32[]{:S(2)}, u32[]{:S(2)}) %collective-permute-start.8) | collective-permute-done | bytes 12320 | tf_op jit(solution)/shard_map/ppermute | solution.py:22
  55.2 2.1 %shard_map.87 = (f32[3,8,128]{2,1,0:T(8,128)S(1)}, f32[3,8,128]{2,1,0:T(8,128)S(1)}, f32[3,8,128]{2,1,0:T(8,128)S(1)}, f32[3,8,128]{2,1,0:T(8,128)S(1)}, f32[3,8,128]{2,1,0:T(8,128)S(1)}, /*index=5*/f32[8,128]{1,0:T(8,128)S(1)}) custom-call(s32[8,8]{1,0:T(8,128)S(1)} %bitcast.28, f32[3,8,128]{2,1,0:T(8,128)S(1)} %select_add_fusion.2.own.k1, ...), custom_call_target="tpu_custom_call" | custom-call | tf_op jit(solution)/shard_map/pallas_call | solution.py:118
  57.3 1.9 %collective-permute-start.12 = (f32[3,8,128]{2,1,0:T(8,128)S(1)}, f32[3,8,128]{2,1,0:T(8,128)S(1)}, u32[]{:S(2)}, u32[]{:S(2)}) collective-permute-start(f32[3,8,128]{2,1,0:T(8,128)S(1)} %get-tuple-element.40), channel_id=1, source_target_pairs={{0,32},{32,64},{64,96},{96,128},{128,160},{160,192},{192,224},{224... | collective-permute-start | bytes 36872 | tf_op jit(solution)/shard_map/ppermute | solution.py:22
  59.2 6.7 %collective-permute-start.13 = (f32[3,8,128]{2,1,0:T(8,128)S(1)}, f32[3,8,128]{2,1,0:T(8,128)S(1)}, u32[]{:S(2)}, u32[]{:S(2)}) collective-permute-start(f32[3,8,128]{2,1,0:T(8,128)S(1)} %get-tuple-element.41), channel_id=1, source_target_pairs={{0,480},{32,0},{64,32},{96,64},{128,96},{160,128},{192,160},{224,1... | collective-permute-start | bytes 36872 | tf_op jit(solution)/shard_map/ppermute | solution.py:22
  65.9 0.0 collective-permute-start.14
  65.9 2.2 %collective-permute-start.15 = (f32[3,8,128]{2,1,0:T(8,128)S(1)}, f32[3,8,128]{2,1,0:T(8,128)S(1)}, u32[]{:S(2)}, u32[]{:S(2)}) collective-permute-start(f32[3,8,128]{2,1,0:T(8,128)S(1)} %get-tuple-element.43), channel_id=1, source_target_pairs={{0,31},{1,0},{2,1},{3,2},{4,3},{5,4},{6,5},{7,6},{8,7},{9,8},{10,9... | collective-permute-start | bytes 36872 | tf_op jit(solution)/shard_map/ppermute | solution.py:22
  68.2 0.1 pad.4.clone
  68.3 0.0 collective-permute-done.12
  68.3 0.0 collective-permute-done.13
  68.3 0.6 collective-permute-done.14
  68.8 0.3 collective-permute-done.15
  69.1 4.6 %collective-permute-start.19 = (f32[3,8,128]{2,1,0:T(8,128)S(1)}, f32[3,8,128]{2,1,0:T(8,128)S(1)}, u32[]{:S(2)}, u32[]{:S(2)}) collective-permute-start(f32[3,8,128]{2,1,0:T(8,128)S(1)} %select_add_fusion.1.own.k2), channel_id=1, source_target_pairs={{0,480},{32,0},{64,32},{96,64},{128,96},{160,128},{192,160},{224,1... | collective-permute-start | bytes 36872 | tf_op jit(solution)/shard_map/ppermute | solution.py:22
  73.7 3.4 %collective-permute-start.18 = (f32[3,8,128]{2,1,0:T(8,128)S(1)}, f32[3,8,128]{2,1,0:T(8,128)S(1)}, u32[]{:S(2)}, u32[]{:S(2)}) collective-permute-start(f32[3,8,128]{2,1,0:T(8,128)S(1)} %select_add_fusion.1.own.k2), channel_id=1, source_target_pairs={{0,31},{1,0},{2,1},{3,2},{4,3},{5,4},{6,5},{7,6},{8,7},{9,8},{10,9... | collective-permute-start | bytes 36872 | tf_op jit(solution)/shard_map/ppermute | solution.py:22
  77.1 0.0 collective-permute-start.17
  77.1 1.9 %collective-permute-start.16 = (f32[3,8,128]{2,1,0:T(8,128)S(1)}, f32[3,8,128]{2,1,0:T(8,128)S(1)}, u32[]{:S(2)}, u32[]{:S(2)}) collective-permute-start(f32[3,8,128]{2,1,0:T(8,128)S(1)} %select_add_fusion.1.own.k2), channel_id=1, source_target_pairs={{0,32},{32,64},{64,96},{96,128},{128,160},{160,192},{192,224},{224... | collective-permute-start | bytes 36872 | tf_op jit(solution)/shard_map/ppermute | solution.py:22
  79.0 0.1 fusion.2
  79.1 0.1 fusion.rest_1_
  79.2 0.0 collective-permute-done.19.from_axial_up
  79.2 0.0 collective-permute-done.18.from_cross_up.u2
  79.2 0.0 collective-permute-done.17.from_cross_dn.d2
  79.2 5.6 %collective-permute-done.16.from_axial_dn = f32[3,8,128]{2,1,0:T(8,128)S(1)} collective-permute-done((f32[3,8,128]{2,1,0:T(8,128)S(1)}, f32[3,8,128]{2,1,0:T(8,128)S(1)}, u32[]{:S(2)}, u32[]{:S(2)}) %collective-permute-start.16) | collective-permute-done | bytes 12320 | tf_op jit(solution)/shard_map/ppermute | solution.py:22
  84.8 2.5 %shard_map.88 = (f32[3,8,128]{2,1,0:T(8,128)S(1)}, f32[4,8,128]{2,1,0:T(8,128)S(1)}, f32[4,8,128]{2,1,0:T(8,128)S(1)}, f32[3,8,128]{2,1,0:T(8,128)S(1)}, f32[3,8...) custom-call(s32[8,8]{1,0:T(8,128)S(1)} %bitcast.29, f32[3,8,128]{2,1,0:T(8,128)S(1)} %select_add_fusion.1.own.k2, ...), custom_call_target="tpu_custom_call" | custom-call | tf_op jit(solution)/shard_map/pallas_call | solution.py:118
  87.3 5.2 %all-to-all-start = ((f32[32,8,128]{2,1,0:T(8,128)}), f32[32,8,128]{2,1,0:T(8,128)S(1)}, u32[]{:S(2)}, u32[]{:S(2)}) async-start(f32[32,8,128]{2,1,0:T(8,128)} %get-tuple-element.48), calls=%async_computation | async-start | bytes 262144 | tf_op jit(solution)/shard_map/all_to_all | solution.py:275
  92.5 0.0 collective-permute-start.20
  92.5 0.5 collective-permute-start.21
  93.0 7.2 %all-to-all-done = f32[32,8,128]{2,1,0:T(8,128)S(1)} async-done(((f32[32,8,128]{2,1,0:T(8,128)}), f32[32,8,128]{2,1,0:T(8,128)S(1)}, u32[]{:S(2)}, u32[]{:S(2)}) %all-to-all-start) | async-done | bytes 131104 | tf_op jit(solution)/shard_map/all_to_all | solution.py:275
  100.3 0.0 collective-permute-done.20.dn_plane
  100.3 0.0 collective-permute-done.21.up_plane
  100.3 0.6 broadcast_in_dim.32
  100.9 6.8 %all-to-all-start.1 = ((f32[16,8,128]{2,1,0:T(8,128)}), f32[16,8,128]{2,1,0:T(8,128)S(1)}, u32[]{:S(2)}, u32[]{:S(2)}) async-start(f32[16,8,128]{2,1,0:T(8,128)} %broadcast_in_dim.32), calls=%async_computation.1 | async-start | bytes 131072 | tf_op jit(solution)/shard_map/all_to_all | solution.py:275
  107.7 2.3 %collective-permute-start.22 = (f32[3,8,128]{2,1,0:T(8,128)S(1)}, f32[3,8,128]{2,1,0:T(8,128)S(1)}, u32[]{:S(2)}, u32[]{:S(2)}) collective-permute-start(f32[3,8,128]{2,1,0:T(8,128)S(1)} %get-tuple-element.56), channel_id=1, source_target_pairs={{0,32},{32,64},{64,96},{96,128},{128,160},{160,192},{192,224},{224... | collective-permute-start | bytes 36872 | tf_op jit(solution)/shard_map/ppermute | solution.py:22
  110.0 6.3 %collective-permute-start.23 = (f32[3,8,128]{2,1,0:T(8,128)S(1)}, f32[3,8,128]{2,1,0:T(8,128)S(1)}, u32[]{:S(2)}, u32[]{:S(2)}) collective-permute-start(f32[3,8,128]{2,1,0:T(8,128)S(1)} %get-tuple-element.57), channel_id=1, source_target_pairs={{0,480},{32,0},{64,32},{96,64},{128,96},{160,128},{192,160},{224,1... | collective-permute-start | bytes 36872 | tf_op jit(solution)/shard_map/ppermute | solution.py:22
  116.3 0.0 collective-permute-done.22
  116.3 0.8 collective-permute-done.23
  117.1 2.2 %all-to-all-done.1.sums = f32[16,8,128]{2,1,0:T(8,128)S(1)} async-done(((f32[16,8,128]{2,1,0:T(8,128)}), f32[16,8,128]{2,1,0:T(8,128)S(1)}, u32[]{:S(2)}, u32[]{:S(2)}) %all-to-all-start.1) | async-done | bytes 65568 | tf_op jit(solution)/shard_map/all_to_all | solution.py:275
  119.3 0.9 shard_map.89
  (15 shorter events, 0.1 us)
Async XLA Ops:
  0.6 18.4 %copy-start = (bf16[1,1,8,8,128,128]{5,4,3,2,1,0:T(8,128)(2,1)S(1)}, bf16[1,1,8,8,128,128]{5,4,3,2,1,0:T(8,128)(2,1)}, u32[]{:S(2)}) copy-start(bf16[1,1,8,8,128,128]{5,4,3,2,1,0:T(8,128)(2,1)} %param.8) | copy-start | bytes 6291460
  0.6 18.3 %copy-start.1 = (f32[1,1,8,3,128]{4,2,3,1,0:T(8,128)S(1)}, f32[1,1,8,3,128]{4,2,3,1,0:T(8,128)}, u32[]{:S(2)}) copy-start(f32[1,1,8,3,128]{4,2,3,1,0:T(8,128)} %param.6) | copy-start | bytes 36868
  0.7 18.3 %copy-start.2 = (s32[1,1,8,8]{3,2,1,0:T(8,128)S(1)}, s32[1,1,8,8]{3,2,1,0:T(8,128)}, u32[]{:S(2)}) copy-start(s32[1,1,8,8]{3,2,1,0:T(8,128)} %param.9) | copy-start | bytes 772
  0.7 18.3 %copy-start.3 = (f32[1,1,8,128]{3,2,1,0:T(8,128)S(1)}, f32[1,1,8,128]{3,2,1,0:T(8,128)}, u32[]{:S(2)}) copy-start(f32[1,1,8,128]{3,2,1,0:T(8,128)} %param.7) | copy-start | bytes 12292
  0.7 12.6 %collective-permute-start.3 = (f32[3,8,128]{2,1,0:T(8,128)}, f32[3,8,128]{2,1,0:T(8,128)S(1)}, u32[]{:S(2)}, u32[]{:S(2)}) collective-permute-start(f32[3,8,128]{2,1,0:T(8,128)} %bitcast.21), channel_id=1, source_target_pairs={{0,480},{32,0},{64,32},{96,64},{128,96},{160,128},{192,160},{224,1... | collective-permute-start | bytes 36872 | tf_op jit(solution)/shard_map/ppermute | solution.py:22
  8.5 4.8 %collective-permute-start.2 = (f32[3,8,128]{2,1,0:T(8,128)}, f32[3,8,128]{2,1,0:T(8,128)S(1)}, u32[]{:S(2)}, u32[]{:S(2)}) collective-permute-start(f32[3,8,128]{2,1,0:T(8,128)} %bitcast.22), channel_id=1, source_target_pairs={{0,31},{1,0},{2,1},{3,2},{4,3},{5,4},{6,5},{7,6},{8,7},{9,8},{10,9... | collective-permute-start | bytes 36872 | tf_op jit(solution)/shard_map/ppermute | solution.py:22
  9.6 9.4 %collective-permute-start.1 = (f32[3,8,128]{2,1,0:T(8,128)}, f32[3,8,128]{2,1,0:T(8,128)S(1)}, u32[]{:S(2)}, u32[]{:S(2)}) collective-permute-start(f32[3,8,128]{2,1,0:T(8,128)} %bitcast.23), channel_id=1, source_target_pairs={{0,1},{1,2},{2,3},{3,4},{4,5},{5,6},{6,7},{7,8},{8,9},{9,10},{10,1... | collective-permute-start | bytes 36872 | tf_op jit(solution)/shard_map/ppermute | solution.py:22
  11.0 8.0 %collective-permute-start = (f32[3,8,128]{2,1,0:T(8,128)}, f32[3,8,128]{2,1,0:T(8,128)S(1)}, u32[]{:S(2)}, u32[]{:S(2)}) collective-permute-start(f32[3,8,128]{2,1,0:T(8,128)} %bitcast.24), channel_id=1, source_target_pairs={{0,32},{32,64},{64,96},{96,128},{128,160},{160,192},{192,224},{224... | collective-permute-start | bytes 36872 | tf_op jit(solution)/shard_map/ppermute | solution.py:22
  19.0 60.0 %copy-start.4 = (s32[1,1,2,64]{3,2,1,0:T(2,128)S(1)}, s32[1,1,2,64]{3,2,1,0:T(2,128)}, u32[]{:S(2)}) copy-start(s32[1,1,2,64]{3,2,1,0:T(2,128)} %param.10) | copy-start | bytes 1540
  19.0 60.0 %copy-start.5 = (s32[1,1,2]{2,1,0:T(1,128)S(1)}, s32[1,1,2]{2,1,0:T(1,128)}, u32[]{:S(2)}) copy-start(s32[1,1,2]{2,1,0:T(1,128)} %param.11) | copy-start | bytes 28
  21.1 17.4 %collective-permute-start.4 = (f32[3,8,128]{2,1,0:T(8,128)S(1)}, f32[3,8,128]{2,1,0:T(8,128)S(1)}, u32[]{:S(2)}, u32[]{:S(2)}) collective-permute-start(f32[3,8,128]{2,1,0:T(8,128)S(1)} %get-tuple-element.34), channel_id=1, source_target_pairs={{0,32},{32,64},{64,96},{96,128},{128,160},{160,192},{192,224},{224... | collective-permute-start | bytes 36872 | tf_op jit(solution)/shard_map/ppermute | solution.py:22
  23.1 15.5 %collective-permute-start.5 = (f32[3,8,128]{2,1,0:T(8,128)S(1)}, f32[3,8,128]{2,1,0:T(8,128)S(1)}, u32[]{:S(2)}, u32[]{:S(2)}) collective-permute-start(f32[3,8,128]{2,1,0:T(8,128)S(1)} %get-tuple-element.35), channel_id=1, source_target_pairs={{0,480},{32,0},{64,32},{96,64},{128,96},{160,128},{192,160},{224,1... | collective-permute-start | bytes 36872 | tf_op jit(solution)/shard_map/ppermute | solution.py:22
  29.7 9.5 %collective-permute-start.6 = (f32[3,8,128]{2,1,0:T(8,128)S(1)}, f32[3,8,128]{2,1,0:T(8,128)S(1)}, u32[]{:S(2)}, u32[]{:S(2)}) collective-permute-start(f32[3,8,128]{2,1,0:T(8,128)S(1)} %get-tuple-element.36), channel_id=1, source_target_pairs={{0,1},{1,2},{2,3},{3,4},{4,5},{5,6},{6,7},{7,8},{8,9},{9,10},{10,1... | collective-permute-start | bytes 36872 | tf_op jit(solution)/shard_map/ppermute | solution.py:22
  31.9 7.5 %collective-permute-start.7 = (f32[3,8,128]{2,1,0:T(8,128)S(1)}, f32[3,8,128]{2,1,0:T(8,128)S(1)}, u32[]{:S(2)}, u32[]{:S(2)}) collective-permute-start(f32[3,8,128]{2,1,0:T(8,128)S(1)} %get-tuple-element.37), channel_id=1, source_target_pairs={{0,31},{1,0},{2,1},{3,2},{4,3},{5,4},{6,5},{7,6},{8,7},{9,8},{10,9... | collective-permute-start | bytes 36872 | tf_op jit(solution)/shard_map/ppermute | solution.py:22
  39.4 10.0 %collective-permute-start.11 = (f32[3,8,128]{2,1,0:T(8,128)S(1)}, f32[3,8,128]{2,1,0:T(8,128)S(1)}, u32[]{:S(2)}, u32[]{:S(2)}) collective-permute-start(f32[3,8,128]{2,1,0:T(8,128)S(1)} %select_add_fusion.2.own.k1), channel_id=1, source_target_pairs={{0,480},{32,0},{64,32},{96,64},{128,96},{160,128},{192,160},{224,1... | collective-permute-start | bytes 36872 | tf_op jit(solution)/shard_map/ppermute | solution.py:22
  41.3 8.1 %collective-permute-start.10 = (f32[3,8,128]{2,1,0:T(8,128)S(1)}, f32[3,8,128]{2,1,0:T(8,128)S(1)}, u32[]{:S(2)}, u32[]{:S(2)}) collective-permute-start(f32[3,8,128]{2,1,0:T(8,128)S(1)} %select_add_fusion.2.own.k1), channel_id=1, source_target_pairs={{0,31},{1,0},{2,1},{3,2},{4,3},{5,4},{6,5},{7,6},{8,7},{9,8},{10,9... | collective-permute-start | bytes 36872 | tf_op jit(solution)/shard_map/ppermute | solution.py:22
  47.5 1.9 %collective-permute-start.9 = (f32[3,8,128]{2,1,0:T(8,128)S(1)}, f32[3,8,128]{2,1,0:T(8,128)S(1)}, u32[]{:S(2)}, u32[]{:S(2)}) collective-permute-start(f32[3,8,128]{2,1,0:T(8,128)S(1)} %select_add_fusion.2.own.k1), channel_id=1, source_target_pairs={{0,1},{1,2},{2,3},{3,4},{4,5},{5,6},{6,7},{7,8},{8,9},{9,10},{10,1... | collective-permute-start | bytes 36872 | tf_op jit(solution)/shard_map/ppermute | solution.py:22
  47.5 7.7 %collective-permute-start.8 = (f32[3,8,128]{2,1,0:T(8,128)S(1)}, f32[3,8,128]{2,1,0:T(8,128)S(1)}, u32[]{:S(2)}, u32[]{:S(2)}) collective-permute-start(f32[3,8,128]{2,1,0:T(8,128)S(1)} %select_add_fusion.2.own.k1), channel_id=1, source_target_pairs={{0,32},{32,64},{64,96},{96,128},{128,160},{160,192},{192,224},{224... | collective-permute-start | bytes 36872 | tf_op jit(solution)/shard_map/ppermute | solution.py:22
  57.3 11.0 %collective-permute-start.12 = (f32[3,8,128]{2,1,0:T(8,128)S(1)}, f32[3,8,128]{2,1,0:T(8,128)S(1)}, u32[]{:S(2)}, u32[]{:S(2)}) collective-permute-start(f32[3,8,128]{2,1,0:T(8,128)S(1)} %get-tuple-element.40), channel_id=1, source_target_pairs={{0,32},{32,64},{64,96},{96,128},{128,160},{160,192},{192,224},{224... | collective-permute-start | bytes 36872 | tf_op jit(solution)/shard_map/ppermute | solution.py:22
  59.2 9.0 %collective-permute-start.13 = (f32[3,8,128]{2,1,0:T(8,128)S(1)}, f32[3,8,128]{2,1,0:T(8,128)S(1)}, u32[]{:S(2)}, u32[]{:S(2)}) collective-permute-start(f32[3,8,128]{2,1,0:T(8,128)S(1)} %get-tuple-element.41), channel_id=1, source_target_pairs={{0,480},{32,0},{64,32},{96,64},{128,96},{160,128},{192,160},{224,1... | collective-permute-start | bytes 36872 | tf_op jit(solution)/shard_map/ppermute | solution.py:22
  65.9 2.9 %collective-permute-start.14 = (f32[3,8,128]{2,1,0:T(8,128)S(1)}, f32[3,8,128]{2,1,0:T(8,128)S(1)}, u32[]{:S(2)}, u32[]{:S(2)}) collective-permute-start(f32[3,8,128]{2,1,0:T(8,128)S(1)} %get-tuple-element.42), channel_id=1, source_target_pairs={{0,1},{1,2},{2,3},{3,4},{4,5},{5,6},{6,7},{7,8},{8,9},{9,10},{10,1... | collective-permute-start | bytes 36872 | tf_op jit(solution)/shard_map/ppermute | solution.py:22
  65.9 3.1 %collective-permute-start.15 = (f32[3,8,128]{2,1,0:T(8,128)S(1)}, f32[3,8,128]{2,1,0:T(8,128)S(1)}, u32[]{:S(2)}, u32[]{:S(2)}) collective-permute-start(f32[3,8,128]{2,1,0:T(8,128)S(1)} %get-tuple-element.43), channel_id=1, source_target_pairs={{0,31},{1,0},{2,1},{3,2},{4,3},{5,4},{6,5},{7,6},{8,7},{9,8},{10,9... | collective-permute-start | bytes 36872 | tf_op jit(solution)/shard_map/ppermute | solution.py:22
  69.1 10.1 %collective-permute-start.19 = (f32[3,8,128]{2,1,0:T(8,128)S(1)}, f32[3,8,128]{2,1,0:T(8,128)S(1)}, u32[]{:S(2)}, u32[]{:S(2)}) collective-permute-start(f32[3,8,128]{2,1,0:T(8,128)S(1)} %select_add_fusion.1.own.k2), channel_id=1, source_target_pairs={{0,480},{32,0},{64,32},{96,64},{128,96},{160,128},{192,160},{224,1... | collective-permute-start | bytes 36872 | tf_op jit(solution)/shard_map/ppermute | solution.py:22
  73.7 5.5 %collective-permute-start.18 = (f32[3,8,128]{2,1,0:T(8,128)S(1)}, f32[3,8,128]{2,1,0:T(8,128)S(1)}, u32[]{:S(2)}, u32[]{:S(2)}) collective-permute-start(f32[3,8,128]{2,1,0:T(8,128)S(1)} %select_add_fusion.1.own.k2), channel_id=1, source_target_pairs={{0,31},{1,0},{2,1},{3,2},{4,3},{5,4},{6,5},{7,6},{8,7},{9,8},{10,9... | collective-permute-start | bytes 36872 | tf_op jit(solution)/shard_map/ppermute | solution.py:22
  77.1 2.1 %collective-permute-start.17 = (f32[3,8,128]{2,1,0:T(8,128)S(1)}, f32[3,8,128]{2,1,0:T(8,128)S(1)}, u32[]{:S(2)}, u32[]{:S(2)}) collective-permute-start(f32[3,8,128]{2,1,0:T(8,128)S(1)} %select_add_fusion.1.own.k2), channel_id=1, source_target_pairs={{0,1},{1,2},{2,3},{3,4},{4,5},{5,6},{6,7},{7,8},{8,9},{9,10},{10,1... | collective-permute-start | bytes 36872 | tf_op jit(solution)/shard_map/ppermute | solution.py:22
  77.1 7.7 %collective-permute-start.16 = (f32[3,8,128]{2,1,0:T(8,128)S(1)}, f32[3,8,128]{2,1,0:T(8,128)S(1)}, u32[]{:S(2)}, u32[]{:S(2)}) collective-permute-start(f32[3,8,128]{2,1,0:T(8,128)S(1)} %select_add_fusion.1.own.k2), channel_id=1, source_target_pairs={{0,32},{32,64},{64,96},{96,128},{128,160},{160,192},{192,224},{224... | collective-permute-start | bytes 36872 | tf_op jit(solution)/shard_map/ppermute | solution.py:22
  87.3 12.9 %all-to-all-start = ((f32[32,8,128]{2,1,0:T(8,128)}), f32[32,8,128]{2,1,0:T(8,128)S(1)}, u32[]{:S(2)}, u32[]{:S(2)}) async-start(f32[32,8,128]{2,1,0:T(8,128)} %get-tuple-element.48), calls=%async_computation | async-start | bytes 262144 | tf_op jit(solution)/shard_map/all_to_all | solution.py:275
  92.5 7.8 %collective-permute-start.20 = (f32[4,8,128]{2,1,0:T(8,128)S(1)}, f32[4,8,128]{2,1,0:T(8,128)S(1)}, u32[]{:S(2)}, u32[]{:S(2)}) collective-permute-start(f32[4,8,128]{2,1,0:T(8,128)S(1)} %get-tuple-element.52), channel_id=1, source_target_pairs={{0,1},{1,2},{2,3},{3,4},{4,5},{5,6},{6,7},{7,8},{8,9},{9,10},{10,1... | collective-permute-start | bytes 49160 | tf_op jit(solution)/shard_map/ppermute | solution.py:22
  92.5 7.8 %collective-permute-start.21 = (f32[4,8,128]{2,1,0:T(8,128)S(1)}, f32[4,8,128]{2,1,0:T(8,128)S(1)}, u32[]{:S(2)}, u32[]{:S(2)}) collective-permute-start(f32[4,8,128]{2,1,0:T(8,128)S(1)} %get-tuple-element.53), channel_id=1, source_target_pairs={{0,31},{1,0},{2,1},{3,2},{4,3},{5,4},{6,5},{7,6},{8,7},{9,8},{10,9... | collective-permute-start | bytes 49160 | tf_op jit(solution)/shard_map/ppermute | solution.py:22
  100.9 18.4 %all-to-all-start.1 = ((f32[16,8,128]{2,1,0:T(8,128)}), f32[16,8,128]{2,1,0:T(8,128)S(1)}, u32[]{:S(2)}, u32[]{:S(2)}) async-start(f32[16,8,128]{2,1,0:T(8,128)} %broadcast_in_dim.32), calls=%async_computation.1 | async-start | bytes 131072 | tf_op jit(solution)/shard_map/all_to_all | solution.py:275
  107.7 8.6 %collective-permute-start.22 = (f32[3,8,128]{2,1,0:T(8,128)S(1)}, f32[3,8,128]{2,1,0:T(8,128)S(1)}, u32[]{:S(2)}, u32[]{:S(2)}) collective-permute-start(f32[3,8,128]{2,1,0:T(8,128)S(1)} %get-tuple-element.56), channel_id=1, source_target_pairs={{0,32},{32,64},{64,96},{96,128},{128,160},{160,192},{192,224},{224... | collective-permute-start | bytes 36872 | tf_op jit(solution)/shard_map/ppermute | solution.py:22
  110.0 7.1 %collective-permute-start.23 = (f32[3,8,128]{2,1,0:T(8,128)S(1)}, f32[3,8,128]{2,1,0:T(8,128)S(1)}, u32[]{:S(2)}, u32[]{:S(2)}) collective-permute-start(f32[3,8,128]{2,1,0:T(8,128)S(1)} %get-tuple-element.57), channel_id=1, source_target_pairs={{0,480},{32,0},{64,32},{96,64},{128,96},{160,128},{192,160},{224,1... | collective-permute-start | bytes 36872 | tf_op jit(solution)/shard_map/ppermute | solution.py:22

commit v8 on v7

--- a/solution.py
+++ b/solution.py
@@ -28,7 +28,7 @@
 
 
 def operator_kernel(
-    sweep, ids, own, from_axial_dn, from_cross_dn, from_cross_up, from_axial_up, tiles, drag, *rest
+    sweep, ids, own, from_cross_up, from_cross_dn, from_axial_up, from_axial_dn, tiles, drag, *rest
 ):
     many = 2 if sweep == ITERS - 1 else 1
     carried, rest = rest[:many], rest[many:]
@@ -293,7 +293,7 @@
         below.append(cross_dn)
         above.append(cross_up)
         r1, r3, r5, r7, kept, sums = operator_call(
-            sweep, ids, (now, axial_dn, cross_dn, cross_up, axial_up), tiles[0, 0], drag, carried,
+            sweep, ids, (now, cross_up, cross_dn, axial_up, axial_dn), tiles[0, 0], drag, carried,
             2 * lax.axis_size("axial") if sweep == ITERS - 1 else None,
         )
         carried = (sums,)

time: 121 us -> 117 us (0.967)
  waiting for transfers between devices: 29 us -> 14.2 us
  starting transfers between devices: 81.8 us -> 93.2 us
    ppermute x24, waiting for transfers between devices: 19.6 us -> 4.93 us  [ring_shift(): return lax.ppermute(shard, axis, ring(lax.axis_size(axis), by))]
    ppermute x24, starting transfers between devices: 69.8 us -> 76.3 us  [ring_shift(): return lax.ppermute(shard, axis, ring(lax.axis_size(axis), by))]
    all_to_all x2, starting transfers between devices: 11.9 us -> 16.9 us  [spread_sum(): lax.all_to_all(part, ('axial', 'cross'), 0, 0, axis_index_groups=groups)]
  transfers between devices with their start and end apart: 26 -> 26, of which waited for: 10 -> 13; matrix products, arithmetic and copies ran while one was open for 0% -> 0% of each run, Pallas kernels for 0% -> 0%
where the time goes in v8:
time: 117 us
  starting transfers between devices  93.2 us (80%)
  waiting for transfers between devices  14.2 us (12%)
  Pallas kernels  7.56 us (6%)
    ppermute x24, starting transfers between devices, ring_shift(): return lax.ppermute(shard, axis, ring(lax.axis_size(axis), by))  76.3 us
    all_to_all x2, starting transfers between devices, spread_sum(): lax.all_to_all(part, ('axial', 'cross'), 0, 0, axis_index_groups=groups)  16.9 us
    all_to_all x2, waiting for transfers between devices, spread_sum(): lax.all_to_all(part, ('axial', 'cross'), 0, 0, axis_index_groups=groups)  9.26 us
    pallas_call x3, Pallas kernels, operator_call(): pl.pallas_call(functools.partial(operator_kernel, sweep), in_specs=[pl.Bl...  6.68 us
    ppermute x24, waiting for transfers between devices, ring_shift(): return lax.ppermute(shard, axis, ring(lax.axis_size(axis), by))  4.93 us
  transfers between devices with their start and end apart: 26, of which 13 were waited for; matrix products, arithmetic and copies ran while one was open for 0% of the time, Pallas kernels for 0%

profile of v8, /device:TPU:1, one launch (start us, length us, event | category | flops | bytes accessed | tf_op | source)
XLA Modules:
  0.0 116.8 jit_solution(1944601524403153610)
XLA Ops:
  0.7 4.1 %collective-permute-start.3 = (f32[3,8,128]{2,1,0:T(8,128)}, f32[3,8,128]{2,1,0:T(8,128)S(1)}, u32[]{:S(2)}, u32[]{:S(2)}) collective-permute-start(f32[3,8,128]{2,1,0:T(8,128)} %bitcast.21), channel_id=1, source_target_pairs={{0,32},{32,64},{64,96},{96,128},{128,160},{160,192},{192,224},{224... | collective-permute-start | bytes 36872 | tf_op jit(solution)/shard_map/ppermute | solution.py:22
  4.8 5.6 %collective-permute-start.2 = (f32[3,8,128]{2,1,0:T(8,128)}, f32[3,8,128]{2,1,0:T(8,128)S(1)}, u32[]{:S(2)}, u32[]{:S(2)}) collective-permute-start(f32[3,8,128]{2,1,0:T(8,128)} %bitcast.22), channel_id=1, source_target_pairs={{0,480},{32,0},{64,32},{96,64},{128,96},{160,128},{192,160},{224,1... | collective-permute-start | bytes 36872 | tf_op jit(solution)/shard_map/ppermute | solution.py:22
  10.4 2.6 %collective-permute-start.1 = (f32[3,8,128]{2,1,0:T(8,128)}, f32[3,8,128]{2,1,0:T(8,128)S(1)}, u32[]{:S(2)}, u32[]{:S(2)}) collective-permute-start(f32[3,8,128]{2,1,0:T(8,128)} %bitcast.23), channel_id=1, source_target_pairs={{0,1},{1,2},{2,3},{3,4},{4,5},{5,6},{6,7},{7,8},{8,9},{9,10},{10,1... | collective-permute-start | bytes 36872 | tf_op jit(solution)/shard_map/ppermute | solution.py:22
  13.0 3.9 %collective-permute-start = (f32[3,8,128]{2,1,0:T(8,128)}, f32[3,8,128]{2,1,0:T(8,128)S(1)}, u32[]{:S(2)}, u32[]{:S(2)}) collective-permute-start(f32[3,8,128]{2,1,0:T(8,128)} %bitcast.24), channel_id=1, source_target_pairs={{0,31},{1,0},{2,1},{3,2},{4,3},{5,4},{6,5},{7,6},{8,7},{9,8},{10,9... | collective-permute-start | bytes 36872 | tf_op jit(solution)/shard_map/ppermute | solution.py:22
  16.9 0.0 collective-permute-done.3.from_axial_dn
  16.9 0.0 collective-permute-done.2.from_axial_up
  16.9 0.8 collective-permute-done.1.from_cross_dn.d0
  17.8 0.2 collective-permute-done.from_cross_up.u0
  17.9 0.0 copy-done.3
  18.0 0.0 copy-start.4
  18.0 0.0 copy-start.5
  18.0 2.1 %shard_map.86 = (f32[3,8,128]{2,1,0:T(8,128)S(1)}, f32[3,8,128]{2,1,0:T(8,128)S(1)}, f32[3,8,128]{2,1,0:T(8,128)S(1)}, f32[3,8,128]{2,1,0:T(8,128)S(1)}, f32[3,8,128]{2,1,0:T(8,128)S(1)}, /*index=5*/f32[8,128]{1,0:T(8,128)S(1)}) custom-call(s32[8,8]{1,0:T(8,128)S(1)} %bitcast.27, f32[3,8,128]{2,1,0:T(8,128)S(1)} %bitcast.25, ...), custom_call_target="tpu_custom_call" | custom-call | tf_op jit(solution)/shard_map/pallas_call | solution.py:118
  20.1 1.9 %collective-permute-start.4 = (f32[3,8,128]{2,1,0:T(8,128)S(1)}, f32[3,8,128]{2,1,0:T(8,128)S(1)}, u32[]{:S(2)}, u32[]{:S(2)}) collective-permute-start(f32[3,8,128]{2,1,0:T(8,128)S(1)} %get-tuple-element.34), channel_id=1, source_target_pairs={{0,32},{32,64},{64,96},{96,128},{128,160},{160,192},{192,224},{224... | collective-permute-start | bytes 36872 | tf_op jit(solution)/shard_map/ppermute | solution.py:22
  22.0 6.7 %collective-permute-start.5 = (f32[3,8,128]{2,1,0:T(8,128)S(1)}, f32[3,8,128]{2,1,0:T(8,128)S(1)}, u32[]{:S(2)}, u32[]{:S(2)}) collective-permute-start(f32[3,8,128]{2,1,0:T(8,128)S(1)} %get-tuple-element.35), channel_id=1, source_target_pairs={{0,480},{32,0},{64,32},{96,64},{128,96},{160,128},{192,160},{224,1... | collective-permute-start | bytes 36872 | tf_op jit(solution)/shard_map/ppermute | solution.py:22
  28.7 0.0 collective-permute-start.6
  28.7 4.3 %collective-permute-start.7 = (f32[3,8,128]{2,1,0:T(8,128)S(1)}, f32[3,8,128]{2,1,0:T(8,128)S(1)}, u32[]{:S(2)}, u32[]{:S(2)}) collective-permute-start(f32[3,8,128]{2,1,0:T(8,128)S(1)} %get-tuple-element.37), channel_id=1, source_target_pairs={{0,31},{1,0},{2,1},{3,2},{4,3},{5,4},{6,5},{7,6},{8,7},{9,8},{10,9... | collective-permute-start | bytes 36872 | tf_op jit(solution)/shard_map/ppermute | solution.py:22
  33.0 0.0 collective-permute-done.4
  33.0 0.0 collective-permute-done.5
  33.0 0.6 collective-permute-done.6
  33.7 0.2 collective-permute-done.7
  33.9 1.9 %collective-permute-start.11 = (f32[3,8,128]{2,1,0:T(8,128)S(1)}, f32[3,8,128]{2,1,0:T(8,128)S(1)}, u32[]{:S(2)}, u32[]{:S(2)}) collective-permute-start(f32[3,8,128]{2,1,0:T(8,128)S(1)} %select_add_fusion.2.own.k1), channel_id=1, source_target_pairs={{0,32},{32,64},{64,96},{96,128},{128,160},{160,192},{192,224},{224... | collective-permute-start | bytes 36872 | tf_op jit(solution)/shard_map/ppermute | solution.py:22
  35.8 6.7 %collective-permute-start.10 = (f32[3,8,128]{2,1,0:T(8,128)S(1)}, f32[3,8,128]{2,1,0:T(8,128)S(1)}, u32[]{:S(2)}, u32[]{:S(2)}) collective-permute-start(f32[3,8,128]{2,1,0:T(8,128)S(1)} %select_add_fusion.2.own.k1), channel_id=1, source_target_pairs={{0,480},{32,0},{64,32},{96,64},{128,96},{160,128},{192,160},{224,1... | collective-permute-start | bytes 36872 | tf_op jit(solution)/shard_map/ppermute | solution.py:22
  42.5 0.0 collective-permute-start.9
  42.5 4.1 %collective-permute-start.8 = (f32[3,8,128]{2,1,0:T(8,128)S(1)}, f32[3,8,128]{2,1,0:T(8,128)S(1)}, u32[]{:S(2)}, u32[]{:S(2)}) collective-permute-start(f32[3,8,128]{2,1,0:T(8,128)S(1)} %select_add_fusion.2.own.k1), channel_id=1, source_target_pairs={{0,31},{1,0},{2,1},{3,2},{4,3},{5,4},{6,5},{7,6},{8,7},{9,8},{10,9... | collective-permute-start | bytes 36872 | tf_op jit(solution)/shard_map/ppermute | solution.py:22
  46.6 0.0 collective-permute-done.11.from_axial_dn
  46.6 0.0 collective-permute-done.10.from_axial_up
  46.6 0.6 collective-permute-done.9.from_cross_dn.d1
  47.2 0.2 collective-permute-done.8.from_cross_up.u1
  47.4 2.1 %shard_map.87 = (f32[3,8,128]{2,1,0:T(8,128)S(1)}, f32[3,8,128]{2,1,0:T(8,128)S(1)}, f32[3,8,128]{2,1,0:T(8,128)S(1)}, f32[3,8,128]{2,1,0:T(8,128)S(1)}, f32[3,8,128]{2,1,0:T(8,128)S(1)}, /*index=5*/f32[8,128]{1,0:T(8,128)S(1)}) custom-call(s32[8,8]{1,0:T(8,128)S(1)} %bitcast.28, f32[3,8,128]{2,1,0:T(8,128)S(1)} %select_add_fusion.2.own.k1, ...), custom_call_target="tpu_custom_call" | custom-call | tf_op jit(solution)/shard_map/pallas_call | solution.py:118
  49.5 1.9 %collective-permute-start.12 = (f32[3,8,128]{2,1,0:T(8,128)S(1)}, f32[3,8,128]{2,1,0:T(8,128)S(1)}, u32[]{:S(2)}, u32[]{:S(2)}) collective-permute-start(f32[3,8,128]{2,1,0:T(8,128)S(1)} %get-tuple-element.40), channel_id=1, source_target_pairs={{0,32},{32,64},{64,96},{96,128},{128,160},{160,192},{192,224},{224... | collective-permute-start | bytes 36872 | tf_op jit(solution)/shard_map/ppermute | solution.py:22
  51.4 6.7 %collective-permute-start.13 = (f32[3,8,128]{2,1,0:T(8,128)S(1)}, f32[3,8,128]{2,1,0:T(8,128)S(1)}, u32[]{:S(2)}, u32[]{:S(2)}) collective-permute-start(f32[3,8,128]{2,1,0:T(8,128)S(1)} %get-tuple-element.41), channel_id=1, source_target_pairs={{0,480},{32,0},{64,32},{96,64},{128,96},{160,128},{192,160},{224,1... | collective-permute-start | bytes 36872 | tf_op jit(solution)/shard_map/ppermute | solution.py:22
  58.1 0.0 collective-permute-start.14
  58.1 4.1 %collective-permute-start.15 = (f32[3,8,128]{2,1,0:T(8,128)S(1)}, f32[3,8,128]{2,1,0:T(8,128)S(1)}, u32[]{:S(2)}, u32[]{:S(2)}) collective-permute-start(f32[3,8,128]{2,1,0:T(8,128)S(1)} %get-tuple-element.43), channel_id=1, source_target_pairs={{0,31},{1,0},{2,1},{3,2},{4,3},{5,4},{6,5},{7,6},{8,7},{9,8},{10,9... | collective-permute-start | bytes 36872 | tf_op jit(solution)/shard_map/ppermute | solution.py:22
  62.2 0.1 pad.4.clone
  62.3 0.0 collective-permute-done.12
  62.3 0.0 collective-permute-done.13
  62.3 0.6 collective-permute-done.14
  62.9 0.2 collective-permute-done.15
  63.0 1.9 %collective-permute-start.19 = (f32[3,8,128]{2,1,0:T(8,128)S(1)}, f32[3,8,128]{2,1,0:T(8,128)S(1)}, u32[]{:S(2)}, u32[]{:S(2)}) collective-permute-start(f32[3,8,128]{2,1,0:T(8,128)S(1)} %select_add_fusion.1.own.k2), channel_id=1, source_target_pairs={{0,32},{32,64},{64,96},{96,128},{128,160},{160,192},{192,224},{224... | collective-permute-start | bytes 36872 | tf_op jit(solution)/shard_map/ppermute | solution.py:22
  65.0 6.7 %collective-permute-start.18 = (f32[3,8,128]{2,1,0:T(8,128)S(1)}, f32[3,8,128]{2,1,0:T(8,128)S(1)}, u32[]{:S(2)}, u32[]{:S(2)}) collective-permute-start(f32[3,8,128]{2,1,0:T(8,128)S(1)} %select_add_fusion.1.own.k2), channel_id=1, source_target_pairs={{0,480},{32,0},{64,32},{96,64},{128,96},{160,128},{192,160},{224,1... | collective-permute-start | bytes 36872 | tf_op jit(solution)/shard_map/ppermute | solution.py:22
  71.7 0.0 collective-permute-start.17
  71.7 4.1 %collective-permute-start.16 = (f32[3,8,128]{2,1,0:T(8,128)S(1)}, f32[3,8,128]{2,1,0:T(8,128)S(1)}, u32[]{:S(2)}, u32[]{:S(2)}) collective-permute-start(f32[3,8,128]{2,1,0:T(8,128)S(1)} %select_add_fusion.1.own.k2), channel_id=1, source_target_pairs={{0,31},{1,0},{2,1},{3,2},{4,3},{5,4},{6,5},{7,6},{8,7},{9,8},{10,9... | collective-permute-start | bytes 36872 | tf_op jit(solution)/shard_map/ppermute | solution.py:22
  75.8 0.0 copy-done.5
  75.8 0.1 fusion.2
  75.8 0.1 fusion.rest_1_
  75.9 0.0 collective-permute-done.19.from_axial_dn
  75.9 0.0 collective-permute-done.18.from_axial_up
  75.9 0.5 collective-permute-done.17.from_cross_dn.d2
  76.4 0.2 collective-permute-done.16.from_cross_up.u2
  76.6 2.5 %shard_map.88 = (f32[3,8,128]{2,1,0:T(8,128)S(1)}, f32[4,8,128]{2,1,0:T(8,128)S(1)}, f32[4,8,128]{2,1,0:T(8,128)S(1)}, f32[3,8,128]{2,1,0:T(8,128)S(1)}, f32[3,8...) custom-call(s32[8,8]{1,0:T(8,128)S(1)} %bitcast.29, f32[3,8,128]{2,1,0:T(8,128)S(1)} %select_add_fusion.1.own.k2, ...), custom_call_target="tpu_custom_call" | custom-call | tf_op jit(solution)/shard_map/pallas_call | solution.py:118
  79.1 7.6 %all-to-all-start = ((f32[32,8,128]{2,1,0:T(8,128)}), f32[32,8,128]{2,1,0:T(8,128)S(1)}, u32[]{:S(2)}, u32[]{:S(2)}) async-start(f32[32,8,128]{2,1,0:T(8,128)} %get-tuple-element.48), calls=%async_computation | async-start | bytes 262144 | tf_op jit(solution)/shard_map/all_to_all | solution.py:275
  86.7 0.0 collective-permute-start.20
  86.7 0.5 collective-permute-start.21
  87.2 7.1 %all-to-all-done = f32[32,8,128]{2,1,0:T(8,128)S(1)} async-done(((f32[32,8,128]{2,1,0:T(8,128)}), f32[32,8,128]{2,1,0:T(8,128)S(1)}, u32[]{:S(2)}, u32[]{:S(2)}) %all-to-all-start) | async-done | bytes 131104 | tf_op jit(solution)/shard_map/all_to_all | solution.py:275
  94.3 0.0 collective-permute-done.20.dn_plane
  94.3 0.0 collective-permute-done.21.up_plane
  94.3 0.6 broadcast_in_dim.32
  95.0 9.3 %all-to-all-start.1 = ((f32[16,8,128]{2,1,0:T(8,128)}), f32[16,8,128]{2,1,0:T(8,128)S(1)}, u32[]{:S(2)}, u32[]{:S(2)}) async-start(f32[16,8,128]{2,1,0:T(8,128)} %broadcast_in_dim.32), calls=%async_computation.1 | async-start | bytes 131072 | tf_op jit(solution)/shard_map/all_to_all | solution.py:275
  104.3 2.3 %collective-permute-start.22 = (f32[3,8,128]{2,1,0:T(8,128)S(1)}, f32[3,8,128]{2,1,0:T(8,128)S(1)}, u32[]{:S(2)}, u32[]{:S(2)}) collective-permute-start(f32[3,8,128]{2,1,0:T(8,128)S(1)} %get-tuple-element.56), channel_id=1, source_target_pairs={{0,32},{32,64},{64,96},{96,128},{128,160},{160,192},{192,224},{224... | collective-permute-start | bytes 36872 | tf_op jit(solution)/shard_map/ppermute | solution.py:22
  106.6 6.3 %collective-permute-start.23 = (f32[3,8,128]{2,1,0:T(8,128)S(1)}, f32[3,8,128]{2,1,0:T(8,128)S(1)}, u32[]{:S(2)}, u32[]{:S(2)}) collective-permute-start(f32[3,8,128]{2,1,0:T(8,128)S(1)} %get-tuple-element.57), channel_id=1, source_target_pairs={{0,480},{32,0},{64,32},{96,64},{128,96},{160,128},{192,160},{224,1... | collective-permute-start | bytes 36872 | tf_op jit(solution)/shard_map/ppermute | solution.py:22
  112.9 0.0 collective-permute-done.22
  112.9 0.8 collective-permute-done.23
  113.7 2.2 %all-to-all-done.1.sums = f32[16,8,128]{2,1,0:T(8,128)S(1)} async-done(((f32[16,8,128]{2,1,0:T(8,128)}), f32[16,8,128]{2,1,0:T(8,128)S(1)}, u32[]{:S(2)}, u32[]{:S(2)}) %all-to-all-start.1) | async-done | bytes 65568 | tf_op jit(solution)/shard_map/all_to_all | solution.py:275
  115.9 0.9 shard_map.89
  (15 shorter events, 0.1 us)
Async XLA Ops:
  0.6 17.3 %copy-start = (bf16[1,1,8,8,128,128]{5,4,3,2,1,0:T(8,128)(2,1)S(1)}, bf16[1,1,8,8,128,128]{5,4,3,2,1,0:T(8,128)(2,1)}, u32[]{:S(2)}) copy-start(bf16[1,1,8,8,128,128]{5,4,3,2,1,0:T(8,128)(2,1)} %param.8) | copy-start | bytes 6291460
  0.6 17.3 %copy-start.1 = (f32[1,1,8,3,128]{4,2,3,1,0:T(8,128)S(1)}, f32[1,1,8,3,128]{4,2,3,1,0:T(8,128)}, u32[]{:S(2)}) copy-start(f32[1,1,8,3,128]{4,2,3,1,0:T(8,128)} %param.6) | copy-start | bytes 36868
  0.7 17.3 %copy-start.2 = (s32[1,1,8,8]{3,2,1,0:T(8,128)S(1)}, s32[1,1,8,8]{3,2,1,0:T(8,128)}, u32[]{:S(2)}) copy-start(s32[1,1,8,8]{3,2,1,0:T(8,128)} %param.9) | copy-start | bytes 772
  0.7 17.3 %copy-start.3 = (f32[1,1,8,128]{3,2,1,0:T(8,128)S(1)}, f32[1,1,8,128]{3,2,1,0:T(8,128)}, u32[]{:S(2)}) copy-start(f32[1,1,8,128]{3,2,1,0:T(8,128)} %param.7) | copy-start | bytes 12292
  0.7 16.2 %collective-permute-start.3 = (f32[3,8,128]{2,1,0:T(8,128)}, f32[3,8,128]{2,1,0:T(8,128)S(1)}, u32[]{:S(2)}, u32[]{:S(2)}) collective-permute-start(f32[3,8,128]{2,1,0:T(8,128)} %bitcast.21), channel_id=1, source_target_pairs={{0,32},{32,64},{64,96},{96,128},{128,160},{160,192},{192,224},{224... | collective-permute-start | bytes 36872 | tf_op jit(solution)/shard_map/ppermute | solution.py:22
  4.8 12.1 %collective-permute-start.2 = (f32[3,8,128]{2,1,0:T(8,128)}, f32[3,8,128]{2,1,0:T(8,128)S(1)}, u32[]{:S(2)}, u32[]{:S(2)}) collective-permute-start(f32[3,8,128]{2,1,0:T(8,128)} %bitcast.22), channel_id=1, source_target_pairs={{0,480},{32,0},{64,32},{96,64},{128,96},{160,128},{192,160},{224,1... | collective-permute-start | bytes 36872 | tf_op jit(solution)/shard_map/ppermute | solution.py:22
  10.4 7.4 %collective-permute-start.1 = (f32[3,8,128]{2,1,0:T(8,128)}, f32[3,8,128]{2,1,0:T(8,128)S(1)}, u32[]{:S(2)}, u32[]{:S(2)}) collective-permute-start(f32[3,8,128]{2,1,0:T(8,128)} %bitcast.23), channel_id=1, source_target_pairs={{0,1},{1,2},{2,3},{3,4},{4,5},{5,6},{6,7},{7,8},{8,9},{9,10},{10,1... | collective-permute-start | bytes 36872 | tf_op jit(solution)/shard_map/ppermute | solution.py:22
  13.0 4.9 %collective-permute-start = (f32[3,8,128]{2,1,0:T(8,128)}, f32[3,8,128]{2,1,0:T(8,128)S(1)}, u32[]{:S(2)}, u32[]{:S(2)}) collective-permute-start(f32[3,8,128]{2,1,0:T(8,128)} %bitcast.24), channel_id=1, source_target_pairs={{0,31},{1,0},{2,1},{3,2},{4,3},{5,4},{6,5},{7,6},{8,7},{9,8},{10,9... | collective-permute-start | bytes 36872 | tf_op jit(solution)/shard_map/ppermute | solution.py:22
  18.0 57.8 %copy-start.4 = (s32[1,1,2,64]{3,2,1,0:T(2,128)S(1)}, s32[1,1,2,64]{3,2,1,0:T(2,128)}, u32[]{:S(2)}) copy-start(s32[1,1,2,64]{3,2,1,0:T(2,128)} %param.10) | copy-start | bytes 1540
  18.0 57.8 %copy-start.5 = (s32[1,1,2]{2,1,0:T(1,128)S(1)}, s32[1,1,2]{2,1,0:T(1,128)}, u32[]{:S(2)}) copy-start(s32[1,1,2]{2,1,0:T(1,128)} %param.11) | copy-start | bytes 28
  20.1 12.9 %collective-permute-start.4 = (f32[3,8,128]{2,1,0:T(8,128)S(1)}, f32[3,8,128]{2,1,0:T(8,128)S(1)}, u32[]{:S(2)}, u32[]{:S(2)}) collective-permute-start(f32[3,8,128]{2,1,0:T(8,128)S(1)} %get-tuple-element.34), channel_id=1, source_target_pairs={{0,32},{32,64},{64,96},{96,128},{128,160},{160,192},{192,224},{224... | collective-permute-start | bytes 36872 | tf_op jit(solution)/shard_map/ppermute | solution.py:22
  22.0 11.0 %collective-permute-start.5 = (f32[3,8,128]{2,1,0:T(8,128)S(1)}, f32[3,8,128]{2,1,0:T(8,128)S(1)}, u32[]{:S(2)}, u32[]{:S(2)}) collective-permute-start(f32[3,8,128]{2,1,0:T(8,128)S(1)} %get-tuple-element.35), channel_id=1, source_target_pairs={{0,480},{32,0},{64,32},{96,64},{128,96},{160,128},{192,160},{224,1... | collective-permute-start | bytes 36872 | tf_op jit(solution)/shard_map/ppermute | solution.py:22
  28.7 5.0 %collective-permute-start.6 = (f32[3,8,128]{2,1,0:T(8,128)S(1)}, f32[3,8,128]{2,1,0:T(8,128)S(1)}, u32[]{:S(2)}, u32[]{:S(2)}) collective-permute-start(f32[3,8,128]{2,1,0:T(8,128)S(1)} %get-tuple-element.36), channel_id=1, source_target_pairs={{0,1},{1,2},{2,3},{3,4},{4,5},{5,6},{6,7},{7,8},{8,9},{9,10},{10,1... | collective-permute-start | bytes 36872 | tf_op jit(solution)/shard_map/ppermute | solution.py:22
  28.7 5.1 %collective-permute-start.7 = (f32[3,8,128]{2,1,0:T(8,128)S(1)}, f32[3,8,128]{2,1,0:T(8,128)S(1)}, u32[]{:S(2)}, u32[]{:S(2)}) collective-permute-start(f32[3,8,128]{2,1,0:T(8,128)S(1)} %get-tuple-element.37), channel_id=1, source_target_pairs={{0,31},{1,0},{2,1},{3,2},{4,3},{5,4},{6,5},{7,6},{8,7},{9,8},{10,9... | collective-permute-start | bytes 36872 | tf_op jit(solution)/shard_map/ppermute | solution.py:22
  33.9 12.7 %collective-permute-start.11 = (f32[3,8,128]{2,1,0:T(8,128)S(1)}, f32[3,8,128]{2,1,0:T(8,128)S(1)}, u32[]{:S(2)}, u32[]{:S(2)}) collective-permute-start(f32[3,8,128]{2,1,0:T(8,128)S(1)} %select_add_fusion.2.own.k1), channel_id=1, source_target_pairs={{0,32},{32,64},{64,96},{96,128},{128,160},{160,192},{192,224},{224... | collective-permute-start | bytes 36872 | tf_op jit(solution)/shard_map/ppermute | solution.py:22
  35.8 10.8 %collective-permute-start.10 = (f32[3,8,128]{2,1,0:T(8,128)S(1)}, f32[3,8,128]{2,1,0:T(8,128)S(1)}, u32[]{:S(2)}, u32[]{:S(2)}) collective-permute-start(f32[3,8,128]{2,1,0:T(8,128)S(1)} %select_add_fusion.2.own.k1), channel_id=1, source_target_pairs={{0,480},{32,0},{64,32},{96,64},{128,96},{160,128},{192,160},{224,1... | collective-permute-start | bytes 36872 | tf_op jit(solution)/shard_map/ppermute | solution.py:22
  42.5 4.7 %collective-permute-start.9 = (f32[3,8,128]{2,1,0:T(8,128)S(1)}, f32[3,8,128]{2,1,0:T(8,128)S(1)}, u32[]{:S(2)}, u32[]{:S(2)}) collective-permute-start(f32[3,8,128]{2,1,0:T(8,128)S(1)} %select_add_fusion.2.own.k1), channel_id=1, source_target_pairs={{0,1},{1,2},{2,3},{3,4},{4,5},{5,6},{6,7},{7,8},{8,9},{9,10},{10,1... | collective-permute-start | bytes 36872 | tf_op jit(solution)/shard_map/ppermute | solution.py:22
  42.5 4.9 %collective-permute-start.8 = (f32[3,8,128]{2,1,0:T(8,128)S(1)}, f32[3,8,128]{2,1,0:T(8,128)S(1)}, u32[]{:S(2)}, u32[]{:S(2)}) collective-permute-start(f32[3,8,128]{2,1,0:T(8,128)S(1)} %select_add_fusion.2.own.k1), channel_id=1, source_target_pairs={{0,31},{1,0},{2,1},{3,2},{4,3},{5,4},{6,5},{7,6},{8,7},{9,8},{10,9... | collective-permute-start | bytes 36872 | tf_op jit(solution)/shard_map/ppermute | solution.py:22
  49.5 12.8 %collective-permute-start.12 = (f32[3,8,128]{2,1,0:T(8,128)S(1)}, f32[3,8,128]{2,1,0:T(8,128)S(1)}, u32[]{:S(2)}, u32[]{:S(2)}) collective-permute-start(f32[3,8,128]{2,1,0:T(8,128)S(1)} %get-tuple-element.40), channel_id=1, source_target_pairs={{0,32},{32,64},{64,96},{96,128},{128,160},{160,192},{192,224},{224... | collective-permute-start | bytes 36872 | tf_op jit(solution)/shard_map/ppermute | solution.py:22
  51.4 10.9 %collective-permute-start.13 = (f32[3,8,128]{2,1,0:T(8,128)S(1)}, f32[3,8,128]{2,1,0:T(8,128)S(1)}, u32[]{:S(2)}, u32[]{:S(2)}) collective-permute-start(f32[3,8,128]{2,1,0:T(8,128)S(1)} %get-tuple-element.41), channel_id=1, source_target_pairs={{0,480},{32,0},{64,32},{96,64},{128,96},{160,128},{192,160},{224,1... | collective-permute-start | bytes 36872 | tf_op jit(solution)/shard_map/ppermute | solution.py:22
  58.1 4.7 %collective-permute-start.14 = (f32[3,8,128]{2,1,0:T(8,128)S(1)}, f32[3,8,128]{2,1,0:T(8,128)S(1)}, u32[]{:S(2)}, u32[]{:S(2)}) collective-permute-start(f32[3,8,128]{2,1,0:T(8,128)S(1)} %get-tuple-element.42), channel_id=1, source_target_pairs={{0,1},{1,2},{2,3},{3,4},{4,5},{5,6},{6,7},{7,8},{8,9},{9,10},{10,1... | collective-permute-start | bytes 36872 | tf_op jit(solution)/shard_map/ppermute | solution.py:22
  58.1 4.9 %collective-permute-start.15 = (f32[3,8,128]{2,1,0:T(8,128)S(1)}, f32[3,8,128]{2,1,0:T(8,128)S(1)}, u32[]{:S(2)}, u32[]{:S(2)}) collective-permute-start(f32[3,8,128]{2,1,0:T(8,128)S(1)} %get-tuple-element.43), channel_id=1, source_target_pairs={{0,31},{1,0},{2,1},{3,2},{4,3},{5,4},{6,5},{7,6},{8,7},{9,8},{10,9... | collective-permute-start | bytes 36872 | tf_op jit(solution)/shard_map/ppermute | solution.py:22
  63.0 12.9 %collective-permute-start.19 = (f32[3,8,128]{2,1,0:T(8,128)S(1)}, f32[3,8,128]{2,1,0:T(8,128)S(1)}, u32[]{:S(2)}, u32[]{:S(2)}) collective-permute-start(f32[3,8,128]{2,1,0:T(8,128)S(1)} %select_add_fusion.1.own.k2), channel_id=1, source_target_pairs={{0,32},{32,64},{64,96},{96,128},{128,160},{160,192},{192,224},{224... | collective-permute-start | bytes 36872 | tf_op jit(solution)/shard_map/ppermute | solution.py:22
  65.0 11.0 %collective-permute-start.18 = (f32[3,8,128]{2,1,0:T(8,128)S(1)}, f32[3,8,128]{2,1,0:T(8,128)S(1)}, u32[]{:S(2)}, u32[]{:S(2)}) collective-permute-start(f32[3,8,128]{2,1,0:T(8,128)S(1)} %select_add_fusion.1.own.k2), channel_id=1, source_target_pairs={{0,480},{32,0},{64,32},{96,64},{128,96},{160,128},{192,160},{224,1... | collective-permute-start | bytes 36872 | tf_op jit(solution)/shard_map/ppermute | solution.py:22
  71.7 4.7 %collective-permute-start.17 = (f32[3,8,128]{2,1,0:T(8,128)S(1)}, f32[3,8,128]{2,1,0:T(8,128)S(1)}, u32[]{:S(2)}, u32[]{:S(2)}) collective-permute-start(f32[3,8,128]{2,1,0:T(8,128)S(1)} %select_add_fusion.1.own.k2), channel_id=1, source_target_pairs={{0,1},{1,2},{2,3},{3,4},{4,5},{5,6},{6,7},{7,8},{8,9},{9,10},{10,1... | collective-permute-start | bytes 36872 | tf_op jit(solution)/shard_map/ppermute | solution.py:22
  71.7 4.9 %collective-permute-start.16 = (f32[3,8,128]{2,1,0:T(8,128)S(1)}, f32[3,8,128]{2,1,0:T(8,128)S(1)}, u32[]{:S(2)}, u32[]{:S(2)}) collective-permute-start(f32[3,8,128]{2,1,0:T(8,128)S(1)} %select_add_fusion.1.own.k2), channel_id=1, source_target_pairs={{0,31},{1,0},{2,1},{3,2},{4,3},{5,4},{6,5},{7,6},{8,7},{9,8},{10,9... | collective-permute-start | bytes 36872 | tf_op jit(solution)/shard_map/ppermute | solution.py:22
  79.1 15.2 %all-to-all-start = ((f32[32,8,128]{2,1,0:T(8,128)}), f32[32,8,128]{2,1,0:T(8,128)S(1)}, u32[]{:S(2)}, u32[]{:S(2)}) async-start(f32[32,8,128]{2,1,0:T(8,128)} %get-tuple-element.48), calls=%async_computation | async-start | bytes 262144 | tf_op jit(solution)/shard_map/all_to_all | solution.py:275
  86.7 7.7 %collective-permute-start.20 = (f32[4,8,128]{2,1,0:T(8,128)S(1)}, f32[4,8,128]{2,1,0:T(8,128)S(1)}, u32[]{:S(2)}, u32[]{:S(2)}) collective-permute-start(f32[4,8,128]{2,1,0:T(8,128)S(1)} %get-tuple-element.52), channel_id=1, source_target_pairs={{0,1},{1,2},{2,3},{3,4},{4,5},{5,6},{6,7},{7,8},{8,9},{9,10},{10,1... | collective-permute-start | bytes 49160 | tf_op jit(solution)/shard_map/ppermute | solution.py:22
  86.7 7.6 %collective-permute-start.21 = (f32[4,8,128]{2,1,0:T(8,128)S(1)}, f32[4,8,128]{2,1,0:T(8,128)S(1)}, u32[]{:S(2)}, u32[]{:S(2)}) collective-permute-start(f32[4,8,128]{2,1,0:T(8,128)S(1)} %get-tuple-element.53), channel_id=1, source_target_pairs={{0,31},{1,0},{2,1},{3,2},{4,3},{5,4},{6,5},{7,6},{8,7},{9,8},{10,9... | collective-permute-start | bytes 49160 | tf_op jit(solution)/shard_map/ppermute | solution.py:22
  95.0 20.9 %all-to-all-start.1 = ((f32[16,8,128]{2,1,0:T(8,128)}), f32[16,8,128]{2,1,0:T(8,128)S(1)}, u32[]{:S(2)}, u32[]{:S(2)}) async-start(f32[16,8,128]{2,1,0:T(8,128)} %broadcast_in_dim.32), calls=%async_computation.1 | async-start | bytes 131072 | tf_op jit(solution)/shard_map/all_to_all | solution.py:275
  104.3 8.6 %collective-permute-start.22 = (f32[3,8,128]{2,1,0:T(8,128)S(1)}, f32[3,8,128]{2,1,0:T(8,128)S(1)}, u32[]{:S(2)}, u32[]{:S(2)}) collective-permute-start(f32[3,8,128]{2,1,0:T(8,128)S(1)} %get-tuple-element.56), channel_id=1, source_target_pairs={{0,32},{32,64},{64,96},{96,128},{128,160},{160,192},{192,224},{224... | collective-permute-start | bytes 36872 | tf_op jit(solution)/shard_map/ppermute | solution.py:22
  106.6 7.1 %collective-permute-start.23 = (f32[3,8,128]{2,1,0:T(8,128)S(1)}, f32[3,8,128]{2,1,0:T(8,128)S(1)}, u32[]{:S(2)}, u32[]{:S(2)}) collective-permute-start(f32[3,8,128]{2,1,0:T(8,128)S(1)} %get-tuple-element.57), channel_id=1, source_target_pairs={{0,480},{32,0},{64,32},{96,64},{128,96},{160,128},{192,160},{224,1... | collective-permute-start | bytes 36872 | tf_op jit(solution)/shard_map/ppermute | solution.py:22

commit v9 on v8

--- a/solution.py
+++ b/solution.py
@@ -28,7 +28,7 @@
 
 
 def operator_kernel(
-    sweep, ids, own, from_cross_up, from_cross_dn, from_axial_up, from_axial_dn, tiles, drag, *rest
+    sweep, ids, own, from_cross_up, from_axial_up, from_cross_dn, from_axial_dn, tiles, drag, *rest
 ):
     many = 2 if sweep == ITERS - 1 else 1
     carried, rest = rest[:many], rest[many:]
@@ -293,7 +293,7 @@
         below.append(cross_dn)
         above.append(cross_up)
         r1, r3, r5, r7, kept, sums = operator_call(
-            sweep, ids, (now, cross_up, cross_dn, axial_up, axial_dn), tiles[0, 0], drag, carried,
+            sweep, ids, (now, cross_up, axial_up, cross_dn, axial_dn), tiles[0, 0], drag, carried,
             2 * lax.axis_size("axial") if sweep == ITERS - 1 else None,
         )
         carried = (sums,)
@@ -311,8 +311,9 @@
         from_upper_axial = ring_shift(r1, "axial", -1)
         if sweep == ITERS - 1:
             planes = [from_lower_cross, from_upper_cross]
-        now = kept + from_lower_axial + from_upper_axial
+        now = kept + from_lower_axial
         now = now + jnp.where(slab > 0, from_lower_cross[:3], 0.0)
+        now = now + from_upper_axial
         now = now + jnp.where(slab < last, from_upper_cross[:3], 0.0)
         if sweep == ITERS - 2:
             now, mig_rows, mig_count = lax.optimization_barrier((now, mig_rows, mig_count))

time: 117 us -> 117 us (level)
  transfers between devices with their start and end apart: 26 -> 26, of which waited for: 13 -> 8; matrix products, arithmetic and copies ran while one was open for 0% -> 0% of each run, Pallas kernels for 0% -> 0%
where the time goes in v9:
time: 117 us; the launch traced here: 116 us
  starting transfers between devices  92.5 us (79%)
  waiting for transfers between devices  14.2 us (12%)
  Pallas kernels  7.54 us (6%)
    ppermute x24, starting transfers between devices, ring_shift(): return lax.ppermute(shard, axis, ring(lax.axis_size(axis), by))  75.5 us
    all_to_all x2, starting transfers between devices, spread_sum(): lax.all_to_all(part, ('axial', 'cross'), 0, 0, axis_index_groups=groups)  17 us
    all_to_all x2, waiting for transfers between devices, spread_sum(): lax.all_to_all(part, ('axial', 'cross'), 0, 0, axis_index_groups=groups)  9.26 us
    pallas_call x3, Pallas kernels, operator_call(): pl.pallas_call(functools.partial(operator_kernel, sweep), in_specs=[pl.Bl...  6.66 us
    ppermute x24, waiting for transfers between devices, ring_shift(): return lax.ppermute(shard, axis, ring(lax.axis_size(axis), by))  4.91 us
  transfers between devices with their start and end apart: 26, of which 8 were waited for; matrix products, arithmetic and copies ran while one was open for 0% of the time, Pallas kernels for 0%

profile of v9, /device:TPU:1, one launch (start us, length us, event | category | flops | bytes accessed | tf_op | source)
XLA Modules:
  0.0 116.0 jit_solution(14262550084023135511)
XLA Ops:
  0.7 4.1 %collective-permute-start.3 = (f32[3,8,128]{2,1,0:T(8,128)}, f32[3,8,128]{2,1,0:T(8,128)S(1)}, u32[]{:S(2)}, u32[]{:S(2)}) collective-permute-start(f32[3,8,128]{2,1,0:T(8,128)} %bitcast.21), channel_id=1, source_target_pairs={{0,32},{32,64},{64,96},{96,128},{128,160},{160,192},{192,224},{224... | collective-permute-start | bytes 36872 | tf_op jit(solution)/shard_map/ppermute | solution.py:22
  4.8 2.5 %collective-permute-start.2 = (f32[3,8,128]{2,1,0:T(8,128)}, f32[3,8,128]{2,1,0:T(8,128)S(1)}, u32[]{:S(2)}, u32[]{:S(2)}) collective-permute-start(f32[3,8,128]{2,1,0:T(8,128)} %bitcast.22), channel_id=1, source_target_pairs={{0,1},{1,2},{2,3},{3,4},{4,5},{5,6},{6,7},{7,8},{8,9},{9,10},{10,1... | collective-permute-start | bytes 36872 | tf_op jit(solution)/shard_map/ppermute | solution.py:22
  7.2 5.5 %collective-permute-start.1 = (f32[3,8,128]{2,1,0:T(8,128)}, f32[3,8,128]{2,1,0:T(8,128)S(1)}, u32[]{:S(2)}, u32[]{:S(2)}) collective-permute-start(f32[3,8,128]{2,1,0:T(8,128)} %bitcast.23), channel_id=1, source_target_pairs={{0,480},{32,0},{64,32},{96,64},{128,96},{160,128},{192,160},{224,1... | collective-permute-start | bytes 36872 | tf_op jit(solution)/shard_map/ppermute | solution.py:22
  12.7 4.2 %collective-permute-start = (f32[3,8,128]{2,1,0:T(8,128)}, f32[3,8,128]{2,1,0:T(8,128)S(1)}, u32[]{:S(2)}, u32[]{:S(2)}) collective-permute-start(f32[3,8,128]{2,1,0:T(8,128)} %bitcast.24), channel_id=1, source_target_pairs={{0,31},{1,0},{2,1},{3,2},{4,3},{5,4},{6,5},{7,6},{8,7},{9,8},{10,9... | collective-permute-start | bytes 36872 | tf_op jit(solution)/shard_map/ppermute | solution.py:22
  16.9 0.0 collective-permute-done.3.from_axial_dn
  16.9 0.0 collective-permute-done.2.from_cross_dn.d0
  16.9 0.0 collective-permute-done.1.from_axial_up
  16.9 1.0 collective-permute-done.from_cross_up.u0
  17.9 0.0 copy-done.3
  18.0 0.0 copy-start.4
  18.0 0.0 copy-start.5
  18.0 2.1 %shard_map.86 = (f32[3,8,128]{2,1,0:T(8,128)S(1)}, f32[3,8,128]{2,1,0:T(8,128)S(1)}, f32[3,8,128]{2,1,0:T(8,128)S(1)}, f32[3,8,128]{2,1,0:T(8,128)S(1)}, f32[3,8,128]{2,1,0:T(8,128)S(1)}, /*index=5*/f32[8,128]{1,0:T(8,128)S(1)}) custom-call(s32[8,8]{1,0:T(8,128)S(1)} %bitcast.27, f32[3,8,128]{2,1,0:T(8,128)S(1)} %bitcast.25, ...), custom_call_target="tpu_custom_call" | custom-call | tf_op jit(solution)/shard_map/pallas_call | solution.py:118
  20.1 1.9 %collective-permute-start.4 = (f32[3,8,128]{2,1,0:T(8,128)S(1)}, f32[3,8,128]{2,1,0:T(8,128)S(1)}, u32[]{:S(2)}, u32[]{:S(2)}) collective-permute-start(f32[3,8,128]{2,1,0:T(8,128)S(1)} %get-tuple-element.34), channel_id=1, source_target_pairs={{0,32},{32,64},{64,96},{96,128},{128,160},{160,192},{192,224},{224... | collective-permute-start | bytes 36872 | tf_op jit(solution)/shard_map/ppermute | solution.py:22
  22.0 0.0 collective-permute-start.5
  22.0 6.7 %collective-permute-start.6 = (f32[3,8,128]{2,1,0:T(8,128)S(1)}, f32[3,8,128]{2,1,0:T(8,128)S(1)}, u32[]{:S(2)}, u32[]{:S(2)}) collective-permute-start(f32[3,8,128]{2,1,0:T(8,128)S(1)} %get-tuple-element.36), channel_id=1, source_target_pairs={{0,480},{32,0},{64,32},{96,64},{128,96},{160,128},{192,160},{224,1... | collective-permute-start | bytes 36872 | tf_op jit(solution)/shard_map/ppermute | solution.py:22
  28.7 4.3 %collective-permute-start.7 = (f32[3,8,128]{2,1,0:T(8,128)S(1)}, f32[3,8,128]{2,1,0:T(8,128)S(1)}, u32[]{:S(2)}, u32[]{:S(2)}) collective-permute-start(f32[3,8,128]{2,1,0:T(8,128)S(1)} %get-tuple-element.37), channel_id=1, source_target_pairs={{0,31},{1,0},{2,1},{3,2},{4,3},{5,4},{6,5},{7,6},{8,7},{9,8},{10,9... | collective-permute-start | bytes 36872 | tf_op jit(solution)/shard_map/ppermute | solution.py:22
  33.0 0.0 collective-permute-done.4
  33.0 0.0 collective-permute-done.5
  33.0 0.0 collective-permute-done.6
  33.0 0.8 collective-permute-done.7
  33.9 1.9 %collective-permute-start.11 = (f32[3,8,128]{2,1,0:T(8,128)S(1)}, f32[3,8,128]{2,1,0:T(8,128)S(1)}, u32[]{:S(2)}, u32[]{:S(2)}) collective-permute-start(f32[3,8,128]{2,1,0:T(8,128)S(1)} %select_add_fusion.2.own.k1), channel_id=1, source_target_pairs={{0,32},{32,64},{64,96},{96,128},{128,160},{160,192},{192,224},{224... | collective-permute-start | bytes 36872 | tf_op jit(solution)/shard_map/ppermute | solution.py:22
  35.8 0.0 collective-permute-start.10
  35.8 6.7 %collective-permute-start.9 = (f32[3,8,128]{2,1,0:T(8,128)S(1)}, f32[3,8,128]{2,1,0:T(8,128)S(1)}, u32[]{:S(2)}, u32[]{:S(2)}) collective-permute-start(f32[3,8,128]{2,1,0:T(8,128)S(1)} %select_add_fusion.2.own.k1), channel_id=1, source_target_pairs={{0,480},{32,0},{64,32},{96,64},{128,96},{160,128},{192,160},{224,1... | collective-permute-start | bytes 36872 | tf_op jit(solution)/shard_map/ppermute | solution.py:22
  42.5 3.8 %collective-permute-start.8 = (f32[3,8,128]{2,1,0:T(8,128)S(1)}, f32[3,8,128]{2,1,0:T(8,128)S(1)}, u32[]{:S(2)}, u32[]{:S(2)}) collective-permute-start(f32[3,8,128]{2,1,0:T(8,128)S(1)} %select_add_fusion.2.own.k1), channel_id=1, source_target_pairs={{0,31},{1,0},{2,1},{3,2},{4,3},{5,4},{6,5},{7,6},{8,7},{9,8},{10,9... | collective-permute-start | bytes 36872 | tf_op jit(solution)/shard_map/ppermute | solution.py:22
  46.3 0.0 collective-permute-done.11.from_axial_dn
  46.3 0.0 collective-permute-done.10.from_cross_dn.d1
  46.3 0.0 collective-permute-done.9.from_axial_up
  46.3 0.8 collective-permute-done.8.from_cross_up.u1
  47.1 2.1 %shard_map.87 = (f32[3,8,128]{2,1,0:T(8,128)S(1)}, f32[3,8,128]{2,1,0:T(8,128)S(1)}, f32[3,8,128]{2,1,0:T(8,128)S(1)}, f32[3,8,128]{2,1,0:T(8,128)S(1)}, f32[3,8,128]{2,1,0:T(8,128)S(1)}, /*index=5*/f32[8,128]{1,0:T(8,128)S(1)}) custom-call(s32[8,8]{1,0:T(8,128)S(1)} %bitcast.28, f32[3,8,128]{2,1,0:T(8,128)S(1)} %select_add_fusion.2.own.k1, ...), custom_call_target="tpu_custom_call" | custom-call | tf_op jit(solution)/shard_map/pallas_call | solution.py:118
  49.2 1.9 %collective-permute-start.12 = (f32[3,8,128]{2,1,0:T(8,128)S(1)}, f32[3,8,128]{2,1,0:T(8,128)S(1)}, u32[]{:S(2)}, u32[]{:S(2)}) collective-permute-start(f32[3,8,128]{2,1,0:T(8,128)S(1)} %get-tuple-element.40), channel_id=1, source_target_pairs={{0,32},{32,64},{64,96},{96,128},{128,160},{160,192},{192,224},{224... | collective-permute-start | bytes 36872 | tf_op jit(solution)/shard_map/ppermute | solution.py:22
  51.1 0.0 collective-permute-start.13
  51.2 6.7 %collective-permute-start.14 = (f32[3,8,128]{2,1,0:T(8,128)S(1)}, f32[3,8,128]{2,1,0:T(8,128)S(1)}, u32[]{:S(2)}, u32[]{:S(2)}) collective-permute-start(f32[3,8,128]{2,1,0:T(8,128)S(1)} %get-tuple-element.42), channel_id=1, source_target_pairs={{0,480},{32,0},{64,32},{96,64},{128,96},{160,128},{192,160},{224,1... | collective-permute-start | bytes 36872 | tf_op jit(solution)/shard_map/ppermute | solution.py:22
  57.8 3.8 %collective-permute-start.15 = (f32[3,8,128]{2,1,0:T(8,128)S(1)}, f32[3,8,128]{2,1,0:T(8,128)S(1)}, u32[]{:S(2)}, u32[]{:S(2)}) collective-permute-start(f32[3,8,128]{2,1,0:T(8,128)S(1)} %get-tuple-element.43), channel_id=1, source_target_pairs={{0,31},{1,0},{2,1},{3,2},{4,3},{5,4},{6,5},{7,6},{8,7},{9,8},{10,9... | collective-permute-start | bytes 36872 | tf_op jit(solution)/shard_map/ppermute | solution.py:22
  61.6 0.1 pad.4.clone
  61.7 0.0 collective-permute-done.12
  61.7 0.0 collective-permute-done.13
  61.7 0.0 collective-permute-done.14
  61.7 0.7 collective-permute-done.15
  62.5 1.9 %collective-permute-start.19 = (f32[3,8,128]{2,1,0:T(8,128)S(1)}, f32[3,8,128]{2,1,0:T(8,128)S(1)}, u32[]{:S(2)}, u32[]{:S(2)}) collective-permute-start(f32[3,8,128]{2,1,0:T(8,128)S(1)} %select_add_fusion.1.own.k2), channel_id=1, source_target_pairs={{0,32},{32,64},{64,96},{96,128},{128,160},{160,192},{192,224},{224... | collective-permute-start | bytes 36872 | tf_op jit(solution)/shard_map/ppermute | solution.py:22
  64.4 0.0 collective-permute-start.18
  64.4 6.7 %collective-permute-start.17 = (f32[3,8,128]{2,1,0:T(8,128)S(1)}, f32[3,8,128]{2,1,0:T(8,128)S(1)}, u32[]{:S(2)}, u32[]{:S(2)}) collective-permute-start(f32[3,8,128]{2,1,0:T(8,128)S(1)} %select_add_fusion.1.own.k2), channel_id=1, source_target_pairs={{0,480},{32,0},{64,32},{96,64},{128,96},{160,128},{192,160},{224,1... | collective-permute-start | bytes 36872 | tf_op jit(solution)/shard_map/ppermute | solution.py:22
  71.1 3.8 %collective-permute-start.16 = (f32[3,8,128]{2,1,0:T(8,128)S(1)}, f32[3,8,128]{2,1,0:T(8,128)S(1)}, u32[]{:S(2)}, u32[]{:S(2)}) collective-permute-start(f32[3,8,128]{2,1,0:T(8,128)S(1)} %select_add_fusion.1.own.k2), channel_id=1, source_target_pairs={{0,31},{1,0},{2,1},{3,2},{4,3},{5,4},{6,5},{7,6},{8,7},{9,8},{10,9... | collective-permute-start | bytes 36872 | tf_op jit(solution)/shard_map/ppermute | solution.py:22
  74.9 0.0 copy-done.5
  74.9 0.1 fusion.2
  75.0 0.1 fusion.rest_1_
  75.1 0.0 collective-permute-done.19.from_axial_dn
  75.1 0.0 collective-permute-done.18.from_cross_dn.d2
  75.1 0.0 collective-permute-done.17.from_axial_up
  75.1 0.7 collective-permute-done.16.from_cross_up.u2
  75.7 2.5 %shard_map.88 = (f32[3,8,128]{2,1,0:T(8,128)S(1)}, f32[4,8,128]{2,1,0:T(8,128)S(1)}, f32[4,8,128]{2,1,0:T(8,128)S(1)}, f32[3,8,128]{2,1,0:T(8,128)S(1)}, f32[3,8...) custom-call(s32[8,8]{1,0:T(8,128)S(1)} %bitcast.29, f32[3,8,128]{2,1,0:T(8,128)S(1)} %select_add_fusion.1.own.k2, ...), custom_call_target="tpu_custom_call" | custom-call | tf_op jit(solution)/shard_map/pallas_call | solution.py:118
  78.3 7.6 %all-to-all-start = ((f32[32,8,128]{2,1,0:T(8,128)}), f32[32,8,128]{2,1,0:T(8,128)S(1)}, u32[]{:S(2)}, u32[]{:S(2)}) async-start(f32[32,8,128]{2,1,0:T(8,128)} %get-tuple-element.48), calls=%async_computation | async-start | bytes 262144 | tf_op jit(solution)/shard_map/all_to_all | solution.py:275
  85.8 0.0 collective-permute-start.20
  85.9 0.5 collective-permute-start.21
  86.4 7.1 %all-to-all-done = f32[32,8,128]{2,1,0:T(8,128)S(1)} async-done(((f32[32,8,128]{2,1,0:T(8,128)}), f32[32,8,128]{2,1,0:T(8,128)S(1)}, u32[]{:S(2)}, u32[]{:S(2)}) %all-to-all-start) | async-done | bytes 131104 | tf_op jit(solution)/shard_map/all_to_all | solution.py:275
  93.5 0.0 collective-permute-done.20.dn_plane
  93.5 0.0 collective-permute-done.21.up_plane
  93.5 0.6 broadcast_in_dim.32
  94.2 9.4 %all-to-all-start.1 = ((f32[16,8,128]{2,1,0:T(8,128)}), f32[16,8,128]{2,1,0:T(8,128)S(1)}, u32[]{:S(2)}, u32[]{:S(2)}) async-start(f32[16,8,128]{2,1,0:T(8,128)} %broadcast_in_dim.32), calls=%async_computation.1 | async-start | bytes 131072 | tf_op jit(solution)/shard_map/all_to_all | solution.py:275
  103.6 2.3 %collective-permute-start.22 = (f32[3,8,128]{2,1,0:T(8,128)S(1)}, f32[3,8,128]{2,1,0:T(8,128)S(1)}, u32[]{:S(2)}, u32[]{:S(2)}) collective-permute-start(f32[3,8,128]{2,1,0:T(8,128)S(1)} %get-tuple-element.56), channel_id=1, source_target_pairs={{0,32},{32,64},{64,96},{96,128},{128,160},{160,192},{192,224},{224... | collective-permute-start | bytes 36872 | tf_op jit(solution)/shard_map/ppermute | solution.py:22
  105.9 6.3 %collective-permute-start.23 = (f32[3,8,128]{2,1,0:T(8,128)S(1)}, f32[3,8,128]{2,1,0:T(8,128)S(1)}, u32[]{:S(2)}, u32[]{:S(2)}) collective-permute-start(f32[3,8,128]{2,1,0:T(8,128)S(1)} %get-tuple-element.58), channel_id=1, source_target_pairs={{0,480},{32,0},{64,32},{96,64},{128,96},{160,128},{192,160},{224,1... | collective-permute-start | bytes 36872 | tf_op jit(solution)/shard_map/ppermute | solution.py:22
  112.2 0.0 collective-permute-done.22
  112.2 0.8 collective-permute-done.23
  113.0 2.2 %all-to-all-done.1.sums = f32[16,8,128]{2,1,0:T(8,128)S(1)} async-done(((f32[16,8,128]{2,1,0:T(8,128)}), f32[16,8,128]{2,1,0:T(8,128)S(1)}, u32[]{:S(2)}, u32[]{:S(2)}) %all-to-all-start.1) | async-done | bytes 65568 | tf_op jit(solution)/shard_map/all_to_all | solution.py:275
  115.2 0.9 shard_map.89
  (15 shorter events, 0.1 us)
Async XLA Ops:
  0.6 17.3 %copy-start = (bf16[1,1,8,8,128,128]{5,4,3,2,1,0:T(8,128)(2,1)S(1)}, bf16[1,1,8,8,128,128]{5,4,3,2,1,0:T(8,128)(2,1)}, u32[]{:S(2)}) copy-start(bf16[1,1,8,8,128,128]{5,4,3,2,1,0:T(8,128)(2,1)} %param.8) | copy-start | bytes 6291460
  0.6 17.3 %copy-start.1 = (f32[1,1,8,3,128]{4,2,3,1,0:T(8,128)S(1)}, f32[1,1,8,3,128]{4,2,3,1,0:T(8,128)}, u32[]{:S(2)}) copy-start(f32[1,1,8,3,128]{4,2,3,1,0:T(8,128)} %param.6) | copy-start | bytes 36868
  0.7 17.3 %copy-start.2 = (s32[1,1,8,8]{3,2,1,0:T(8,128)S(1)}, s32[1,1,8,8]{3,2,1,0:T(8,128)}, u32[]{:S(2)}) copy-start(s32[1,1,8,8]{3,2,1,0:T(8,128)} %param.9) | copy-start | bytes 772
  0.7 17.3 %copy-start.3 = (f32[1,1,8,128]{3,2,1,0:T(8,128)S(1)}, f32[1,1,8,128]{3,2,1,0:T(8,128)}, u32[]{:S(2)}) copy-start(f32[1,1,8,128]{3,2,1,0:T(8,128)} %param.7) | copy-start | bytes 12292
  0.7 16.2 %collective-permute-start.3 = (f32[3,8,128]{2,1,0:T(8,128)}, f32[3,8,128]{2,1,0:T(8,128)S(1)}, u32[]{:S(2)}, u32[]{:S(2)}) collective-permute-start(f32[3,8,128]{2,1,0:T(8,128)} %bitcast.21), channel_id=1, source_target_pairs={{0,32},{32,64},{64,96},{96,128},{128,160},{160,192},{192,224},{224... | collective-permute-start | bytes 36872 | tf_op jit(solution)/shard_map/ppermute | solution.py:22
  4.8 12.1 %collective-permute-start.2 = (f32[3,8,128]{2,1,0:T(8,128)}, f32[3,8,128]{2,1,0:T(8,128)S(1)}, u32[]{:S(2)}, u32[]{:S(2)}) collective-permute-start(f32[3,8,128]{2,1,0:T(8,128)} %bitcast.22), channel_id=1, source_target_pairs={{0,1},{1,2},{2,3},{3,4},{4,5},{5,6},{6,7},{7,8},{8,9},{9,10},{10,1... | collective-permute-start | bytes 36872 | tf_op jit(solution)/shard_map/ppermute | solution.py:22
  7.2 9.7 %collective-permute-start.1 = (f32[3,8,128]{2,1,0:T(8,128)}, f32[3,8,128]{2,1,0:T(8,128)S(1)}, u32[]{:S(2)}, u32[]{:S(2)}) collective-permute-start(f32[3,8,128]{2,1,0:T(8,128)} %bitcast.23), channel_id=1, source_target_pairs={{0,480},{32,0},{64,32},{96,64},{128,96},{160,128},{192,160},{224,1... | collective-permute-start | bytes 36872 | tf_op jit(solution)/shard_map/ppermute | solution.py:22
  12.7 5.2 %collective-permute-start = (f32[3,8,128]{2,1,0:T(8,128)}, f32[3,8,128]{2,1,0:T(8,128)S(1)}, u32[]{:S(2)}, u32[]{:S(2)}) collective-permute-start(f32[3,8,128]{2,1,0:T(8,128)} %bitcast.24), channel_id=1, source_target_pairs={{0,31},{1,0},{2,1},{3,2},{4,3},{5,4},{6,5},{7,6},{8,7},{9,8},{10,9... | collective-permute-start | bytes 36872 | tf_op jit(solution)/shard_map/ppermute | solution.py:22
  18.0 57.0 %copy-start.4 = (s32[1,1,2,64]{3,2,1,0:T(2,128)S(1)}, s32[1,1,2,64]{3,2,1,0:T(2,128)}, u32[]{:S(2)}) copy-start(s32[1,1,2,64]{3,2,1,0:T(2,128)} %param.10) | copy-start | bytes 1540
  18.0 57.0 %copy-start.5 = (s32[1,1,2]{2,1,0:T(1,128)S(1)}, s32[1,1,2]{2,1,0:T(1,128)}, u32[]{:S(2)}) copy-start(s32[1,1,2]{2,1,0:T(1,128)} %param.11) | copy-start | bytes 28
  20.1 12.9 %collective-permute-start.4 = (f32[3,8,128]{2,1,0:T(8,128)S(1)}, f32[3,8,128]{2,1,0:T(8,128)S(1)}, u32[]{:S(2)}, u32[]{:S(2)}) collective-permute-start(f32[3,8,128]{2,1,0:T(8,128)S(1)} %get-tuple-element.34), channel_id=1, source_target_pairs={{0,32},{32,64},{64,96},{96,128},{128,160},{160,192},{192,224},{224... | collective-permute-start | bytes 36872 | tf_op jit(solution)/shard_map/ppermute | solution.py:22
  22.0 11.0 %collective-permute-start.5 = (f32[3,8,128]{2,1,0:T(8,128)S(1)}, f32[3,8,128]{2,1,0:T(8,128)S(1)}, u32[]{:S(2)}, u32[]{:S(2)}) collective-permute-start(f32[3,8,128]{2,1,0:T(8,128)S(1)} %get-tuple-element.35), channel_id=1, source_target_pairs={{0,1},{1,2},{2,3},{3,4},{4,5},{5,6},{6,7},{7,8},{8,9},{9,10},{10,1... | collective-permute-start | bytes 36872 | tf_op jit(solution)/shard_map/ppermute | solution.py:22
  22.0 11.0 %collective-permute-start.6 = (f32[3,8,128]{2,1,0:T(8,128)S(1)}, f32[3,8,128]{2,1,0:T(8,128)S(1)}, u32[]{:S(2)}, u32[]{:S(2)}) collective-permute-start(f32[3,8,128]{2,1,0:T(8,128)S(1)} %get-tuple-element.36), channel_id=1, source_target_pairs={{0,480},{32,0},{64,32},{96,64},{128,96},{160,128},{192,160},{224,1... | collective-permute-start | bytes 36872 | tf_op jit(solution)/shard_map/ppermute | solution.py:22
  28.7 5.1 %collective-permute-start.7 = (f32[3,8,128]{2,1,0:T(8,128)S(1)}, f32[3,8,128]{2,1,0:T(8,128)S(1)}, u32[]{:S(2)}, u32[]{:S(2)}) collective-permute-start(f32[3,8,128]{2,1,0:T(8,128)S(1)} %get-tuple-element.37), channel_id=1, source_target_pairs={{0,31},{1,0},{2,1},{3,2},{4,3},{5,4},{6,5},{7,6},{8,7},{9,8},{10,9... | collective-permute-start | bytes 36872 | tf_op jit(solution)/shard_map/ppermute | solution.py:22
  33.9 12.4 %collective-permute-start.11 = (f32[3,8,128]{2,1,0:T(8,128)S(1)}, f32[3,8,128]{2,1,0:T(8,128)S(1)}, u32[]{:S(2)}, u32[]{:S(2)}) collective-permute-start(f32[3,8,128]{2,1,0:T(8,128)S(1)} %select_add_fusion.2.own.k1), channel_id=1, source_target_pairs={{0,32},{32,64},{64,96},{96,128},{128,160},{160,192},{192,224},{224... | collective-permute-start | bytes 36872 | tf_op jit(solution)/shard_map/ppermute | solution.py:22
  35.8 10.5 %collective-permute-start.10 = (f32[3,8,128]{2,1,0:T(8,128)S(1)}, f32[3,8,128]{2,1,0:T(8,128)S(1)}, u32[]{:S(2)}, u32[]{:S(2)}) collective-permute-start(f32[3,8,128]{2,1,0:T(8,128)S(1)} %select_add_fusion.2.own.k1), channel_id=1, source_target_pairs={{0,1},{1,2},{2,3},{3,4},{4,5},{5,6},{6,7},{7,8},{8,9},{9,10},{10,1... | collective-permute-start | bytes 36872 | tf_op jit(solution)/shard_map/ppermute | solution.py:22
  35.8 10.5 %collective-permute-start.9 = (f32[3,8,128]{2,1,0:T(8,128)S(1)}, f32[3,8,128]{2,1,0:T(8,128)S(1)}, u32[]{:S(2)}, u32[]{:S(2)}) collective-permute-start(f32[3,8,128]{2,1,0:T(8,128)S(1)} %select_add_fusion.2.own.k1), channel_id=1, source_target_pairs={{0,480},{32,0},{64,32},{96,64},{128,96},{160,128},{192,160},{224,1... | collective-permute-start | bytes 36872 | tf_op jit(solution)/shard_map/ppermute | solution.py:22
  42.5 4.6 %collective-permute-start.8 = (f32[3,8,128]{2,1,0:T(8,128)S(1)}, f32[3,8,128]{2,1,0:T(8,128)S(1)}, u32[]{:S(2)}, u32[]{:S(2)}) collective-permute-start(f32[3,8,128]{2,1,0:T(8,128)S(1)} %select_add_fusion.2.own.k1), channel_id=1, source_target_pairs={{0,31},{1,0},{2,1},{3,2},{4,3},{5,4},{6,5},{7,6},{8,7},{9,8},{10,9... | collective-permute-start | bytes 36872 | tf_op jit(solution)/shard_map/ppermute | solution.py:22
  49.2 12.5 %collective-permute-start.12 = (f32[3,8,128]{2,1,0:T(8,128)S(1)}, f32[3,8,128]{2,1,0:T(8,128)S(1)}, u32[]{:S(2)}, u32[]{:S(2)}) collective-permute-start(f32[3,8,128]{2,1,0:T(8,128)S(1)} %get-tuple-element.40), channel_id=1, source_target_pairs={{0,32},{32,64},{64,96},{96,128},{128,160},{160,192},{192,224},{224... | collective-permute-start | bytes 36872 | tf_op jit(solution)/shard_map/ppermute | solution.py:22
  51.1 10.6 %collective-permute-start.13 = (f32[3,8,128]{2,1,0:T(8,128)S(1)}, f32[3,8,128]{2,1,0:T(8,128)S(1)}, u32[]{:S(2)}, u32[]{:S(2)}) collective-permute-start(f32[3,8,128]{2,1,0:T(8,128)S(1)} %get-tuple-element.41), channel_id=1, source_target_pairs={{0,1},{1,2},{2,3},{3,4},{4,5},{5,6},{6,7},{7,8},{8,9},{9,10},{10,1... | collective-permute-start | bytes 36872 | tf_op jit(solution)/shard_map/ppermute | solution.py:22
  51.2 10.6 %collective-permute-start.14 = (f32[3,8,128]{2,1,0:T(8,128)S(1)}, f32[3,8,128]{2,1,0:T(8,128)S(1)}, u32[]{:S(2)}, u32[]{:S(2)}) collective-permute-start(f32[3,8,128]{2,1,0:T(8,128)S(1)} %get-tuple-element.42), channel_id=1, source_target_pairs={{0,480},{32,0},{64,32},{96,64},{128,96},{160,128},{192,160},{224,1... | collective-permute-start | bytes 36872 | tf_op jit(solution)/shard_map/ppermute | solution.py:22
  57.8 4.6 %collective-permute-start.15 = (f32[3,8,128]{2,1,0:T(8,128)S(1)}, f32[3,8,128]{2,1,0:T(8,128)S(1)}, u32[]{:S(2)}, u32[]{:S(2)}) collective-permute-start(f32[3,8,128]{2,1,0:T(8,128)S(1)} %get-tuple-element.43), channel_id=1, source_target_pairs={{0,31},{1,0},{2,1},{3,2},{4,3},{5,4},{6,5},{7,6},{8,7},{9,8},{10,9... | collective-permute-start | bytes 36872 | tf_op jit(solution)/shard_map/ppermute | solution.py:22
  62.5 12.6 %collective-permute-start.19 = (f32[3,8,128]{2,1,0:T(8,128)S(1)}, f32[3,8,128]{2,1,0:T(8,128)S(1)}, u32[]{:S(2)}, u32[]{:S(2)}) collective-permute-start(f32[3,8,128]{2,1,0:T(8,128)S(1)} %select_add_fusion.1.own.k2), channel_id=1, source_target_pairs={{0,32},{32,64},{64,96},{96,128},{128,160},{160,192},{192,224},{224... | collective-permute-start | bytes 36872 | tf_op jit(solution)/shard_map/ppermute | solution.py:22
  64.4 10.7 %collective-permute-start.18 = (f32[3,8,128]{2,1,0:T(8,128)S(1)}, f32[3,8,128]{2,1,0:T(8,128)S(1)}, u32[]{:S(2)}, u32[]{:S(2)}) collective-permute-start(f32[3,8,128]{2,1,0:T(8,128)S(1)} %select_add_fusion.1.own.k2), channel_id=1, source_target_pairs={{0,1},{1,2},{2,3},{3,4},{4,5},{5,6},{6,7},{7,8},{8,9},{9,10},{10,1... | collective-permute-start | bytes 36872 | tf_op jit(solution)/shard_map/ppermute | solution.py:22
  64.4 10.7 %collective-permute-start.17 = (f32[3,8,128]{2,1,0:T(8,128)S(1)}, f32[3,8,128]{2,1,0:T(8,128)S(1)}, u32[]{:S(2)}, u32[]{:S(2)}) collective-permute-start(f32[3,8,128]{2,1,0:T(8,128)S(1)} %select_add_fusion.1.own.k2), channel_id=1, source_target_pairs={{0,480},{32,0},{64,32},{96,64},{128,96},{160,128},{192,160},{224,1... | collective-permute-start | bytes 36872 | tf_op jit(solution)/shard_map/ppermute | solution.py:22
  71.1 4.6 %collective-permute-start.16 = (f32[3,8,128]{2,1,0:T(8,128)S(1)}, f32[3,8,128]{2,1,0:T(8,128)S(1)}, u32[]{:S(2)}, u32[]{:S(2)}) collective-permute-start(f32[3,8,128]{2,1,0:T(8,128)S(1)} %select_add_fusion.1.own.k2), channel_id=1, source_target_pairs={{0,31},{1,0},{2,1},{3,2},{4,3},{5,4},{6,5},{7,6},{8,7},{9,8},{10,9... | collective-permute-start | bytes 36872 | tf_op jit(solution)/shard_map/ppermute | solution.py:22
  78.3 15.2 %all-to-all-start = ((f32[32,8,128]{2,1,0:T(8,128)}), f32[32,8,128]{2,1,0:T(8,128)S(1)}, u32[]{:S(2)}, u32[]{:S(2)}) async-start(f32[32,8,128]{2,1,0:T(8,128)} %get-tuple-element.48), calls=%async_computation | async-start | bytes 262144 | tf_op jit(solution)/shard_map/all_to_all | solution.py:275
  85.8 7.7 %collective-permute-start.20 = (f32[4,8,128]{2,1,0:T(8,128)S(1)}, f32[4,8,128]{2,1,0:T(8,128)S(1)}, u32[]{:S(2)}, u32[]{:S(2)}) collective-permute-start(f32[4,8,128]{2,1,0:T(8,128)S(1)} %get-tuple-element.52), channel_id=1, source_target_pairs={{0,1},{1,2},{2,3},{3,4},{4,5},{5,6},{6,7},{7,8},{8,9},{9,10},{10,1... | collective-permute-start | bytes 49160 | tf_op jit(solution)/shard_map/ppermute | solution.py:22
  85.9 7.6 %collective-permute-start.21 = (f32[4,8,128]{2,1,0:T(8,128)S(1)}, f32[4,8,128]{2,1,0:T(8,128)S(1)}, u32[]{:S(2)}, u32[]{:S(2)}) collective-permute-start(f32[4,8,128]{2,1,0:T(8,128)S(1)} %get-tuple-element.53), channel_id=1, source_target_pairs={{0,31},{1,0},{2,1},{3,2},{4,3},{5,4},{6,5},{7,6},{8,7},{9,8},{10,9... | collective-permute-start | bytes 49160 | tf_op jit(solution)/shard_map/ppermute | solution.py:22
  94.2 21.0 %all-to-all-start.1 = ((f32[16,8,128]{2,1,0:T(8,128)}), f32[16,8,128]{2,1,0:T(8,128)S(1)}, u32[]{:S(2)}, u32[]{:S(2)}) async-start(f32[16,8,128]{2,1,0:T(8,128)} %broadcast_in_dim.32), calls=%async_computation.1 | async-start | bytes 131072 | tf_op jit(solution)/shard_map/all_to_all | solution.py:275
  103.6 8.6 %collective-permute-start.22 = (f32[3,8,128]{2,1,0:T(8,128)S(1)}, f32[3,8,128]{2,1,0:T(8,128)S(1)}, u32[]{:S(2)}, u32[]{:S(2)}) collective-permute-start(f32[3,8,128]{2,1,0:T(8,128)S(1)} %get-tuple-element.56), channel_id=1, source_target_pairs={{0,32},{32,64},{64,96},{96,128},{128,160},{160,192},{192,224},{224... | collective-permute-start | bytes 36872 | tf_op jit(solution)/shard_map/ppermute | solution.py:22
  105.9 7.1 %collective-permute-start.23 = (f32[3,8,128]{2,1,0:T(8,128)S(1)}, f32[3,8,128]{2,1,0:T(8,128)S(1)}, u32[]{:S(2)}, u32[]{:S(2)}) collective-permute-start(f32[3,8,128]{2,1,0:T(8,128)S(1)} %get-tuple-element.58), channel_id=1, source_target_pairs={{0,480},{32,0},{64,32},{96,64},{128,96},{160,128},{192,160},{224,1... | collective-permute-start | bytes 36872 | tf_op jit(solution)/shard_map/ppermute | solution.py:22

commit v10 on v9

--- a/solution.py
+++ b/solution.py
@@ -113,7 +113,7 @@
     across = jax.ShapeDtypeStruct((4 if sweep == ITERS - 1 else 3, blocks, width), jnp.float32)
     plane = (SUB, width) if copies is None else (copies, SUB, width)
     plane = jax.ShapeDtypeStruct(plane, jnp.float32)
-    rows = 8 * blocks * SUB
+    rows = (8 * blocks + 1) * SUB
     scratch = [pltpu.VMEM((rows, width), jnp.float32), pltpu.VMEM((rows, width), jnp.float32)]
     return pl.pallas_call(
         functools.partial(operator_kernel, sweep),

time: 117 us -> 117 us (level)
  no operation moved by 1% of the time
where the time goes in v10:
time: 117 us; the launch traced here: 116 us
  starting transfers between devices  92.4 us (79%)
  waiting for transfers between devices  14.2 us (12%)
  Pallas kernels  7.55 us (6%)
    ppermute x24, starting transfers between devices, ring_shift(): return lax.ppermute(shard, axis, ring(lax.axis_size(axis), by))  75.5 us
    all_to_all x2, starting transfers between devices, spread_sum(): lax.all_to_all(part, ('axial', 'cross'), 0, 0, axis_index_groups=groups)  17 us
    all_to_all x2, waiting for transfers between devices, spread_sum(): lax.all_to_all(part, ('axial', 'cross'), 0, 0, axis_index_groups=groups)  9.26 us
    pallas_call x3, Pallas kernels, operator_call(): pl.pallas_call(functools.partial(operator_kernel, sweep), in_specs=[pl.Bl...  6.67 us
    ppermute x24, waiting for transfers between devices, ring_shift(): return lax.ppermute(shard, axis, ring(lax.axis_size(axis), by))  4.91 us
  transfers between devices with their start and end apart: 26, of which 8 were waited for; matrix products, arithmetic and copies ran while one was open for 0% of the time, Pallas kernels for 0%

profile of v10, /device:TPU:1, one launch (start us, length us, event | category | flops | bytes accessed | tf_op | source)
XLA Modules:
  0.0 116.0 jit_solution(11891005208534516987)
XLA Ops:
  0.6 0.0 copy-start
  0.7 4.1 %collective-permute-start.3 = (f32[3,8,128]{2,1,0:T(8,128)}, f32[3,8,128]{2,1,0:T(8,128)S(1)}, u32[]{:S(2)}, u32[]{:S(2)}) collective-permute-start(f32[3,8,128]{2,1,0:T(8,128)} %bitcast.21), channel_id=1, source_target_pairs={{0,32},{32,64},{64,96},{96,128},{128,160},{160,192},{192,224},{224... | collective-permute-start | bytes 36872 | tf_op jit(solution)/shard_map/ppermute | solution.py:22
  4.8 2.5 %collective-permute-start.2 = (f32[3,8,128]{2,1,0:T(8,128)}, f32[3,8,128]{2,1,0:T(8,128)S(1)}, u32[]{:S(2)}, u32[]{:S(2)}) collective-permute-start(f32[3,8,128]{2,1,0:T(8,128)} %bitcast.22), channel_id=1, source_target_pairs={{0,1},{1,2},{2,3},{3,4},{4,5},{5,6},{6,7},{7,8},{8,9},{9,10},{10,1... | collective-permute-start | bytes 36872 | tf_op jit(solution)/shard_map/ppermute | solution.py:22
  7.2 5.5 %collective-permute-start.1 = (f32[3,8,128]{2,1,0:T(8,128)}, f32[3,8,128]{2,1,0:T(8,128)S(1)}, u32[]{:S(2)}, u32[]{:S(2)}) collective-permute-start(f32[3,8,128]{2,1,0:T(8,128)} %bitcast.23), channel_id=1, source_target_pairs={{0,480},{32,0},{64,32},{96,64},{128,96},{160,128},{192,160},{224,1... | collective-permute-start | bytes 36872 | tf_op jit(solution)/shard_map/ppermute | solution.py:22
  12.7 4.2 %collective-permute-start = (f32[3,8,128]{2,1,0:T(8,128)}, f32[3,8,128]{2,1,0:T(8,128)S(1)}, u32[]{:S(2)}, u32[]{:S(2)}) collective-permute-start(f32[3,8,128]{2,1,0:T(8,128)} %bitcast.24), channel_id=1, source_target_pairs={{0,31},{1,0},{2,1},{3,2},{4,3},{5,4},{6,5},{7,6},{8,7},{9,8},{10,9... | collective-permute-start | bytes 36872 | tf_op jit(solution)/shard_map/ppermute | solution.py:22
  16.9 0.0 collective-permute-done.3.from_axial_dn
  16.9 0.0 collective-permute-done.2.from_cross_dn.d0
  16.9 0.0 collective-permute-done.1.from_axial_up
  16.9 1.0 collective-permute-done.from_cross_up.u0
  17.9 0.0 copy-done.3
  18.0 0.0 copy-start.4
  18.0 0.0 copy-start.5
  18.0 2.1 %shard_map.86 = (f32[3,8,128]{2,1,0:T(8,128)S(1)}, f32[3,8,128]{2,1,0:T(8,128)S(1)}, f32[3,8,128]{2,1,0:T(8,128)S(1)}, f32[3,8,128]{2,1,0:T(8,128)S(1)}, f32[3,8,128]{2,1,0:T(8,128)S(1)}, /*index=5*/f32[8,128]{1,0:T(8,128)S(1)}) custom-call(s32[8,8]{1,0:T(8,128)S(1)} %bitcast.27, f32[3,8,128]{2,1,0:T(8,128)S(1)} %bitcast.25, ...), custom_call_target="tpu_custom_call" | custom-call | tf_op jit(solution)/shard_map/pallas_call | solution.py:118
  20.1 1.9 %collective-permute-start.4 = (f32[3,8,128]{2,1,0:T(8,128)S(1)}, f32[3,8,128]{2,1,0:T(8,128)S(1)}, u32[]{:S(2)}, u32[]{:S(2)}) collective-permute-start(f32[3,8,128]{2,1,0:T(8,128)S(1)} %get-tuple-element.34), channel_id=1, source_target_pairs={{0,32},{32,64},{64,96},{96,128},{128,160},{160,192},{192,224},{224... | collective-permute-start | bytes 36872 | tf_op jit(solution)/shard_map/ppermute | solution.py:22
  22.0 0.0 collective-permute-start.5
  22.0 6.7 %collective-permute-start.6 = (f32[3,8,128]{2,1,0:T(8,128)S(1)}, f32[3,8,128]{2,1,0:T(8,128)S(1)}, u32[]{:S(2)}, u32[]{:S(2)}) collective-permute-start(f32[3,8,128]{2,1,0:T(8,128)S(1)} %get-tuple-element.36), channel_id=1, source_target_pairs={{0,480},{32,0},{64,32},{96,64},{128,96},{160,128},{192,160},{224,1... | collective-permute-start | bytes 36872 | tf_op jit(solution)/shard_map/ppermute | solution.py:22
  28.7 4.3 %collective-permute-start.7 = (f32[3,8,128]{2,1,0:T(8,128)S(1)}, f32[3,8,128]{2,1,0:T(8,128)S(1)}, u32[]{:S(2)}, u32[]{:S(2)}) collective-permute-start(f32[3,8,128]{2,1,0:T(8,128)S(1)} %get-tuple-element.37), channel_id=1, source_target_pairs={{0,31},{1,0},{2,1},{3,2},{4,3},{5,4},{6,5},{7,6},{8,7},{9,8},{10,9... | collective-permute-start | bytes 36872 | tf_op jit(solution)/shard_map/ppermute | solution.py:22
  33.0 0.0 collective-permute-done.4
  33.0 0.0 collective-permute-done.5
  33.0 0.0 collective-permute-done.6
  33.0 0.8 collective-permute-done.7
  33.9 1.9 %collective-permute-start.11 = (f32[3,8,128]{2,1,0:T(8,128)S(1)}, f32[3,8,128]{2,1,0:T(8,128)S(1)}, u32[]{:S(2)}, u32[]{:S(2)}) collective-permute-start(f32[3,8,128]{2,1,0:T(8,128)S(1)} %select_add_fusion.2.own.k1), channel_id=1, source_target_pairs={{0,32},{32,64},{64,96},{96,128},{128,160},{160,192},{192,224},{224... | collective-permute-start | bytes 36872 | tf_op jit(solution)/shard_map/ppermute | solution.py:22
  35.8 0.0 collective-permute-start.10
  35.8 6.7 %collective-permute-start.9 = (f32[3,8,128]{2,1,0:T(8,128)S(1)}, f32[3,8,128]{2,1,0:T(8,128)S(1)}, u32[]{:S(2)}, u32[]{:S(2)}) collective-permute-start(f32[3,8,128]{2,1,0:T(8,128)S(1)} %select_add_fusion.2.own.k1), channel_id=1, source_target_pairs={{0,480},{32,0},{64,32},{96,64},{128,96},{160,128},{192,160},{224,1... | collective-permute-start | bytes 36872 | tf_op jit(solution)/shard_map/ppermute | solution.py:22
  42.5 3.8 %collective-permute-start.8 = (f32[3,8,128]{2,1,0:T(8,128)S(1)}, f32[3,8,128]{2,1,0:T(8,128)S(1)}, u32[]{:S(2)}, u32[]{:S(2)}) collective-permute-start(f32[3,8,128]{2,1,0:T(8,128)S(1)} %select_add_fusion.2.own.k1), channel_id=1, source_target_pairs={{0,31},{1,0},{2,1},{3,2},{4,3},{5,4},{6,5},{7,6},{8,7},{9,8},{10,9... | collective-permute-start | bytes 36872 | tf_op jit(solution)/shard_map/ppermute | solution.py:22
  46.3 0.0 collective-permute-done.11.from_axial_dn
  46.3 0.0 collective-permute-done.10.from_cross_dn.d1
  46.3 0.0 collective-permute-done.9.from_axial_up
  46.3 0.8 collective-permute-done.8.from_cross_up.u1
  47.1 2.1 %shard_map.87 = (f32[3,8,128]{2,1,0:T(8,128)S(1)}, f32[3,8,128]{2,1,0:T(8,128)S(1)}, f32[3,8,128]{2,1,0:T(8,128)S(1)}, f32[3,8,128]{2,1,0:T(8,128)S(1)}, f32[3,8,128]{2,1,0:T(8,128)S(1)}, /*index=5*/f32[8,128]{1,0:T(8,128)S(1)}) custom-call(s32[8,8]{1,0:T(8,128)S(1)} %bitcast.28, f32[3,8,128]{2,1,0:T(8,128)S(1)} %select_add_fusion.2.own.k1, ...), custom_call_target="tpu_custom_call" | custom-call | tf_op jit(solution)/shard_map/pallas_call | solution.py:118
  49.2 1.9 %collective-permute-start.12 = (f32[3,8,128]{2,1,0:T(8,128)S(1)}, f32[3,8,128]{2,1,0:T(8,128)S(1)}, u32[]{:S(2)}, u32[]{:S(2)}) collective-permute-start(f32[3,8,128]{2,1,0:T(8,128)S(1)} %get-tuple-element.40), channel_id=1, source_target_pairs={{0,32},{32,64},{64,96},{96,128},{128,160},{160,192},{192,224},{224... | collective-permute-start | bytes 36872 | tf_op jit(solution)/shard_map/ppermute | solution.py:22
  51.1 0.0 collective-permute-start.13
  51.2 6.7 %collective-permute-start.14 = (f32[3,8,128]{2,1,0:T(8,128)S(1)}, f32[3,8,128]{2,1,0:T(8,128)S(1)}, u32[]{:S(2)}, u32[]{:S(2)}) collective-permute-start(f32[3,8,128]{2,1,0:T(8,128)S(1)} %get-tuple-element.42), channel_id=1, source_target_pairs={{0,480},{32,0},{64,32},{96,64},{128,96},{160,128},{192,160},{224,1... | collective-permute-start | bytes 36872 | tf_op jit(solution)/shard_map/ppermute | solution.py:22
  57.9 3.8 %collective-permute-start.15 = (f32[3,8,128]{2,1,0:T(8,128)S(1)}, f32[3,8,128]{2,1,0:T(8,128)S(1)}, u32[]{:S(2)}, u32[]{:S(2)}) collective-permute-start(f32[3,8,128]{2,1,0:T(8,128)S(1)} %get-tuple-element.43), channel_id=1, source_target_pairs={{0,31},{1,0},{2,1},{3,2},{4,3},{5,4},{6,5},{7,6},{8,7},{9,8},{10,9... | collective-permute-start | bytes 36872 | tf_op jit(solution)/shard_map/ppermute | solution.py:22
  61.7 0.1 pad.4.clone
  61.7 0.0 collective-permute-done.12
  61.7 0.0 collective-permute-done.13
  61.7 0.0 collective-permute-done.14
  61.7 0.7 collective-permute-done.15
  62.5 1.9 %collective-permute-start.19 = (f32[3,8,128]{2,1,0:T(8,128)S(1)}, f32[3,8,128]{2,1,0:T(8,128)S(1)}, u32[]{:S(2)}, u32[]{:S(2)}) collective-permute-start(f32[3,8,128]{2,1,0:T(8,128)S(1)} %select_add_fusion.1.own.k2), channel_id=1, source_target_pairs={{0,32},{32,64},{64,96},{96,128},{128,160},{160,192},{192,224},{224... | collective-permute-start | bytes 36872 | tf_op jit(solution)/shard_map/ppermute | solution.py:22
  64.4 0.0 collective-permute-start.18
  64.4 6.7 %collective-permute-start.17 = (f32[3,8,128]{2,1,0:T(8,128)S(1)}, f32[3,8,128]{2,1,0:T(8,128)S(1)}, u32[]{:S(2)}, u32[]{:S(2)}) collective-permute-start(f32[3,8,128]{2,1,0:T(8,128)S(1)} %select_add_fusion.1.own.k2), channel_id=1, source_target_pairs={{0,480},{32,0},{64,32},{96,64},{128,96},{160,128},{192,160},{224,1... | collective-permute-start | bytes 36872 | tf_op jit(solution)/shard_map/ppermute | solution.py:22
  71.1 3.8 %collective-permute-start.16 = (f32[3,8,128]{2,1,0:T(8,128)S(1)}, f32[3,8,128]{2,1,0:T(8,128)S(1)}, u32[]{:S(2)}, u32[]{:S(2)}) collective-permute-start(f32[3,8,128]{2,1,0:T(8,128)S(1)} %select_add_fusion.1.own.k2), channel_id=1, source_target_pairs={{0,31},{1,0},{2,1},{3,2},{4,3},{5,4},{6,5},{7,6},{8,7},{9,8},{10,9... | collective-permute-start | bytes 36872 | tf_op jit(solution)/shard_map/ppermute | solution.py:22
  74.9 0.1 fusion.2
  75.0 0.1 fusion.rest_1_
  75.1 0.0 collective-permute-done.19.from_axial_dn
  75.1 0.0 collective-permute-done.18.from_cross_dn.d2
  75.1 0.0 collective-permute-done.17.from_axial_up
  75.1 0.7 collective-permute-done.16.from_cross_up.u2
  75.8 2.5 %shard_map.88 = (f32[3,8,128]{2,1,0:T(8,128)S(1)}, f32[4,8,128]{2,1,0:T(8,128)S(1)}, f32[4,8,128]{2,1,0:T(8,128)S(1)}, f32[3,8,128]{2,1,0:T(8,128)S(1)}, f32[3,8...) custom-call(s32[8,8]{1,0:T(8,128)S(1)} %bitcast.29, f32[3,8,128]{2,1,0:T(8,128)S(1)} %select_add_fusion.1.own.k2, ...), custom_call_target="tpu_custom_call" | custom-call | tf_op jit(solution)/shard_map/pallas_call | solution.py:118
  78.3 7.6 %all-to-all-start = ((f32[32,8,128]{2,1,0:T(8,128)}), f32[32,8,128]{2,1,0:T(8,128)S(1)}, u32[]{:S(2)}, u32[]{:S(2)}) async-start(f32[32,8,128]{2,1,0:T(8,128)} %get-tuple-element.48), calls=%async_computation | async-start | bytes 262144 | tf_op jit(solution)/shard_map/all_to_all | solution.py:275
  85.9 0.0 collective-permute-start.20
  85.9 0.5 collective-permute-start.21
  86.4 7.1 %all-to-all-done = f32[32,8,128]{2,1,0:T(8,128)S(1)} async-done(((f32[32,8,128]{2,1,0:T(8,128)}), f32[32,8,128]{2,1,0:T(8,128)S(1)}, u32[]{:S(2)}, u32[]{:S(2)}) %all-to-all-start) | async-done | bytes 131104 | tf_op jit(solution)/shard_map/all_to_all | solution.py:275
  93.5 0.0 collective-permute-done.20.dn_plane
  93.5 0.0 collective-permute-done.21.up_plane
  93.5 0.6 broadcast_in_dim.32
  94.2 9.4 %all-to-all-start.1 = ((f32[16,8,128]{2,1,0:T(8,128)}), f32[16,8,128]{2,1,0:T(8,128)S(1)}, u32[]{:S(2)}, u32[]{:S(2)}) async-start(f32[16,8,128]{2,1,0:T(8,128)} %broadcast_in_dim.32), calls=%async_computation.1 | async-start | bytes 131072 | tf_op jit(solution)/shard_map/all_to_all | solution.py:275
  103.6 2.3 %collective-permute-start.22 = (f32[3,8,128]{2,1,0:T(8,128)S(1)}, f32[3,8,128]{2,1,0:T(8,128)S(1)}, u32[]{:S(2)}, u32[]{:S(2)}) collective-permute-start(f32[3,8,128]{2,1,0:T(8,128)S(1)} %get-tuple-element.56), channel_id=1, source_target_pairs={{0,32},{32,64},{64,96},{96,128},{128,160},{160,192},{192,224},{224... | collective-permute-start | bytes 36872 | tf_op jit(solution)/shard_map/ppermute | solution.py:22
  105.9 6.3 %collective-permute-start.23 = (f32[3,8,128]{2,1,0:T(8,128)S(1)}, f32[3,8,128]{2,1,0:T(8,128)S(1)}, u32[]{:S(2)}, u32[]{:S(2)}) collective-permute-start(f32[3,8,128]{2,1,0:T(8,128)S(1)} %get-tuple-element.58), channel_id=1, source_target_pairs={{0,480},{32,0},{64,32},{96,64},{128,96},{160,128},{192,160},{224,1... | collective-permute-start | bytes 36872 | tf_op jit(solution)/shard_map/ppermute | solution.py:22
  112.2 0.0 collective-permute-done.22
  112.2 0.8 collective-permute-done.23
  113.0 2.2 %all-to-all-done.1.sums = f32[16,8,128]{2,1,0:T(8,128)S(1)} async-done(((f32[16,8,128]{2,1,0:T(8,128)}), f32[16,8,128]{2,1,0:T(8,128)S(1)}, u32[]{:S(2)}, u32[]{:S(2)}) %all-to-all-start.1) | async-done | bytes 65568 | tf_op jit(solution)/shard_map/all_to_all | solution.py:275
  115.2 0.9 shard_map.89
  (15 shorter events, 0.1 us)
Async XLA Ops:
  0.6 17.3 %copy-start = (bf16[1,1,8,8,128,128]{5,4,3,2,1,0:T(8,128)(2,1)S(1)}, bf16[1,1,8,8,128,128]{5,4,3,2,1,0:T(8,128)(2,1)}, u32[]{:S(2)}) copy-start(bf16[1,1,8,8,128,128]{5,4,3,2,1,0:T(8,128)(2,1)} %param.8) | copy-start | bytes 6291460
  0.6 17.3 %copy-start.1 = (f32[1,1,8,3,128]{4,2,3,1,0:T(8,128)S(1)}, f32[1,1,8,3,128]{4,2,3,1,0:T(8,128)}, u32[]{:S(2)}) copy-start(f32[1,1,8,3,128]{4,2,3,1,0:T(8,128)} %param.6) | copy-start | bytes 36868
  0.7 17.3 %copy-start.2 = (s32[1,1,8,8]{3,2,1,0:T(8,128)S(1)}, s32[1,1,8,8]{3,2,1,0:T(8,128)}, u32[]{:S(2)}) copy-start(s32[1,1,8,8]{3,2,1,0:T(8,128)} %param.9) | copy-start | bytes 772
  0.7 17.3 %copy-start.3 = (f32[1,1,8,128]{3,2,1,0:T(8,128)S(1)}, f32[1,1,8,128]{3,2,1,0:T(8,128)}, u32[]{:S(2)}) copy-start(f32[1,1,8,128]{3,2,1,0:T(8,128)} %param.7) | copy-start | bytes 12292
  0.7 16.2 %collective-permute-start.3 = (f32[3,8,128]{2,1,0:T(8,128)}, f32[3,8,128]{2,1,0:T(8,128)S(1)}, u32[]{:S(2)}, u32[]{:S(2)}) collective-permute-start(f32[3,8,128]{2,1,0:T(8,128)} %bitcast.21), channel_id=1, source_target_pairs={{0,32},{32,64},{64,96},{96,128},{128,160},{160,192},{192,224},{224... | collective-permute-start | bytes 36872 | tf_op jit(solution)/shard_map/ppermute | solution.py:22
  4.8 12.1 %collective-permute-start.2 = (f32[3,8,128]{2,1,0:T(8,128)}, f32[3,8,128]{2,1,0:T(8,128)S(1)}, u32[]{:S(2)}, u32[]{:S(2)}) collective-permute-start(f32[3,8,128]{2,1,0:T(8,128)} %bitcast.22), channel_id=1, source_target_pairs={{0,1},{1,2},{2,3},{3,4},{4,5},{5,6},{6,7},{7,8},{8,9},{9,10},{10,1... | collective-permute-start | bytes 36872 | tf_op jit(solution)/shard_map/ppermute | solution.py:22
  7.2 9.7 %collective-permute-start.1 = (f32[3,8,128]{2,1,0:T(8,128)}, f32[3,8,128]{2,1,0:T(8,128)S(1)}, u32[]{:S(2)}, u32[]{:S(2)}) collective-permute-start(f32[3,8,128]{2,1,0:T(8,128)} %bitcast.23), channel_id=1, source_target_pairs={{0,480},{32,0},{64,32},{96,64},{128,96},{160,128},{192,160},{224,1... | collective-permute-start | bytes 36872 | tf_op jit(solution)/shard_map/ppermute | solution.py:22
  12.7 5.2 %collective-permute-start = (f32[3,8,128]{2,1,0:T(8,128)}, f32[3,8,128]{2,1,0:T(8,128)S(1)}, u32[]{:S(2)}, u32[]{:S(2)}) collective-permute-start(f32[3,8,128]{2,1,0:T(8,128)} %bitcast.24), channel_id=1, source_target_pairs={{0,31},{1,0},{2,1},{3,2},{4,3},{5,4},{6,5},{7,6},{8,7},{9,8},{10,9... | collective-permute-start | bytes 36872 | tf_op jit(solution)/shard_map/ppermute | solution.py:22
  18.0 57.0 %copy-start.4 = (s32[1,1,2,64]{3,2,1,0:T(2,128)S(1)}, s32[1,1,2,64]{3,2,1,0:T(2,128)}, u32[]{:S(2)}) copy-start(s32[1,1,2,64]{3,2,1,0:T(2,128)} %param.10) | copy-start | bytes 1540
  18.0 57.0 %copy-start.5 = (s32[1,1,2]{2,1,0:T(1,128)S(1)}, s32[1,1,2]{2,1,0:T(1,128)}, u32[]{:S(2)}) copy-start(s32[1,1,2]{2,1,0:T(1,128)} %param.11) | copy-start | bytes 28
  20.1 12.9 %collective-permute-start.4 = (f32[3,8,128]{2,1,0:T(8,128)S(1)}, f32[3,8,128]{2,1,0:T(8,128)S(1)}, u32[]{:S(2)}, u32[]{:S(2)}) collective-permute-start(f32[3,8,128]{2,1,0:T(8,128)S(1)} %get-tuple-element.34), channel_id=1, source_target_pairs={{0,32},{32,64},{64,96},{96,128},{128,160},{160,192},{192,224},{224... | collective-permute-start | bytes 36872 | tf_op jit(solution)/shard_map/ppermute | solution.py:22
  22.0 11.0 %collective-permute-start.5 = (f32[3,8,128]{2,1,0:T(8,128)S(1)}, f32[3,8,128]{2,1,0:T(8,128)S(1)}, u32[]{:S(2)}, u32[]{:S(2)}) collective-permute-start(f32[3,8,128]{2,1,0:T(8,128)S(1)} %get-tuple-element.35), channel_id=1, source_target_pairs={{0,1},{1,2},{2,3},{3,4},{4,5},{5,6},{6,7},{7,8},{8,9},{9,10},{10,1... | collective-permute-start | bytes 36872 | tf_op jit(solution)/shard_map/ppermute | solution.py:22
  22.0 11.0 %collective-permute-start.6 = (f32[3,8,128]{2,1,0:T(8,128)S(1)}, f32[3,8,128]{2,1,0:T(8,128)S(1)}, u32[]{:S(2)}, u32[]{:S(2)}) collective-permute-start(f32[3,8,128]{2,1,0:T(8,128)S(1)} %get-tuple-element.36), channel_id=1, source_target_pairs={{0,480},{32,0},{64,32},{96,64},{128,96},{160,128},{192,160},{224,1... | collective-permute-start | bytes 36872 | tf_op jit(solution)/shard_map/ppermute | solution.py:22
  28.7 5.1 %collective-permute-start.7 = (f32[3,8,128]{2,1,0:T(8,128)S(1)}, f32[3,8,128]{2,1,0:T(8,128)S(1)}, u32[]{:S(2)}, u32[]{:S(2)}) collective-permute-start(f32[3,8,128]{2,1,0:T(8,128)S(1)} %get-tuple-element.37), channel_id=1, source_target_pairs={{0,31},{1,0},{2,1},{3,2},{4,3},{5,4},{6,5},{7,6},{8,7},{9,8},{10,9... | collective-permute-start | bytes 36872 | tf_op jit(solution)/shard_map/ppermute | solution.py:22
  33.9 12.4 %collective-permute-start.11 = (f32[3,8,128]{2,1,0:T(8,128)S(1)}, f32[3,8,128]{2,1,0:T(8,128)S(1)}, u32[]{:S(2)}, u32[]{:S(2)}) collective-permute-start(f32[3,8,128]{2,1,0:T(8,128)S(1)} %select_add_fusion.2.own.k1), channel_id=1, source_target_pairs={{0,32},{32,64},{64,96},{96,128},{128,160},{160,192},{192,224},{224... | collective-permute-start | bytes 36872 | tf_op jit(solution)/shard_map/ppermute | solution.py:22
  35.8 10.5 %collective-permute-start.10 = (f32[3,8,128]{2,1,0:T(8,128)S(1)}, f32[3,8,128]{2,1,0:T(8,128)S(1)}, u32[]{:S(2)}, u32[]{:S(2)}) collective-permute-start(f32[3,8,128]{2,1,0:T(8,128)S(1)} %select_add_fusion.2.own.k1), channel_id=1, source_target_pairs={{0,1},{1,2},{2,3},{3,4},{4,5},{5,6},{6,7},{7,8},{8,9},{9,10},{10,1... | collective-permute-start | bytes 36872 | tf_op jit(solution)/shard_map/ppermute | solution.py:22
  35.8 10.5 %collective-permute-start.9 = (f32[3,8,128]{2,1,0:T(8,128)S(1)}, f32[3,8,128]{2,1,0:T(8,128)S(1)}, u32[]{:S(2)}, u32[]{:S(2)}) collective-permute-start(f32[3,8,128]{2,1,0:T(8,128)S(1)} %select_add_fusion.2.own.k1), channel_id=1, source_target_pairs={{0,480},{32,0},{64,32},{96,64},{128,96},{160,128},{192,160},{224,1... | collective-permute-start | bytes 36872 | tf_op jit(solution)/shard_map/ppermute | solution.py:22
  42.5 4.6 %collective-permute-start.8 = (f32[3,8,128]{2,1,0:T(8,128)S(1)}, f32[3,8,128]{2,1,0:T(8,128)S(1)}, u32[]{:S(2)}, u32[]{:S(2)}) collective-permute-start(f32[3,8,128]{2,1,0:T(8,128)S(1)} %select_add_fusion.2.own.k1), channel_id=1, source_target_pairs={{0,31},{1,0},{2,1},{3,2},{4,3},{5,4},{6,5},{7,6},{8,7},{9,8},{10,9... | collective-permute-start | bytes 36872 | tf_op jit(solution)/shard_map/ppermute | solution.py:22
  49.2 12.5 %collective-permute-start.12 = (f32[3,8,128]{2,1,0:T(8,128)S(1)}, f32[3,8,128]{2,1,0:T(8,128)S(1)}, u32[]{:S(2)}, u32[]{:S(2)}) collective-permute-start(f32[3,8,128]{2,1,0:T(8,128)S(1)} %get-tuple-element.40), channel_id=1, source_target_pairs={{0,32},{32,64},{64,96},{96,128},{128,160},{160,192},{192,224},{224... | collective-permute-start | bytes 36872 | tf_op jit(solution)/shard_map/ppermute | solution.py:22
  51.1 10.6 %collective-permute-start.13 = (f32[3,8,128]{2,1,0:T(8,128)S(1)}, f32[3,8,128]{2,1,0:T(8,128)S(1)}, u32[]{:S(2)}, u32[]{:S(2)}) collective-permute-start(f32[3,8,128]{2,1,0:T(8,128)S(1)} %get-tuple-element.41), channel_id=1, source_target_pairs={{0,1},{1,2},{2,3},{3,4},{4,5},{5,6},{6,7},{7,8},{8,9},{9,10},{10,1... | collective-permute-start | bytes 36872 | tf_op jit(solution)/shard_map/ppermute | solution.py:22
  51.2 10.6 %collective-permute-start.14 = (f32[3,8,128]{2,1,0:T(8,128)S(1)}, f32[3,8,128]{2,1,0:T(8,128)S(1)}, u32[]{:S(2)}, u32[]{:S(2)}) collective-permute-start(f32[3,8,128]{2,1,0:T(8,128)S(1)} %get-tuple-element.42), channel_id=1, source_target_pairs={{0,480},{32,0},{64,32},{96,64},{128,96},{160,128},{192,160},{224,1... | collective-permute-start | bytes 36872 | tf_op jit(solution)/shard_map/ppermute | solution.py:22
  57.9 4.6 %collective-permute-start.15 = (f32[3,8,128]{2,1,0:T(8,128)S(1)}, f32[3,8,128]{2,1,0:T(8,128)S(1)}, u32[]{:S(2)}, u32[]{:S(2)}) collective-permute-start(f32[3,8,128]{2,1,0:T(8,128)S(1)} %get-tuple-element.43), channel_id=1, source_target_pairs={{0,31},{1,0},{2,1},{3,2},{4,3},{5,4},{6,5},{7,6},{8,7},{9,8},{10,9... | collective-permute-start | bytes 36872 | tf_op jit(solution)/shard_map/ppermute | solution.py:22
  62.5 12.6 %collective-permute-start.19 = (f32[3,8,128]{2,1,0:T(8,128)S(1)}, f32[3,8,128]{2,1,0:T(8,128)S(1)}, u32[]{:S(2)}, u32[]{:S(2)}) collective-permute-start(f32[3,8,128]{2,1,0:T(8,128)S(1)} %select_add_fusion.1.own.k2), channel_id=1, source_target_pairs={{0,32},{32,64},{64,96},{96,128},{128,160},{160,192},{192,224},{224... | collective-permute-start | bytes 36872 | tf_op jit(solution)/shard_map/ppermute | solution.py:22
  64.4 10.7 %collective-permute-start.18 = (f32[3,8,128]{2,1,0:T(8,128)S(1)}, f32[3,8,128]{2,1,0:T(8,128)S(1)}, u32[]{:S(2)}, u32[]{:S(2)}) collective-permute-start(f32[3,8,128]{2,1,0:T(8,128)S(1)} %select_add_fusion.1.own.k2), channel_id=1, source_target_pairs={{0,1},{1,2},{2,3},{3,4},{4,5},{5,6},{6,7},{7,8},{8,9},{9,10},{10,1... | collective-permute-start | bytes 36872 | tf_op jit(solution)/shard_map/ppermute | solution.py:22
  64.4 10.7 %collective-permute-start.17 = (f32[3,8,128]{2,1,0:T(8,128)S(1)}, f32[3,8,128]{2,1,0:T(8,128)S(1)}, u32[]{:S(2)}, u32[]{:S(2)}) collective-permute-start(f32[3,8,128]{2,1,0:T(8,128)S(1)} %select_add_fusion.1.own.k2), channel_id=1, source_target_pairs={{0,480},{32,0},{64,32},{96,64},{128,96},{160,128},{192,160},{224,1... | collective-permute-start | bytes 36872 | tf_op jit(solution)/shard_map/ppermute | solution.py:22
  71.1 4.6 %collective-permute-start.16 = (f32[3,8,128]{2,1,0:T(8,128)S(1)}, f32[3,8,128]{2,1,0:T(8,128)S(1)}, u32[]{:S(2)}, u32[]{:S(2)}) collective-permute-start(f32[3,8,128]{2,1,0:T(8,128)S(1)} %select_add_fusion.1.own.k2), channel_id=1, source_target_pairs={{0,31},{1,0},{2,1},{3,2},{4,3},{5,4},{6,5},{7,6},{8,7},{9,8},{10,9... | collective-permute-start | bytes 36872 | tf_op jit(solution)/shard_map/ppermute | solution.py:22
  78.3 15.2 %all-to-all-start = ((f32[32,8,128]{2,1,0:T(8,128)}), f32[32,8,128]{2,1,0:T(8,128)S(1)}, u32[]{:S(2)}, u32[]{:S(2)}) async-start(f32[32,8,128]{2,1,0:T(8,128)} %get-tuple-element.48), calls=%async_computation | async-start | bytes 262144 | tf_op jit(solution)/shard_map/all_to_all | solution.py:275
  85.9 7.7 %collective-permute-start.20 = (f32[4,8,128]{2,1,0:T(8,128)S(1)}, f32[4,8,128]{2,1,0:T(8,128)S(1)}, u32[]{:S(2)}, u32[]{:S(2)}) collective-permute-start(f32[4,8,128]{2,1,0:T(8,128)S(1)} %get-tuple-element.52), channel_id=1, source_target_pairs={{0,1},{1,2},{2,3},{3,4},{4,5},{5,6},{6,7},{7,8},{8,9},{9,10},{10,1... | collective-permute-start | bytes 49160 | tf_op jit(solution)/shard_map/ppermute | solution.py:22
  85.9 7.6 %collective-permute-start.21 = (f32[4,8,128]{2,1,0:T(8,128)S(1)}, f32[4,8,128]{2,1,0:T(8,128)S(1)}, u32[]{:S(2)}, u32[]{:S(2)}) collective-permute-start(f32[4,8,128]{2,1,0:T(8,128)S(1)} %get-tuple-element.53), channel_id=1, source_target_pairs={{0,31},{1,0},{2,1},{3,2},{4,3},{5,4},{6,5},{7,6},{8,7},{9,8},{10,9... | collective-permute-start | bytes 49160 | tf_op jit(solution)/shard_map/ppermute | solution.py:22
  94.2 21.0 %all-to-all-start.1 = ((f32[16,8,128]{2,1,0:T(8,128)}), f32[16,8,128]{2,1,0:T(8,128)S(1)}, u32[]{:S(2)}, u32[]{:S(2)}) async-start(f32[16,8,128]{2,1,0:T(8,128)} %broadcast_in_dim.32), calls=%async_computation.1 | async-start | bytes 131072 | tf_op jit(solution)/shard_map/all_to_all | solution.py:275
  103.6 8.6 %collective-permute-start.22 = (f32[3,8,128]{2,1,0:T(8,128)S(1)}, f32[3,8,128]{2,1,0:T(8,128)S(1)}, u32[]{:S(2)}, u32[]{:S(2)}) collective-permute-start(f32[3,8,128]{2,1,0:T(8,128)S(1)} %get-tuple-element.56), channel_id=1, source_target_pairs={{0,32},{32,64},{64,96},{96,128},{128,160},{160,192},{192,224},{224... | collective-permute-start | bytes 36872 | tf_op jit(solution)/shard_map/ppermute | solution.py:22
  105.9 7.1 %collective-permute-start.23 = (f32[3,8,128]{2,1,0:T(8,128)S(1)}, f32[3,8,128]{2,1,0:T(8,128)S(1)}, u32[]{:S(2)}, u32[]{:S(2)}) collective-permute-start(f32[3,8,128]{2,1,0:T(8,128)S(1)} %get-tuple-element.58), channel_id=1, source_target_pairs={{0,480},{32,0},{64,32},{96,64},{128,96},{160,128},{192,160},{224,1... | collective-permute-start | bytes 36872 | tf_op jit(solution)/shard_map/ppermute | solution.py:22

commit v11 on v10

--- a/solution.py
+++ b/solution.py
@@ -299,16 +299,16 @@
         carried = (sums,)
         if sweep == ITERS - 1:
             part = jnp.sum(spread_sum(sums, lambda a, c: c // 2), axis=0)
-            part, r1, r7 = lax.optimization_barrier((part, r1, r7))
+            part, r3, r5 = lax.optimization_barrier((part, r3, r5))
+        from_lower_axial = ring_shift(r7, "axial", 1)
+        from_upper_axial = ring_shift(r1, "axial", -1)
+        if sweep == ITERS - 1:
+            part, from_lower_axial, from_upper_axial = lax.optimization_barrier(
+                (part, from_lower_axial, from_upper_axial)
+            )
+            sums = spread_sum(part, lambda a, c: (a, c % 2))
         from_lower_cross = ring_shift(r5, "cross", 1)
         from_upper_cross = ring_shift(r3, "cross", -1)
-        if sweep == ITERS - 1:
-            part, from_lower_cross, from_upper_cross = lax.optimization_barrier(
-                (part, from_lower_cross, from_upper_cross)
-            )
-            sums = spread_sum(part, lambda a, c: (a, c % 2))
-        from_lower_axial = ring_shift(r7, "axial", 1)
-        from_upper_axial = ring_shift(r1, "axial", -1)
         if sweep == ITERS - 1:
             planes = [from_lower_cross, from_upper_cross]
         now = kept + from_lower_axial

time: 117 us -> 120 us (1.026)
  the two profiles are of different devices: /device:TPU:1 before, /device:TPU:6 now
where the time goes in v11:
time: 120 us
  starting transfers between devices  82.8 us (69%)
  waiting for transfers between devices  27.7 us (23%)
  Pallas kernels  7.55 us (6%)
    ppermute x24, starting transfers between devices, ring_shift(): return lax.ppermute(shard, axis, ring(lax.axis_size(axis), by))  61.2 us
    all_to_all x2, starting transfers between devices, spread_sum(): lax.all_to_all(part, ('axial', 'cross'), 0, 0, axis_index_groups=groups)  21.7 us
    ppermute x24, waiting for transfers between devices, ring_shift(): return lax.ppermute(shard, axis, ring(lax.axis_size(axis), by))  19.2 us
    all_to_all x2, waiting for transfers between devices, spread_sum(): lax.all_to_all(part, ('axial', 'cross'), 0, 0, axis_index_groups=groups)  8.45 us
    pallas_call x3, Pallas kernels, operator_call(): pl.pallas_call(functools.partial(operator_kernel, sweep), in_specs=[pl.Bl...  6.67 us
  transfers between devices with their start and end apart: 26, of which 9 were waited for; matrix products, arithmetic and copies ran while one was open for 0% of the time, Pallas kernels for 0%

profile of v11, /device:TPU:6, one launch (start us, length us, event | category | flops | bytes accessed | tf_op | source)
XLA Modules:
  0.0 119.9 jit_solution(5780039548173009763)
XLA Ops:
  0.7 3.5 %collective-permute-start.3 = (f32[3,8,128]{2,1,0:T(8,128)}, f32[3,8,128]{2,1,0:T(8,128)S(1)}, u32[]{:S(2)}, u32[]{:S(2)}) collective-permute-start(f32[3,8,128]{2,1,0:T(8,128)} %bitcast.21), channel_id=1, source_target_pairs={{0,32},{32,64},{64,96},{96,128},{128,160},{160,192},{192,224},{224... | collective-permute-start | bytes 36872 | tf_op jit(solution)/shard_map/ppermute | solution.py:22
  4.2 0.0 collective-permute-start.2
  4.2 2.4 %collective-permute-start.1 = (f32[3,8,128]{2,1,0:T(8,128)}, f32[3,8,128]{2,1,0:T(8,128)S(1)}, u32[]{:S(2)}, u32[]{:S(2)}) collective-permute-start(f32[3,8,128]{2,1,0:T(8,128)} %bitcast.23), channel_id=1, source_target_pairs={{0,480},{32,0},{64,32},{96,64},{128,96},{160,128},{192,160},{224,1... | collective-permute-start | bytes 36872 | tf_op jit(solution)/shard_map/ppermute | solution.py:22
  6.7 8.4 %collective-permute-start = (f32[3,8,128]{2,1,0:T(8,128)}, f32[3,8,128]{2,1,0:T(8,128)S(1)}, u32[]{:S(2)}, u32[]{:S(2)}) collective-permute-start(f32[3,8,128]{2,1,0:T(8,128)} %bitcast.24), channel_id=1, source_target_pairs={{0,31},{1,0},{2,1},{3,2},{4,3},{5,4},{6,5},{7,6},{8,7},{9,8},{10,9... | collective-permute-start | bytes 36872 | tf_op jit(solution)/shard_map/ppermute | solution.py:22
  15.1 0.0 collective-permute-done.3.from_axial_dn
  15.1 0.0 collective-permute-done.2.from_cross_dn.d0
  15.1 0.0 collective-permute-done.1.from_axial_up
  15.1 1.6 %collective-permute-done.from_cross_up.u0 = f32[3,8,128]{2,1,0:T(8,128)S(1)} collective-permute-done((f32[3,8,128]{2,1,0:T(8,128)}, f32[3,8,128]{2,1,0:T(8,128)S(1)}, u32[]{:S(2)}, u32[]{:S(2)}) %collective-permute-start) | collective-permute-done | bytes 12320 | tf_op jit(solution)/shard_map/ppermute | solution.py:22
  16.7 0.0 copy-done.3
  16.7 0.0 copy-start.4
  16.7 0.0 copy-start.5
  16.7 2.1 %shard_map.86 = (f32[3,8,128]{2,1,0:T(8,128)S(1)}, f32[3,8,128]{2,1,0:T(8,128)S(1)}, f32[3,8,128]{2,1,0:T(8,128)S(1)}, f32[3,8,128]{2,1,0:T(8,128)S(1)}, f32[3,8,128]{2,1,0:T(8,128)S(1)}, /*index=5*/f32[8,128]{1,0:T(8,128)S(1)}) custom-call(s32[8,8]{1,0:T(8,128)S(1)} %bitcast.27, f32[3,8,128]{2,1,0:T(8,128)S(1)} %bitcast.25, ...), custom_call_target="tpu_custom_call" | custom-call | tf_op jit(solution)/shard_map/pallas_call | solution.py:118
  18.8 5.5 %collective-permute-start.4 = (f32[3,8,128]{2,1,0:T(8,128)S(1)}, f32[3,8,128]{2,1,0:T(8,128)S(1)}, u32[]{:S(2)}, u32[]{:S(2)}) collective-permute-start(f32[3,8,128]{2,1,0:T(8,128)S(1)} %get-tuple-element.34), channel_id=1, source_target_pairs={{0,32},{32,64},{64,96},{96,128},{128,160},{160,192},{192,224},{224... | collective-permute-start | bytes 36872 | tf_op jit(solution)/shard_map/ppermute | solution.py:22
  24.3 0.0 collective-permute-start.5
  24.4 1.9 %collective-permute-start.6 = (f32[3,8,128]{2,1,0:T(8,128)S(1)}, f32[3,8,128]{2,1,0:T(8,128)S(1)}, u32[]{:S(2)}, u32[]{:S(2)}) collective-permute-start(f32[3,8,128]{2,1,0:T(8,128)S(1)} %get-tuple-element.36), channel_id=1, source_target_pairs={{0,480},{32,0},{64,32},{96,64},{128,96},{160,128},{192,160},{224,1... | collective-permute-start | bytes 36872 | tf_op jit(solution)/shard_map/ppermute | solution.py:22
  26.3 2.9 %collective-permute-start.7 = (f32[3,8,128]{2,1,0:T(8,128)S(1)}, f32[3,8,128]{2,1,0:T(8,128)S(1)}, u32[]{:S(2)}, u32[]{:S(2)}) collective-permute-start(f32[3,8,128]{2,1,0:T(8,128)S(1)} %get-tuple-element.37), channel_id=1, source_target_pairs={{0,31},{1,0},{2,1},{3,2},{4,3},{5,4},{6,5},{7,6},{8,7},{9,8},{10,9... | collective-permute-start | bytes 36872 | tf_op jit(solution)/shard_map/ppermute | solution.py:22
  29.2 0.0 collective-permute-done.4
  29.2 0.0 collective-permute-done.5
  29.2 2.8 %collective-permute-done.6 = f32[3,8,128]{2,1,0:T(8,128)S(1)} collective-permute-done((f32[3,8,128]{2,1,0:T(8,128)S(1)}, f32[3,8,128]{2,1,0:T(8,128)S(1)}, u32[]{:S(2)}, u32[]{:S(2)}) %collective-permute-start.6) | collective-permute-done | bytes 12320 | tf_op jit(solution)/shard_map/ppermute | solution.py:22
  32.1 0.0 collective-permute-done.7
  32.1 4.3 %collective-permute-start.11 = (f32[3,8,128]{2,1,0:T(8,128)S(1)}, f32[3,8,128]{2,1,0:T(8,128)S(1)}, u32[]{:S(2)}, u32[]{:S(2)}) collective-permute-start(f32[3,8,128]{2,1,0:T(8,128)S(1)} %select_add_fusion.1.own.k1), channel_id=1, source_target_pairs={{0,32},{32,64},{64,96},{96,128},{128,160},{160,192},{192,224},{224... | collective-permute-start | bytes 36872 | tf_op jit(solution)/shard_map/ppermute | solution.py:22
  36.4 0.0 collective-permute-start.10
  36.4 1.9 %collective-permute-start.9 = (f32[3,8,128]{2,1,0:T(8,128)S(1)}, f32[3,8,128]{2,1,0:T(8,128)S(1)}, u32[]{:S(2)}, u32[]{:S(2)}) collective-permute-start(f32[3,8,128]{2,1,0:T(8,128)S(1)} %select_add_fusion.1.own.k1), channel_id=1, source_target_pairs={{0,480},{32,0},{64,32},{96,64},{128,96},{160,128},{192,160},{224,1... | collective-permute-start | bytes 36872 | tf_op jit(solution)/shard_map/ppermute | solution.py:22
  38.4 2.9 %collective-permute-start.8 = (f32[3,8,128]{2,1,0:T(8,128)S(1)}, f32[3,8,128]{2,1,0:T(8,128)S(1)}, u32[]{:S(2)}, u32[]{:S(2)}) collective-permute-start(f32[3,8,128]{2,1,0:T(8,128)S(1)} %select_add_fusion.1.own.k1), channel_id=1, source_target_pairs={{0,31},{1,0},{2,1},{3,2},{4,3},{5,4},{6,5},{7,6},{8,7},{9,8},{10,9... | collective-permute-start | bytes 36872 | tf_op jit(solution)/shard_map/ppermute | solution.py:22
  41.3 0.0 collective-permute-done.11.from_axial_dn
  41.3 0.0 collective-permute-done.10.from_cross_dn.d1
  41.3 2.8 %collective-permute-done.9.from_axial_up = f32[3,8,128]{2,1,0:T(8,128)S(1)} collective-permute-done((f32[3,8,128]{2,1,0:T(8,128)S(1)}, f32[3,8,128]{2,1,0:T(8,128)S(1)}, u32[]{:S(2)}, u32[]{:S(2)}) %collective-permute-start.9) | collective-permute-done | bytes 12320 | tf_op jit(solution)/shard_map/ppermute | solution.py:22
  44.1 0.0 collective-permute-done.8.from_cross_up.u1
  44.1 2.1 %shard_map.87 = (f32[3,8,128]{2,1,0:T(8,128)S(1)}, f32[3,8,128]{2,1,0:T(8,128)S(1)}, f32[3,8,128]{2,1,0:T(8,128)S(1)}, f32[3,8,128]{2,1,0:T(8,128)S(1)}, f32[3,8,128]{2,1,0:T(8,128)S(1)}, /*index=5*/f32[8,128]{1,0:T(8,128)S(1)}) custom-call(s32[8,8]{1,0:T(8,128)S(1)} %bitcast.28, f32[3,8,128]{2,1,0:T(8,128)S(1)} %select_add_fusion.1.own.k1, ...), custom_call_target="tpu_custom_call" | custom-call | tf_op jit(solution)/shard_map/pallas_call | solution.py:118
  46.2 4.3 %collective-permute-start.12 = (f32[3,8,128]{2,1,0:T(8,128)S(1)}, f32[3,8,128]{2,1,0:T(8,128)S(1)}, u32[]{:S(2)}, u32[]{:S(2)}) collective-permute-start(f32[3,8,128]{2,1,0:T(8,128)S(1)} %get-tuple-element.40), channel_id=1, source_target_pairs={{0,32},{32,64},{64,96},{96,128},{128,160},{160,192},{192,224},{224... | collective-permute-start | bytes 36872 | tf_op jit(solution)/shard_map/ppermute | solution.py:22
  50.5 0.0 collective-permute-start.13
  50.6 1.9 %collective-permute-start.14 = (f32[3,8,128]{2,1,0:T(8,128)S(1)}, f32[3,8,128]{2,1,0:T(8,128)S(1)}, u32[]{:S(2)}, u32[]{:S(2)}) collective-permute-start(f32[3,8,128]{2,1,0:T(8,128)S(1)} %get-tuple-element.42), channel_id=1, source_target_pairs={{0,480},{32,0},{64,32},{96,64},{128,96},{160,128},{192,160},{224,1... | collective-permute-start | bytes 36872 | tf_op jit(solution)/shard_map/ppermute | solution.py:22
  52.5 2.9 %collective-permute-start.15 = (f32[3,8,128]{2,1,0:T(8,128)S(1)}, f32[3,8,128]{2,1,0:T(8,128)S(1)}, u32[]{:S(2)}, u32[]{:S(2)}) collective-permute-start(f32[3,8,128]{2,1,0:T(8,128)S(1)} %get-tuple-element.43), channel_id=1, source_target_pairs={{0,31},{1,0},{2,1},{3,2},{4,3},{5,4},{6,5},{7,6},{8,7},{9,8},{10,9... | collective-permute-start | bytes 36872 | tf_op jit(solution)/shard_map/ppermute | solution.py:22
  55.4 0.1 pad.4.clone
  55.5 0.0 collective-permute-done.12
  55.5 0.0 collective-permute-done.13
  55.5 2.7 %collective-permute-done.14 = f32[3,8,128]{2,1,0:T(8,128)S(1)} collective-permute-done((f32[3,8,128]{2,1,0:T(8,128)S(1)}, f32[3,8,128]{2,1,0:T(8,128)S(1)}, u32[]{:S(2)}, u32[]{:S(2)}) %collective-permute-start.14) | collective-permute-done | bytes 12320 | tf_op jit(solution)/shard_map/ppermute | solution.py:22
  58.3 0.0 collective-permute-done.15
  58.3 4.3 %collective-permute-start.19 = (f32[3,8,128]{2,1,0:T(8,128)S(1)}, f32[3,8,128]{2,1,0:T(8,128)S(1)}, u32[]{:S(2)}, u32[]{:S(2)}) collective-permute-start(f32[3,8,128]{2,1,0:T(8,128)S(1)} %select_add_fusion.own.k2), channel_id=1, source_target_pairs={{0,32},{32,64},{64,96},{96,128},{128,160},{160,192},{192,224},{224... | collective-permute-start | bytes 36872 | tf_op jit(solution)/shard_map/ppermute | solution.py:22
  62.6 0.0 collective-permute-start.18
  62.6 1.9 %collective-permute-start.17 = (f32[3,8,128]{2,1,0:T(8,128)S(1)}, f32[3,8,128]{2,1,0:T(8,128)S(1)}, u32[]{:S(2)}, u32[]{:S(2)}) collective-permute-start(f32[3,8,128]{2,1,0:T(8,128)S(1)} %select_add_fusion.own.k2), channel_id=1, source_target_pairs={{0,480},{32,0},{64,32},{96,64},{128,96},{160,128},{192,160},{224,1... | collective-permute-start | bytes 36872 | tf_op jit(solution)/shard_map/ppermute | solution.py:22
  64.6 2.9 %collective-permute-start.16 = (f32[3,8,128]{2,1,0:T(8,128)S(1)}, f32[3,8,128]{2,1,0:T(8,128)S(1)}, u32[]{:S(2)}, u32[]{:S(2)}) collective-permute-start(f32[3,8,128]{2,1,0:T(8,128)S(1)} %select_add_fusion.own.k2), channel_id=1, source_target_pairs={{0,31},{1,0},{2,1},{3,2},{4,3},{5,4},{6,5},{7,6},{8,7},{9,8},{10,9... | collective-permute-start | bytes 36872 | tf_op jit(solution)/shard_map/ppermute | solution.py:22
  67.5 0.0 copy-done.5
  67.5 0.1 fusion.5
  67.6 0.1 fusion.3.rest_1_
  67.7 0.0 collective-permute-done.19.from_axial_dn
  67.7 0.0 collective-permute-done.18.from_cross_dn.d2
  67.7 2.7 %collective-permute-done.17.from_axial_up = f32[3,8,128]{2,1,0:T(8,128)S(1)} collective-permute-done((f32[3,8,128]{2,1,0:T(8,128)S(1)}, f32[3,8,128]{2,1,0:T(8,128)S(1)}, u32[]{:S(2)}, u32[]{:S(2)}) %collective-permute-start.17) | collective-permute-done | bytes 12320 | tf_op jit(solution)/shard_map/ppermute | solution.py:22
  70.3 0.0 collective-permute-done.16.from_cross_up.u2
  70.3 2.5 %shard_map.88 = (f32[3,8,128]{2,1,0:T(8,128)S(1)}, f32[4,8,128]{2,1,0:T(8,128)S(1)}, f32[4,8,128]{2,1,0:T(8,128)S(1)}, f32[3,8,128]{2,1,0:T(8,128)S(1)}, f32[3,8...) custom-call(s32[8,8]{1,0:T(8,128)S(1)} %bitcast.29, f32[3,8,128]{2,1,0:T(8,128)S(1)} %select_add_fusion.own.k2, ...), custom_call_target="tpu_custom_call" | custom-call | tf_op jit(solution)/shard_map/pallas_call | solution.py:118
  72.8 12.0 %all-to-all-start = ((f32[32,8,128]{2,1,0:T(8,128)}), f32[32,8,128]{2,1,0:T(8,128)S(1)}, u32[]{:S(2)}, u32[]{:S(2)}) async-start(f32[32,8,128]{2,1,0:T(8,128)} %get-tuple-element.48), calls=%async_computation | async-start | bytes 262144 | tf_op jit(solution)/shard_map/all_to_all | solution.py:275
  84.8 3.4 %collective-permute-start.20 = (f32[3,8,128]{2,1,0:T(8,128)S(1)}, f32[3,8,128]{2,1,0:T(8,128)S(1)}, u32[]{:S(2)}, u32[]{:S(2)}) collective-permute-start(f32[3,8,128]{2,1,0:T(8,128)S(1)} %get-tuple-element.52), channel_id=1, source_target_pairs={{0,32},{32,64},{64,96},{96,128},{128,160},{160,192},{192,224},{224... | collective-permute-start | bytes 36872 | tf_op jit(solution)/shard_map/ppermute | solution.py:22
  88.2 2.5 %collective-permute-start.21 = (f32[3,8,128]{2,1,0:T(8,128)S(1)}, f32[3,8,128]{2,1,0:T(8,128)S(1)}, u32[]{:S(2)}, u32[]{:S(2)}) collective-permute-start(f32[3,8,128]{2,1,0:T(8,128)S(1)} %get-tuple-element.53), channel_id=1, source_target_pairs={{0,480},{32,0},{64,32},{96,64},{128,96},{160,128},{192,160},{224,1... | collective-permute-start | bytes 36872 | tf_op jit(solution)/shard_map/ppermute | solution.py:22
  90.7 0.2 all-to-all-done
  90.9 0.0 collective-permute-done.20
  91.0 5.0 %collective-permute-done.21 = f32[3,8,128]{2,1,0:T(8,128)S(1)} collective-permute-done((f32[3,8,128]{2,1,0:T(8,128)S(1)}, f32[3,8,128]{2,1,0:T(8,128)S(1)}, u32[]{:S(2)}, u32[]{:S(2)}) %collective-permute-start.21) | collective-permute-done | bytes 12320 | tf_op jit(solution)/shard_map/ppermute | solution.py:22
  95.9 0.6 broadcast_in_dim.32
  96.5 9.7 %all-to-all-start.1 = ((f32[16,8,128]{2,1,0:T(8,128)}), f32[16,8,128]{2,1,0:T(8,128)S(1)}, u32[]{:S(2)}, u32[]{:S(2)}) async-start(f32[16,8,128]{2,1,0:T(8,128)} %broadcast_in_dim.32), calls=%async_computation.1 | async-start | bytes 131072 | tf_op jit(solution)/shard_map/all_to_all | solution.py:275
  106.2 0.0 collective-permute-start.22
  106.3 2.9 %collective-permute-start.23 = (f32[4,8,128]{2,1,0:T(8,128)S(1)}, f32[4,8,128]{2,1,0:T(8,128)S(1)}, u32[]{:S(2)}, u32[]{:S(2)}) collective-permute-start(f32[4,8,128]{2,1,0:T(8,128)S(1)} %get-tuple-element.59), channel_id=1, source_target_pairs={{0,31},{1,0},{2,1},{3,2},{4,3},{5,4},{6,5},{7,6},{8,7},{9,8},{10,9... | collective-permute-start | bytes 49160 | tf_op jit(solution)/shard_map/ppermute | solution.py:22
  109.2 1.6 %collective-permute-done.22.dn_plane = f32[4,8,128]{2,1,0:T(8,128)S(1)} collective-permute-done((f32[4,8,128]{2,1,0:T(8,128)S(1)}, f32[4,8,128]{2,1,0:T(8,128)S(1)}, u32[]{:S(2)}, u32[]{:S(2)}) %collective-permute-start.22) | collective-permute-done | bytes 16416 | tf_op jit(solution)/shard_map/ppermute | solution.py:22
  110.8 0.0 collective-permute-done.23.up_plane
  110.8 8.2 %all-to-all-done.1.sums = f32[16,8,128]{2,1,0:T(8,128)S(1)} async-done(((f32[16,8,128]{2,1,0:T(8,128)}), f32[16,8,128]{2,1,0:T(8,128)S(1)}, u32[]{:S(2)}, u32[]{:S(2)}) %all-to-all-start.1) | async-done | bytes 65568 | tf_op jit(solution)/shard_map/all_to_all | solution.py:275
  119.0 0.9 shard_map.89
  (15 shorter events, 0.1 us)
Async XLA Ops:
  0.6 16.1 %copy-start = (bf16[1,1,8,8,128,128]{5,4,3,2,1,0:T(8,128)(2,1)S(1)}, bf16[1,1,8,8,128,128]{5,4,3,2,1,0:T(8,128)(2,1)}, u32[]{:S(2)}) copy-start(bf16[1,1,8,8,128,128]{5,4,3,2,1,0:T(8,128)(2,1)} %param.8) | copy-start | bytes 6291460
  0.6 16.1 %copy-start.1 = (f32[1,1,8,3,128]{4,2,3,1,0:T(8,128)S(1)}, f32[1,1,8,3,128]{4,2,3,1,0:T(8,128)}, u32[]{:S(2)}) copy-start(f32[1,1,8,3,128]{4,2,3,1,0:T(8,128)} %param.6) | copy-start | bytes 36868
  0.7 16.0 %copy-start.2 = (s32[1,1,8,8]{3,2,1,0:T(8,128)S(1)}, s32[1,1,8,8]{3,2,1,0:T(8,128)}, u32[]{:S(2)}) copy-start(s32[1,1,8,8]{3,2,1,0:T(8,128)} %param.9) | copy-start | bytes 772
  0.7 16.0 %copy-start.3 = (f32[1,1,8,128]{3,2,1,0:T(8,128)S(1)}, f32[1,1,8,128]{3,2,1,0:T(8,128)}, u32[]{:S(2)}) copy-start(f32[1,1,8,128]{3,2,1,0:T(8,128)} %param.7) | copy-start | bytes 12292
  0.7 14.4 %collective-permute-start.3 = (f32[3,8,128]{2,1,0:T(8,128)}, f32[3,8,128]{2,1,0:T(8,128)S(1)}, u32[]{:S(2)}, u32[]{:S(2)}) collective-permute-start(f32[3,8,128]{2,1,0:T(8,128)} %bitcast.21), channel_id=1, source_target_pairs={{0,32},{32,64},{64,96},{96,128},{128,160},{160,192},{192,224},{224... | collective-permute-start | bytes 36872 | tf_op jit(solution)/shard_map/ppermute | solution.py:22
  4.2 10.9 %collective-permute-start.2 = (f32[3,8,128]{2,1,0:T(8,128)}, f32[3,8,128]{2,1,0:T(8,128)S(1)}, u32[]{:S(2)}, u32[]{:S(2)}) collective-permute-start(f32[3,8,128]{2,1,0:T(8,128)} %bitcast.22), channel_id=1, source_target_pairs={{0,1},{1,2},{2,3},{3,4},{4,5},{5,6},{6,7},{7,8},{8,9},{9,10},{10,1... | collective-permute-start | bytes 36872 | tf_op jit(solution)/shard_map/ppermute | solution.py:22
  4.2 10.9 %collective-permute-start.1 = (f32[3,8,128]{2,1,0:T(8,128)}, f32[3,8,128]{2,1,0:T(8,128)S(1)}, u32[]{:S(2)}, u32[]{:S(2)}) collective-permute-start(f32[3,8,128]{2,1,0:T(8,128)} %bitcast.23), channel_id=1, source_target_pairs={{0,480},{32,0},{64,32},{96,64},{128,96},{160,128},{192,160},{224,1... | collective-permute-start | bytes 36872 | tf_op jit(solution)/shard_map/ppermute | solution.py:22
  6.7 10.0 %collective-permute-start = (f32[3,8,128]{2,1,0:T(8,128)}, f32[3,8,128]{2,1,0:T(8,128)S(1)}, u32[]{:S(2)}, u32[]{:S(2)}) collective-permute-start(f32[3,8,128]{2,1,0:T(8,128)} %bitcast.24), channel_id=1, source_target_pairs={{0,31},{1,0},{2,1},{3,2},{4,3},{5,4},{6,5},{7,6},{8,7},{9,8},{10,9... | collective-permute-start | bytes 36872 | tf_op jit(solution)/shard_map/ppermute | solution.py:22
  16.7 50.8 %copy-start.4 = (s32[1,1,2,64]{3,2,1,0:T(2,128)S(1)}, s32[1,1,2,64]{3,2,1,0:T(2,128)}, u32[]{:S(2)}) copy-start(s32[1,1,2,64]{3,2,1,0:T(2,128)} %param.10) | copy-start | bytes 1540
  16.7 50.8 %copy-start.5 = (s32[1,1,2]{2,1,0:T(1,128)S(1)}, s32[1,1,2]{2,1,0:T(1,128)}, u32[]{:S(2)}) copy-start(s32[1,1,2]{2,1,0:T(1,128)} %param.11) | copy-start | bytes 28
  18.8 10.4 %collective-permute-start.4 = (f32[3,8,128]{2,1,0:T(8,128)S(1)}, f32[3,8,128]{2,1,0:T(8,128)S(1)}, u32[]{:S(2)}, u32[]{:S(2)}) collective-permute-start(f32[3,8,128]{2,1,0:T(8,128)S(1)} %get-tuple-element.34), channel_id=1, source_target_pairs={{0,32},{32,64},{64,96},{96,128},{128,160},{160,192},{192,224},{224... | collective-permute-start | bytes 36872 | tf_op jit(solution)/shard_map/ppermute | solution.py:22
  24.3 4.9 %collective-permute-start.5 = (f32[3,8,128]{2,1,0:T(8,128)S(1)}, f32[3,8,128]{2,1,0:T(8,128)S(1)}, u32[]{:S(2)}, u32[]{:S(2)}) collective-permute-start(f32[3,8,128]{2,1,0:T(8,128)S(1)} %get-tuple-element.35), channel_id=1, source_target_pairs={{0,1},{1,2},{2,3},{3,4},{4,5},{5,6},{6,7},{7,8},{8,9},{9,10},{10,1... | collective-permute-start | bytes 36872 | tf_op jit(solution)/shard_map/ppermute | solution.py:22
  24.4 7.7 %collective-permute-start.6 = (f32[3,8,128]{2,1,0:T(8,128)S(1)}, f32[3,8,128]{2,1,0:T(8,128)S(1)}, u32[]{:S(2)}, u32[]{:S(2)}) collective-permute-start(f32[3,8,128]{2,1,0:T(8,128)S(1)} %get-tuple-element.36), channel_id=1, source_target_pairs={{0,480},{32,0},{64,32},{96,64},{128,96},{160,128},{192,160},{224,1... | collective-permute-start | bytes 36872 | tf_op jit(solution)/shard_map/ppermute | solution.py:22
  26.3 5.8 %collective-permute-start.7 = (f32[3,8,128]{2,1,0:T(8,128)S(1)}, f32[3,8,128]{2,1,0:T(8,128)S(1)}, u32[]{:S(2)}, u32[]{:S(2)}) collective-permute-start(f32[3,8,128]{2,1,0:T(8,128)S(1)} %get-tuple-element.37), channel_id=1, source_target_pairs={{0,31},{1,0},{2,1},{3,2},{4,3},{5,4},{6,5},{7,6},{8,7},{9,8},{10,9... | collective-permute-start | bytes 36872 | tf_op jit(solution)/shard_map/ppermute | solution.py:22
  32.1 9.2 %collective-permute-start.11 = (f32[3,8,128]{2,1,0:T(8,128)S(1)}, f32[3,8,128]{2,1,0:T(8,128)S(1)}, u32[]{:S(2)}, u32[]{:S(2)}) collective-permute-start(f32[3,8,128]{2,1,0:T(8,128)S(1)} %select_add_fusion.1.own.k1), channel_id=1, source_target_pairs={{0,32},{32,64},{64,96},{96,128},{128,160},{160,192},{192,224},{224... | collective-permute-start | bytes 36872 | tf_op jit(solution)/shard_map/ppermute | solution.py:22
  36.4 4.9 %collective-permute-start.10 = (f32[3,8,128]{2,1,0:T(8,128)S(1)}, f32[3,8,128]{2,1,0:T(8,128)S(1)}, u32[]{:S(2)}, u32[]{:S(2)}) collective-permute-start(f32[3,8,128]{2,1,0:T(8,128)S(1)} %select_add_fusion.1.own.k1), channel_id=1, source_target_pairs={{0,1},{1,2},{2,3},{3,4},{4,5},{5,6},{6,7},{7,8},{8,9},{9,10},{10,1... | collective-permute-start | bytes 36872 | tf_op jit(solution)/shard_map/ppermute | solution.py:22
  36.4 7.7 %collective-permute-start.9 = (f32[3,8,128]{2,1,0:T(8,128)S(1)}, f32[3,8,128]{2,1,0:T(8,128)S(1)}, u32[]{:S(2)}, u32[]{:S(2)}) collective-permute-start(f32[3,8,128]{2,1,0:T(8,128)S(1)} %select_add_fusion.1.own.k1), channel_id=1, source_target_pairs={{0,480},{32,0},{64,32},{96,64},{128,96},{160,128},{192,160},{224,1... | collective-permute-start | bytes 36872 | tf_op jit(solution)/shard_map/ppermute | solution.py:22
  38.4 5.8 %collective-permute-start.8 = (f32[3,8,128]{2,1,0:T(8,128)S(1)}, f32[3,8,128]{2,1,0:T(8,128)S(1)}, u32[]{:S(2)}, u32[]{:S(2)}) collective-permute-start(f32[3,8,128]{2,1,0:T(8,128)S(1)} %select_add_fusion.1.own.k1), channel_id=1, source_target_pairs={{0,31},{1,0},{2,1},{3,2},{4,3},{5,4},{6,5},{7,6},{8,7},{9,8},{10,9... | collective-permute-start | bytes 36872 | tf_op jit(solution)/shard_map/ppermute | solution.py:22
  46.2 9.3 %collective-permute-start.12 = (f32[3,8,128]{2,1,0:T(8,128)S(1)}, f32[3,8,128]{2,1,0:T(8,128)S(1)}, u32[]{:S(2)}, u32[]{:S(2)}) collective-permute-start(f32[3,8,128]{2,1,0:T(8,128)S(1)} %get-tuple-element.40), channel_id=1, source_target_pairs={{0,32},{32,64},{64,96},{96,128},{128,160},{160,192},{192,224},{224... | collective-permute-start | bytes 36872 | tf_op jit(solution)/shard_map/ppermute | solution.py:22
  50.5 5.0 %collective-permute-start.13 = (f32[3,8,128]{2,1,0:T(8,128)S(1)}, f32[3,8,128]{2,1,0:T(8,128)S(1)}, u32[]{:S(2)}, u32[]{:S(2)}) collective-permute-start(f32[3,8,128]{2,1,0:T(8,128)S(1)} %get-tuple-element.41), channel_id=1, source_target_pairs={{0,1},{1,2},{2,3},{3,4},{4,5},{5,6},{6,7},{7,8},{8,9},{9,10},{10,1... | collective-permute-start | bytes 36872 | tf_op jit(solution)/shard_map/ppermute | solution.py:22
  50.6 7.7 %collective-permute-start.14 = (f32[3,8,128]{2,1,0:T(8,128)S(1)}, f32[3,8,128]{2,1,0:T(8,128)S(1)}, u32[]{:S(2)}, u32[]{:S(2)}) collective-permute-start(f32[3,8,128]{2,1,0:T(8,128)S(1)} %get-tuple-element.42), channel_id=1, source_target_pairs={{0,480},{32,0},{64,32},{96,64},{128,96},{160,128},{192,160},{224,1... | collective-permute-start | bytes 36872 | tf_op jit(solution)/shard_map/ppermute | solution.py:22
  52.5 5.8 %collective-permute-start.15 = (f32[3,8,128]{2,1,0:T(8,128)S(1)}, f32[3,8,128]{2,1,0:T(8,128)S(1)}, u32[]{:S(2)}, u32[]{:S(2)}) collective-permute-start(f32[3,8,128]{2,1,0:T(8,128)S(1)} %get-tuple-element.43), channel_id=1, source_target_pairs={{0,31},{1,0},{2,1},{3,2},{4,3},{5,4},{6,5},{7,6},{8,7},{9,8},{10,9... | collective-permute-start | bytes 36872 | tf_op jit(solution)/shard_map/ppermute | solution.py:22
  58.3 9.4 %collective-permute-start.19 = (f32[3,8,128]{2,1,0:T(8,128)S(1)}, f32[3,8,128]{2,1,0:T(8,128)S(1)}, u32[]{:S(2)}, u32[]{:S(2)}) collective-permute-start(f32[3,8,128]{2,1,0:T(8,128)S(1)} %select_add_fusion.own.k2), channel_id=1, source_target_pairs={{0,32},{32,64},{64,96},{96,128},{128,160},{160,192},{192,224},{224... | collective-permute-start | bytes 36872 | tf_op jit(solution)/shard_map/ppermute | solution.py:22
  62.6 5.1 %collective-permute-start.18 = (f32[3,8,128]{2,1,0:T(8,128)S(1)}, f32[3,8,128]{2,1,0:T(8,128)S(1)}, u32[]{:S(2)}, u32[]{:S(2)}) collective-permute-start(f32[3,8,128]{2,1,0:T(8,128)S(1)} %select_add_fusion.own.k2), channel_id=1, source_target_pairs={{0,1},{1,2},{2,3},{3,4},{4,5},{5,6},{6,7},{7,8},{8,9},{9,10},{10,1... | collective-permute-start | bytes 36872 | tf_op jit(solution)/shard_map/ppermute | solution.py:22
  62.6 7.7 %collective-permute-start.17 = (f32[3,8,128]{2,1,0:T(8,128)S(1)}, f32[3,8,128]{2,1,0:T(8,128)S(1)}, u32[]{:S(2)}, u32[]{:S(2)}) collective-permute-start(f32[3,8,128]{2,1,0:T(8,128)S(1)} %select_add_fusion.own.k2), channel_id=1, source_target_pairs={{0,480},{32,0},{64,32},{96,64},{128,96},{160,128},{192,160},{224,1... | collective-permute-start | bytes 36872 | tf_op jit(solution)/shard_map/ppermute | solution.py:22
  64.6 5.8 %collective-permute-start.16 = (f32[3,8,128]{2,1,0:T(8,128)S(1)}, f32[3,8,128]{2,1,0:T(8,128)S(1)}, u32[]{:S(2)}, u32[]{:S(2)}) collective-permute-start(f32[3,8,128]{2,1,0:T(8,128)S(1)} %select_add_fusion.own.k2), channel_id=1, source_target_pairs={{0,31},{1,0},{2,1},{3,2},{4,3},{5,4},{6,5},{7,6},{8,7},{9,8},{10,9... | collective-permute-start | bytes 36872 | tf_op jit(solution)/shard_map/ppermute | solution.py:22
  72.8 18.1 %all-to-all-start = ((f32[32,8,128]{2,1,0:T(8,128)}), f32[32,8,128]{2,1,0:T(8,128)S(1)}, u32[]{:S(2)}, u32[]{:S(2)}) async-start(f32[32,8,128]{2,1,0:T(8,128)} %get-tuple-element.48), calls=%async_computation | async-start | bytes 262144 | tf_op jit(solution)/shard_map/all_to_all | solution.py:275
  84.8 6.1 %collective-permute-start.20 = (f32[3,8,128]{2,1,0:T(8,128)S(1)}, f32[3,8,128]{2,1,0:T(8,128)S(1)}, u32[]{:S(2)}, u32[]{:S(2)}) collective-permute-start(f32[3,8,128]{2,1,0:T(8,128)S(1)} %get-tuple-element.52), channel_id=1, source_target_pairs={{0,32},{32,64},{64,96},{96,128},{128,160},{160,192},{192,224},{224... | collective-permute-start | bytes 36872 | tf_op jit(solution)/shard_map/ppermute | solution.py:22
  88.2 7.7 %collective-permute-start.21 = (f32[3,8,128]{2,1,0:T(8,128)S(1)}, f32[3,8,128]{2,1,0:T(8,128)S(1)}, u32[]{:S(2)}, u32[]{:S(2)}) collective-permute-start(f32[3,8,128]{2,1,0:T(8,128)S(1)} %get-tuple-element.53), channel_id=1, source_target_pairs={{0,480},{32,0},{64,32},{96,64},{128,96},{160,128},{192,160},{224,1... | collective-permute-start | bytes 36872 | tf_op jit(solution)/shard_map/ppermute | solution.py:22
  96.5 22.5 %all-to-all-start.1 = ((f32[16,8,128]{2,1,0:T(8,128)}), f32[16,8,128]{2,1,0:T(8,128)S(1)}, u32[]{:S(2)}, u32[]{:S(2)}) async-start(f32[16,8,128]{2,1,0:T(8,128)} %broadcast_in_dim.32), calls=%async_computation.1 | async-start | bytes 131072 | tf_op jit(solution)/shard_map/all_to_all | solution.py:275
  106.2 4.5 %collective-permute-start.22 = (f32[4,8,128]{2,1,0:T(8,128)S(1)}, f32[4,8,128]{2,1,0:T(8,128)S(1)}, u32[]{:S(2)}, u32[]{:S(2)}) collective-permute-start(f32[4,8,128]{2,1,0:T(8,128)S(1)} %get-tuple-element.57), channel_id=1, source_target_pairs={{0,1},{1,2},{2,3},{3,4},{4,5},{5,6},{6,7},{7,8},{8,9},{9,10},{10,1... | collective-permute-start | bytes 49160 | tf_op jit(solution)/shard_map/ppermute | solution.py:22
  106.3 4.5 %collective-permute-start.23 = (f32[4,8,128]{2,1,0:T(8,128)S(1)}, f32[4,8,128]{2,1,0:T(8,128)S(1)}, u32[]{:S(2)}, u32[]{:S(2)}) collective-permute-start(f32[4,8,128]{2,1,0:T(8,128)S(1)} %get-tuple-element.59), channel_id=1, source_target_pairs={{0,31},{1,0},{2,1},{3,2},{4,3},{5,4},{6,5},{7,6},{8,7},{9,8},{10,9... | collective-permute-start | bytes 49160 | tf_op jit(solution)/shard_map/ppermute | solution.py:22
